TPU v7x, 512 devices: a whole 4x4x16 slice. The times are simulated.
512 devices in a mesh: dp: 64 (over y_hi, z, core), tensor: 8 (over y_lo, x).
Axes of the slice: x: 4, y: 4 (y_hi: 2, y_lo: 2; y = y_hi * 2 + y_lo), z: 16, core: 2. Of those that a mesh axis runs over, the one named last changes fastest.
Arguments:
- tokens: bfloat16 [512, 8192], P('dp', 'tensor'), may hold values from -6 to 6
- gate_weight: bfloat16 [8192, 16384], P('tensor', 'dp'), may hold values from -0.125 to 0.125
- up_weight: bfloat16 [8192, 16384], P('tensor', 'dp'), may hold values from -0.125 to 0.125
- down_weight: bfloat16 [16384, 8192], P('dp', 'tensor'), may hold values from -0.09375 to 0.09375
- gate_mask: int32 [64, 128], P('tensor', 'dp'), may hold values 0 or 1
- up_mask: int32 [64, 128], P('tensor', 'dp'), may hold values 0 or 1
- down_mask: int32 [128, 64], P('dp', 'tensor'), may hold values 0 or 1
- probe_gate: bfloat16 [8192, 16384], P('tensor', 'dp'), may hold values from -1 to 1, as said below
- probe_up: bfloat16 [8192, 16384], P('tensor', 'dp'), may hold values from -1 to 1, as said below
- probe_down: bfloat16 [16384, 8192], P('dp', 'tensor'), may hold values from -1 to 1, as said below
Outputs:
- fisher_gate: bfloat16 [8192, 16384], P('tensor', 'dp')
- fisher_up: bfloat16 [8192, 16384], P('tensor', 'dp')
- fisher_down: bfloat16 [16384, 8192], P('dp', 'tensor')
Inputs may be any that keep to these rules, and one draw needn't show every extreme that they name: `probe_gate`: every entry is -1 or +1. `probe_up`: every entry is -1 or +1. `probe_down`: every entry is -1 or +1.
All inputs are finite; a program needn't handle non-finite values. No bound on the sum of `gate_mask` or of `up_mask` or of `down_mask` on one device may be relied on, other than what follows from the above.
Results may differ from a plain program's by a relative error of at most 0.008.
Values may be sent and summed in bfloat16 or wider, within the bound.
No kernel may reach another device: no remote copies, remote signals or barrier semaphores. Data moves between devices by JAX's collectives and lax.ppermute only.
A program may use at most 64 MiB of HBM per device.

v0:
```python
import jax
import jax.numpy as jnp
from jax import lax
from jax.sharding import PartitionSpec as P

D = 8192
HID = 16384


def widen(mask, rows, cols):
    grown = jnp.repeat(mask, rows // mask.shape[0], axis=0)
    grown = jnp.repeat(grown, cols // mask.shape[1], axis=1)
    return grown.astype(jnp.bfloat16)


def gating(pre, width):
    gate = pre[:, :width]
    up = pre[:, width : 2 * width]
    tangent_gate = pre[:, 2 * width : 3 * width]
    tangent_up = pre[:, 3 * width :]
    sig = jax.nn.sigmoid(gate)
    act = gate * sig
    slope = sig * (1.0 + gate * (1.0 - sig))
    hidden = (act * up).astype(jnp.bfloat16)
    tangent_hidden = (slope * tangent_gate * up + act * tangent_up).astype(jnp.bfloat16)
    return (hidden, tangent_hidden, up * slope, act)


def on_device(
    tokens,
    gate_weight,
    up_weight,
    down_weight,
    gate_mask,
    up_mask,
    down_mask,
    probe_gate,
    probe_up,
    probe_down,
):
    feat_rows = gate_weight.shape[0]
    width = gate_weight.shape[1]
    kept_gate = gate_weight * widen(gate_mask, feat_rows, width)
    kept_up = up_weight * widen(up_mask, feat_rows, width)
    kept_down = down_weight * widen(down_mask, width, feat_rows)
    stacked = jnp.concatenate([kept_gate, kept_up, probe_gate, probe_up], axis=1)
    gathered = lax.all_gather(tokens, "dp", axis=0, tiled=True)
    column_scale = jnp.concatenate(
        [jnp.ones((2 * width,), jnp.float32), jnp.full((2 * width,), D ** (-0.5), jnp.float32)]
    )
    partial_value = jnp.dot(gathered, stacked, preferred_element_type=jnp.float32) * column_scale
    pre = lax.psum(partial_value, "tensor")
    hidden, tangent_hidden, up_slope, act = gating(pre, width)
    term = jnp.dot(tangent_hidden, kept_down, preferred_element_type=jnp.float32)
    term = term + jnp.dot(hidden, probe_down, preferred_element_type=jnp.float32) * HID ** (-0.5)
    tangent_out = lax.psum(term, "dp").astype(jnp.bfloat16)
    back_part = lax.dot_general(
        tangent_out, kept_down, (((1,), (1,)), ((), ())), preferred_element_type=jnp.float32
    )
    back = lax.psum(back_part, "tensor")
    gate_bar = (back * up_slope).astype(jnp.bfloat16)
    up_bar = (back * act).astype(jnp.bfloat16)
    factor = gathered.shape[0] ** (-0.5)
    bars = jnp.concatenate([gate_bar, up_bar], axis=1)
    grads = lax.dot_general(
        gathered, bars, (((0,), (0,)), ((), ())), preferred_element_type=jnp.float32
    )
    grad_down = lax.dot_general(
        hidden, tangent_out, (((0,), (0,)), ((), ())), preferred_element_type=jnp.float32
    )
    fisher_gate = (probe_gate.astype(jnp.float32) * grads[:, :width] * factor).astype(jnp.bfloat16)
    fisher_up = (probe_up.astype(jnp.float32) * grads[:, width:] * factor).astype(jnp.bfloat16)
    fisher_down = (probe_down.astype(jnp.float32) * grad_down * factor).astype(jnp.bfloat16)
    return (fisher_gate, fisher_up, fisher_down)


def solution(mesh):
    return jax.shard_map(
        on_device,
        mesh=mesh,
        in_specs=(
            P("dp", "tensor"),
            P("tensor", "dp"),
            P("tensor", "dp"),
            P("dp", "tensor"),
            P("tensor", "dp"),
            P("tensor", "dp"),
            P("dp", "tensor"),
            P("tensor", "dp"),
            P("tensor", "dp"),
            P("dp", "tensor"),
        ),
        out_specs=(P("tensor", "dp"), P("tensor", "dp"), P("dp", "tensor")),
        check_vma=False,
    )
```

profile of v0, /device:TPU:1, one launch (start us, length us, event | category | flops | bytes accessed | tf_op | source)
XLA Modules:
  0.0 624.4 jit_solution(5196570887902048595)
XLA Ops:
  7.2 0.0 copy-start.10
  7.2 0.0 copy-start.9
  7.2 0.0 all-gather.2.cloned.1.call-start
  7.2 0.7 all-gather.2.cloned.1.call-update
  7.9 0.0 all-reduce.4.cloned.1.call-start
  8.0 0.7 convert_element_type.67
  8.6 0.1 copy.14
  8.7 0.7 convert_element_type.70
  9.4 0.1 copy.15
  9.6 2.9 broadcast_in_dim.19
  12.5 0.0 copy-start.7
  12.5 0.0 copy-start.8
  12.5 0.0 copy-start.12
  12.6 2.9 broadcast_in_dim.21
  15.5 0.0 copy-done.10
  15.6 0.0 copy-done.9
  15.6 0.2 bitcast_multiply_fusion.1
  15.7 141.1 %all-gather.2.cloned.1.call-done = bf16[512,1024]{1,0:T(8,128)(2,1)} async-done(((bf16[8,1024]{1,0:T(8,128)(2,1)}), bf16[512,1024]{1,0:T(8,128)(2,1)}) %all-gather.2.cloned.1.call-update) | async-done | bytes 1048592 | tf_op jit(solution)/shard_map/all_gather | solution.py:47
  156.8 0.0 copy-done.7
  156.8 0.0 copy-done.8
  156.8 0.0 copy-done.12
  156.8 4.3 multiply_bitcast_fusion
  161.1 0.0 copy-start.11
  161.1 0.0 copy-start.6
  161.1 0.0 all-reduce.4.cloned.1.call-update
  161.1 0.0 all-reduce.6.cloned.1.call-start
  161.2 0.6 copy-done.11
  161.8 88.3 %all-reduce.4.cloned.1.call-done = f32[512,1024]{0,1:T(8,128)} async-done(((f32[512,1024]{0,1:T(8,128)}), f32[512,1024]{0,1:T(8,128)}) %all-reduce.4.cloned.1.call-update) | async-done | bytes 2097168 | tf_op jit(solution)/shard_map/psum | solution.py:52
  250.0 1.4 multiply_convert_fusion.2
  251.4 0.3 broadcast_in_dim.23
  251.8 0.0 copy-start
  251.8 0.0 copy-done.6
  251.8 0.0 copy-start.2
  251.8 2.4 fusion.26
  254.2 0.0 copy-done
  254.2 0.0 copy-done.2
  254.2 0.5 multiply_add_fusion
  254.7 276.3 %all-reduce.7 = bf16[512,1024]{1,0:T(8,128)(2,1)S(1)} all-reduce(f32[512,1024]{1,0:T(8,128)S(1)} %multiply_add_fusion), channel_id=1, replica_groups=mesh['dp'=64,'tensor'=8] {'dp'}, use_global_device_ids=true, to_apply=%region_1.0 | all-reduce | flops 524288 | bytes 3145728 | tf_op jit(solution)/shard_map/psum | solution.py:56
  531.1 2.5 fusion.23
  533.5 0.0 all-reduce.6.cloned.1.call-update
  533.6 0.0 copy-start.1
  533.6 2.2 copy.13
  535.8 2.0 copy.17
  537.8 2.3 fusion.11
  540.1 0.0 copy-start.5
  540.1 72.9 %all-reduce.6.cloned.1.call-done = f32[512,256]{0,1:T(8,128)} async-done(((f32[512,256]{0,1:T(8,128)}), f32[512,256]{0,1:T(8,128)}) %all-reduce.6.cloned.1.call-update) | async-done | bytes 524304 | tf_op jit(solution)/shard_map/psum | solution.py:60
  613.0 0.0 copy-done.1
  613.0 1.3 multiply_convert_fusion.1
  614.3 0.0 copy-start.3
  614.3 0.0 copy-start.4
  614.3 0.0 copy-done.5
  614.3 0.7 convolution_bitcast_fusion
  615.0 0.3 copy-done.3
  615.3 0.2 copy-done.4
  615.5 0.4 fusion.13
  615.9 1.0 copy.18
  616.9 1.0 copy.19
  (4 shorter events, 0.1 us)
Async XLA Ops:
  7.2 8.4 %copy-start.10 = (bf16[1024,256]{1,0:T(8,128)(2,1)S(1)}, bf16[1024,256]{1,0:T(8,128)(2,1)}, u32[]{:S(2)}) copy-start(bf16[1024,256]{1,0:T(8,128)(2,1)} %param.11) | copy-start | bytes 1572868
  7.2 8.4 %copy-start.9 = (bf16[1024,256]{1,0:T(8,128)(2,1)S(1)}, bf16[1024,256]{1,0:T(8,128)(2,1)}, u32[]{:S(2)}) copy-start(bf16[1024,256]{1,0:T(8,128)(2,1)} %param.12) | copy-start | bytes 1572868
  7.2 149.6 %all-gather.2.cloned.1.call-start = ((), (), s32[]{:S(2)}) async-start(), calls=%async_computation | async-start | bytes 1064960 | tf_op jit(solution)/shard_map/all_gather | solution.py:47
  7.9 242.1 %all-reduce.4.cloned.1.call-start = ((), (), s32[]{:S(2)}) async-start(), calls=%async_computation.1 | async-start | bytes 4194304 | tf_op jit(solution)/shard_map/psum | solution.py:52
  12.5 144.3 %copy-start.7 = (bf16[1024,256]{1,0:T(8,128)(2,1)S(1)}, bf16[1024,256]{1,0:T(8,128)(2,1)}, u32[]{:S(2)}) copy-start(bf16[1024,256]{1,0:T(8,128)(2,1)} %param.17) | copy-start | bytes 1572868
  12.5 144.3 %copy-start.8 = (bf16[1024,256]{1,0:T(8,128)(2,1)S(1)}, bf16[1024,256]{1,0:T(8,128)(2,1)}, u32[]{:S(2)}) copy-start(bf16[1024,256]{1,0:T(8,128)(2,1)} %param.18) | copy-start | bytes 1572868
  12.5 144.3 %copy-start.12 = (f32[1024]{0:T(1024)S(1)}, f32[1024]{0:T(1024)}, u32[]{:S(2)}) copy-start(f32[1024]{0:T(1024)} %constant.1.clone.1) | copy-start | bytes 12292
  161.1 0.7 copy-start.11
  161.1 90.7 %copy-start.6 = (bf16[256,1024]{1,0:T(8,128)(2,1)S(1)}, bf16[256,1024]{1,0:T(8,128)(2,1)}, u32[]{:S(2)}) copy-start(bf16[256,1024]{1,0:T(8,128)(2,1)} %param.13) | copy-start | bytes 1572868
  161.1 451.8 %all-reduce.6.cloned.1.call-start = ((), (), s32[]{:S(2)}) async-start(), calls=%async_computation.2 | async-start | bytes 1048576 | tf_op jit(solution)/shard_map/psum | solution.py:60
  251.8 2.5 copy-start
  251.8 2.5 copy-start.2
  533.6 79.4 %copy-start.1 = (f32[512,1024]{0,1:T(8,128)S(1)}, f32[512,1024]{0,1:T(8,128)}, u32[]{:S(2)}) copy-start(f32[512,1024]{0,1:T(8,128)} %all-reduce.4.cloned.1.call-done) | copy-start | bytes 6291460
  540.1 74.2 %copy-start.5 = (bf16[512,1024]{1,0:T(8,128)(2,1)S(1)}, bf16[512,1024]{1,0:T(8,128)(2,1)}, u32[]{:S(2)}) copy-start(bf16[512,1024]{1,0:T(8,128)(2,1)} %all-gather.2.cloned.1.call-done) | copy-start | bytes 3145732
  614.3 1.0 copy-start.3
  614.3 1.2 copy-start.4
Sparse Core Ops, SparseCore 0:
  11.3 145.4 all-gather.1
  161.2 88.7 all-reduce.3
  533.7 79.2 all-reduce.5
where the time goes:
time: 629 us; the launch traced here: 624 us
  waiting for transfers between devices  303 us (48%)
  blocking collectives  276 us (44%)
  between operations  14 us (2%)
  local copies, waits for them, and re-layouts  13.9 us (2%)
  matrix products  12.6 us (2%)
    psum x1, blocking collectives, on_device(): tangent_out = lax.psum(term, 'dp').astype(jnp.bfloat16)  276 us
    all_gather x1, waiting for transfers between devices, on_device(): gathered = lax.all_gather(tokens, 'dp', axis=0, tiled=True)  141 us
    psum x1, waiting for transfers between devices, on_device(): pre = lax.psum(partial_value, 'tensor')  88.3 us
    psum x1, waiting for transfers between devices, on_device(): back = lax.psum(back_part, 'tensor')  72.9 us
  transfers between devices with their start and end apart: 3, of which 3 were waited for; matrix products, arithmetic and copies ran while one was open for 2% of the time, Pallas kernels for 0%

commit v1 on v0

v1 whole, which is shorter than its diff:
```python
import jax
import jax.numpy as jnp
from jax import lax
from jax.sharding import Mesh, PartitionSpec as P

D = 8192
HID = 16384
BF16 = jnp.bfloat16
F32 = jnp.float32
DP = ("yh", "z", "c")
TP = ("yl", "x")


def kept(weight, mask):
    rows, cols = weight.shape
    wide = jnp.repeat(mask.astype(BF16), cols // mask.shape[1], axis=1)
    blocks = weight.reshape(mask.shape[0], rows // mask.shape[0], cols)
    return (blocks * wide[:, None, :]).reshape(rows, cols)


def swap(x, axis):
    return lax.ppermute(x, axis, [(0, 1), (1, 0)])


def spread(x, axes, n):
    copies = jnp.broadcast_to(x[None], (n,) + x.shape)
    out = lax.all_to_all(copies, axes, 0, 0, tiled=True)
    return out.reshape((n * x.shape[0],) + x.shape[1:])


def scatter_sum(x, axes, n):
    pieces = x.reshape((n, x.shape[0] // n) + x.shape[1:])
    out = lax.all_to_all(pieces, axes, 0, 0, tiled=True)
    return jnp.sum(out.astype(F32), axis=0)


def gather_dp(x):
    x = spread(x, "z", 16)
    x = jnp.concatenate([x, swap(x, "yh")], axis=0)
    return jnp.concatenate([x, swap(x, "c")], axis=0)


def fold(x, axis):
    half = x.shape[0] // 2
    return x[:half] + swap(x[half:].astype(BF16), axis).astype(F32)


def on_device(
    tokens,
    gate_weight,
    up_weight,
    down_weight,
    gate_mask,
    up_mask,
    down_mask,
    probe_gate,
    probe_up,
    probe_down,
):
    width = gate_weight.shape[1]
    gathered = gather_dp(tokens)
    kept_gate = kept(gate_weight, gate_mask)
    kept_up = kept(up_weight, up_mask)
    kept_down = kept(down_weight, down_mask)
    stacked = jnp.concatenate([kept_gate, kept_up, probe_gate, probe_up], axis=1)
    partial = jnp.dot(gathered, stacked, preferred_element_type=F32).astype(BF16)
    pre = scatter_sum(partial, TP, 8)
    gate = pre[:, :width]
    up = pre[:, width : 2 * width]
    tangent_gate = pre[:, 2 * width : 3 * width] * D**-0.5
    tangent_up = pre[:, 3 * width :] * D**-0.5
    sig = jax.nn.sigmoid(gate)
    act = gate * sig
    slope = sig * (1.0 + gate * (1.0 - sig))
    hid = (act * up).astype(BF16)
    tan = (slope * tangent_gate * up + act * tangent_up).astype(BF16)
    both = spread(jnp.concatenate([tan, hid], axis=1), TP, 8)
    hidden = both[:, width:]
    down = jnp.concatenate([kept_down, probe_down * HID**-0.5], axis=0)
    term = jnp.dot(both, down, preferred_element_type=F32)
    term = fold(term, "c")
    term = fold(term, "yh")
    chunk = scatter_sum(term.astype(BF16), "z", 16).astype(BF16)
    tangent_out = gather_dp(chunk)
    back = lax.dot_general(
        tangent_out, kept_down, (((1,), (1,)), ((), ())), preferred_element_type=F32
    )
    back = scatter_sum(back.astype(BF16), TP, 8)
    bars = jnp.concatenate([(back * up * slope).astype(BF16), (back * act).astype(BF16)], axis=1)
    bars = spread(bars, TP, 8)
    factor = gathered.shape[0] ** -0.5
    contract = (((0,), (0,)), ((), ()))
    grads = lax.dot_general(gathered, bars, contract, preferred_element_type=F32)
    grad_down = lax.dot_general(hidden, tangent_out, contract, preferred_element_type=F32)
    fisher_gate = (probe_gate.astype(F32) * grads[:, :width] * factor).astype(BF16)
    fisher_up = (probe_up.astype(F32) * grads[:, width:] * factor).astype(BF16)
    fisher_down = (probe_down.astype(F32) * grad_down * factor).astype(BF16)
    return (fisher_gate, fisher_up, fisher_down)


def solution(mesh):
    fine = Mesh(mesh.devices.reshape(2, 16, 2, 2, 4), DP + TP)
    col = P(TP, DP)
    row = P(DP, TP)
    return jax.shard_map(
        on_device,
        mesh=fine,
        in_specs=(row, col, col, row, col, col, row, col, col, row),
        out_specs=(col, col, row),
        check_vma=False,
    )
```

time: 629 us -> 194 us (0.31)
  waiting for transfers between devices: 303 us -> 35 us
  blocking collectives: 276 us -> 103 us
  starting transfers between devices: 0.12 us -> 42.2 us
  between operations: 14 us -> 0.94 us
  local copies, waits for them, and re-layouts: 13.9 us -> 3.39 us
  matrix products: 12.6 us -> 5.56 us
    psum x1 -> x0, blocking collectives: 276 us -> none  [on_device(): tangent_out = lax.psum(term, 'dp').astype(jnp.bfloat16)]
    psum x2 -> x0, waiting for transfers between devices: 161 us -> none  [the longest x1 88.3 us: on_device(): pre = lax.psum(partial_value, 'tensor')]
    all_gather x1 -> x0, waiting for transfers between devices: 141 us -> none  [on_device(): gathered = lax.all_gather(tokens, 'dp', axis=0, tiled=True)]
    all_to_all x0 -> x5, blocking collectives: none -> 103 us  [the longest x2 52.8 us: spread(): out = lax.all_to_all(copies, axes, 0, 0, tiled=True)]
    ppermute x0 -> x6, starting transfers between devices: none -> 35.3 us  [swap(): return lax.ppermute(x, axis, [(0, 1), (1, 0)])]
    all_to_all x0 -> x2, waiting for transfers between devices: none -> 17.7 us  [spread(): out = lax.all_to_all(copies, axes, 0, 0, tiled=True)]
    ppermute x0 -> x6, waiting for transfers between devices: none -> 17.3 us  [swap(): return lax.ppermute(x, axis, [(0, 1), (1, 0)])]
    all_to_all x0 -> x2, starting transfers between devices: none -> 6.99 us  [spread(): out = lax.all_to_all(copies, axes, 0, 0, tiled=True)]
  transfers between devices with their start and end apart: 3 -> 8, of which waited for: 3 -> 7; matrix products, arithmetic and copies ran while one was open for 2% -> 2% of each run, Pallas kernels for 0% -> 0%
where the time goes in v1:
time: 194 us
  blocking collectives  103 us (53%)
  starting transfers between devices  42.2 us (22%)
  waiting for transfers between devices  35 us (18%)
  matrix products  5.56 us (3%)
  other arithmetic  3.54 us (2%)
  local copies, waits for them, and re-layouts  3.39 us (2%)
    all_to_all x2, blocking collectives, spread(): out = lax.all_to_all(copies, axes, 0, 0, tiled=True)  52.8 us
    all_to_all x3, blocking collectives, scatter_sum(): out = lax.all_to_all(pieces, axes, 0, 0, tiled=True)  50.2 us
    ppermute x6, starting transfers between devices, swap(): return lax.ppermute(x, axis, [(0, 1), (1, 0)])  35.3 us
    all_to_all x2, waiting for transfers between devices, spread(): out = lax.all_to_all(copies, axes, 0, 0, tiled=True)  17.7 us
    ppermute x6, waiting for transfers between devices, swap(): return lax.ppermute(x, axis, [(0, 1), (1, 0)])  17.3 us
    all_to_all x2, starting transfers between devices, spread(): out = lax.all_to_all(copies, axes, 0, 0, tiled=True)  6.99 us
  transfers between devices with their start and end apart: 8, of which 7 were waited for; matrix products, arithmetic and copies ran while one was open for 2% of the time, Pallas kernels for 0%

profile of v1, /device:TPU:1, one launch (start us, length us, event | category | flops | bytes accessed | tf_op | source)
XLA Modules:
  0.0 193.8 jit_solution(2917680285703363870)
XLA Ops:
  0.6 0.0 copy-start
  0.6 0.0 copy-start.1
  0.7 0.0 copy-start.4
  0.7 0.0 copy-start.6
  0.7 0.9 broadcast_in_dim.14
  1.6 28.7 %all_to_all.35 = bf16[16,8,1024]{2,1,0:T(8,128)(2,1)S(1)} all-to-all(bf16[16,8,1024]{2,1,0:T(8,128)(2,1)S(1)} %broadcast_in_dim.14), channel_id=1, replica_groups=mesh['yh'=2,'z'=16,'c'=2,'yl'=2,'x'=4] {'z'}, dimensions={0} | all-to-all | bytes 524288 | tf_op jit(solution)/shard_map/all_to_all | solution.py:27
  30.2 4.8 %collective-permute-start = (bf16[128,1024]{1,0:T(8,128)(2,1)S(1)}, bf16[128,1024]{1,0:T(8,128)(2,1)S(1)}, u32[]{:S(2)}, u32[]{:S(2)}) collective-permute-start(bf16[128,1024]{1,0:T(8,128)(2,1)S(1)} %bitcast.29), channel_id=1, source_target_pairs={{0,256},{256,0},{1,257},{257,1},{2,258},{258,2},{3,259},{259,3},{4... | collective-permute-start | bytes 786440 | tf_op jit(solution)/shard_map/ppermute | solution.py:22
  35.1 3.8 %collective-permute-done = bf16[128,1024]{1,0:T(8,128)(2,1)S(1)} collective-permute-done((bf16[128,1024]{1,0:T(8,128)(2,1)S(1)}, bf16[128,1024]{1,0:T(8,128)(2,1)S(1)}, u32[]{:S(2)}, u32[]{:S(2)}) %collective-permute-start) | collective-permute-done | bytes 262176 | tf_op jit(solution)/shard_map/ppermute | solution.py:22
  38.9 9.2 %collective-permute-start.1 = (bf16[256,1024]{1,0:T(8,128)(2,1)S(1)}, bf16[256,1024]{1,0:T(8,128)(2,1)S(1)}, u32[]{:S(2)}, u32[]{:S(2)}) collective-permute-start(bf16[256,1024]{1,0:T(8,128)(2,1)S(1)} %pad_maximum_fusion.2), channel_id=1, source_target_pairs={{0,8},{8,0},{1,9},{9,1},{2,10},{10,2},{3,11},{11,3},{4,12},{12,4},... | collective-permute-start | bytes 1572872 | tf_op jit(solution)/shard_map/ppermute | solution.py:22
  48.1 0.7 convert_element_type.65
  48.8 0.7 convert_element_type.66
  49.5 0.1 broadcast_bitcast_fusion.1
  49.6 0.1 broadcast_bitcast_fusion.2
  49.6 0.0 copy-done
  49.6 0.0 copy-done.1
  49.6 0.1 bitcast_multiply_fusion.1
  49.7 0.0 collective-permute-done.1
  49.7 0.0 copy-start.8
  49.8 0.0 copy-done.4
  49.8 0.0 copy-done.6
  49.8 1.3 fusion.8
  51.0 0.0 copy-done.8
  51.1 20.7 %all_to_all.36 = bf16[8,64,1024]{2,1,0:T(8,128)(2,1)S(1)} all-to-all(bf16[8,64,1024]{2,1,0:T(8,128)(2,1)S(1)} %bitcast.28), channel_id=1, replica_groups=mesh['yh'=2,'z'=16,'c'=2,'yl'=2,'x'=4] {'yl','x'}, dimensions={0} | all-to-all | bytes 2097152 | tf_op jit(solution)/shard_map/all_to_all | solution.py:33
  71.7 0.0 copy-start.11
  71.7 0.0 copy-start.2
  71.7 0.0 copy-start.3
  71.7 0.2 convert_reduce_fusion
  71.9 0.1 fusion.27
  72.0 0.8 broadcast_in_dim.17
  72.8 3.5 %all-to-all-start.2 = ((bf16[8,64,512]{2,1,0:T(8,128)(2,1)}), bf16[8,64,512]{2,1,0:T(8,128)(2,1)S(1)}, u32[]{:S(2)}, u32[]{:S(2)}) async-start(bf16[8,64,512]{2,1,0:T(8,128)(2,1)} %broadcast_in_dim.17), calls=%async_computation.2 | async-start | bytes 1048576 | tf_op jit(solution)/shard_map/all_to_all | solution.py:27
  76.3 0.0 copy-done.11
  76.3 0.1 broadcast_bitcast_fusion
  76.4 0.0 copy-done.2
  76.4 0.0 copy-done.3
  76.4 0.1 bitcast_multiply_fusion
  76.5 9.9 %all-to-all-done.2 = bf16[8,64,512]{2,1,0:T(8,128)(2,1)S(1)} async-done(((bf16[8,64,512]{2,1,0:T(8,128)(2,1)}), bf16[8,64,512]{2,1,0:T(8,128)(2,1)S(1)}, u32[]{:S(2)}, u32[]{:S(2)}) %all-to-all-start.2) | async-done | bytes 524320 | tf_op jit(solution)/shard_map/all_to_all | solution.py:27
  86.5 0.7 fusion.17
  87.2 0.1 slice.106
  87.3 2.7 %collective-permute-start.2 = (bf16[256,1024]{1,0:T(8,128)(2,1)S(1)}, bf16[256,1024]{1,0:T(8,128)(2,1)S(1)}, u32[]{:S(2)}, u32[]{:S(2)}) collective-permute-start(bf16[256,1024]{1,0:T(8,128)(2,1)S(1)} %slice.106), channel_id=1, source_target_pairs={{0,8},{8,0},{1,9},{9,1},{2,10},{10,2},{3,11},{11,3},{4,12},{12,4},... | collective-permute-start | bytes 1572872 | tf_op jit(solution)/shard_map/ppermute | solution.py:22
  90.0 1.5 collective-permute-done.2
  91.5 0.2 slice_add_fusion
  91.7 4.5 %collective-permute-start.3 = (bf16[128,1024]{1,0:T(8,128)(2,1)S(1)}, bf16[128,1024]{1,0:T(8,128)(2,1)S(1)}, u32[]{:S(2)}, u32[]{:S(2)}) collective-permute-start(bf16[128,1024]{1,0:T(8,128)(2,1)S(1)} %slice.107), channel_id=1, source_target_pairs={{0,256},{256,0},{1,257},{257,1},{2,258},{258,2},{3,259},{259,3},{4... | collective-permute-start | bytes 786440 | tf_op jit(solution)/shard_map/ppermute | solution.py:22
  96.3 6.4 %collective-permute-done.3 = bf16[128,1024]{1,0:T(8,128)(2,1)S(1)} collective-permute-done((bf16[128,1024]{1,0:T(8,128)(2,1)S(1)}, bf16[128,1024]{1,0:T(8,128)(2,1)S(1)}, u32[]{:S(2)}, u32[]{:S(2)}) %collective-permute-start.3) | collective-permute-done | bytes 262176 | tf_op jit(solution)/shard_map/ppermute | solution.py:22
  102.7 0.1 fusion.23
  102.7 19.7 %all_to_all.37 = bf16[16,8,1024]{2,1,0:T(8,128)(2,1)S(1)} all-to-all(bf16[16,8,1024]{2,1,0:T(8,128)(2,1)S(1)} %fusion.23), channel_id=1, replica_groups=mesh['yh'=2,'z'=16,'c'=2,'yl'=2,'x'=4] {'z'}, dimensions={0} | all-to-all | bytes 524288 | tf_op jit(solution)/shard_map/all_to_all | solution.py:33
  122.5 24.2 %all_to_all.38 = bf16[16,8,1024]{2,1,0:T(8,128)(2,1)S(1)} all-to-all(bf16[16,8,1024]{2,1,0:T(8,128)(2,1)S(1)} %broadcast_in_dim.38), channel_id=1, replica_groups=mesh['yh'=2,'z'=16,'c'=2,'yl'=2,'x'=4] {'z'}, dimensions={0} | all-to-all | bytes 524288 | tf_op jit(solution)/shard_map/all_to_all | solution.py:27
  146.7 4.5 %collective-permute-start.4 = (bf16[128,1024]{1,0:T(8,128)(2,1)S(1)}, bf16[128,1024]{1,0:T(8,128)(2,1)S(1)}, u32[]{:S(2)}, u32[]{:S(2)}) collective-permute-start(bf16[128,1024]{1,0:T(8,128)(2,1)S(1)} %bitcast.33), channel_id=1, source_target_pairs={{0,256},{256,0},{1,257},{257,1},{2,258},{258,2},{3,259},{259,3},{4... | collective-permute-start | bytes 786440 | tf_op jit(solution)/shard_map/ppermute | solution.py:22
  151.2 4.1 %collective-permute-done.4 = bf16[128,1024]{1,0:T(8,128)(2,1)S(1)} collective-permute-done((bf16[128,1024]{1,0:T(8,128)(2,1)S(1)}, bf16[128,1024]{1,0:T(8,128)(2,1)S(1)}, u32[]{:S(2)}, u32[]{:S(2)}) %collective-permute-start.4) | collective-permute-done | bytes 262176 | tf_op jit(solution)/shard_map/ppermute | solution.py:22
  155.3 9.4 %collective-permute-start.5 = (bf16[256,1024]{1,0:T(8,128)(2,1)S(1)}, bf16[256,1024]{1,0:T(8,128)(2,1)S(1)}, u32[]{:S(2)}, u32[]{:S(2)}) collective-permute-start(bf16[256,1024]{1,0:T(8,128)(2,1)S(1)} %pad_maximum_fusion.3), channel_id=1, source_target_pairs={{0,8},{8,0},{1,9},{9,1},{2,10},{10,2},{3,11},{11,3},{4,12},{12,4},... | collective-permute-start | bytes 1572872 | tf_op jit(solution)/shard_map/ppermute | solution.py:22
  164.8 1.5 collective-permute-done.5
  166.3 0.5 convolution_convert_fusion
  166.8 9.8 %all_to_all.39 = bf16[8,64,256]{2,1,0:T(8,128)(2,1)S(1)} all-to-all(bf16[8,64,256]{2,1,0:T(8,128)(2,1)S(1)} %bitcast.38), channel_id=1, replica_groups=mesh['yh'=2,'z'=16,'c'=2,'yl'=2,'x'=4] {'yl','x'}, dimensions={0} | all-to-all | bytes 524288 | tf_op jit(solution)/shard_map/all_to_all | solution.py:33
  176.6 0.0 copy-done.10
  176.6 0.1 multiply_convert_fusion.1
  176.7 0.8 broadcast_in_dim.39
  177.6 3.5 %all-to-all-start.6 = ((bf16[8,64,512]{2,1,0:T(8,128)(2,1)}), bf16[8,64,512]{2,1,0:T(8,128)(2,1)S(1)}, u32[]{:S(2)}, u32[]{:S(2)}) async-start(bf16[8,64,512]{2,1,0:T(8,128)(2,1)} %broadcast_in_dim.39), calls=%async_computation.6 | async-start | bytes 1048576 | tf_op jit(solution)/shard_map/all_to_all | solution.py:27
  181.1 0.0 copy-start.9
  181.1 2.4 %fusion.12 = bf16[256,1024]{1,0:T(8,128)(2,1)} fusion(bf16[256,1024]{1,0:T(8,128)(2,1)S(1)} %copy-done.3, bf16[256,1024]{1,0:T(8,128)(2,1)} %copy-done.10, bf16[128,1024]{1,0:T(8,128)(2,1)S(1)} %collective-permute-done.4, bf16[128,1024]{1,0:T(8,128)(2,1)S(1)} %bitcast.36, bf16[512,512]{1,0:T(8,128)(2,1)S(1)} %bitcast.27), kind=kOutput, calls=%fused_computation.12 | convolution fusion | flops 272629760 | bytes 2359296 | tf_op jit(solution)/shard_map/dot_general | solution.py:94
  183.4 7.8 %all-to-all-done.6 = bf16[8,64,512]{2,1,0:T(8,128)(2,1)S(1)} async-done(((bf16[8,64,512]{2,1,0:T(8,128)(2,1)}), bf16[8,64,512]{2,1,0:T(8,128)(2,1)S(1)}, u32[]{:S(2)}, u32[]{:S(2)}) %all-to-all-start.6) | async-done | bytes 524320 | tf_op jit(solution)/shard_map/all_to_all | solution.py:27
  191.2 0.0 copy-done.9
  191.2 0.7 fusion.22
  192.0 0.3 copy-done.5
  192.3 0.2 copy-done.7
  192.4 1.3 fusion.14
  (13 shorter events, 0.2 us)
Async XLA Ops:
  0.6 49.0 %copy-start = (bf16[1024,256]{1,0:T(8,128)(2,1)S(1)}, bf16[1024,256]{1,0:T(8,128)(2,1)}, u32[]{:S(2)}) copy-start(bf16[1024,256]{1,0:T(8,128)(2,1)} %param.12) | copy-start | bytes 1572868
  0.6 49.0 %copy-start.1 = (bf16[1024,256]{1,0:T(8,128)(2,1)S(1)}, bf16[1024,256]{1,0:T(8,128)(2,1)}, u32[]{:S(2)}) copy-start(bf16[1024,256]{1,0:T(8,128)(2,1)} %param.11) | copy-start | bytes 1572868
  0.7 49.1 %copy-start.4 = (bf16[1024,256]{1,0:T(8,128)(2,1)S(1)}, bf16[1024,256]{1,0:T(8,128)(2,1)}, u32[]{:S(2)}) copy-start(bf16[1024,256]{1,0:T(8,128)(2,1)} %param.18) | copy-start | bytes 1572868
  0.7 49.1 %copy-start.6 = (bf16[1024,256]{1,0:T(8,128)(2,1)S(1)}, bf16[1024,256]{1,0:T(8,128)(2,1)}, u32[]{:S(2)}) copy-start(bf16[1024,256]{1,0:T(8,128)(2,1)} %param.17) | copy-start | bytes 1572868
  30.2 8.6 %collective-permute-start = (bf16[128,1024]{1,0:T(8,128)(2,1)S(1)}, bf16[128,1024]{1,0:T(8,128)(2,1)S(1)}, u32[]{:S(2)}, u32[]{:S(2)}) collective-permute-start(bf16[128,1024]{1,0:T(8,128)(2,1)S(1)} %bitcast.29), channel_id=1, source_target_pairs={{0,256},{256,0},{1,257},{257,1},{2,258},{258,2},{3,259},{259,3},{4... | collective-permute-start | bytes 786440 | tf_op jit(solution)/shard_map/ppermute | solution.py:22
  38.9 10.8 %collective-permute-start.1 = (bf16[256,1024]{1,0:T(8,128)(2,1)S(1)}, bf16[256,1024]{1,0:T(8,128)(2,1)S(1)}, u32[]{:S(2)}, u32[]{:S(2)}) collective-permute-start(bf16[256,1024]{1,0:T(8,128)(2,1)S(1)} %pad_maximum_fusion.2), channel_id=1, source_target_pairs={{0,8},{8,0},{1,9},{9,1},{2,10},{10,2},{3,11},{11,3},{4,12},{12,4},... | collective-permute-start | bytes 1572872 | tf_op jit(solution)/shard_map/ppermute | solution.py:22
  49.7 1.3 copy-start.8
  71.7 4.6 %copy-start.11 = (s32[2,8]{1,0:T(2,128)S(1)}, s32[2,8]{1,0:T(2,128)}, u32[]{:S(2)}) copy-start(s32[2,8]{1,0:T(2,128)} %param.16) | copy-start | bytes 196
  71.7 4.7 %copy-start.2 = (bf16[256,1024]{1,0:T(8,128)(2,1)S(1)}, bf16[256,1024]{1,0:T(8,128)(2,1)}, u32[]{:S(2)}) copy-start(bf16[256,1024]{1,0:T(8,128)(2,1)} %param.13) | copy-start | bytes 1572868
  71.7 4.7 %copy-start.3 = (bf16[256,1024]{1,0:T(8,128)(2,1)S(1)}, bf16[256,1024]{1,0:T(8,128)(2,1)}, u32[]{:S(2)}) copy-start(bf16[256,1024]{1,0:T(8,128)(2,1)} %param.19) | copy-start | bytes 1572868
  72.8 13.7 %all-to-all-start.2 = ((bf16[8,64,512]{2,1,0:T(8,128)(2,1)}), bf16[8,64,512]{2,1,0:T(8,128)(2,1)S(1)}, u32[]{:S(2)}, u32[]{:S(2)}) async-start(bf16[8,64,512]{2,1,0:T(8,128)(2,1)} %broadcast_in_dim.17), calls=%async_computation.2 | async-start | bytes 1048576 | tf_op jit(solution)/shard_map/all_to_all | solution.py:27
  87.3 4.2 %collective-permute-start.2 = (bf16[256,1024]{1,0:T(8,128)(2,1)S(1)}, bf16[256,1024]{1,0:T(8,128)(2,1)S(1)}, u32[]{:S(2)}, u32[]{:S(2)}) collective-permute-start(bf16[256,1024]{1,0:T(8,128)(2,1)S(1)} %slice.106), channel_id=1, source_target_pairs={{0,8},{8,0},{1,9},{9,1},{2,10},{10,2},{3,11},{11,3},{4,12},{12,4},... | collective-permute-start | bytes 1572872 | tf_op jit(solution)/shard_map/ppermute | solution.py:22
  91.7 10.9 %collective-permute-start.3 = (bf16[128,1024]{1,0:T(8,128)(2,1)S(1)}, bf16[128,1024]{1,0:T(8,128)(2,1)S(1)}, u32[]{:S(2)}, u32[]{:S(2)}) collective-permute-start(bf16[128,1024]{1,0:T(8,128)(2,1)S(1)} %slice.107), channel_id=1, source_target_pairs={{0,256},{256,0},{1,257},{257,1},{2,258},{258,2},{3,259},{259,3},{4... | collective-permute-start | bytes 786440 | tf_op jit(solution)/shard_map/ppermute | solution.py:22
  146.7 8.6 %collective-permute-start.4 = (bf16[128,1024]{1,0:T(8,128)(2,1)S(1)}, bf16[128,1024]{1,0:T(8,128)(2,1)S(1)}, u32[]{:S(2)}, u32[]{:S(2)}) collective-permute-start(bf16[128,1024]{1,0:T(8,128)(2,1)S(1)} %bitcast.33), channel_id=1, source_target_pairs={{0,256},{256,0},{1,257},{257,1},{2,258},{258,2},{3,259},{259,3},{4... | collective-permute-start | bytes 786440 | tf_op jit(solution)/shard_map/ppermute | solution.py:22
  155.3 11.0 %collective-permute-start.5 = (bf16[256,1024]{1,0:T(8,128)(2,1)S(1)}, bf16[256,1024]{1,0:T(8,128)(2,1)S(1)}, u32[]{:S(2)}, u32[]{:S(2)}) collective-permute-start(bf16[256,1024]{1,0:T(8,128)(2,1)S(1)} %pad_maximum_fusion.3), channel_id=1, source_target_pairs={{0,8},{8,0},{1,9},{9,1},{2,10},{10,2},{3,11},{11,3},{4,12},{12,4},... | collective-permute-start | bytes 1572872 | tf_op jit(solution)/shard_map/ppermute | solution.py:22
  166.3 10.3 %copy-start.10 = (bf16[256,1024]{1,0:T(8,128)(2,1)}, bf16[256,1024]{1,0:T(8,128)(2,1)S(1)}, u32[]{:S(2)}) copy-start(bf16[256,1024]{1,0:T(8,128)(2,1)S(1)} %collective-permute-done.5) | copy-start | bytes 1572868
  177.6 13.7 %all-to-all-start.6 = ((bf16[8,64,512]{2,1,0:T(8,128)(2,1)}), bf16[8,64,512]{2,1,0:T(8,128)(2,1)S(1)}, u32[]{:S(2)}, u32[]{:S(2)}) async-start(bf16[8,64,512]{2,1,0:T(8,128)(2,1)} %broadcast_in_dim.39), calls=%async_computation.6 | async-start | bytes 1048576 | tf_op jit(solution)/shard_map/all_to_all | solution.py:27
  181.1 10.2 %copy-start.9 = (bf16[256,1024]{1,0:T(8,128)(2,1)S(1)}, bf16[256,1024]{1,0:T(8,128)(2,1)}, u32[]{:S(2)}) copy-start(bf16[256,1024]{1,0:T(8,128)(2,1)} %copy-done.8) | copy-start | bytes 1572868
  191.2 1.0 copy-start.5
  191.2 1.2 copy-start.7

commit v2 on v1

v2 whole, which is shorter than its diff:
```python
import jax
import jax.numpy as jnp
from jax import lax
from jax.sharding import Mesh, PartitionSpec as P

D = 8192
HID = 16384
BF16 = jnp.bfloat16
F32 = jnp.float32
DP = ("yh", "zh", "zl", "c")
TP = ("yl", "x")


def kept(weight, mask):
    rows, cols = weight.shape
    wide = jnp.repeat(mask.astype(BF16), cols // mask.shape[1], axis=1)
    blocks = weight.reshape(mask.shape[0], rows // mask.shape[0], cols)
    return (blocks * wide[:, None, :]).reshape(rows, cols)


def swap(x, axis):
    return lax.ppermute(x, axis, [(0, 1), (1, 0)])


def exchange(pieces, axes):
    return lax.all_to_all(pieces, axes, 0, 0, tiled=True)


def copies(x, n):
    return jnp.broadcast_to(x[None], (n,) + x.shape)


def total(pieces):
    return jnp.sum(pieces.astype(F32), axis=0)


def own_first(x, axis):
    return jnp.where(lax.axis_index(axis) == 0, x, x[::-1])


def split_rows(x, own):
    first = x[:own].reshape((8, own // 8) + x.shape[1:])
    rest = x[own:].reshape((8, -1) + x.shape[1:])
    return jnp.concatenate([first, rest], axis=1)


def join_rows(x, own):
    first = x[:, : own // 8].reshape((own,) + x.shape[2:])
    rest = x[:, own // 8 :].reshape((-1,) + x.shape[2:])
    return jnp.concatenate([first, rest], axis=0)


def on_device(
    tokens,
    gate_weight,
    up_weight,
    down_weight,
    gate_mask,
    up_mask,
    down_mask,
    probe_gate,
    probe_up,
    probe_down,
):
    width = gate_weight.shape[1]
    feats = tokens.shape[1]
    kept_gate = kept(gate_weight, gate_mask)
    kept_up = kept(up_weight, up_mask)
    kept_down = kept(down_weight, down_mask)
    stacked = jnp.concatenate([kept_gate, kept_up, probe_gate, probe_up], axis=1)
    down = jnp.concatenate([kept_down, probe_down * HID**-0.5], axis=0)

    tok0 = exchange(copies(tokens, 16), ("zl", "zh")).reshape(128, feats)
    own = tok0.shape[0]
    tok1 = swap(tok0, "yh")
    pre0 = jnp.dot(tok0, stacked, preferred_element_type=F32).astype(BF16)
    pre0 = total(exchange(pre0.reshape(8, own // 8, 4 * width), TP))
    tok1, pre0 = lax.optimization_barrier((tok1, pre0))
    tok01 = jnp.concatenate([tok0, tok1], axis=0)
    tok23 = swap(tok01, "c")
    rest = jnp.concatenate([tok1, tok23], axis=0)
    pre1 = jnp.dot(rest, stacked, preferred_element_type=F32).astype(BF16)
    pre1 = total(exchange(pre1.reshape(8, -1, 4 * width), TP))
    gathered = jnp.concatenate([tok01, tok23], axis=0)
    shuffled = split_rows(gathered, own).reshape(gathered.shape)

    pre = jnp.concatenate([pre0, pre1], axis=0)
    gate = pre[:, :width]
    up = pre[:, width : 2 * width]
    tangent_gate = pre[:, 2 * width : 3 * width] * D**-0.5
    tangent_up = pre[:, 3 * width :] * D**-0.5
    sig = jax.nn.sigmoid(gate)
    act = gate * sig
    slope = sig * (1.0 + gate * (1.0 - sig))
    hid = (act * up).astype(BF16)
    tan = (slope * tangent_gate * up + act * tangent_up).astype(BF16)
    both = exchange(copies(jnp.concatenate([tan, hid], axis=1), 8), TP)
    hidden = both[:, :, width:].reshape(-1, width)
    both = join_rows(both, own)

    half = both.shape[0] // 2
    away = jnp.dot(both[half:], down, preferred_element_type=F32).astype(BF16)
    away = swap(away, "c")
    term = jnp.dot(both[:half], down, preferred_element_type=F32) + away.astype(F32)
    term = own_first(term.astype(BF16).reshape(2, 4, 32, feats), "yh")
    term = exchange(term.transpose(1, 0, 2, 3).reshape(8, 32, feats), ("zl", "yh"))
    chunk = total(term).astype(BF16)
    chunk = total(exchange(copies(chunk, 4), "zh")).astype(BF16)
    out01 = exchange(copies(chunk, 8), ("zl", "yh")).reshape(4, 2, 32, feats)
    out01 = own_first(out01.transpose(1, 0, 2, 3), "yh").reshape(half, feats)
    out23 = swap(out01, "c")
    tangent_out = jnp.concatenate([out01, out23], axis=0)

    back = lax.dot_general(
        tangent_out, kept_down, (((1,), (1,)), ((), ())), preferred_element_type=F32
    )
    back = total(exchange(split_rows(back.astype(BF16), own), TP))
    bars = jnp.concatenate([(back * up * slope).astype(BF16), (back * act).astype(BF16)], axis=1)
    bars = exchange(copies(bars, 8), TP).reshape(gathered.shape[0], 2 * width)
    factor = gathered.shape[0] ** -0.5
    contract = (((0,), (0,)), ((), ()))
    out_shuffled = split_rows(tangent_out, own).reshape(gathered.shape)
    grad_down = lax.dot_general(hidden, out_shuffled, contract, preferred_element_type=F32)
    grads = lax.dot_general(shuffled, bars, contract, preferred_element_type=F32)
    fisher_gate = (probe_gate.astype(F32) * grads[:, :width] * factor).astype(BF16)
    fisher_up = (probe_up.astype(F32) * grads[:, width:] * factor).astype(BF16)
    fisher_down = (probe_down.astype(F32) * grad_down * factor).astype(BF16)
    return (fisher_gate, fisher_up, fisher_down)


def solution(mesh):
    fine = Mesh(mesh.devices.reshape(2, 4, 4, 2, 2, 4), DP + TP)
    col = P(TP, DP)
    row = P(DP, TP)
    return jax.shard_map(
        on_device,
        mesh=fine,
        in_specs=(row, col, col, row, col, col, row, col, col, row),
        out_specs=(col, col, row),
        check_vma=False,
    )
```

time: 194 us -> 195 us (level)
  blocking collectives: 103 us -> 90 us
  waiting for transfers between devices: 35 us -> 40.7 us
  starting transfers between devices: 42.2 us -> 46.1 us
    all_to_all x2 -> x4, starting transfers between devices: 6.99 us -> 27.8 us  [exchange(): return lax.all_to_all(pieces, axes, 0, 0, tiled=True)]
    ppermute x6 -> x4, starting transfers between devices: 35.3 us -> 18.3 us  [swap(): return lax.ppermute(x, axis, [(0, 1), (1, 0)])]
    all_to_all x2 -> x4, waiting for transfers between devices: 17.7 us -> 31.5 us  [exchange(): return lax.all_to_all(pieces, axes, 0, 0, tiled=True)]
    all_to_all x5, blocking collectives: 103 us -> 90 us  [exchange(): return lax.all_to_all(pieces, axes, 0, 0, tiled=True)]
    ppermute x6 -> x4, waiting for transfers between devices: 17.3 us -> 9.12 us  [swap(): return lax.ppermute(x, axis, [(0, 1), (1, 0)])]
    dot_general x4 -> x6, matrix products: 5.08 us -> 6.94 us  [the longest x1 2.37 us: on_device(): lax.dot_general(hidden, out_shuffled, contract, preferred_element_type=F32)]
  transfers between devices with their start and end apart: 8 -> 8, of which waited for: 7 -> 8; matrix products, arithmetic and copies ran while one was open for 2% -> 3% of each run, Pallas kernels for 0% -> 0%
where the time goes in v2:
time: 195 us; the launch traced here: 194 us
  blocking collectives  90 us (46%)
  starting transfers between devices  46.1 us (24%)
  waiting for transfers between devices  40.7 us (21%)
  matrix products  7.42 us (4%)
  other arithmetic  4.85 us (2%)
  local copies, waits for them, and re-layouts  4.18 us (2%)
    all_to_all x5, blocking collectives, exchange(): return lax.all_to_all(pieces, axes, 0, 0, tiled=True)  90 us
    all_to_all x4, waiting for transfers between devices, exchange(): return lax.all_to_all(pieces, axes, 0, 0, tiled=True)  31.5 us
    all_to_all x4, starting transfers between devices, exchange(): return lax.all_to_all(pieces, axes, 0, 0, tiled=True)  27.8 us
    ppermute x4, starting transfers between devices, swap(): return lax.ppermute(x, axis, [(0, 1), (1, 0)])  18.3 us
    ppermute x4, waiting for transfers between devices, swap(): return lax.ppermute(x, axis, [(0, 1), (1, 0)])  9.12 us
  transfers between devices with their start and end apart: 8, of which 8 were waited for; matrix products, arithmetic and copies ran while one was open for 3% of the time, Pallas kernels for 0%

profile of v2, /device:TPU:1, one launch (start us, length us, event | category | flops | bytes accessed | tf_op | source)
XLA Modules:
  0.0 194.1 jit_solution(17513875077879433674)
XLA Ops:
  0.6 0.0 copy-start.2
  0.6 0.0 copy-start.4
  0.7 1.5 broadcast_in_dim.16
  2.2 15.7 %all-to-all-start = ((bf16[16,8,1024]{2,1,0:T(8,128)(2,1)}), bf16[16,8,1024]{2,1,0:T(8,128)(2,1)S(1)}, u32[]{:S(2)}, u32[]{:S(2)}) async-start(bf16[16,8,1024]{2,1,0:T(8,128)(2,1)} %broadcast_in_dim.16), calls=%async_computation | async-start | bytes 524288 | tf_op jit(solution)/shard_map/all_to_all | solution.py:26
  17.9 0.7 convert_element_type.74
  18.6 0.7 convert_element_type.75
  19.3 0.1 broadcast_bitcast_fusion.1
  19.4 0.1 broadcast_bitcast_fusion.2
  19.4 1.3 bitcast_multiply_fusion.1
  20.7 12.5 %all-to-all-done = bf16[16,8,1024]{2,1,0:T(8,128)(2,1)S(1)} async-done(((bf16[16,8,1024]{2,1,0:T(8,128)(2,1)}), bf16[16,8,1024]{2,1,0:T(8,128)(2,1)S(1)}, u32[]{:S(2)}, u32[]{:S(2)}) %all-to-all-start) | async-done | bytes 262176 | tf_op jit(solution)/shard_map/all_to_all | solution.py:26
  33.3 0.0 copy-done.2
  33.3 0.0 copy-done.4
  33.3 1.2 convolution_convert_fusion.2
  34.4 5.0 %all-to-all-start.1 = ((bf16[8,16,1024]{2,1,0:T(8,128)(2,1)}), bf16[8,16,1024]{2,1,0:T(8,128)(2,1)S(1)}, u32[]{:S(2)}, u32[]{:S(2)}) async-start(bf16[8,16,1024]{2,1,0:T(8,128)(2,1)} %bitcast.7), calls=%async_computation.1 | async-start | bytes 524288 | tf_op jit(solution)/shard_map/all_to_all | solution.py:26
  39.5 4.5 %collective-permute-start = (bf16[128,1024]{1,0:T(8,128)(2,1)S(1)}, bf16[128,1024]{1,0:T(8,128)(2,1)S(1)}, u32[]{:S(2)}, u32[]{:S(2)}) collective-permute-start(bf16[128,1024]{1,0:T(8,128)(2,1)S(1)} %bitcast.56), channel_id=1, source_target_pairs={{0,256},{256,0},{1,257},{257,1},{2,258},{258,2},{3,259},{259,3},{4... | collective-permute-start | bytes 786440 | tf_op jit(solution)/shard_map/ppermute | solution.py:22
  44.0 1.6 all-to-all-done.1
  45.6 4.4 %collective-permute-done = bf16[128,1024]{1,0:T(8,128)(2,1)S(1)} collective-permute-done((bf16[128,1024]{1,0:T(8,128)(2,1)S(1)}, bf16[128,1024]{1,0:T(8,128)(2,1)S(1)}, u32[]{:S(2)}, u32[]{:S(2)}) %collective-permute-start) | collective-permute-done | bytes 262176 | tf_op jit(solution)/shard_map/ppermute | solution.py:22
  50.1 5.5 %collective-permute-start.1 = (bf16[256,1024]{1,0:T(8,128)(2,1)S(1)}, bf16[256,1024]{1,0:T(8,128)(2,1)S(1)}, u32[]{:S(2)}, u32[]{:S(2)}) collective-permute-start(bf16[256,1024]{1,0:T(8,128)(2,1)S(1)} %pad_maximum_fusion.7), channel_id=1, source_target_pairs={{0,8},{8,0},{1,9},{9,1},{2,10},{10,2},{3,11},{11,3},{4,12},{12,4},... | collective-permute-start | bytes 1572872 | tf_op jit(solution)/shard_map/ppermute | solution.py:22
  55.7 1.5 collective-permute-done.1
  57.2 0.0 copy-start.6
  57.2 1.0 convolution_convert_fusion
  58.2 0.0 copy-done.6
  58.2 16.5 %all_to_all.45 = bf16[8,48,1024]{2,1,0:T(8,128)(2,1)S(1)} all-to-all(bf16[8,48,1024]{2,1,0:T(8,128)(2,1)S(1)} %bitcast.60), channel_id=1, replica_groups=mesh['yh'=2,'zh'=4,'zl'=4,'c'=2,'yl'=2,'x'=4] {'yl','x'}, dimensions={0} | all-to-all | bytes 1572864 | tf_op jit(solution)/shard_map/all_to_all | solution.py:26
  74.7 0.0 copy-start.8
  74.7 0.0 copy-start
  74.8 0.0 copy-start.1
  74.8 0.1 convert_reduce_fusion
  74.9 0.1 fusion.27
  75.0 0.8 broadcast_in_dim.19
  75.8 3.5 %all-to-all-start.3 = ((bf16[8,64,512]{2,1,0:T(8,128)(2,1)}), bf16[8,64,512]{2,1,0:T(8,128)(2,1)S(1)}, u32[]{:S(2)}, u32[]{:S(2)}) async-start(bf16[8,64,512]{2,1,0:T(8,128)(2,1)} %broadcast_in_dim.19), calls=%async_computation.3 | async-start | bytes 1048576 | tf_op jit(solution)/shard_map/all_to_all | solution.py:26
  79.3 0.0 copy-done.8
  79.3 0.1 broadcast_bitcast_fusion
  79.4 0.0 copy-done
  79.4 0.0 copy-done.1
  79.4 0.1 bitcast_multiply_fusion
  79.5 9.7 %all-to-all-done.3 = bf16[8,64,512]{2,1,0:T(8,128)(2,1)S(1)} async-done(((bf16[8,64,512]{2,1,0:T(8,128)(2,1)}), bf16[8,64,512]{2,1,0:T(8,128)(2,1)S(1)}, u32[]{:S(2)}, u32[]{:S(2)}) %all-to-all-start.3) | async-done | bytes 524320 | tf_op jit(solution)/shard_map/all_to_all | solution.py:26
  89.3 1.2 convolution_convert_fusion.1
  90.5 3.0 %collective-permute-start.2 = (bf16[256,1024]{1,0:T(8,128)(2,1)}, bf16[256,1024]{1,0:T(8,128)(2,1)S(1)}, u32[]{:S(2)}, u32[]{:S(2)}) collective-permute-start(bf16[256,1024]{1,0:T(8,128)(2,1)} %convolution_convert_fusion.1), channel_id=1, source_target_pairs={{0,8},{8,0},{1,9},{9,1},{2,10},{10,2},{3,11},{11,3},{4,12},{12,4},... | collective-permute-start | bytes 1572872 | tf_op jit(solution)/shard_map/ppermute | solution.py:22
  93.5 1.7 collective-permute-done.2
  95.2 0.4 add_convert_fusion
  95.7 0.1 reverse_select_fusion.1
  95.8 22.3 %all_to_all.46 = bf16[8,32,1024]{2,1,0:T(8,128)(2,1)S(1)} all-to-all(bf16[8,32,1024]{2,1,0:T(8,128)(2,1)S(1)} %bitcast.55), channel_id=1, replica_groups=mesh['yh'=2,'zh'=4,'zl'=4,'c'=2,'yl'=2,'x'=4] {'zl','yh'}, dimensions={0} | all-to-all | bytes 1048576 | tf_op jit(solution)/shard_map/all_to_all | solution.py:26
  118.1 0.1 reduce_sum.53
  118.3 19.3 %all_to_all.47 = bf16[4,32,1024]{2,1,0:T(8,128)(2,1)S(1)} all-to-all(bf16[4,32,1024]{2,1,0:T(8,128)(2,1)S(1)} %broadcast_in_dim.21), channel_id=1, replica_groups=mesh['yh'=2,'zh'=4,'zl'=4,'c'=2,'yl'=2,'x'=4] {'zh'}, dimensions={0} | all-to-all | bytes 524288 | tf_op jit(solution)/shard_map/all_to_all | solution.py:26
  137.6 0.1 broadcast_in_dim.22
  137.7 22.0 %all_to_all.48 = bf16[8,32,1024]{2,1,0:T(8,128)(2,1)S(1)} all-to-all(bf16[8,32,1024]{2,1,0:T(8,128)(2,1)S(1)} %broadcast_in_dim.22), channel_id=1, replica_groups=mesh['yh'=2,'zh'=4,'zl'=4,'c'=2,'yl'=2,'x'=4] {'zl','yh'}, dimensions={0} | all-to-all | bytes 1048576 | tf_op jit(solution)/shard_map/all_to_all | solution.py:26
  159.6 0.1 reverse_select_fusion
  159.8 5.3 %collective-permute-start.3 = (bf16[256,1024]{1,0:T(8,128)(2,1)S(1)}, bf16[256,1024]{1,0:T(8,128)(2,1)S(1)}, u32[]{:S(2)}, u32[]{:S(2)}) collective-permute-start(bf16[256,1024]{1,0:T(8,128)(2,1)S(1)} %bitcast.51), channel_id=1, source_target_pairs={{0,8},{8,0},{1,9},{9,1},{2,10},{10,2},{3,11},{11,3},{4,12},{12,4},... | collective-permute-start | bytes 1572872 | tf_op jit(solution)/shard_map/ppermute | solution.py:22
  165.1 1.5 collective-permute-done.3
  166.6 0.5 convolution_convert_fusion.3
  167.2 9.8 %all_to_all.49 = bf16[8,64,256]{2,1,0:T(8,128)(2,1)S(1)} all-to-all(bf16[8,64,256]{2,1,0:T(8,128)(2,1)S(1)} %pad_maximum_fusion.12), channel_id=1, replica_groups=mesh['yh'=2,'zh'=4,'zl'=4,'c'=2,'yl'=2,'x'=4] {'yl','x'}, dimensions={0} | all-to-all | bytes 524288 | tf_op jit(solution)/shard_map/all_to_all | solution.py:26
  177.0 0.1 multiply_convert_fusion.1
  177.1 0.8 broadcast_in_dim.46
  178.0 3.5 %all-to-all-start.8 = ((bf16[8,64,512]{2,1,0:T(8,128)(2,1)}), bf16[8,64,512]{2,1,0:T(8,128)(2,1)S(1)}, u32[]{:S(2)}, u32[]{:S(2)}) async-start(bf16[8,64,512]{2,1,0:T(8,128)(2,1)} %broadcast_in_dim.46), calls=%async_computation.8 | async-start | bytes 1048576 | tf_op jit(solution)/shard_map/all_to_all | solution.py:26
  181.5 0.1 pad_maximum_fusion.2
  181.5 0.0 copy-start.7
  181.6 2.4 %fusion.2 = bf16[256,1024]{1,0:T(8,128)(2,1)} fusion(bf16[8,48,1024]{2,1,0:T(8,128)(2,1)S(1)} %bitcast.59, bf16[8,16,1024]{2,1,0:T(8,128)(2,1)S(1)} %bitcast.65, bf16[256,1024]{1,0:T(8,128)(2,1)} %param.19, bf16[8,64,512]{2,1,0:T(8,128)(2,1)S(1)} %all-to-all-done.3), kind=kOutput, calls=%fused_computation.8 | convolution fusion | flops 271581184 | bytes 2359296 | tf_op jit(solution)/shard_map/dot_general | solution.py:123
  183.9 7.7 %all-to-all-done.8 = bf16[8,64,512]{2,1,0:T(8,128)(2,1)S(1)} async-done(((bf16[8,64,512]{2,1,0:T(8,128)(2,1)}), bf16[8,64,512]{2,1,0:T(8,128)(2,1)S(1)}, u32[]{:S(2)}, u32[]{:S(2)}) %all-to-all-start.8) | async-done | bytes 524320 | tf_op jit(solution)/shard_map/all_to_all | solution.py:26
  191.6 0.0 copy-done.7
  191.6 0.0 copy-start.3
  191.6 0.7 convolution_bitcast_fusion
  192.4 0.3 copy-done.3
  192.7 0.2 copy-done.5
  192.8 1.3 fusion.4
  (21 shorter events, 0.5 us)
Async XLA Ops:
  0.6 32.6 %copy-start.2 = (bf16[1024,256]{1,0:T(8,128)(2,1)S(1)}, bf16[1024,256]{1,0:T(8,128)(2,1)}, u32[]{:S(2)}) copy-start(bf16[1024,256]{1,0:T(8,128)(2,1)} %param.18) | copy-start | bytes 1572868
  0.6 32.6 %copy-start.4 = (bf16[1024,256]{1,0:T(8,128)(2,1)S(1)}, bf16[1024,256]{1,0:T(8,128)(2,1)}, u32[]{:S(2)}) copy-start(bf16[1024,256]{1,0:T(8,128)(2,1)} %param.17) | copy-start | bytes 1572868
  2.2 31.1 %all-to-all-start = ((bf16[16,8,1024]{2,1,0:T(8,128)(2,1)}), bf16[16,8,1024]{2,1,0:T(8,128)(2,1)S(1)}, u32[]{:S(2)}, u32[]{:S(2)}) async-start(bf16[16,8,1024]{2,1,0:T(8,128)(2,1)} %broadcast_in_dim.16), calls=%async_computation | async-start | bytes 524288 | tf_op jit(solution)/shard_map/all_to_all | solution.py:26
  34.4 11.2 %all-to-all-start.1 = ((bf16[8,16,1024]{2,1,0:T(8,128)(2,1)}), bf16[8,16,1024]{2,1,0:T(8,128)(2,1)S(1)}, u32[]{:S(2)}, u32[]{:S(2)}) async-start(bf16[8,16,1024]{2,1,0:T(8,128)(2,1)} %bitcast.7), calls=%async_computation.1 | async-start | bytes 524288 | tf_op jit(solution)/shard_map/all_to_all | solution.py:26
  39.5 10.6 %collective-permute-start = (bf16[128,1024]{1,0:T(8,128)(2,1)S(1)}, bf16[128,1024]{1,0:T(8,128)(2,1)S(1)}, u32[]{:S(2)}, u32[]{:S(2)}) collective-permute-start(bf16[128,1024]{1,0:T(8,128)(2,1)S(1)} %bitcast.56), channel_id=1, source_target_pairs={{0,256},{256,0},{1,257},{257,1},{2,258},{258,2},{3,259},{259,3},{4... | collective-permute-start | bytes 786440 | tf_op jit(solution)/shard_map/ppermute | solution.py:22
  50.1 7.0 %collective-permute-start.1 = (bf16[256,1024]{1,0:T(8,128)(2,1)S(1)}, bf16[256,1024]{1,0:T(8,128)(2,1)S(1)}, u32[]{:S(2)}, u32[]{:S(2)}) collective-permute-start(bf16[256,1024]{1,0:T(8,128)(2,1)S(1)} %pad_maximum_fusion.7), channel_id=1, source_target_pairs={{0,8},{8,0},{1,9},{9,1},{2,10},{10,2},{3,11},{11,3},{4,12},{12,4},... | collective-permute-start | bytes 1572872 | tf_op jit(solution)/shard_map/ppermute | solution.py:22
  57.2 1.0 copy-start.6
  74.7 4.6 %copy-start.8 = (s32[2,8]{1,0:T(2,128)S(1)}, s32[2,8]{1,0:T(2,128)}, u32[]{:S(2)}) copy-start(s32[2,8]{1,0:T(2,128)} %param.16) | copy-start | bytes 196
  74.7 4.7 %copy-start = (bf16[256,1024]{1,0:T(8,128)(2,1)S(1)}, bf16[256,1024]{1,0:T(8,128)(2,1)}, u32[]{:S(2)}) copy-start(bf16[256,1024]{1,0:T(8,128)(2,1)} %param.13) | copy-start | bytes 1572868
  74.8 4.7 %copy-start.1 = (bf16[256,1024]{1,0:T(8,128)(2,1)S(1)}, bf16[256,1024]{1,0:T(8,128)(2,1)}, u32[]{:S(2)}) copy-start(bf16[256,1024]{1,0:T(8,128)(2,1)} %param.19) | copy-start | bytes 1572868
  75.8 13.4 %all-to-all-start.3 = ((bf16[8,64,512]{2,1,0:T(8,128)(2,1)}), bf16[8,64,512]{2,1,0:T(8,128)(2,1)S(1)}, u32[]{:S(2)}, u32[]{:S(2)}) async-start(bf16[8,64,512]{2,1,0:T(8,128)(2,1)} %broadcast_in_dim.19), calls=%async_computation.3 | async-start | bytes 1048576 | tf_op jit(solution)/shard_map/all_to_all | solution.py:26
  90.5 4.7 %collective-permute-start.2 = (bf16[256,1024]{1,0:T(8,128)(2,1)}, bf16[256,1024]{1,0:T(8,128)(2,1)S(1)}, u32[]{:S(2)}, u32[]{:S(2)}) collective-permute-start(bf16[256,1024]{1,0:T(8,128)(2,1)} %convolution_convert_fusion.1), channel_id=1, source_target_pairs={{0,8},{8,0},{1,9},{9,1},{2,10},{10,2},{3,11},{11,3},{4,12},{12,4},... | collective-permute-start | bytes 1572872 | tf_op jit(solution)/shard_map/ppermute | solution.py:22
  159.8 6.8 %collective-permute-start.3 = (bf16[256,1024]{1,0:T(8,128)(2,1)S(1)}, bf16[256,1024]{1,0:T(8,128)(2,1)S(1)}, u32[]{:S(2)}, u32[]{:S(2)}) collective-permute-start(bf16[256,1024]{1,0:T(8,128)(2,1)S(1)} %bitcast.51), channel_id=1, source_target_pairs={{0,8},{8,0},{1,9},{9,1},{2,10},{10,2},{3,11},{11,3},{4,12},{12,4},... | collective-permute-start | bytes 1572872 | tf_op jit(solution)/shard_map/ppermute | solution.py:22
  178.0 13.7 %all-to-all-start.8 = ((bf16[8,64,512]{2,1,0:T(8,128)(2,1)}), bf16[8,64,512]{2,1,0:T(8,128)(2,1)S(1)}, u32[]{:S(2)}, u32[]{:S(2)}) async-start(bf16[8,64,512]{2,1,0:T(8,128)(2,1)} %broadcast_in_dim.46), calls=%async_computation.8 | async-start | bytes 1048576 | tf_op jit(solution)/shard_map/all_to_all | solution.py:26
  181.5 10.1 %copy-start.7 = (bf16[384,1024]{1,0:T(8,128)(2,1)S(1)}, bf16[384,1024]{1,0:T(8,128)(2,1)}, u32[]{:S(2)}) copy-start(bf16[384,1024]{1,0:T(8,128)(2,1)} %copy-done.6) | copy-start | bytes 2359300
  191.6 1.0 copy-start.3
  191.6 1.2 copy-start.5

commit v3 on v1

v3 whole, which is shorter than its diff:
```python
import jax
import jax.numpy as jnp
from jax import lax
from jax.sharding import Mesh, PartitionSpec as P

D = 8192
HID = 16384
BF16 = jnp.bfloat16
F32 = jnp.float32
DP = ("yh", "zh", "zl", "c")
TP = ("yl", "x")
NEAR = ("yh", "c", "yl", "x")


def kept(weight, mask):
    rows, cols = weight.shape
    wide = jnp.repeat(mask.astype(BF16), cols // mask.shape[1], axis=1)
    blocks = weight.reshape(mask.shape[0], rows // mask.shape[0], cols)
    return (blocks * wide[:, None, :]).reshape(rows, cols)


def swap(x, axis):
    return lax.ppermute(x, axis, [(0, 1), (1, 0)])


def step_y(x, way):
    return lax.ppermute(x, ("yh", "yl"), [(i, (i + way) % 4) for i in range(4)])


def exchange(pieces, axes):
    return lax.all_to_all(pieces, axes, 0, 0, tiled=True)


def together(arrays):
    return lax.optimization_barrier(arrays)


def copies(x, n):
    return jnp.broadcast_to(x[None], (n,) + x.shape)


def total(pieces, axis=0):
    return jnp.sum(pieces.astype(F32), axis=axis)


def reorder(x):
    x = jnp.where(lax.axis_index("c") == 0, x, x[:, ::-1])
    return jnp.where(lax.axis_index("yh") == 0, x, x[::-1])


def by_position(own, over_c, over_y, over_both):
    x = reorder(jnp.stack([own, over_c, over_y, over_both]).reshape((2, 2) + own.shape))
    return x.reshape((4 * own.shape[0],) + own.shape[1:])


def dot(a, b, dims=((1,), (0,))):
    return lax.dot_general(a, b, (dims, ((), ())), preferred_element_type=F32)


def on_device(
    tokens,
    gate_weight,
    up_weight,
    down_weight,
    gate_mask,
    up_mask,
    down_mask,
    probe_gate,
    probe_up,
    probe_down,
):
    width = gate_weight.shape[1]
    feats = tokens.shape[1]

    tok0 = exchange(copies(tokens, 16), ("zl", "zh")).reshape(8, 16, feats)
    kept_down = kept(down_weight, down_mask)
    kept_gate = kept(gate_weight, gate_mask)
    kept_up = kept(up_weight, up_mask)
    kept_c, probe_c = swap(kept_down, "c"), swap(probe_down, "c")
    kept_y, probe_y = step_y(kept_down, 1), step_y(probe_down, -1)
    tok0, kept_gate, kept_up, kept_c, probe_c, kept_y, probe_y = together(
        (tok0, kept_gate, kept_up, kept_c, probe_c, kept_y, probe_y)
    )
    stacked = jnp.concatenate([kept_gate, kept_up, probe_gate, probe_up], axis=1)

    tok1 = swap(tok0, "yh")
    pair = jnp.stack([tok0, tok1], axis=1)
    other = swap(pair, "c")
    gathered = jnp.stack([pair, other], axis=2).reshape(-1, feats)
    partial = dot(gathered, stacked).astype(BF16)
    partial, kept_y, probe_y = together((partial, kept_y, probe_y))
    pre = exchange(partial.reshape(8, -1, 4 * width), TP)
    pre, kept_y, probe_y = together((pre, step_y(kept_y, 1), step_y(probe_y, -1)))
    pre = total(pre)

    gate = pre[:, :width]
    up = pre[:, width : 2 * width]
    tangent_gate = pre[:, 2 * width : 3 * width] * D**-0.5
    tangent_up = pre[:, 3 * width :] * D**-0.5
    sig = jax.nn.sigmoid(gate)
    act = gate * sig
    slope = sig * (1.0 + gate * (1.0 - sig))
    hid = (act * up).astype(BF16)
    tan = (slope * tangent_gate * up + act * tangent_up).astype(BF16)
    both = jnp.concatenate([tan, hid], axis=1).reshape(2, 2, 16, 2 * width)
    both = reorder(both).reshape(4, 1, 16, 2 * width)
    both = jnp.broadcast_to(both, (4, 8, 16, 2 * width)).reshape(32, 16, 2 * width)
    both, kept_y, probe_y = together((both, kept_y, probe_y))
    both = exchange(both, NEAR).reshape(4, 128, 2 * width)
    kept4 = by_position(kept_down, kept_c, kept_y, swap(kept_y, "c"))
    probe4 = by_position(probe_down, probe_c, probe_y, swap(probe_y, "c"))
    both, kept4, probe4 = together((both, kept4, probe4))
    tan4 = jnp.concatenate([both[i, :, :width] for i in range(4)], axis=1)
    hid4 = jnp.concatenate([both[i, :, width:] for i in range(4)], axis=1)

    term = dot(tan4, kept4) + dot(hid4, probe4) * HID**-0.5
    term, both = together((term.astype(BF16), both))
    mine = reorder(both[:, :, width:].reshape(2, 2, 128, width))
    term = exchange(term.reshape(4, 32, feats), "zl")
    term, mine = together((term, jnp.stack([mine[:, 0], swap(mine[:, 1], "c")])))
    chunk = exchange(copies(total(term).astype(BF16), 4), "zh")
    chunk, hidden = together((chunk, jnp.stack([mine[:, 0], swap(mine[:, 1], "yh")], axis=1)))
    hidden = hidden.reshape(-1, width)
    chunk = exchange(copies(total(chunk).astype(BF16), 4), "zl")
    out0 = chunk.reshape(128, feats)

    back = dot(out0, kept4, ((1,), (1,))).astype(BF16)
    back = jnp.stack([back[:, i * width : (i + 1) * width] for i in range(4)])
    back, out0 = together((back, out0))
    back = exchange(back.reshape(32, 16, width), NEAR)
    back, out1 = together((back, jnp.stack([out0, swap(out0, "yh")])))
    back = total(back.reshape(4, 8, 16, width), 1).reshape(2, 2, 16, width)
    back = reorder(back).reshape(64, width)
    bars = jnp.concatenate([(back * up * slope).astype(BF16), (back * act).astype(BF16)], axis=1)
    bars, out1 = together((bars, out1))
    bars = exchange(copies(bars, 8), TP).reshape(gathered.shape[0], 2 * width)
    tangent_out = jnp.stack([out1, swap(out1, "c")]).reshape(gathered.shape)

    factor = gathered.shape[0] ** -0.5
    grad_down = dot(hidden, tangent_out, ((0,), (0,)))
    grads = dot(gathered, bars, ((0,), (0,)))
    fisher_gate = (probe_gate.astype(F32) * grads[:, :width] * factor).astype(BF16)
    fisher_up = (probe_up.astype(F32) * grads[:, width:] * factor).astype(BF16)
    fisher_down = (probe_down.astype(F32) * grad_down * factor).astype(BF16)
    return (fisher_gate, fisher_up, fisher_down)


def solution(mesh):
    fine = Mesh(mesh.devices.reshape(2, 4, 4, 2, 2, 4), DP + TP)
    col = P(TP, DP)
    row = P(DP, TP)
    return jax.shard_map(
        on_device,
        mesh=fine,
        in_specs=(row, col, col, row, col, col, row, col, col, row),
        out_specs=(col, col, row),
        check_vma=False,
    )
```

time: 194 us -> 213 us (1.098)
  blocking collectives: 103 us -> 8.36 us
  starting transfers between devices: 42.2 us -> 98.5 us
  waiting for transfers between devices: 35 us -> 71.7 us
  other arithmetic: 3.54 us -> 15.2 us
  local copies, waits for them, and re-layouts: 3.39 us -> 7.92 us
  matrix products: 5.56 us -> 8.75 us
    all_to_all x5 -> x1, blocking collectives: 103 us -> 8.36 us  [exchange(): return lax.all_to_all(pieces, axes, 0, 0, tiled=True)]
    all_to_all x2 -> x7, starting transfers between devices: 6.99 us -> 56.2 us  [exchange(): return lax.all_to_all(pieces, axes, 0, 0, tiled=True)]
    ppermute x0 -> x4, waiting for transfers between devices: none -> 27.8 us  [step_y(): return lax.ppermute(x, ('yh', 'yl'), [(i, (i + way) % 4) for i in range(4)])]
    ppermute x0 -> x4, starting transfers between devices: none -> 13.2 us  [step_y(): return lax.ppermute(x, ('yh', 'yl'), [(i, (i + way) % 4) for i in range(4)])]
    all_to_all x2 -> x7, waiting for transfers between devices: 17.7 us -> 30.3 us  [exchange(): return lax.all_to_all(pieces, axes, 0, 0, tiled=True)]
    ppermute x6 -> x10, starting transfers between devices: 35.3 us -> 29.1 us  [swap(): return lax.ppermute(x, axis, [(0, 1), (1, 0)])]
    another operation x0 -> x8, other arithmetic: none -> 4.48 us  [the longest x2 2.77 us: by_position(): jnp.stack([own, over_c, over_y, over_both]).reshape((2, 2) + own.shape)]
    select_n x0 -> x10, other arithmetic: none -> 3.83 us  [the longest x5 2.58 us: reorder(): return jnp.where(lax.axis_index('yh') == 0, x, x[::-1])]
  transfers between devices with their start and end apart: 8 -> 21, of which waited for: 7 -> 13; matrix products, arithmetic and copies ran while one was open for 2% -> 7% of each run, Pallas kernels for 0% -> 0%
where the time goes in v3:
time: 213 us; the launch traced here: 212 us
  starting transfers between devices  98.5 us (46%)
  waiting for transfers between devices  71.7 us (34%)
  other arithmetic  15.2 us (7%)
  matrix products  8.75 us (4%)
  blocking collectives  8.36 us (4%)
  local copies, waits for them, and re-layouts  7.92 us (4%)
    all_to_all x7, starting transfers between devices, exchange(): return lax.all_to_all(pieces, axes, 0, 0, tiled=True)  56.2 us
    all_to_all x7, waiting for transfers between devices, exchange(): return lax.all_to_all(pieces, axes, 0, 0, tiled=True)  30.3 us
    ppermute x10, starting transfers between devices, swap(): return lax.ppermute(x, axis, [(0, 1), (1, 0)])  29.1 us
    ppermute x4, waiting for transfers between devices, step_y(): return lax.ppermute(x, ('yh', 'yl'), [(i, (i + way) % 4) for i in range(4)])  27.8 us
    ppermute x10, waiting for transfers between devices, swap(): return lax.ppermute(x, axis, [(0, 1), (1, 0)])  13.6 us
    ppermute x4, starting transfers between devices, step_y(): return lax.ppermute(x, ('yh', 'yl'), [(i, (i + way) % 4) for i in range(4)])  13.2 us
    dot_general x6, matrix products, dot(): return lax.dot_general(a, b, (dims, ((), ())), preferred_element_type=F32)  8.75 us
    all_to_all x1, blocking collectives, exchange(): return lax.all_to_all(pieces, axes, 0, 0, tiled=True)  8.36 us
  transfers between devices with their start and end apart: 21, of which 13 were waited for; matrix products, arithmetic and copies ran while one was open for 7% of the time, Pallas kernels for 0%

profile of v3, /device:TPU:1, one launch (start us, length us, event | category | flops | bytes accessed | tf_op | source)
XLA Modules:
  0.0 211.6 jit_solution(5316621141618294432)
XLA Ops:
  0.7 1.5 broadcast_in_dim.18
  2.2 15.7 %all-to-all-start = ((bf16[16,8,1024]{2,1,0:T(8,128)(2,1)}), bf16[16,8,1024]{2,1,0:T(8,128)(2,1)S(1)}, u32[]{:S(2)}, u32[]{:S(2)}) async-start(bf16[16,8,1024]{2,1,0:T(8,128)(2,1)} %broadcast_in_dim.18), calls=%async_computation | async-start | bytes 524288 | tf_op jit(solution)/shard_map/all_to_all | solution.py:31
  17.9 0.7 convert_element_type.64
  18.7 1.1 bitcast_multiply_fusion
  19.8 3.2 %collective-permute-start.2 = (bf16[256,1024]{1,0:T(8,128)(2,1)S(1)}, bf16[256,1024]{1,0:T(8,128)(2,1)S(1)}, u32[]{:S(2)}, u32[]{:S(2)}) collective-permute-start(bf16[256,1024]{1,0:T(8,128)(2,1)S(1)} %bitcast_multiply_fusion), channel_id=1, source_target_pairs={{0,4},{4,256},{256,260},{260,0},{1,5},{5,257},{257,261},{261,1},{2... | collective-permute-start | bytes 1572872 | tf_op jit(solution)/shard_map/ppermute | solution.py:27
  23.0 3.1 %collective-permute-start = (bf16[256,1024]{1,0:T(8,128)(2,1)S(1)}, bf16[256,1024]{1,0:T(8,128)(2,1)S(1)}, u32[]{:S(2)}, u32[]{:S(2)}) collective-permute-start(bf16[256,1024]{1,0:T(8,128)(2,1)S(1)} %bitcast_multiply_fusion), channel_id=1, source_target_pairs={{0,8},{8,0},{1,9},{9,1},{2,10},{10,2},{3,11},{11,3},{4,12},{12,4},... | collective-permute-start | bytes 1572872 | tf_op jit(solution)/shard_map/ppermute | solution.py:23
  26.1 3.3 %collective-permute-start.3 = (bf16[256,1024]{1,0:T(8,128)(2,1)}, bf16[256,1024]{1,0:T(8,128)(2,1)S(1)}, u32[]{:S(2)}, u32[]{:S(2)}) collective-permute-start(bf16[256,1024]{1,0:T(8,128)(2,1)} %param.19), channel_id=1, source_target_pairs={{0,260},{4,0},{256,4},{260,256},{1,261},{5,1},{257,5},{261,257},{2... | collective-permute-start | bytes 1572872 | tf_op jit(solution)/shard_map/ppermute | solution.py:27
  29.4 2.2 %collective-permute-start.1 = (bf16[256,1024]{1,0:T(8,128)(2,1)}, bf16[256,1024]{1,0:T(8,128)(2,1)}, u32[]{:S(2)}, u32[]{:S(2)}) collective-permute-start(bf16[256,1024]{1,0:T(8,128)(2,1)} %param.19), channel_id=1, source_target_pairs={{0,8},{8,0},{1,9},{9,1},{2,10},{10,2},{3,11},{11,3},{4,12},{12,4},... | collective-permute-start | bytes 1572872 | tf_op jit(solution)/shard_map/ppermute | solution.py:23
  31.7 0.7 convert_element_type.62
  32.3 0.7 convert_element_type.63
  33.3 2.2 %collective-permute-done.2 = bf16[256,1024]{1,0:T(8,128)(2,1)S(1)} collective-permute-done((bf16[256,1024]{1,0:T(8,128)(2,1)S(1)}, bf16[256,1024]{1,0:T(8,128)(2,1)S(1)}, u32[]{:S(2)}, u32[]{:S(2)}) %collective-permute-start.2) | collective-permute-done | bytes 524320 | tf_op jit(solution)/shard_map/ppermute | solution.py:27
  35.5 6.3 %collective-permute-done.3 = bf16[256,1024]{1,0:T(8,128)(2,1)S(1)} collective-permute-done((bf16[256,1024]{1,0:T(8,128)(2,1)}, bf16[256,1024]{1,0:T(8,128)(2,1)S(1)}, u32[]{:S(2)}, u32[]{:S(2)}) %collective-permute-start.3) | collective-permute-done | bytes 524320 | tf_op jit(solution)/shard_map/ppermute | solution.py:27
  41.8 0.8 copy-done.14
  42.6 4.5 %collective-permute-start.4 = (bf16[8,16,1024]{2,1,0:T(8,128)(2,1)S(1)}, bf16[8,16,1024]{2,1,0:T(8,128)(2,1)S(1)}, u32[]{:S(2)}, u32[]{:S(2)}) collective-permute-start(bf16[8,16,1024]{2,1,0:T(8,128)(2,1)S(1)} %bitcast.130), channel_id=1, source_target_pairs={{0,256},{256,0},{1,257},{257,1},{2,258},{258,2},{3,259},{259,3},{4... | collective-permute-start | bytes 786440 | tf_op jit(solution)/shard_map/ppermute | solution.py:23
  47.1 5.9 %collective-permute-done.4 = bf16[8,16,1024]{2,1,0:T(8,128)(2,1)S(1)} collective-permute-done((bf16[8,16,1024]{2,1,0:T(8,128)(2,1)S(1)}, bf16[8,16,1024]{2,1,0:T(8,128)(2,1)S(1)}, u32[]{:S(2)}, u32[]{:S(2)}) %collective-permute-start.4) | collective-permute-done | bytes 262176 | tf_op jit(solution)/shard_map/ppermute | solution.py:23
  53.1 3.6 %collective-permute-start.5 = (bf16[8,2,16,1024]{3,2,1,0:T(8,128)(2,1)S(1)}, bf16[8,2,16,1024]{3,2,1,0:T(8,128)(2,1)S(1)}, u32[]{:S(2)}, u32[]{:S(2)}) collective-permute-start(bf16[8,2,16,1024]{3,2,1,0:T(8,128)(2,1)S(1)} %get-tuple-element.76), channel_id=1, source_target_pairs={{0,8},{8,0},{1,9},{9,1},{2,10},{10,2},{3,11},{11,3},{4,12},{12,4},... | collective-permute-start | bytes 1572872 | tf_op jit(solution)/shard_map/ppermute | solution.py:23
  56.7 1.5 collective-permute-done.5
  58.3 3.3 %fusion.8 = bf16[512,1024]{1,0:T(8,128)(2,1)} fusion(bf16[512,1024]{1,0:T(8,128)(2,1)S(1)} %bitcast.121, bf16[1024,256]{1,0:T(8,128)(2,1)S(1)} %copy-done.5, bf16[1024,256]{1,0:T(8,128)(2,1)} %param.17, bf16[1024,256]{1,0:T(8,128)(2,1)S(1)} %get-tuple-element.36, bf16[1024,256]{1,0:T(8,128)(2,1)S(1)} %get-tuple-element.35), kind=kOutput, calls=%fused_computation.15 | convolution fusion | flops 1082654720 | bytes 4194304 | tf_op jit(solution)/shard_map/dot_general | solution.py:57
  61.6 5.0 %all-to-all-start.1 = ((bf16[8,64,1024]{2,1,0:T(8,128)(2,1)}), bf16[8,64,1024]{2,1,0:T(8,128)(2,1)S(1)}, u32[]{:S(2)}, u32[]{:S(2)}) async-start(bf16[8,64,1024]{2,1,0:T(8,128)(2,1)} %bitcast.129), calls=%async_computation.1 | async-start | bytes 2097152 | tf_op jit(solution)/shard_map/all_to_all | solution.py:31
  66.6 3.5 %collective-permute-start.6 = (bf16[256,1024]{1,0:T(8,128)(2,1)}, bf16[256,1024]{1,0:T(8,128)(2,1)}, u32[]{:S(2)}, u32[]{:S(2)}) collective-permute-start(bf16[256,1024]{1,0:T(8,128)(2,1)} %copy-done.13), channel_id=1, source_target_pairs={{0,4},{4,256},{256,260},{260,0},{1,5},{5,257},{257,261},{261,1},{2... | collective-permute-start | bytes 1572872 | tf_op jit(solution)/shard_map/ppermute | solution.py:27
  70.1 3.2 %collective-permute-start.7 = (bf16[256,1024]{1,0:T(8,128)(2,1)}, bf16[256,1024]{1,0:T(8,128)(2,1)}, u32[]{:S(2)}, u32[]{:S(2)}) collective-permute-start(bf16[256,1024]{1,0:T(8,128)(2,1)} %copy-done.14), channel_id=1, source_target_pairs={{0,260},{4,0},{256,4},{260,256},{1,261},{5,1},{257,5},{261,257},{2... | collective-permute-start | bytes 1572872 | tf_op jit(solution)/shard_map/ppermute | solution.py:27
  73.4 16.2 %collective-permute-done.6 = bf16[256,1024]{1,0:T(8,128)(2,1)} collective-permute-done((bf16[256,1024]{1,0:T(8,128)(2,1)}, bf16[256,1024]{1,0:T(8,128)(2,1)}, u32[]{:S(2)}, u32[]{:S(2)}) %collective-permute-start.6) | collective-permute-done | bytes 524320 | tf_op jit(solution)/shard_map/ppermute | solution.py:27
  89.6 3.0 %collective-permute-done.7 = bf16[256,1024]{1,0:T(8,128)(2,1)} collective-permute-done((bf16[256,1024]{1,0:T(8,128)(2,1)}, bf16[256,1024]{1,0:T(8,128)(2,1)}, u32[]{:S(2)}, u32[]{:S(2)}) %collective-permute-start.7) | collective-permute-done | bytes 524320 | tf_op jit(solution)/shard_map/ppermute | solution.py:27
  92.9 0.9 broadcast_in_dim.45
  93.8 2.4 %collective-permute-start.8 = (bf16[256,1024]{1,0:T(8,128)(2,1)}, bf16[256,1024]{1,0:T(8,128)(2,1)S(1)}, u32[]{:S(2)}, u32[]{:S(2)}) collective-permute-start(bf16[256,1024]{1,0:T(8,128)(2,1)} %collective-permute-done.6), channel_id=1, source_target_pairs={{0,8},{8,0},{1,9},{9,1},{2,10},{10,2},{3,11},{11,3},{4,12},{12,4},... | collective-permute-start | bytes 1572872 | tf_op jit(solution)/shard_map/ppermute | solution.py:23
  96.2 6.2 %all-to-all-start.2 = ((bf16[32,16,512]{2,1,0:T(8,128)(2,1)}), bf16[32,16,512]{2,1,0:T(8,128)(2,1)}, u32[]{:S(2)}, u32[]{:S(2)}) async-start(bf16[32,16,512]{2,1,0:T(8,128)(2,1)} %bitcast.16), calls=%async_computation.2 | async-start | bytes 1048576 | tf_op jit(solution)/shard_map/all_to_all | solution.py:31
  102.4 2.2 %collective-permute-start.9 = (bf16[256,1024]{1,0:T(8,128)(2,1)}, bf16[256,1024]{1,0:T(8,128)(2,1)S(1)}, u32[]{:S(2)}, u32[]{:S(2)}) collective-permute-start(bf16[256,1024]{1,0:T(8,128)(2,1)} %collective-permute-done.7), channel_id=1, source_target_pairs={{0,8},{8,0},{1,9},{9,1},{2,10},{10,2},{3,11},{11,3},{4,12},{12,4},... | collective-permute-start | bytes 1572872 | tf_op jit(solution)/shard_map/ppermute | solution.py:23
  104.6 1.3 pad_maximum_fusion
  105.9 0.6 reverse_select_fusion.3
  106.5 0.6 reverse_select_fusion.2
  107.1 0.4 copy-done.8
  107.6 1.5 pad_maximum_fusion.1
  109.0 0.6 reverse_select_fusion.1
  109.6 1.9 reverse_select_fusion
  111.6 2.4 %all-to-all-done.2 = bf16[32,16,512]{2,1,0:T(8,128)(2,1)} async-done(((bf16[32,16,512]{2,1,0:T(8,128)(2,1)}), bf16[32,16,512]{2,1,0:T(8,128)(2,1)}, u32[]{:S(2)}, u32[]{:S(2)}) %all-to-all-start.2) | async-done | bytes 524320 | tf_op jit(solution)/shard_map/all_to_all | solution.py:31
  114.0 1.2 slice_bitcast_fusion.10
  115.3 0.4 fusion.23
  115.9 1.2 fusion.15
  117.0 4.7 %all-to-all-start.3 = ((bf16[4,32,1024]{2,1,0:T(8,128)(2,1)}), bf16[4,32,1024]{2,1,0:T(8,128)(2,1)}, u32[]{:S(2)}, u32[]{:S(2)}) async-start(bf16[4,32,1024]{2,1,0:T(8,128)(2,1)} %bitcast.38), calls=%async_computation.3 | async-start | bytes 524288 | tf_op jit(solution)/shard_map/all_to_all | solution.py:31
  121.7 1.0 slice.81
  122.8 2.6 %collective-permute-start.10 = (bf16[2,128,256]{2,1,0:T(8,128)(2,1)S(1)}, bf16[2,128,256]{2,1,0:T(8,128)(2,1)S(1)}, u32[]{:S(2)}, u32[]{:S(2)}) collective-permute-start(bf16[2,128,256]{2,1,0:T(8,128)(2,1)S(1)} %get-tuple-element.84), channel_id=1, source_target_pairs={{0,8},{8,0},{1,9},{9,1},{2,10},{10,2},{3,11},{11,3},{4,12},{12,4},... | collective-permute-start | bytes 393224 | tf_op jit(solution)/shard_map/ppermute | solution.py:23
  125.4 1.0 collective-permute-done.10
  126.4 2.9 %all-to-all-done.3 = bf16[4,32,1024]{2,1,0:T(8,128)(2,1)} async-done(((bf16[4,32,1024]{2,1,0:T(8,128)(2,1)}), bf16[4,32,1024]{2,1,0:T(8,128)(2,1)}, u32[]{:S(2)}, u32[]{:S(2)}) %all-to-all-start.3) | async-done | bytes 262176 | tf_op jit(solution)/shard_map/all_to_all | solution.py:31
  129.3 1.0 reduce_sum.43
  130.3 0.7 broadcast_in_dim.46
  131.0 10.9 %all-to-all-start.4 = ((bf16[4,32,1024]{2,1,0:T(8,128)(2,1)}), bf16[4,32,1024]{2,1,0:T(8,128)(2,1)}, u32[]{:S(2)}, u32[]{:S(2)}) async-start(bf16[4,32,1024]{2,1,0:T(8,128)(2,1)} %broadcast_in_dim.46), calls=%async_computation.4 | async-start | bytes 524288 | tf_op jit(solution)/shard_map/all_to_all | solution.py:31
  141.9 1.9 collective-permute-start.11
  143.8 5.2 %collective-permute-done.11 = bf16[2,128,256]{2,1,0:T(8,128)(2,1)S(1)} collective-permute-done((bf16[2,128,256]{2,1,0:T(8,128)(2,1)S(1)}, bf16[2,128,256]{2,1,0:T(8,128)(2,1)S(1)}, u32[]{:S(2)}, u32[]{:S(2)}) %collective-permute-start.11) | collective-permute-done | bytes 131104 | tf_op jit(solution)/shard_map/ppermute | solution.py:23
  149.1 0.7 pad_maximum_fusion.6
  149.8 8.6 %all-to-all-done.4 = bf16[4,32,1024]{2,1,0:T(8,128)(2,1)} async-done(((bf16[4,32,1024]{2,1,0:T(8,128)(2,1)}), bf16[4,32,1024]{2,1,0:T(8,128)(2,1)}, u32[]{:S(2)}, u32[]{:S(2)}) %all-to-all-start.4) | async-done | bytes 262176 | tf_op jit(solution)/shard_map/all_to_all | solution.py:31
  158.4 1.0 reduce_sum.44
  159.4 8.4 %all_to_all.40 = bf16[4,32,1024]{2,1,0:T(8,128)(2,1)S(1)} all-to-all(bf16[4,32,1024]{2,1,0:T(8,128)(2,1)S(1)} %broadcast_in_dim.47), channel_id=1, replica_groups=mesh['yh'=2,'zh'=4,'zl'=4,'c'=2,'yl'=2,'x'=4] {'zl'}, dimensions={0} | all-to-all | bytes 524288 | tf_op jit(solution)/shard_map/all_to_all | solution.py:31
  167.8 0.8 convolution_convert_fusion
  168.7 0.7 pad_maximum_fusion.7
  169.4 4.1 %collective-permute-start.12 = (bf16[128,1024]{1,0:T(8,128)(2,1)S(1)}, bf16[128,1024]{1,0:T(8,128)(2,1)S(1)}, u32[]{:S(2)}, u32[]{:S(2)}) collective-permute-start(bf16[128,1024]{1,0:T(8,128)(2,1)S(1)} %bitcast.124), channel_id=1, source_target_pairs={{0,256},{256,0},{1,257},{257,1},{2,258},{258,2},{3,259},{259,3},{4... | collective-permute-start | bytes 786440 | tf_op jit(solution)/shard_map/ppermute | solution.py:23
  173.6 10.1 %all-to-all-start.6 = ((bf16[32,16,256]{2,1,0:T(8,128)(2,1)}), bf16[32,16,256]{2,1,0:T(8,128)(2,1)S(1)}, u32[]{:S(2)}, u32[]{:S(2)}) async-start(bf16[32,16,256]{2,1,0:T(8,128)(2,1)} %bitcast.50), calls=%async_computation.6 | async-start | bytes 524288 | tf_op jit(solution)/shard_map/all_to_all | solution.py:31
  183.8 8.7 %all-to-all-done.6 = bf16[32,16,256]{2,1,0:T(8,128)(2,1)S(1)} async-done(((bf16[32,16,256]{2,1,0:T(8,128)(2,1)}), bf16[32,16,256]{2,1,0:T(8,128)(2,1)S(1)}, u32[]{:S(2)}, u32[]{:S(2)}) %all-to-all-start.6) | async-done | bytes 262176 | tf_op jit(solution)/shard_map/all_to_all | solution.py:31
  192.6 0.8 broadcast_in_dim.48
  193.4 3.5 %all-to-all-start.7 = ((bf16[8,64,512]{2,1,0:T(8,128)(2,1)}), bf16[8,64,512]{2,1,0:T(8,128)(2,1)S(1)}, u32[]{:S(2)}, u32[]{:S(2)}) async-start(bf16[8,64,512]{2,1,0:T(8,128)(2,1)} %broadcast_in_dim.48), calls=%async_computation.7 | async-start | bytes 1048576 | tf_op jit(solution)/shard_map/all_to_all | solution.py:31
  197.0 2.4 %collective-permute-start.13 = (bf16[2,128,1024]{2,1,0:T(8,128)(2,1)S(1)}, bf16[2,128,1024]{2,1,0:T(8,128)(2,1)}, u32[]{:S(2)}, u32[]{:S(2)}) collective-permute-start(bf16[2,128,1024]{2,1,0:T(8,128)(2,1)S(1)} %pad_maximum_fusion.4), channel_id=1, source_target_pairs={{0,8},{8,0},{1,9},{9,1},{2,10},{10,2},{3,11},{11,3},{4,12},{12,4},... | collective-permute-start | bytes 1572872 | tf_op jit(solution)/shard_map/ppermute | solution.py:23
  199.4 7.7 %all-to-all-done.7 = bf16[8,64,512]{2,1,0:T(8,128)(2,1)S(1)} async-done(((bf16[8,64,512]{2,1,0:T(8,128)(2,1)}), bf16[8,64,512]{2,1,0:T(8,128)(2,1)S(1)}, u32[]{:S(2)}, u32[]{:S(2)}) %all-to-all-start.7) | async-done | bytes 524320 | tf_op jit(solution)/shard_map/all_to_all | solution.py:31
  207.2 0.7 fusion.53
  208.0 1.3 fusion.17
  209.3 2.3 %fusion.13 = bf16[256,1024]{1,0:T(8,128)(2,1)} fusion(bf16[1,2,128,1024]{3,2,1,0:T(8,128)(2,1)} %bitcast.58, bf16[1,2,128,1024]{3,2,1,0:T(8,128)(2,1)S(1)} %bitcast.132, bf16[256,1024]{1,0:T(8,128)(2,1)S(1)} %copy-done.9, bf16[2,2,128,256]{3,2,0,1:T(8,128)(2,1)S(1)} %copy-done.12), kind=kOutput, calls=%fused_computation.19 | convolution fusion | flops 270008320 | bytes 2359296 | tf_op jit(solution)/shard_map/dot_general | solution.py:57
  (63 shorter events, 1.3 us)
Async XLA Ops:
  0.6 32.5 %copy-start.3 = (bf16[1024,256]{1,0:T(8,128)(2,1)S(1)}, bf16[1024,256]{1,0:T(8,128)(2,1)}, u32[]{:S(2)}) copy-start(bf16[1024,256]{1,0:T(8,128)(2,1)} %param.12) | copy-start | bytes 1572868
  0.6 32.5 %copy-start.4 = (bf16[1024,256]{1,0:T(8,128)(2,1)S(1)}, bf16[1024,256]{1,0:T(8,128)(2,1)}, u32[]{:S(2)}) copy-start(bf16[1024,256]{1,0:T(8,128)(2,1)} %param.11) | copy-start | bytes 1572868
  2.2 40.4 %all-to-all-start = ((bf16[16,8,1024]{2,1,0:T(8,128)(2,1)}), bf16[16,8,1024]{2,1,0:T(8,128)(2,1)S(1)}, u32[]{:S(2)}, u32[]{:S(2)}) async-start(bf16[16,8,1024]{2,1,0:T(8,128)(2,1)} %broadcast_in_dim.18), calls=%async_computation | async-start | bytes 524288 | tf_op jit(solution)/shard_map/all_to_all | solution.py:31
  19.8 15.7 %collective-permute-start.2 = (bf16[256,1024]{1,0:T(8,128)(2,1)S(1)}, bf16[256,1024]{1,0:T(8,128)(2,1)S(1)}, u32[]{:S(2)}, u32[]{:S(2)}) collective-permute-start(bf16[256,1024]{1,0:T(8,128)(2,1)S(1)} %bitcast_multiply_fusion), channel_id=1, source_target_pairs={{0,4},{4,256},{256,260},{260,0},{1,5},{5,257},{257,261},{261,1},{2... | collective-permute-start | bytes 1572872 | tf_op jit(solution)/shard_map/ppermute | solution.py:27
  23.0 12.5 %collective-permute-start = (bf16[256,1024]{1,0:T(8,128)(2,1)S(1)}, bf16[256,1024]{1,0:T(8,128)(2,1)S(1)}, u32[]{:S(2)}, u32[]{:S(2)}) collective-permute-start(bf16[256,1024]{1,0:T(8,128)(2,1)S(1)} %bitcast_multiply_fusion), channel_id=1, source_target_pairs={{0,8},{8,0},{1,9},{9,1},{2,10},{10,2},{3,11},{11,3},{4,12},{12,4},... | collective-permute-start | bytes 1572872 | tf_op jit(solution)/shard_map/ppermute | solution.py:23
  26.1 15.7 %collective-permute-start.3 = (bf16[256,1024]{1,0:T(8,128)(2,1)}, bf16[256,1024]{1,0:T(8,128)(2,1)S(1)}, u32[]{:S(2)}, u32[]{:S(2)}) collective-permute-start(bf16[256,1024]{1,0:T(8,128)(2,1)} %param.19), channel_id=1, source_target_pairs={{0,260},{4,0},{256,4},{260,256},{1,261},{5,1},{257,5},{261,257},{2... | collective-permute-start | bytes 1572872 | tf_op jit(solution)/shard_map/ppermute | solution.py:27
  29.4 13.2 %collective-permute-start.1 = (bf16[256,1024]{1,0:T(8,128)(2,1)}, bf16[256,1024]{1,0:T(8,128)(2,1)}, u32[]{:S(2)}, u32[]{:S(2)}) collective-permute-start(bf16[256,1024]{1,0:T(8,128)(2,1)} %param.19), channel_id=1, source_target_pairs={{0,8},{8,0},{1,9},{9,1},{2,10},{10,2},{3,11},{11,3},{4,12},{12,4},... | collective-permute-start | bytes 1572872 | tf_op jit(solution)/shard_map/ppermute | solution.py:23
  33.3 25.1 %copy-start.5 = (bf16[1024,256]{1,0:T(8,128)(2,1)S(1)}, bf16[1024,256]{1,0:T(8,128)(2,1)}, u32[]{:S(2)}) copy-start(bf16[1024,256]{1,0:T(8,128)(2,1)} %param.18) | copy-start | bytes 1572868
  35.5 6.3 %copy-start.13 = (bf16[256,1024]{1,0:T(8,128)(2,1)}, bf16[256,1024]{1,0:T(8,128)(2,1)S(1)}, u32[]{:S(2)}) copy-start(bf16[256,1024]{1,0:T(8,128)(2,1)S(1)} %collective-permute-done.2) | copy-start | bytes 1572868
  35.5 6.3 %copy-start.10 = (bf16[256,1024]{1,0:T(8,128)(2,1)}, bf16[256,1024]{1,0:T(8,128)(2,1)S(1)}, u32[]{:S(2)}) copy-start(bf16[256,1024]{1,0:T(8,128)(2,1)S(1)} %collective-permute-done) | copy-start | bytes 1572868
  41.8 0.8 copy-start.14
  42.6 10.4 %collective-permute-start.4 = (bf16[8,16,1024]{2,1,0:T(8,128)(2,1)S(1)}, bf16[8,16,1024]{2,1,0:T(8,128)(2,1)S(1)}, u32[]{:S(2)}, u32[]{:S(2)}) collective-permute-start(bf16[8,16,1024]{2,1,0:T(8,128)(2,1)S(1)} %bitcast.130), channel_id=1, source_target_pairs={{0,256},{256,0},{1,257},{257,1},{2,258},{258,2},{3,259},{259,3},{4... | collective-permute-start | bytes 786440 | tf_op jit(solution)/shard_map/ppermute | solution.py:23
  53.1 5.1 %collective-permute-start.5 = (bf16[8,2,16,1024]{3,2,1,0:T(8,128)(2,1)S(1)}, bf16[8,2,16,1024]{3,2,1,0:T(8,128)(2,1)S(1)}, u32[]{:S(2)}, u32[]{:S(2)}) collective-permute-start(bf16[8,2,16,1024]{3,2,1,0:T(8,128)(2,1)S(1)} %get-tuple-element.76), channel_id=1, source_target_pairs={{0,8},{8,0},{1,9},{9,1},{2,10},{10,2},{3,11},{11,3},{4,12},{12,4},... | collective-permute-start | bytes 1572872 | tf_op jit(solution)/shard_map/ppermute | solution.py:23
  61.6 31.0 %all-to-all-start.1 = ((bf16[8,64,1024]{2,1,0:T(8,128)(2,1)}), bf16[8,64,1024]{2,1,0:T(8,128)(2,1)S(1)}, u32[]{:S(2)}, u32[]{:S(2)}) async-start(bf16[8,64,1024]{2,1,0:T(8,128)(2,1)} %bitcast.129), calls=%async_computation.1 | async-start | bytes 2097152 | tf_op jit(solution)/shard_map/all_to_all | solution.py:31
  66.6 38.0 %copy-start.11 = (bf16[256,1024]{1,0:T(8,128)(2,1)S(1)}, bf16[256,1024]{1,0:T(8,128)(2,1)}, u32[]{:S(2)}) copy-start(bf16[256,1024]{1,0:T(8,128)(2,1)} %copy-done.10) | copy-start | bytes 1572868
  66.6 23.0 %collective-permute-start.6 = (bf16[256,1024]{1,0:T(8,128)(2,1)}, bf16[256,1024]{1,0:T(8,128)(2,1)}, u32[]{:S(2)}, u32[]{:S(2)}) collective-permute-start(bf16[256,1024]{1,0:T(8,128)(2,1)} %copy-done.13), channel_id=1, source_target_pairs={{0,4},{4,256},{256,260},{260,0},{1,5},{5,257},{257,261},{261,1},{2... | collective-permute-start | bytes 1572872 | tf_op jit(solution)/shard_map/ppermute | solution.py:27
  70.1 22.5 %collective-permute-start.7 = (bf16[256,1024]{1,0:T(8,128)(2,1)}, bf16[256,1024]{1,0:T(8,128)(2,1)}, u32[]{:S(2)}, u32[]{:S(2)}) collective-permute-start(bf16[256,1024]{1,0:T(8,128)(2,1)} %copy-done.14), channel_id=1, source_target_pairs={{0,260},{4,0},{256,4},{260,256},{1,261},{5,1},{257,5},{261,257},{2... | collective-permute-start | bytes 1572872 | tf_op jit(solution)/shard_map/ppermute | solution.py:27
  92.8 13.1 %copy-start.1 = (f32[64,1024]{1,0:T(8,128)}, f32[64,1024]{1,0:T(8,128)S(1)}, u32[]{:S(2)}) copy-start(f32[64,1024]{1,0:T(8,128)S(1)} %convert_reduce_fusion) | copy-start | bytes 786436
  93.8 10.8 %collective-permute-start.8 = (bf16[256,1024]{1,0:T(8,128)(2,1)}, bf16[256,1024]{1,0:T(8,128)(2,1)S(1)}, u32[]{:S(2)}, u32[]{:S(2)}) collective-permute-start(bf16[256,1024]{1,0:T(8,128)(2,1)} %collective-permute-done.6), channel_id=1, source_target_pairs={{0,8},{8,0},{1,9},{9,1},{2,10},{10,2},{3,11},{11,3},{4,12},{12,4},... | collective-permute-start | bytes 1572872 | tf_op jit(solution)/shard_map/ppermute | solution.py:23
  96.2 17.8 %all-to-all-start.2 = ((bf16[32,16,512]{2,1,0:T(8,128)(2,1)}), bf16[32,16,512]{2,1,0:T(8,128)(2,1)}, u32[]{:S(2)}, u32[]{:S(2)}) async-start(bf16[32,16,512]{2,1,0:T(8,128)(2,1)} %bitcast.16), calls=%async_computation.2 | async-start | bytes 1048576 | tf_op jit(solution)/shard_map/all_to_all | solution.py:31
  102.4 4.7 %collective-permute-start.9 = (bf16[256,1024]{1,0:T(8,128)(2,1)}, bf16[256,1024]{1,0:T(8,128)(2,1)S(1)}, u32[]{:S(2)}, u32[]{:S(2)}) collective-permute-start(bf16[256,1024]{1,0:T(8,128)(2,1)} %collective-permute-done.7), channel_id=1, source_target_pairs={{0,8},{8,0},{1,9},{9,1},{2,10},{10,2},{3,11},{11,3},{4,12},{12,4},... | collective-permute-start | bytes 1572872 | tf_op jit(solution)/shard_map/ppermute | solution.py:23
  106.5 1.0 copy-start.8
  114.0 1.8 copy-start
  117.0 12.3 %all-to-all-start.3 = ((bf16[4,32,1024]{2,1,0:T(8,128)(2,1)}), bf16[4,32,1024]{2,1,0:T(8,128)(2,1)}, u32[]{:S(2)}, u32[]{:S(2)}) async-start(bf16[4,32,1024]{2,1,0:T(8,128)(2,1)} %bitcast.38), calls=%async_computation.3 | async-start | bytes 524288 | tf_op jit(solution)/shard_map/all_to_all | solution.py:31
  122.8 3.6 %collective-permute-start.10 = (bf16[2,128,256]{2,1,0:T(8,128)(2,1)S(1)}, bf16[2,128,256]{2,1,0:T(8,128)(2,1)S(1)}, u32[]{:S(2)}, u32[]{:S(2)}) collective-permute-start(bf16[2,128,256]{2,1,0:T(8,128)(2,1)S(1)} %get-tuple-element.84), channel_id=1, source_target_pairs={{0,8},{8,0},{1,9},{9,1},{2,10},{10,2},{3,11},{11,3},{4,12},{12,4},... | collective-permute-start | bytes 393224 | tf_op jit(solution)/shard_map/ppermute | solution.py:23
  131.0 27.4 %all-to-all-start.4 = ((bf16[4,32,1024]{2,1,0:T(8,128)(2,1)}), bf16[4,32,1024]{2,1,0:T(8,128)(2,1)}, u32[]{:S(2)}, u32[]{:S(2)}) async-start(bf16[4,32,1024]{2,1,0:T(8,128)(2,1)} %broadcast_in_dim.46), calls=%async_computation.4 | async-start | bytes 524288 | tf_op jit(solution)/shard_map/all_to_all | solution.py:31
  141.9 7.2 %collective-permute-start.11 = (bf16[2,128,256]{2,1,0:T(8,128)(2,1)S(1)}, bf16[2,128,256]{2,1,0:T(8,128)(2,1)S(1)}, u32[]{:S(2)}, u32[]{:S(2)}) collective-permute-start(bf16[2,128,256]{2,1,0:T(8,128)(2,1)S(1)} %slice_bitcast_fusion.2), channel_id=1, source_target_pairs={{0,256},{256,0},{1,257},{257,1},{2,258},{258,2},{3,259},{259,3},{4... | collective-permute-start | bytes 393224 | tf_op jit(solution)/shard_map/ppermute | solution.py:23
  168.6 23.9 %copy-start.2 = (f32[64,1024]{1,0:T(8,128)S(1)}, f32[64,1024]{1,0:T(8,128)}, u32[]{:S(2)}) copy-start(f32[64,1024]{1,0:T(8,128)} %copy-done.1) | copy-start | bytes 786436
  169.4 14.3 %collective-permute-start.12 = (bf16[128,1024]{1,0:T(8,128)(2,1)S(1)}, bf16[128,1024]{1,0:T(8,128)(2,1)S(1)}, u32[]{:S(2)}, u32[]{:S(2)}) collective-permute-start(bf16[128,1024]{1,0:T(8,128)(2,1)S(1)} %bitcast.124), channel_id=1, source_target_pairs={{0,256},{256,0},{1,257},{257,1},{2,258},{258,2},{3,259},{259,3},{4... | collective-permute-start | bytes 786440 | tf_op jit(solution)/shard_map/ppermute | solution.py:23
  173.6 18.9 %all-to-all-start.6 = ((bf16[32,16,256]{2,1,0:T(8,128)(2,1)}), bf16[32,16,256]{2,1,0:T(8,128)(2,1)S(1)}, u32[]{:S(2)}, u32[]{:S(2)}) async-start(bf16[32,16,256]{2,1,0:T(8,128)(2,1)} %bitcast.50), calls=%async_computation.6 | async-start | bytes 524288 | tf_op jit(solution)/shard_map/all_to_all | solution.py:31
  193.4 13.7 %all-to-all-start.7 = ((bf16[8,64,512]{2,1,0:T(8,128)(2,1)}), bf16[8,64,512]{2,1,0:T(8,128)(2,1)S(1)}, u32[]{:S(2)}, u32[]{:S(2)}) async-start(bf16[8,64,512]{2,1,0:T(8,128)(2,1)} %broadcast_in_dim.48), calls=%async_computation.7 | async-start | bytes 1048576 | tf_op jit(solution)/shard_map/all_to_all | solution.py:31
  197.0 11.0 %copy-start.6 = (bf16[1024,256]{1,0:T(8,128)(2,1)S(1)}, bf16[1024,256]{1,0:T(8,128)(2,1)}, u32[]{:S(2)}) copy-start(bf16[1024,256]{1,0:T(8,128)(2,1)} %param.18) | copy-start | bytes 1572868
  197.0 11.0 %copy-start.7 = (bf16[1024,256]{1,0:T(8,128)(2,1)S(1)}, bf16[1024,256]{1,0:T(8,128)(2,1)}, u32[]{:S(2)}) copy-start(bf16[1024,256]{1,0:T(8,128)(2,1)} %param.17) | copy-start | bytes 1572868
  197.0 12.3 %collective-permute-start.13 = (bf16[2,128,1024]{2,1,0:T(8,128)(2,1)S(1)}, bf16[2,128,1024]{2,1,0:T(8,128)(2,1)}, u32[]{:S(2)}, u32[]{:S(2)}) collective-permute-start(bf16[2,128,1024]{2,1,0:T(8,128)(2,1)S(1)} %pad_maximum_fusion.4), channel_id=1, source_target_pairs={{0,8},{8,0},{1,9},{9,1},{2,10},{10,2},{3,11},{11,3},{4,12},{12,4},... | collective-permute-start | bytes 1572872 | tf_op jit(solution)/shard_map/ppermute | solution.py:23
  207.9 1.4 copy-start.9
  207.9 1.4 copy-start.12

commit v4 on v1

v4 whole, which is shorter than its diff:
```python
import jax
import jax.numpy as jnp
from jax import lax
from jax.sharding import Mesh, PartitionSpec as P

D = 8192
HID = 16384
BF16 = jnp.bfloat16
F32 = jnp.float32
DP = ("yh", "zh", "zl", "c")
TP = ("yl", "x")
NEAR = ("c", "yl", "x")


def kept(weight, mask):
    rows, cols = weight.shape
    wide = jnp.repeat(mask.astype(BF16), cols // mask.shape[1], axis=1)
    blocks = weight.reshape(mask.shape[0], rows // mask.shape[0], cols)
    return (blocks * wide[:, None, :]).reshape(rows, cols)


def swap(x, axis):
    return lax.ppermute(x, axis, [(0, 1), (1, 0)])


def exchange(pieces, axes):
    return lax.all_to_all(pieces, axes, 0, 0, tiled=True)


def together(arrays):
    return lax.optimization_barrier(arrays)


def copies(x, n):
    return jnp.broadcast_to(x[None], (n,) + x.shape)


def total(pieces, axis=0):
    return jnp.sum(pieces.astype(F32), axis=axis)


def in_order(own, other, axis):
    first = lax.axis_index(axis) == 0
    return jnp.where(first, own, other), jnp.where(first, other, own)


def dot(a, b, dims=((1,), (0,))):
    return lax.dot_general(a, b, (dims, ((), ())), preferred_element_type=F32)


def on_device(
    tokens,
    gate_weight,
    up_weight,
    down_weight,
    gate_mask,
    up_mask,
    down_mask,
    probe_gate,
    probe_up,
    probe_down,
):
    width = gate_weight.shape[1]
    feats = tokens.shape[1]

    tok0 = exchange(copies(tokens, 16), ("zl", "zh")).reshape(8, 16, feats)

    kept_gate = kept(gate_weight, gate_mask)
    kept_up = kept(up_weight, up_mask)
    kept_down = kept(down_weight, down_mask)
    stacked = jnp.concatenate([kept_gate, kept_up, probe_gate, probe_up], axis=1)
    down = jnp.concatenate([kept_down, probe_down * HID**-0.5], axis=0)
    stacked0, stacked1 = in_order(stacked, swap(stacked, "c"), "c")
    down0, down1 = in_order(down, swap(down, "c"), "c")
    tok0, stacked0, stacked1, down0, down1 = together((tok0, stacked0, stacked1, down0, down1))

    pair = jnp.stack([tok0, swap(tok0, "yh")], axis=1).reshape(-1, feats)
    partial = jnp.stack([dot(pair, stacked0).astype(BF16), dot(pair, stacked1).astype(BF16)])
    partial, pair = together((partial, pair))
    pre = exchange(partial.reshape(16, -1, 4 * width), NEAR)
    pre, pair2 = together((pre, swap(pair, "c")))
    pre = total(pre.reshape(2, 8, -1, 4 * width), 1).reshape(-1, 4 * width)

    gate = pre[:, :width]
    up = pre[:, width : 2 * width]
    tangent_gate = pre[:, 2 * width : 3 * width] * D**-0.5
    tangent_up = pre[:, 3 * width :] * D**-0.5
    sig = jax.nn.sigmoid(gate)
    act = gate * sig
    slope = sig * (1.0 + gate * (1.0 - sig))
    hid = (act * up).astype(BF16)
    tan = (slope * tangent_gate * up + act * tangent_up).astype(BF16)
    both = jnp.concatenate([tan, hid], axis=1).reshape(2, 1, 32, 2 * width)
    both = jnp.broadcast_to(both, (2, 8, 32, 2 * width)).reshape(16, 32, 2 * width)
    both = exchange(both, NEAR).reshape(2, 256, 2 * width)

    term = dot(
        jnp.concatenate([both[0], both[1]], axis=1), jnp.concatenate([down0, down1], axis=0)
    )
    term = term.astype(BF16).reshape(4, 2, 2, 16, feats)
    term = jnp.stack(in_order(term[:, :, 0], term[:, :, 1], "yh"), axis=1)
    hid0, hid1 = in_order(both[0, :, width:], both[1, :, width:], "c")
    term, hid0, hid1 = together((term.reshape(8, 32, feats), hid0, hid1))
    term = exchange(term, ("zl", "yh"))
    term, hid1 = together((term, swap(hid1, "c")))
    chunk = exchange(copies(total(term).astype(BF16), 4), "zh")
    chunk = exchange(copies(total(chunk).astype(BF16), 8), ("zl", "yh"))
    chunk = chunk.reshape(4, 2, 2, 16, feats)
    out0 = jnp.stack(in_order(chunk[:, 0], chunk[:, 1], "yh"), axis=2).reshape(-1, feats)
    out0 = together(out0)

    back = [dot(out0, d[:width], ((1,), (1,))).astype(BF16) for d in (down0, down1)]
    back = exchange(jnp.stack(back).reshape(16, 32, width), NEAR)
    back = total(back.reshape(2, 8, 32, width), 1).reshape(-1, width)
    bars = jnp.concatenate([(back * up * slope).astype(BF16), (back * act).astype(BF16)], axis=1)
    bars, out0 = together((bars, out0))
    bars = exchange(copies(bars, 8), TP).reshape(-1, 2 * width)
    out1 = swap(out0, "c")

    gathered = in_order(pair.reshape(8, 32, feats), pair2.reshape(8, 32, feats), "c")
    gathered = jnp.stack(gathered, axis=1).reshape(-1, feats)
    factor = gathered.shape[0] ** -0.5
    along = ((0,), (0,))
    grad_down = dot(
        jnp.concatenate([hid0, hid1], axis=0), jnp.concatenate([out0, out1], axis=0), along
    )
    grads = dot(gathered, bars, along)
    fisher_gate = (probe_gate.astype(F32) * grads[:, :width] * factor).astype(BF16)
    fisher_up = (probe_up.astype(F32) * grads[:, width:] * factor).astype(BF16)
    fisher_down = (probe_down.astype(F32) * grad_down * factor).astype(BF16)
    return (fisher_gate, fisher_up, fisher_down)


def solution(mesh):
    fine = Mesh(mesh.devices.reshape(2, 4, 4, 2, 2, 4), DP + TP)
    col = P(TP, DP)
    row = P(DP, TP)
    return jax.shard_map(
        on_device,
        mesh=fine,
        in_specs=(row, col, col, row, col, col, row, col, col, row),
        out_specs=(col, col, row),
        check_vma=False,
    )
```

time: 194 us -> 203 us (1.046)
  blocking collectives: 103 us -> 53.8 us
  waiting for transfers between devices: 35 us -> 55.9 us
  starting transfers between devices: 42.2 us -> 57.3 us
  other arithmetic: 3.54 us -> 18.2 us
  matrix products: 5.56 us -> 11.2 us
    all_to_all x5 -> x3, blocking collectives: 103 us -> 53.8 us  [exchange(): return lax.all_to_all(pieces, axes, 0, 0, tiled=True)]
    all_to_all x2 -> x5, waiting for transfers between devices: 17.7 us -> 49.1 us  [exchange(): return lax.all_to_all(pieces, axes, 0, 0, tiled=True)]
    all_to_all x2 -> x5, starting transfers between devices: 6.99 us -> 35.2 us  [exchange(): return lax.all_to_all(pieces, axes, 0, 0, tiled=True)]
    ppermute x6, starting transfers between devices: 35.3 us -> 22.1 us  [swap(): return lax.ppermute(x, axis, [(0, 1), (1, 0)])]
    ppermute x6, waiting for transfers between devices: 17.3 us -> 6.8 us  [swap(): return lax.ppermute(x, axis, [(0, 1), (1, 0)])]
    select_n x0 -> x7, other arithmetic: none -> 8.77 us  [in_order(): return (jnp.where(first, own, other), jnp.where(first, other, own))]
    dot_general x5 -> x7, matrix products: 5.56 us -> 11.2 us  [dot(): return lax.dot_general(a, b, (dims, ((), ())), preferred_element_type=F32)]
    concatenate x3, other arithmetic: 0.08 us -> 2.65 us  [the longest x1 1.59 us: on_device(): jnp.concatenate([kept_gate, kept_up, probe_gate, probe_up], axis=1)]
  transfers between devices with their start and end apart: 8 -> 11, of which waited for: 7 -> 8; matrix products, arithmetic and copies ran while one was open for 2% -> 6% of each run, Pallas kernels for 0% -> 0%
where the time goes in v4:
time: 203 us; the launch traced here: 202 us
  starting transfers between devices  57.3 us (28%)
  waiting for transfers between devices  55.9 us (28%)
  blocking collectives  53.8 us (27%)
  other arithmetic  18.2 us (9%)
  matrix products  11.2 us (6%)
  local copies, waits for them, and re-layouts  4.07 us (2%)
    all_to_all x3, blocking collectives, exchange(): return lax.all_to_all(pieces, axes, 0, 0, tiled=True)  53.8 us
    all_to_all x5, waiting for transfers between devices, exchange(): return lax.all_to_all(pieces, axes, 0, 0, tiled=True)  49.1 us
    all_to_all x5, starting transfers between devices, exchange(): return lax.all_to_all(pieces, axes, 0, 0, tiled=True)  35.2 us
    ppermute x6, starting transfers between devices, swap(): return lax.ppermute(x, axis, [(0, 1), (1, 0)])  22.1 us
    dot_general x7, matrix products, dot(): return lax.dot_general(a, b, (dims, ((), ())), preferred_element_type=F32)  11.2 us
    select_n x7, other arithmetic, in_order(): return (jnp.where(first, own, other), jnp.where(first, other, own))  8.77 us
    ppermute x6, waiting for transfers between devices, swap(): return lax.ppermute(x, axis, [(0, 1), (1, 0)])  6.8 us
  transfers between devices with their start and end apart: 11, of which 8 were waited for; matrix products, arithmetic and copies ran while one was open for 6% of the time, Pallas kernels for 0%

profile of v4, /device:TPU:1, one launch (start us, length us, event | category | flops | bytes accessed | tf_op | source)
XLA Modules:
  0.0 201.5 jit_solution(1772167989522157117)
XLA Ops:
  0.7 0.8 convert_element_type.72
  1.4 0.1 broadcast_bitcast_fusion.1
  1.5 0.7 convert_element_type.71
  2.2 0.1 broadcast_bitcast_fusion.2
  2.3 1.3 bitcast_multiply_fusion.1
  3.6 0.0 copy-start.10
  3.6 0.0 copy-start.5
  3.6 0.0 copy-start.6
  3.6 1.6 pad_maximum_fusion
  5.2 8.8 %collective-permute-start = (bf16[1024,1024]{1,0:T(8,128)(2,1)}, bf16[1024,1024]{1,0:T(8,128)(2,1)}, u32[]{:S(2)}, u32[]{:S(2)}) collective-permute-start(bf16[1024,1024]{1,0:T(8,128)(2,1)} %pad_maximum_fusion), channel_id=1, source_target_pairs={{0,8},{8,0},{1,9},{9,1},{2,10},{10,2},{3,11},{11,3},{4,12},{12,4},... | collective-permute-start | bytes 6291464 | tf_op jit(solution)/shard_map/ppermute | solution.py:23
  14.0 0.1 broadcast_bitcast_fusion
  14.1 0.0 copy-start.9
  14.1 0.1 bitcast_multiply_fusion
  14.2 1.0 pad_maximum_fusion.1
  15.2 1.9 collective-permute-start.1
  17.2 0.7 broadcast_in_dim.18
  17.9 9.5 %all-to-all-start = ((bf16[16,8,1024]{2,1,0:T(8,128)(2,1)}), bf16[16,8,1024]{2,1,0:T(8,128)(2,1)S(1)}, u32[]{:S(2)}, u32[]{:S(2)}) async-start(bf16[16,8,1024]{2,1,0:T(8,128)(2,1)} %broadcast_in_dim.18), calls=%async_computation | async-start | bytes 524288 | tf_op jit(solution)/shard_map/all_to_all | solution.py:27
  27.4 0.0 collective-permute-done.1
  27.5 3.1 %broadcast_select_fusion.2 = (bf16[512,1024]{1,0:T(8,128)(2,1)}, bf16[512,1024]{1,0:T(8,128)(2,1)}) fusion(bf16[512,1024]{1,0:T(8,128)(2,1)} %collective-permute-done.1, pred[]{:T(512)S(6)} %eq.4, bf16[256,1024]{1,0:T(8,128)(2,1)S(1)} %get-tuple-element.56, bf16[256,1024]{1,0:T(8,128)(2,1)S(1)} %get-tuple-element.55), kind=kLoop, calls=%fused_computation.32 | loop fusion | flops 3145728 | bytes 4194305 | tf_op jit(solution)/shard_map/jit(_where)/select_n | solution.py:44
  30.6 0.0 collective-permute-done
  30.6 3.8 %broadcast_select_fusion = (bf16[1024,1024]{1,0:T(8,128)(2,1)}, bf16[1024,1024]{1,0:T(8,128)(2,1)}) fusion(bf16[1024,1024]{1,0:T(8,128)(2,1)} %collective-permute-done, pred[]{:T(512)S(6)} %eq.4, bf16[1024,256]{1,0:T(8,128)(2,1)S(1)} %copy-done, bf16[1024,256]{1,0:T(8,128)(2,1)S(1)} %copy-done.1, bf16[1024,256]{1,0:T(8,128)(2,1)S(1)} %get-tuple-element.53, ...), kind=kLoop, calls=%fused_computation.6 | loop fusion | flops 10485760 | bytes 8388609 | tf_op jit(solution)/shard_map/jit(_where)/select_n | solution.py:44
  34.4 8.8 %all-to-all-done = bf16[16,8,1024]{2,1,0:T(8,128)(2,1)S(1)} async-done(((bf16[16,8,1024]{2,1,0:T(8,128)(2,1)}), bf16[16,8,1024]{2,1,0:T(8,128)(2,1)S(1)}, u32[]{:S(2)}, u32[]{:S(2)}) %all-to-all-start) | async-done | bytes 262176 | tf_op jit(solution)/shard_map/all_to_all | solution.py:27
  43.2 4.8 %collective-permute-start.2 = (bf16[8,16,1024]{2,1,0:T(8,128)(2,1)S(1)}, bf16[8,16,1024]{2,1,0:T(8,128)(2,1)S(1)}, u32[]{:S(2)}, u32[]{:S(2)}) collective-permute-start(bf16[8,16,1024]{2,1,0:T(8,128)(2,1)S(1)} %bitcast.120), channel_id=1, source_target_pairs={{0,256},{256,0},{1,257},{257,1},{2,258},{258,2},{3,259},{259,3},{4... | collective-permute-start | bytes 786440 | tf_op jit(solution)/shard_map/ppermute | solution.py:23
  48.0 3.8 %collective-permute-done.2 = bf16[8,16,1024]{2,1,0:T(8,128)(2,1)S(1)} collective-permute-done((bf16[8,16,1024]{2,1,0:T(8,128)(2,1)S(1)}, bf16[8,16,1024]{2,1,0:T(8,128)(2,1)S(1)}, u32[]{:S(2)}, u32[]{:S(2)}) %collective-permute-start.2) | collective-permute-done | bytes 262176 | tf_op jit(solution)/shard_map/ppermute | solution.py:23
  51.8 0.1 pad_maximum_fusion.4
  51.9 2.4 %fusion.9 = bf16[1,256,1024]{2,1,0:T(8,128)(2,1)S(1)} fusion(bf16[256,1024]{1,0:T(8,128)(2,1)S(1)} %bitcast.110, bf16[1024,1024]{1,0:T(8,128)(2,1)} %get-tuple-element.20), kind=kOutput, calls=%fused_computation.14 | convolution fusion | flops 537133056 | bytes 3145728 | tf_op jit(solution)/shard_map/dot_general | solution.py:48
  54.3 0.7 fusion.10
  55.0 1.1 pad_maximum_fusion.2
  56.2 8.9 %all-to-all-start.1 = ((bf16[16,32,1024]{2,1,0:T(8,128)(2,1)}), bf16[16,32,1024]{2,1,0:T(8,128)(2,1)S(1)}, u32[]{:S(2)}, u32[]{:S(2)}) async-start(bf16[16,32,1024]{2,1,0:T(8,128)(2,1)} %bitcast.12), calls=%async_computation.1 | async-start | bytes 2097152 | tf_op jit(solution)/shard_map/all_to_all | solution.py:27
  65.1 2.0 collective-permute-start.3
  67.1 1.9 collective-permute-done.3
  69.0 12.3 %all-to-all-done.1 = bf16[16,32,1024]{2,1,0:T(8,128)(2,1)S(1)} async-done(((bf16[16,32,1024]{2,1,0:T(8,128)(2,1)}), bf16[16,32,1024]{2,1,0:T(8,128)(2,1)S(1)}, u32[]{:S(2)}, u32[]{:S(2)}) %all-to-all-start.1) | async-done | bytes 1048608 | tf_op jit(solution)/shard_map/all_to_all | solution.py:27
  81.3 0.2 convert_reduce_fusion
  81.5 0.1 fusion.32
  81.6 0.8 broadcast_in_dim.45
  82.4 3.6 %all-to-all-start.2 = ((bf16[16,32,512]{2,1,0:T(8,128)(2,1)}), bf16[16,32,512]{2,1,0:T(8,128)(2,1)S(1)}, u32[]{:S(2)}, u32[]{:S(2)}) async-start(bf16[16,32,512]{2,1,0:T(8,128)(2,1)} %bitcast.19), calls=%async_computation.2 | async-start | bytes 1048576 | tf_op jit(solution)/shard_map/all_to_all | solution.py:27
  86.0 10.6 %all-to-all-done.2 = bf16[16,32,512]{2,1,0:T(8,128)(2,1)S(1)} async-done(((bf16[16,32,512]{2,1,0:T(8,128)(2,1)}), bf16[16,32,512]{2,1,0:T(8,128)(2,1)S(1)}, u32[]{:S(2)}, u32[]{:S(2)}) %all-to-all-start.2) | async-done | bytes 524320 | tf_op jit(solution)/shard_map/all_to_all | solution.py:27
  96.6 0.7 select_bitcast_fusion.2
  97.3 2.0 fusion.6
  99.4 0.8 pad_maximum_fusion.5
  100.2 9.6 %all-to-all-start.3 = ((bf16[8,32,1024]{2,1,0:T(8,128)(2,1)}), bf16[8,32,1024]{2,1,0:T(8,128)(2,1)S(1)}, u32[]{:S(2)}, u32[]{:S(2)}) async-start(bf16[8,32,1024]{2,1,0:T(8,128)(2,1)} %bitcast.26), calls=%async_computation.3 | async-start | bytes 1048576 | tf_op jit(solution)/shard_map/all_to_all | solution.py:27
  109.9 2.4 %collective-permute-start.4 = (bf16[256,256]{1,0:T(8,128)(2,1)S(1)}, bf16[256,256]{1,0:T(8,128)(2,1)}, u32[]{:S(2)}, u32[]{:S(2)}) collective-permute-start(bf16[256,256]{1,0:T(8,128)(2,1)S(1)} %get-tuple-element.29), channel_id=1, source_target_pairs={{0,8},{8,0},{1,9},{9,1},{2,10},{10,2},{3,11},{11,3},{4,12},{12,4},... | collective-permute-start | bytes 393224 | tf_op jit(solution)/shard_map/ppermute | solution.py:23
  112.3 1.1 collective-permute-done.4
  113.4 10.5 %all-to-all-done.3 = bf16[8,32,1024]{2,1,0:T(8,128)(2,1)S(1)} async-done(((bf16[8,32,1024]{2,1,0:T(8,128)(2,1)}), bf16[8,32,1024]{2,1,0:T(8,128)(2,1)S(1)}, u32[]{:S(2)}, u32[]{:S(2)}) %all-to-all-start.3) | async-done | bytes 524320 | tf_op jit(solution)/shard_map/all_to_all | solution.py:27
  123.9 0.1 reduce_sum.43
  124.0 17.0 %all_to_all.40 = bf16[4,32,1024]{2,1,0:T(8,128)(2,1)S(1)} all-to-all(bf16[4,32,1024]{2,1,0:T(8,128)(2,1)S(1)} %broadcast_in_dim.46), channel_id=1, replica_groups=mesh['yh'=2,'zh'=4,'zl'=4,'c'=2,'yl'=2,'x'=4] {'zh'}, dimensions={0} | all-to-all | bytes 524288 | tf_op jit(solution)/shard_map/all_to_all | solution.py:27
  141.0 0.1 broadcast_in_dim.47
  141.1 23.2 %all_to_all.41 = bf16[8,32,1024]{2,1,0:T(8,128)(2,1)S(1)} all-to-all(bf16[8,32,1024]{2,1,0:T(8,128)(2,1)S(1)} %broadcast_in_dim.47), channel_id=1, replica_groups=mesh['yh'=2,'zh'=4,'zl'=4,'c'=2,'yl'=2,'x'=4] {'zl','yh'}, dimensions={0} | all-to-all | bytes 1048576 | tf_op jit(solution)/shard_map/all_to_all | solution.py:27
  164.4 0.1 pad_maximum_fusion.6
  164.5 0.8 copy.38
  165.3 0.4 copy-done.4
  165.7 1.4 fusion.11
  167.1 1.4 fusion.12
  168.5 13.6 %all_to_all.42 = bf16[16,32,256]{2,1,0:T(8,128)(2,1)S(1)} all-to-all(bf16[16,32,256]{2,1,0:T(8,128)(2,1)S(1)} %bitcast.119), channel_id=1, replica_groups=mesh['yh'=2,'zh'=4,'zl'=4,'c'=2,'yl'=2,'x'=4] {'c','yl','x'}, dimensions={0} | all-to-all | bytes 524288 | tf_op jit(solution)/shard_map/all_to_all | solution.py:27
  182.3 0.8 broadcast_in_dim.48
  183.1 3.5 %all-to-all-start.7 = ((bf16[8,64,512]{2,1,0:T(8,128)(2,1)}), bf16[8,64,512]{2,1,0:T(8,128)(2,1)S(1)}, u32[]{:S(2)}, u32[]{:S(2)}) async-start(bf16[8,64,512]{2,1,0:T(8,128)(2,1)} %broadcast_in_dim.48), calls=%async_computation.7 | async-start | bytes 1048576 | tf_op jit(solution)/shard_map/all_to_all | solution.py:27
  186.6 1.1 broadcast_select_fusion.5
  187.8 0.1 pad_maximum_fusion.3
  187.9 2.1 %collective-permute-start.5 = (bf16[256,1024]{1,0:T(8,128)(2,1)}, bf16[256,1024]{1,0:T(8,128)(2,1)}, u32[]{:S(2)}, u32[]{:S(2)}) collective-permute-start(bf16[256,1024]{1,0:T(8,128)(2,1)} %bitcast.36), channel_id=1, source_target_pairs={{0,8},{8,0},{1,9},{9,1},{2,10},{10,2},{3,11},{11,3},{4,12},{12,4},... | collective-permute-start | bytes 1572872 | tf_op jit(solution)/shard_map/ppermute | solution.py:23
  190.0 6.8 %all-to-all-done.7 = bf16[8,64,512]{2,1,0:T(8,128)(2,1)S(1)} async-done(((bf16[8,64,512]{2,1,0:T(8,128)(2,1)}), bf16[8,64,512]{2,1,0:T(8,128)(2,1)S(1)}, u32[]{:S(2)}, u32[]{:S(2)}) %all-to-all-start.7) | async-done | bytes 524320 | tf_op jit(solution)/shard_map/all_to_all | solution.py:27
  196.9 0.7 fusion.42
  197.6 0.0 copy-start.7
  197.6 1.3 fusion.14
  199.0 2.5 %fusion.5 = bf16[256,1024]{1,0:T(8,128)(2,1)} fusion(bf16[256,1024]{1,0:T(8,128)(2,1)} %collective-permute-done.5, bf16[256,1024]{1,0:T(8,128)(2,1)} %bitcast.36, bf16[256,1024]{1,0:T(8,128)(2,1)S(1)} %copy-done.7, bf16[256,256]{1,0:T(8,128)(2,1)} %collective-permute-done.4, bf16[256,256]{1,0:T(8,128)(2,1)S(1)} %copy-done.8), kind=kOutput, calls=%fused_computation.10 | convolution fusion | flops 272105472 | bytes 2359296 | tf_op jit(solution)/shard_map/dot_general | solution.py:48
  (30 shorter events, 0.4 us)
Async XLA Ops:
  0.6 2.9 %copy-start.1 = (bf16[1024,256]{1,0:T(8,128)(2,1)S(1)}, bf16[1024,256]{1,0:T(8,128)(2,1)}, u32[]{:S(2)}) copy-start(bf16[1024,256]{1,0:T(8,128)(2,1)} %param.17) | copy-start | bytes 1572868
  0.6 2.9 %copy-start = (bf16[1024,256]{1,0:T(8,128)(2,1)S(1)}, bf16[1024,256]{1,0:T(8,128)(2,1)}, u32[]{:S(2)}) copy-start(bf16[1024,256]{1,0:T(8,128)(2,1)} %param.18) | copy-start | bytes 1572868
  3.6 10.4 %copy-start.10 = (s32[2,8]{1,0:T(2,128)S(1)}, s32[2,8]{1,0:T(2,128)}, u32[]{:S(2)}) copy-start(s32[2,8]{1,0:T(2,128)} %param.16) | copy-start | bytes 196
  3.6 10.5 %copy-start.5 = (bf16[256,1024]{1,0:T(8,128)(2,1)S(1)}, bf16[256,1024]{1,0:T(8,128)(2,1)}, u32[]{:S(2)}) copy-start(bf16[256,1024]{1,0:T(8,128)(2,1)} %param.13) | copy-start | bytes 1572868
  3.6 10.5 %copy-start.6 = (bf16[256,1024]{1,0:T(8,128)(2,1)S(1)}, bf16[256,1024]{1,0:T(8,128)(2,1)}, u32[]{:S(2)}) copy-start(bf16[256,1024]{1,0:T(8,128)(2,1)} %param.19) | copy-start | bytes 1572868
  5.2 25.4 %collective-permute-start = (bf16[1024,1024]{1,0:T(8,128)(2,1)}, bf16[1024,1024]{1,0:T(8,128)(2,1)}, u32[]{:S(2)}, u32[]{:S(2)}) collective-permute-start(bf16[1024,1024]{1,0:T(8,128)(2,1)} %pad_maximum_fusion), channel_id=1, source_target_pairs={{0,8},{8,0},{1,9},{9,1},{2,10},{10,2},{3,11},{11,3},{4,12},{12,4},... | collective-permute-start | bytes 6291464 | tf_op jit(solution)/shard_map/ppermute | solution.py:23
  14.1 3.1 %copy-start.9 = (bf16[8,1024]{1,0:T(8,128)(2,1)S(1)}, bf16[8,1024]{1,0:T(8,128)(2,1)}, u32[]{:S(2)}) copy-start(bf16[8,1024]{1,0:T(8,128)(2,1)} %param.10) | copy-start | bytes 49156
  15.2 12.2 %collective-permute-start.1 = (bf16[512,1024]{1,0:T(8,128)(2,1)}, bf16[512,1024]{1,0:T(8,128)(2,1)}, u32[]{:S(2)}, u32[]{:S(2)}) collective-permute-start(bf16[512,1024]{1,0:T(8,128)(2,1)} %pad_maximum_fusion.1), channel_id=1, source_target_pairs={{0,8},{8,0},{1,9},{9,1},{2,10},{10,2},{3,11},{11,3},{4,12},{12,4},... | collective-permute-start | bytes 3145736 | tf_op jit(solution)/shard_map/ppermute | solution.py:23
  17.9 25.3 %all-to-all-start = ((bf16[16,8,1024]{2,1,0:T(8,128)(2,1)}), bf16[16,8,1024]{2,1,0:T(8,128)(2,1)S(1)}, u32[]{:S(2)}, u32[]{:S(2)}) async-start(bf16[16,8,1024]{2,1,0:T(8,128)(2,1)} %broadcast_in_dim.18), calls=%async_computation | async-start | bytes 524288 | tf_op jit(solution)/shard_map/all_to_all | solution.py:27
  43.2 8.6 %collective-permute-start.2 = (bf16[8,16,1024]{2,1,0:T(8,128)(2,1)S(1)}, bf16[8,16,1024]{2,1,0:T(8,128)(2,1)S(1)}, u32[]{:S(2)}, u32[]{:S(2)}) collective-permute-start(bf16[8,16,1024]{2,1,0:T(8,128)(2,1)S(1)} %bitcast.120), channel_id=1, source_target_pairs={{0,256},{256,0},{1,257},{257,1},{2,258},{258,2},{3,259},{259,3},{4... | collective-permute-start | bytes 786440 | tf_op jit(solution)/shard_map/ppermute | solution.py:23
  51.8 2.5 %copy-start.2 = (bf16[1024,1024]{1,0:T(8,128)(2,1)S(1)}, bf16[1024,1024]{1,0:T(8,128)(2,1)}, u32[]{:S(2)}) copy-start(bf16[1024,1024]{1,0:T(8,128)(2,1)} %get-tuple-element.21) | copy-start | bytes 6291460
  56.2 25.1 %all-to-all-start.1 = ((bf16[16,32,1024]{2,1,0:T(8,128)(2,1)}), bf16[16,32,1024]{2,1,0:T(8,128)(2,1)S(1)}, u32[]{:S(2)}, u32[]{:S(2)}) async-start(bf16[16,32,1024]{2,1,0:T(8,128)(2,1)} %bitcast.12), calls=%async_computation.1 | async-start | bytes 2097152 | tf_op jit(solution)/shard_map/all_to_all | solution.py:27
  65.1 3.9 %collective-permute-start.3 = (bf16[256,1024]{1,0:T(8,128)(2,1)S(1)}, bf16[256,1024]{1,0:T(8,128)(2,1)}, u32[]{:S(2)}, u32[]{:S(2)}) collective-permute-start(bf16[256,1024]{1,0:T(8,128)(2,1)S(1)} %bitcast.112), channel_id=1, source_target_pairs={{0,8},{8,0},{1,9},{9,1},{2,10},{10,2},{3,11},{11,3},{4,12},{12,4},... | collective-permute-start | bytes 1572872 | tf_op jit(solution)/shard_map/ppermute | solution.py:23
  81.5 15.9 %copy-start.3 = (bf16[512,1024]{1,0:T(8,128)(2,1)S(1)}, bf16[512,1024]{1,0:T(8,128)(2,1)}, u32[]{:S(2)}) copy-start(bf16[512,1024]{1,0:T(8,128)(2,1)} %get-tuple-element.27) | copy-start | bytes 3145732
  82.4 14.2 %all-to-all-start.2 = ((bf16[16,32,512]{2,1,0:T(8,128)(2,1)}), bf16[16,32,512]{2,1,0:T(8,128)(2,1)S(1)}, u32[]{:S(2)}, u32[]{:S(2)}) async-start(bf16[16,32,512]{2,1,0:T(8,128)(2,1)} %bitcast.19), calls=%async_computation.2 | async-start | bytes 1048576 | tf_op jit(solution)/shard_map/all_to_all | solution.py:27
  100.2 23.7 %all-to-all-start.3 = ((bf16[8,32,1024]{2,1,0:T(8,128)(2,1)}), bf16[8,32,1024]{2,1,0:T(8,128)(2,1)S(1)}, u32[]{:S(2)}, u32[]{:S(2)}) async-start(bf16[8,32,1024]{2,1,0:T(8,128)(2,1)} %bitcast.26), calls=%async_computation.3 | async-start | bytes 1048576 | tf_op jit(solution)/shard_map/all_to_all | solution.py:27
  109.9 3.5 %collective-permute-start.4 = (bf16[256,256]{1,0:T(8,128)(2,1)S(1)}, bf16[256,256]{1,0:T(8,128)(2,1)}, u32[]{:S(2)}, u32[]{:S(2)}) collective-permute-start(bf16[256,256]{1,0:T(8,128)(2,1)S(1)} %get-tuple-element.29), channel_id=1, source_target_pairs={{0,8},{8,0},{1,9},{9,1},{2,10},{10,2},{3,11},{11,3},{4,12},{12,4},... | collective-permute-start | bytes 393224 | tf_op jit(solution)/shard_map/ppermute | solution.py:23
  164.3 1.4 copy-start.4
  183.1 13.7 %all-to-all-start.7 = ((bf16[8,64,512]{2,1,0:T(8,128)(2,1)}), bf16[8,64,512]{2,1,0:T(8,128)(2,1)S(1)}, u32[]{:S(2)}, u32[]{:S(2)}) async-start(bf16[8,64,512]{2,1,0:T(8,128)(2,1)} %broadcast_in_dim.48), calls=%async_computation.7 | async-start | bytes 1048576 | tf_op jit(solution)/shard_map/all_to_all | solution.py:27
  187.9 11.1 %collective-permute-start.5 = (bf16[256,1024]{1,0:T(8,128)(2,1)}, bf16[256,1024]{1,0:T(8,128)(2,1)}, u32[]{:S(2)}, u32[]{:S(2)}) collective-permute-start(bf16[256,1024]{1,0:T(8,128)(2,1)} %bitcast.36), channel_id=1, source_target_pairs={{0,8},{8,0},{1,9},{9,1},{2,10},{10,2},{3,11},{11,3},{4,12},{12,4},... | collective-permute-start | bytes 1572872 | tf_op jit(solution)/shard_map/ppermute | solution.py:23
  197.6 1.4 copy-start.7
  197.6 1.4 copy-start.8

commit v5 on v1

v5 whole, which is shorter than its diff:
```python
import jax
import jax.numpy as jnp
from jax import lax
from jax.experimental import pallas as pl
from jax.experimental.pallas import tpu as pltpu
from jax.sharding import Mesh, PartitionSpec as P

D = 8192
HID = 16384
TOKENS = 512
BF16 = jnp.bfloat16
F32 = jnp.float32
DP = ("yh", "zh", "zl", "c")
TP = ("yl", "x")
NEAR = ("c", "yl", "x")


def swap(x, axis):
    return lax.ppermute(x, axis, [(0, 1), (1, 0)])


def exchange(pieces, axes):
    return lax.all_to_all(pieces, axes, 0, 0, tiled=True)


def dot(a, b, dims=((1,), (0,))):
    return lax.dot_general(a, b, (dims, ((), ())), preferred_element_type=F32)


def local(kernel, outs, *args, scalars=0):
    spec = pl.BlockSpec(memory_space=pltpu.VMEM)
    small = pl.BlockSpec(memory_space=pltpu.SMEM)
    return pl.pallas_call(
        kernel,
        out_shape=[jax.ShapeDtypeStruct(shape, dtype) for shape, dtype in outs],
        in_specs=[small] * scalars + [spec] * (len(args) - scalars),
        out_specs=[spec] * len(outs),
        compiler_params=pltpu.CompilerParams(vmem_limit_bytes=32 * 2**20),
    )(*args)


def copies_kernel(x_ref, o_ref):
    for i in range(o_ref.shape[0]):
        o_ref[i] = x_ref[...]


def keep(mask_ref, w_ref, o_ref):
    for i in range(mask_ref.shape[0]):
        for j in range(mask_ref.shape[1]):
            block = (slice(i * 128, (i + 1) * 128), slice(j * 128, (j + 1) * 128))
            o_ref[block] = (w_ref[block].astype(F32) * mask_ref[i, j].astype(F32)).astype(BF16)


def kept_kernel(gmask_ref, umask_ref, gate_ref, up_ref, kgate_ref, kup_ref):
    keep(gmask_ref, gate_ref, kgate_ref)
    keep(umask_ref, up_ref, kup_ref)


def pre_kernel(
    dmask_ref,
    own_ref,
    other_ref,
    gate_ref,
    up_ref,
    pgate_ref,
    pup_ref,
    down_ref,
    pdown_ref,
    o_ref,
    down2_ref,
):
    width = gate_ref.shape[1]
    keep(dmask_ref, down_ref, down2_ref)
    down2_ref[width:, :] = pdown_ref[...]
    for half, tok_ref in enumerate((own_ref, other_ref)):
        for j, w_ref in enumerate((gate_ref, up_ref, pgate_ref, pup_ref)):
            y = dot(tok_ref[...], w_ref[...]).astype(BF16)
            for r in range(2):
                q = 16 * (2 * half + r)
                o_ref[:, q : q + 16, j * width : (j + 1) * width] = y[
                    r * 128 : (r + 1) * 128
                ].reshape(8, 16, width)


def gate_kernel(x_ref, o_ref, up_slope_ref, act_ref):
    width = act_ref.shape[1]

    def part(j):
        cols = slice(j * width, (j + 1) * width)
        acc = x_ref[0, :, cols].astype(F32)
        for i in range(1, 8):
            acc = acc + x_ref[i, :, cols].astype(F32)
        return acc

    gate = part(0)
    up = part(1)
    tangent_gate = part(2) * D**-0.5
    tangent_up = part(3) * D**-0.5
    sig = jax.nn.sigmoid(gate)
    act = gate * sig
    slope = sig * (1.0 + gate * (1.0 - sig))
    hid = (act * up).astype(BF16)
    tan = (slope * tangent_gate * up + act * tangent_up).astype(BF16)
    c = lax.axis_index("c")
    for r in range(2):
        rows = slice(r * 32, (r + 1) * 32)
        place = c if r == 0 else 1 - c
        for i in range(8):
            o_ref[place, i, :, :width] = tan[rows]
            o_ref[place, i, :, width:] = hid[rows]
    up_slope_ref[...] = up * slope
    act_ref[...] = act


def term_kernel(x_ref, down_ref, down2_ref, o_ref, hid_ref, hid2_ref):
    width = hid_ref.shape[1]
    c = lax.axis_index("c")
    yh = lax.axis_index("yh")

    def rows(src):
        parts = [x_ref[src, :, 16 * r : 16 * r + 16, :].reshape(128, 2 * width) for r in range(2)]
        return jnp.concatenate(parts, axis=0)

    own = rows(c)
    other = rows(1 - c)
    hid_ref[...] = own[:, width:]
    hid2_ref[...] = other[:, width:]
    for j in range(4):
        cols = slice(j * 256, (j + 1) * 256)
        y = dot(own[:, width:], down_ref[width:, cols]) + dot(other[:, width:], down2_ref[width:, cols])
        y = y * HID**-0.5
        y = y + dot(own[:, :width], down_ref[:width, cols])
        y = y + dot(other[:, :width], down2_ref[:width, cols])
        y = y.astype(BF16)
        for r in range(2):
            place = yh if r == 0 else 1 - yh
            o_ref[:, place, :, cols] = y[r * 128 : (r + 1) * 128].reshape(4, 32, 256)


def spread_kernel(x_ref, o_ref):
    acc = x_ref[0].astype(F32)
    for i in range(1, x_ref.shape[0]):
        acc = acc + x_ref[i].astype(F32)
    acc = acc.astype(BF16)
    for i in range(o_ref.shape[0]):
        o_ref[i] = acc


def back_kernel(x_ref, down_ref, down2_ref, o_ref, out_ref):
    width = o_ref.shape[3]
    c = lax.axis_index("c")
    yh = lax.axis_index("yh")
    for r in range(2):
        place = yh if r == 0 else 1 - yh
        out_ref[r * 128 : (r + 1) * 128, :] = x_ref[:, place].reshape(128, x_ref.shape[3])
    for w_ref, place in ((down_ref, c), (down2_ref, 1 - c)):
        y = dot(out_ref[...], w_ref[:width, :], ((1,), (1,))).astype(BF16)
        for r in range(2):
            o_ref[place, :, 16 * r : 16 * r + 16, :] = y[r * 128 : (r + 1) * 128].reshape(
                8, 16, width
            )


def bars_kernel(x_ref, up_slope_ref, act_ref, o_ref):
    width = act_ref.shape[1]
    c = lax.axis_index("c")
    for r in range(2):
        place = c if r == 0 else 1 - c
        rows = slice(r * 32, (r + 1) * 32)
        back = x_ref[place, 0].astype(F32)
        for i in range(1, 8):
            back = back + x_ref[place, i].astype(F32)
        gate_bar = (back * up_slope_ref[rows]).astype(BF16)
        up_bar = (back * act_ref[rows]).astype(BF16)
        for i in range(8):
            o_ref[i, rows, :width] = gate_bar
            o_ref[i, rows, width:] = up_bar


def fisher_kernel(own_ref, other_ref, bars_ref, pgate_ref, pup_ref, gate_ref, up_ref):
    width = gate_ref.shape[1]
    factor = TOKENS**-0.5
    bars = [bars_ref[:, 16 * q : 16 * q + 16, :].reshape(128, 2 * width) for q in range(4)]
    y = dot(own_ref[...], jnp.concatenate(bars[:2], axis=0), ((0,), (0,)))
    y = y + dot(other_ref[...], jnp.concatenate(bars[2:], axis=0), ((0,), (0,)))
    gate_ref[...] = (pgate_ref[...].astype(F32) * y[:, :width] * factor).astype(BF16)
    up_ref[...] = (pup_ref[...].astype(F32) * y[:, width:] * factor).astype(BF16)


def fisher(own, other, bars, probe_gate, probe_up):
    rows, width = probe_gate.shape
    block = 256
    weight = pl.BlockSpec((block, width), lambda i: (i, 0))
    return pl.pallas_call(
        fisher_kernel,
        grid=(rows // block,),
        out_shape=[jax.ShapeDtypeStruct((rows, width), BF16)] * 2,
        in_specs=[
            pl.BlockSpec((own.shape[0], block), lambda i: (0, i)),
            pl.BlockSpec((own.shape[0], block), lambda i: (0, i)),
            pl.BlockSpec(bars.shape, lambda i: (0, 0, 0)),
            weight,
            weight,
        ],
        out_specs=[weight, weight],
        compiler_params=pltpu.CompilerParams(vmem_limit_bytes=32 * 2**20),
    )(own, other, bars, probe_gate, probe_up)


def on_device(
    tokens,
    gate_weight,
    up_weight,
    down_weight,
    gate_mask,
    up_mask,
    down_mask,
    probe_gate,
    probe_up,
    probe_down,
):
    width = gate_weight.shape[1]
    feats = tokens.shape[1]

    (mine,) = local(copies_kernel, [((16, 8, feats), BF16)], tokens)
    tok0 = exchange(mine, ("zl", "zh")).reshape(128, feats)
    kept_gate, kept_up = local(
        kept_kernel,
        [(gate_weight.shape, BF16), (up_weight.shape, BF16)],
        gate_mask,
        up_mask,
        gate_weight,
        up_weight,
        scalars=2,
    )
    pair = jnp.concatenate([tok0, swap(tok0, "yh")], axis=0)
    pair2 = swap(pair, "c")
    partial, down = local(
        pre_kernel,
        [((8, 64, 4 * width), BF16), ((2 * width, feats), BF16)],
        down_mask,
        pair,
        pair2,
        kept_gate,
        kept_up,
        probe_gate,
        probe_up,
        down_weight,
        probe_down,
        scalars=1,
    )
    pre = exchange(partial, TP)
    down2 = swap(down, "c")
    send, up_slope, act = local(
        gate_kernel,
        [((2, 8, 32, 2 * width), BF16), ((64, width), F32), ((64, width), F32)],
        pre,
    )
    both = exchange(send.reshape(16, 32, 2 * width), NEAR).reshape(2, 8, 32, 2 * width)
    term, hid, hid2 = local(
        term_kernel,
        [((4, 2, 32, feats), BF16), ((256, width), BF16), ((256, width), BF16)],
        both,
        down,
        down2,
    )
    term = exchange(term.reshape(8, 32, feats), ("zl", "yh"))
    (chunk,) = local(spread_kernel, [((4, 32, feats), BF16)], term)
    chunk = exchange(chunk, "zh")
    (chunk,) = local(spread_kernel, [((8, 32, feats), BF16)], chunk)
    chunk = exchange(chunk, ("zl", "yh")).reshape(4, 2, 32, feats)
    back, out = local(
        back_kernel, [((2, 8, 32, width), BF16), ((256, feats), BF16)], chunk, down, down2
    )
    back = exchange(back.reshape(16, 32, width), NEAR).reshape(2, 8, 32, width)
    (bars,) = local(bars_kernel, [((8, 64, 2 * width), BF16)], back, up_slope, act)
    bars = exchange(bars, TP)

    grad_down = dot(
        jnp.concatenate([hid, swap(hid2, "c")], axis=0),
        jnp.concatenate([out, swap(out, "c")], axis=0),
        ((0,), (0,)),
    )
    fisher_down = (probe_down.astype(F32) * grad_down * TOKENS**-0.5).astype(BF16)
    fisher_gate, fisher_up = fisher(pair, pair2, bars, probe_gate, probe_up)
    return (fisher_gate, fisher_up, fisher_down)


def solution(mesh):
    fine = Mesh(mesh.devices.reshape(2, 4, 4, 2, 2, 4), DP + TP)
    col = P(TP, DP)
    row = P(DP, TP)
    return jax.shard_map(
        on_device,
        mesh=fine,
        in_specs=(row, col, col, row, col, col, row, col, col, row),
        out_specs=(col, col, row),
        check_vma=False,
    )
```

time: 194 us -> 193 us (level)
  Pallas kernels: 0 us -> 10.5 us
  starting transfers between devices: 42.2 us -> 34.6 us
  other arithmetic: 3.54 us -> 0.03 us
  matrix products: 5.56 us -> 2.56 us
  local copies, waits for them, and re-layouts: 3.39 us -> 5.83 us
  blocking collectives: 103 us -> 105 us
    ppermute x6 -> x5, starting transfers between devices: 35.3 us -> 21.2 us  [swap(): return lax.ppermute(x, axis, [(0, 1), (1, 0)])]
    ppermute x6 -> x5, waiting for transfers between devices: 17.3 us -> 5.34 us  [swap(): return lax.ppermute(x, axis, [(0, 1), (1, 0)])]
    pallas_call x0 -> x10, Pallas kernels: none -> 10.5 us  [the longest x9 8.01 us: local(): pl.pallas_call(kernel, out_shape=[jax.ShapeDtypeStruct(shape, dtype) for...]
    all_to_all x2 -> x3, waiting for transfers between devices: 17.7 us -> 27.7 us  [exchange(): return lax.all_to_all(pieces, axes, 0, 0, tiled=True)]
    all_to_all x2 -> x3, starting transfers between devices: 6.99 us -> 13.3 us  [exchange(): return lax.all_to_all(pieces, axes, 0, 0, tiled=True)]
    unnamed x26 -> x36, local copies, waits for them, and re-layouts: 0.58 us -> 5.83 us
    dot_general x5 -> x1, matrix products: 5.56 us -> 2.56 us  [dot(): return lax.dot_general(a, b, (dims, ((), ())), preferred_element_type=F32)]
    convert_element_type x6 -> x0, other arithmetic: 2.81 us -> none  [the longest x3 1.37 us: kept(): wide = jnp.repeat(mask.astype(BF16), cols // mask.shape[1], axis=1)]
  transfers between devices with their start and end apart: 8 -> 8, of which waited for: 7 -> 6; matrix products, arithmetic and copies ran while one was open for 2% -> 1% of each run, Pallas kernels for 0% -> 2%
where the time goes in v5:
time: 193 us; the launch traced here: 192 us
  blocking collectives  105 us (54%)
  starting transfers between devices  34.6 us (18%)
  waiting for transfers between devices  33.1 us (17%)
  Pallas kernels  10.5 us (5%)
  local copies, waits for them, and re-layouts  5.83 us (3%)
  matrix products  2.56 us (1%)
    all_to_all x5, blocking collectives, exchange(): return lax.all_to_all(pieces, axes, 0, 0, tiled=True)  105 us
    all_to_all x3, waiting for transfers between devices, exchange(): return lax.all_to_all(pieces, axes, 0, 0, tiled=True)  27.7 us
    ppermute x5, starting transfers between devices, swap(): return lax.ppermute(x, axis, [(0, 1), (1, 0)])  21.2 us
    all_to_all x3, starting transfers between devices, exchange(): return lax.all_to_all(pieces, axes, 0, 0, tiled=True)  13.3 us
    pallas_call x9, Pallas kernels, local(): pl.pallas_call(kernel, out_shape=[jax.ShapeDtypeStruct(shape, dtype) for...  8.01 us
    unnamed x36, local copies, waits for them, and re-layouts  5.83 us
    ppermute x5, waiting for transfers between devices, swap(): return lax.ppermute(x, axis, [(0, 1), (1, 0)])  5.34 us
  transfers between devices with their start and end apart: 8, of which 6 were waited for; matrix products, arithmetic and copies ran while one was open for 1% of the time, Pallas kernels for 2%

profile of v5, /device:TPU:1, one launch (start us, length us, event | category | flops | bytes accessed | tf_op | source)
XLA Modules:
  0.0 192.2 jit_solution(13577688567969668096)
XLA Ops:
  0.6 0.0 copy-start.10
  0.6 0.0 copy-start.9
  0.7 0.0 copy-start.12
  0.7 0.8 copy-done.12
  1.5 0.0 copy-start.14
  1.5 0.0 copy-start.15
  1.5 30.9 %all_to_all.40 = bf16[16,8,1024]{2,1,0:T(8,128)(2,1)S(1)} all-to-all(bf16[16,8,1024]{2,1,0:T(8,128)(2,1)S(1)} %shard_map.121), channel_id=1, replica_groups=mesh['yh'=2,'zh'=4,'zl'=4,'c'=2,'yl'=2,'x'=4] {'zl','zh'}, dimensions={0} | all-to-all | bytes 524288 | tf_op jit(solution)/shard_map/all_to_all | solution.py:23
  32.4 0.0 copy-start
  32.4 0.0 copy-start.1
  32.4 0.0 copy-start.13
  32.4 4.9 %collective-permute-start = (bf16[128,1024]{1,0:T(8,128)(2,1)S(1)}, bf16[128,1024]{1,0:T(8,128)(2,1)S(1)}, u32[]{:S(2)}, u32[]{:S(2)}) collective-permute-start(bf16[128,1024]{1,0:T(8,128)(2,1)S(1)} %bitcast.12), channel_id=1, source_target_pairs={{0,256},{256,0},{1,257},{257,1},{2,258},{258,2},{3,259},{259,3},{4... | collective-permute-start | bytes 786440 | tf_op jit(solution)/shard_map/ppermute | solution.py:19
  37.3 3.8 %collective-permute-done = bf16[128,1024]{1,0:T(8,128)(2,1)S(1)} collective-permute-done((bf16[128,1024]{1,0:T(8,128)(2,1)S(1)}, bf16[128,1024]{1,0:T(8,128)(2,1)S(1)}, u32[]{:S(2)}, u32[]{:S(2)}) %collective-permute-start) | collective-permute-done | bytes 262176 | tf_op jit(solution)/shard_map/ppermute | solution.py:19
  41.1 6.2 %collective-permute-start.1 = (bf16[256,1024]{1,0:T(8,128)(2,1)S(1)}, bf16[256,1024]{1,0:T(8,128)(2,1)S(1)}, u32[]{:S(2)}, u32[]{:S(2)}) collective-permute-start(bf16[256,1024]{1,0:T(8,128)(2,1)S(1)} %pad_maximum_fusion.own_ref), channel_id=1, source_target_pairs={{0,8},{8,0},{1,9},{9,1},{2,10},{10,2},{3,11},{11,3},{4,12},{12,4},... | collective-permute-start | bytes 1572872 | tf_op jit(solution)/shard_map/ppermute | solution.py:19
  47.3 0.0 copy-done.14
  47.3 0.1 copy.13.gmask_ref
  47.4 0.0 copy-done.15
  47.4 0.1 copy.14.umask_ref
  47.5 0.0 copy-done.10
  47.5 0.0 copy-done.9
  47.5 0.9 shard_map.122
  48.4 0.5 collective-permute-done.1.other_ref
  48.8 0.0 copy-start.3
  48.8 0.0 copy-done
  48.9 0.0 copy-done.1
  48.9 0.0 copy-done.13
  48.9 0.0 copy-start.6
  48.9 1.2 copy-done.6
  50.1 0.0 copy-start.7
  50.1 1.0 copy-done.7
  51.1 1.9 %shard_map.123 = (bf16[8,64,1024]{2,1,0:T(8,128)(2,1)S(1)}, bf16[512,1024]{1,0:T(8,128)(2,1)S(1)}) custom-call(s32[2,8]{1,0:T(2,128)S(1)} %copy-done.13, bf16[256,1024]{1,0:T(8,128)(2,1)S(1)} %pad_maximum_fusion.own_ref, bf16[256,1024]{1,0:T(8,128)(2,1)S(1)} %collective-permute-done.1.other_ref, bf16[1024,256]{1,0:T(8,128)(2,1)S(1)} %get-tuple-element.17.gate_ref, ...), custom_call_target="tpu_custom_call" | custom-call | tf_op jit(solution)/shard_map/pallas_call | solution.py:33
  53.1 0.0 copy-done.3
  53.1 0.0 copy-start.5
  53.1 1.0 copy-done.5
  54.1 5.0 %all-to-all-start.1 = ((bf16[8,64,1024]{2,1,0:T(8,128)(2,1)}), bf16[8,64,1024]{2,1,0:T(8,128)(2,1)}, u32[]{:S(2)}, u32[]{:S(2)}) async-start(bf16[8,64,1024]{2,1,0:T(8,128)(2,1)} %copy-done.5), calls=%async_computation.1 | async-start | bytes 2097152 | tf_op jit(solution)/shard_map/all_to_all | solution.py:23
  59.1 2.5 %collective-permute-start.2 = (bf16[512,1024]{1,0:T(8,128)(2,1)S(1)}, bf16[512,1024]{1,0:T(8,128)(2,1)S(1)}, u32[]{:S(2)}, u32[]{:S(2)}) collective-permute-start(bf16[512,1024]{1,0:T(8,128)(2,1)S(1)} %get-tuple-element.21.down_ref), channel_id=1, source_target_pairs={{0,8},{8,0},{1,9},{9,1},{2,10},{10,2},{3,11},{11,3},{4,12},{12,4},... | collective-permute-start | bytes 3145736 | tf_op jit(solution)/shard_map/ppermute | solution.py:19
  61.7 13.4 %all-to-all-done.1.x_ref = bf16[8,64,1024]{2,1,0:T(8,128)(2,1)} async-done(((bf16[8,64,1024]{2,1,0:T(8,128)(2,1)}), bf16[8,64,1024]{2,1,0:T(8,128)(2,1)}, u32[]{:S(2)}, u32[]{:S(2)}) %all-to-all-start.1) | async-done | bytes 1048608 | tf_op jit(solution)/shard_map/all_to_all | solution.py:23
  75.1 1.4 shard_map.124
  76.5 0.0 copy-start.11
  76.5 0.8 copy-done.11
  77.3 4.8 %all-to-all-start.2 = ((bf16[16,32,512]{2,1,0:T(8,128)(2,1)}), bf16[16,32,512]{2,1,0:T(8,128)(2,1)}, u32[]{:S(2)}, u32[]{:S(2)}) async-start(bf16[16,32,512]{2,1,0:T(8,128)(2,1)} %bitcast.9), calls=%async_computation.2 | async-start | bytes 1048576 | tf_op jit(solution)/shard_map/all_to_all | solution.py:23
  82.1 0.0 collective-permute-done.2.down2_ref
  82.1 10.7 %all-to-all-done.2 = bf16[16,32,512]{2,1,0:T(8,128)(2,1)} async-done(((bf16[16,32,512]{2,1,0:T(8,128)(2,1)}), bf16[16,32,512]{2,1,0:T(8,128)(2,1)}, u32[]{:S(2)}, u32[]{:S(2)}) %all-to-all-start.2) | async-done | bytes 524320 | tf_op jit(solution)/shard_map/all_to_all | solution.py:23
  92.8 1.8 shard_map.125
  94.5 22.5 %all_to_all.41.x_ref = bf16[8,32,1024]{2,1,0:T(8,128)(2,1)S(1)} all-to-all(bf16[8,32,1024]{2,1,0:T(8,128)(2,1)S(1)} %bitcast.10), channel_id=1, replica_groups=mesh['yh'=2,'zh'=4,'zl'=4,'c'=2,'yl'=2,'x'=4] {'zl','yh'}, dimensions={0} | all-to-all | bytes 1048576 | tf_op jit(solution)/shard_map/all_to_all | solution.py:23
  117.0 0.1 shard_map.126
  117.1 19.8 %all_to_all.42.x_ref = bf16[4,32,1024]{2,1,0:T(8,128)(2,1)S(1)} all-to-all(bf16[4,32,1024]{2,1,0:T(8,128)(2,1)S(1)} %shard_map.126), channel_id=1, replica_groups=mesh['yh'=2,'zh'=4,'zl'=4,'c'=2,'yl'=2,'x'=4] {'zh'}, dimensions={0} | all-to-all | bytes 524288 | tf_op jit(solution)/shard_map/all_to_all | solution.py:23
  136.9 21.4 %all_to_all.43 = bf16[8,32,1024]{2,1,0:T(8,128)(2,1)S(1)} all-to-all(bf16[8,32,1024]{2,1,0:T(8,128)(2,1)S(1)} %shard_map.127), channel_id=1, replica_groups=mesh['yh'=2,'zh'=4,'zl'=4,'c'=2,'yl'=2,'x'=4] {'zl','yh'}, dimensions={0} | all-to-all | bytes 1048576 | tf_op jit(solution)/shard_map/all_to_all | solution.py:23
  158.3 1.1 shard_map.128
  159.4 5.4 %collective-permute-start.4 = (bf16[256,1024]{1,0:T(8,128)(2,1)}, bf16[256,1024]{1,0:T(8,128)(2,1)S(1)}, u32[]{:S(2)}, u32[]{:S(2)}) collective-permute-start(bf16[256,1024]{1,0:T(8,128)(2,1)} %get-tuple-element.30), channel_id=1, source_target_pairs={{0,8},{8,0},{1,9},{9,1},{2,10},{10,2},{3,11},{11,3},{4,12},{12,4},... | collective-permute-start | bytes 1572872 | tf_op jit(solution)/shard_map/ppermute | solution.py:19
  164.8 10.2 %all_to_all.44 = bf16[16,32,256]{2,1,0:T(8,128)(2,1)S(1)} all-to-all(bf16[16,32,256]{2,1,0:T(8,128)(2,1)S(1)} %bitcast.11), channel_id=1, replica_groups=mesh['yh'=2,'zh'=4,'zl'=4,'c'=2,'yl'=2,'x'=4] {'c','yl','x'}, dimensions={0} | all-to-all | bytes 524288 | tf_op jit(solution)/shard_map/all_to_all | solution.py:23
  175.0 0.0 copy-start.8
  175.0 0.8 shard_map.129
  175.9 3.5 %all-to-all-start.7 = ((bf16[8,64,512]{2,1,0:T(8,128)(2,1)}), bf16[8,64,512]{2,1,0:T(8,128)(2,1)S(1)}, u32[]{:S(2)}, u32[]{:S(2)}) async-start(bf16[8,64,512]{2,1,0:T(8,128)(2,1)} %shard_map.129), calls=%async_computation.7 | async-start | bytes 1048576 | tf_op jit(solution)/shard_map/all_to_all | solution.py:23
  179.4 2.1 %collective-permute-start.3 = (bf16[256,256]{1,0:T(8,128)(2,1)S(1)}, bf16[256,256]{1,0:T(8,128)(2,1)S(1)}, u32[]{:S(2)}, u32[]{:S(2)}) collective-permute-start(bf16[256,256]{1,0:T(8,128)(2,1)S(1)} %get-tuple-element.29), channel_id=1, source_target_pairs={{0,8},{8,0},{1,9},{9,1},{2,10},{10,2},{3,11},{11,3},{4,12},{12,4},... | collective-permute-start | bytes 393224 | tf_op jit(solution)/shard_map/ppermute | solution.py:19
  181.5 1.1 collective-permute-done.3
  182.6 0.0 collective-permute-done.4
  182.6 0.0 copy-start.16
  182.6 0.8 copy-done.16
  183.4 0.0 copy-done.8
  183.5 2.6 %fusion.1 = bf16[256,1024]{1,0:T(8,128)(2,1)} fusion(bf16[256,1024]{1,0:T(8,128)(2,1)} %copy-done.16, bf16[256,1024]{1,0:T(8,128)(2,1)} %get-tuple-element.30, bf16[256,1024]{1,0:T(8,128)(2,1)S(1)} %copy-done.8, bf16[256,256]{1,0:T(8,128)(2,1)S(1)} %collective-permute-done.3, bf16[256,256]{1,0:T(8,128)(2,1)S(1)} %get-tuple-element.28), kind=kOutput, calls=%fused_computation.2 | convolution fusion | flops 272105472 | bytes 2359296 | tf_op jit(solution)/shard_map/dot_general | solution.py:27
  186.0 3.6 %all-to-all-done.7.bars_ref = bf16[8,64,512]{2,1,0:T(8,128)(2,1)S(1)} async-done(((bf16[8,64,512]{2,1,0:T(8,128)(2,1)}), bf16[8,64,512]{2,1,0:T(8,128)(2,1)S(1)}, u32[]{:S(2)}, u32[]{:S(2)}) %all-to-all-start.7) | async-done | bytes 524320 | tf_op jit(solution)/shard_map/all_to_all | solution.py:23
  189.6 0.0 copy-done.2
  189.6 0.0 copy-done.4
  189.6 2.5 %shard_map.130 = (bf16[1024,256]{1,0:T(8,128)(2,1)}, bf16[1024,256]{1,0:T(8,128)(2,1)}) custom-call(bf16[256,1024]{1,0:T(8,128)(2,1)S(1)} %pad_maximum_fusion.own_ref, bf16[256,1024]{1,0:T(8,128)(2,1)S(1)} %copy-done.4, bf16[8,64,512]{2,1,0:T(8,128)(2,1)S(1)} %all-to-all-done.7.bars_ref, bf16[1024,256]{1,0:T(8,128)(2,1)S(1)} %copy-done, ...), custom_call_target="tpu_custom_call" | custom-call | tf_op jit(solution)/shard_map/pallas_call | solution.py:194
  (5 shorter events, 0.1 us)
Async XLA Ops:
  0.6 46.9 %copy-start.10 = (bf16[1024,256]{1,0:T(8,128)(2,1)S(1)}, bf16[1024,256]{1,0:T(8,128)(2,1)}, u32[]{:S(2)}) copy-start(bf16[1024,256]{1,0:T(8,128)(2,1)} %up_ref.1) | copy-start | bytes 1572868
  0.6 46.9 %copy-start.9 = (bf16[1024,256]{1,0:T(8,128)(2,1)S(1)}, bf16[1024,256]{1,0:T(8,128)(2,1)}, u32[]{:S(2)}) copy-start(bf16[1024,256]{1,0:T(8,128)(2,1)} %gate_ref.1) | copy-start | bytes 1572868
  0.7 0.8 copy-start.12
  1.5 45.9 %copy-start.14 = (s32[8,2]{0,1:T(2,128)S(1)}, s32[8,2]{0,1:T(2,128)}, u32[]{:S(2)}) copy-start(s32[8,2]{0,1:T(2,128)} %param.14) | copy-start | bytes 196
  1.5 46.0 %copy-start.15 = (s32[8,2]{0,1:T(2,128)S(1)}, s32[8,2]{0,1:T(2,128)}, u32[]{:S(2)}) copy-start(s32[8,2]{0,1:T(2,128)} %param.15) | copy-start | bytes 196
  32.4 16.5 %copy-start = (bf16[1024,256]{1,0:T(8,128)(2,1)S(1)}, bf16[1024,256]{1,0:T(8,128)(2,1)}, u32[]{:S(2)}) copy-start(bf16[1024,256]{1,0:T(8,128)(2,1)} %pgate_ref.3) | copy-start | bytes 1572868
  32.4 16.5 %copy-start.1 = (bf16[1024,256]{1,0:T(8,128)(2,1)S(1)}, bf16[1024,256]{1,0:T(8,128)(2,1)}, u32[]{:S(2)}) copy-start(bf16[1024,256]{1,0:T(8,128)(2,1)} %pup_ref.3) | copy-start | bytes 1572868
  32.4 16.5 %copy-start.13 = (s32[2,8]{1,0:T(2,128)S(1)}, s32[2,8]{1,0:T(2,128)}, u32[]{:S(2)}) copy-start(s32[2,8]{1,0:T(2,128)} %dmask_ref.1) | copy-start | bytes 196
  32.4 8.7 %collective-permute-start = (bf16[128,1024]{1,0:T(8,128)(2,1)S(1)}, bf16[128,1024]{1,0:T(8,128)(2,1)S(1)}, u32[]{:S(2)}, u32[]{:S(2)}) collective-permute-start(bf16[128,1024]{1,0:T(8,128)(2,1)S(1)} %bitcast.12), channel_id=1, source_target_pairs={{0,256},{256,0},{1,257},{257,1},{2,258},{258,2},{3,259},{259,3},{4... | collective-permute-start | bytes 786440 | tf_op jit(solution)/shard_map/ppermute | solution.py:19
  41.1 7.7 %collective-permute-start.1 = (bf16[256,1024]{1,0:T(8,128)(2,1)S(1)}, bf16[256,1024]{1,0:T(8,128)(2,1)S(1)}, u32[]{:S(2)}, u32[]{:S(2)}) collective-permute-start(bf16[256,1024]{1,0:T(8,128)(2,1)S(1)} %pad_maximum_fusion.own_ref), channel_id=1, source_target_pairs={{0,8},{8,0},{1,9},{9,1},{2,10},{10,2},{3,11},{11,3},{4,12},{12,4},... | collective-permute-start | bytes 1572872 | tf_op jit(solution)/shard_map/ppermute | solution.py:19
  48.8 4.2 %copy-start.3 = (bf16[256,1024]{1,0:T(8,128)(2,1)}, bf16[256,1024]{1,0:T(8,128)(2,1)S(1)}, u32[]{:S(2)}) copy-start(bf16[256,1024]{1,0:T(8,128)(2,1)S(1)} %collective-permute-done.1.other_ref) | copy-start | bytes 1572868
  48.9 1.2 copy-start.6
  50.1 1.0 copy-start.7
  53.1 1.0 copy-start.5
  54.1 21.0 %all-to-all-start.1 = ((bf16[8,64,1024]{2,1,0:T(8,128)(2,1)}), bf16[8,64,1024]{2,1,0:T(8,128)(2,1)}, u32[]{:S(2)}, u32[]{:S(2)}) async-start(bf16[8,64,1024]{2,1,0:T(8,128)(2,1)} %copy-done.5), calls=%async_computation.1 | async-start | bytes 2097152 | tf_op jit(solution)/shard_map/all_to_all | solution.py:23
  59.1 23.0 %collective-permute-start.2 = (bf16[512,1024]{1,0:T(8,128)(2,1)S(1)}, bf16[512,1024]{1,0:T(8,128)(2,1)S(1)}, u32[]{:S(2)}, u32[]{:S(2)}) collective-permute-start(bf16[512,1024]{1,0:T(8,128)(2,1)S(1)} %get-tuple-element.21.down_ref), channel_id=1, source_target_pairs={{0,8},{8,0},{1,9},{9,1},{2,10},{10,2},{3,11},{11,3},{4,12},{12,4},... | collective-permute-start | bytes 3145736 | tf_op jit(solution)/shard_map/ppermute | solution.py:19
  76.5 0.8 copy-start.11
  77.3 15.5 %all-to-all-start.2 = ((bf16[16,32,512]{2,1,0:T(8,128)(2,1)}), bf16[16,32,512]{2,1,0:T(8,128)(2,1)}, u32[]{:S(2)}, u32[]{:S(2)}) async-start(bf16[16,32,512]{2,1,0:T(8,128)(2,1)} %bitcast.9), calls=%async_computation.2 | async-start | bytes 1048576 | tf_op jit(solution)/shard_map/all_to_all | solution.py:23
  159.4 23.3 %collective-permute-start.4 = (bf16[256,1024]{1,0:T(8,128)(2,1)}, bf16[256,1024]{1,0:T(8,128)(2,1)S(1)}, u32[]{:S(2)}, u32[]{:S(2)}) collective-permute-start(bf16[256,1024]{1,0:T(8,128)(2,1)} %get-tuple-element.30), channel_id=1, source_target_pairs={{0,8},{8,0},{1,9},{9,1},{2,10},{10,2},{3,11},{11,3},{4,12},{12,4},... | collective-permute-start | bytes 1572872 | tf_op jit(solution)/shard_map/ppermute | solution.py:19
  175.0 8.4 %copy-start.8 = (bf16[256,1024]{1,0:T(8,128)(2,1)S(1)}, bf16[256,1024]{1,0:T(8,128)(2,1)}, u32[]{:S(2)}) copy-start(bf16[256,1024]{1,0:T(8,128)(2,1)} %pdown_ref.1) | copy-start | bytes 1572868
  175.9 13.7 %all-to-all-start.7 = ((bf16[8,64,512]{2,1,0:T(8,128)(2,1)}), bf16[8,64,512]{2,1,0:T(8,128)(2,1)S(1)}, u32[]{:S(2)}, u32[]{:S(2)}) async-start(bf16[8,64,512]{2,1,0:T(8,128)(2,1)} %shard_map.129), calls=%async_computation.7 | async-start | bytes 1048576 | tf_op jit(solution)/shard_map/all_to_all | solution.py:23
  179.4 3.2 %collective-permute-start.3 = (bf16[256,256]{1,0:T(8,128)(2,1)S(1)}, bf16[256,256]{1,0:T(8,128)(2,1)S(1)}, u32[]{:S(2)}, u32[]{:S(2)}) collective-permute-start(bf16[256,256]{1,0:T(8,128)(2,1)S(1)} %get-tuple-element.29), channel_id=1, source_target_pairs={{0,8},{8,0},{1,9},{9,1},{2,10},{10,2},{3,11},{11,3},{4,12},{12,4},... | collective-permute-start | bytes 393224 | tf_op jit(solution)/shard_map/ppermute | solution.py:19
  182.6 0.8 copy-start.16
  183.4 6.2 %copy-start.2 = (bf16[1024,256]{1,0:T(8,128)(2,1)S(1)}, bf16[1024,256]{1,0:T(8,128)(2,1)}, u32[]{:S(2)}) copy-start(bf16[1024,256]{1,0:T(8,128)(2,1)} %pup_ref.3) | copy-start | bytes 1572868
  183.5 6.2 %copy-start.4 = (bf16[256,1024]{1,0:T(8,128)(2,1)S(1)}, bf16[256,1024]{1,0:T(8,128)(2,1)}, u32[]{:S(2)}) copy-start(bf16[256,1024]{1,0:T(8,128)(2,1)} %copy-done.3) | copy-start | bytes 1572868

commit v6 on v5

v6 whole, which is shorter than its diff:
```python
import jax
import jax.numpy as jnp
from jax import lax
from jax.experimental import pallas as pl
from jax.experimental.pallas import tpu as pltpu
from jax.sharding import Mesh, PartitionSpec as P

D = 8192
HID = 16384
TOKENS = 512
BF16 = jnp.bfloat16
F32 = jnp.float32
DP = ("yh", "zh", "zl", "c")
TP = ("yl", "x")
NEAR = ("yh", "c", "yl", "x")


def swap(x, axis):
    return lax.ppermute(x, axis, [(0, 1), (1, 0)])


def step_y(x, way):
    return lax.ppermute(x, ("yh", "yl"), [(i, (i + way) % 4) for i in range(4)])


def exchange(pieces, axes):
    return lax.all_to_all(pieces, axes, 0, 0, tiled=True)


def dot(a, b, dims=((1,), (0,))):
    return lax.dot_general(a, b, (dims, ((), ())), preferred_element_type=F32)


def local(kernel, outs, *args, scalars=0, after=0):
    spec = pl.BlockSpec(memory_space=pltpu.VMEM)
    small = pl.BlockSpec(memory_space=pltpu.SMEM)
    unread = pl.BlockSpec(memory_space=pl.ANY)
    return pl.pallas_call(
        kernel,
        out_shape=[jax.ShapeDtypeStruct(shape, dtype) for shape, dtype in outs],
        in_specs=[small] * scalars + [spec] * (len(args) - scalars - after) + [unread] * after,
        out_specs=[spec] * len(outs),
        compiler_params=pltpu.CompilerParams(vmem_limit_bytes=32 * 2**20),
    )(*args)


def relatives():
    c = lax.axis_index("c")
    yh = lax.axis_index("yh")
    for dy, y in enumerate((yh, 1 - yh)):
        for dc, core in enumerate((c, 1 - c)):
            yield dy, dc, 2 * y + core


def copies_kernel(x_ref, o_ref):
    for i in range(o_ref.shape[0]):
        o_ref[i] = x_ref[...]


def keep(mask_ref, w_ref, o_ref):
    for i in range(mask_ref.shape[0]):
        for j in range(mask_ref.shape[1]):
            block = (slice(i * 128, (i + 1) * 128), slice(j * 128, (j + 1) * 128))
            o_ref[block] = (w_ref[block].astype(F32) * mask_ref[i, j].astype(F32)).astype(BF16)


def keep_kernel(mask_ref, w_ref, o_ref):
    keep(mask_ref, w_ref, o_ref)


def stack_kernel(gmask_ref, umask_ref, gate_ref, up_ref, pgate_ref, pup_ref, o_ref):
    width = gate_ref.shape[1]
    keep(gmask_ref, gate_ref, o_ref.at[:, :width])
    keep(umask_ref, up_ref, o_ref.at[:, width : 2 * width])
    o_ref[:, 2 * width : 3 * width] = pgate_ref[...]
    o_ref[:, 3 * width :] = pup_ref[...]


def pair_kernel(a_ref, b_ref, *refs):
    o_ref = refs[-1]
    rows = a_ref.shape[0]
    o_ref[:rows] = a_ref[...]
    o_ref[rows:] = b_ref[...]


def pre_kernel(own_ref, other_ref, w_ref, o_ref):
    width = w_ref.shape[1] // 4
    for half, tok_ref in enumerate((own_ref, other_ref)):
        for j in range(4):
            cols = slice(j * width, (j + 1) * width)
            y = dot(tok_ref[...], w_ref[:, cols]).astype(BF16)
            for r in range(2):
                q = 16 * (2 * half + r)
                o_ref[:, q : q + 16, cols] = y[r * 128 : (r + 1) * 128].reshape(8, 16, width)


def pack_kernel(kept_ref, probe_ref, kept2_ref, probe2_ref, after_ref, o_ref):
    width = kept_ref.shape[0]
    scale = HID**-0.5
    o_ref[:width] = kept_ref[...]
    o_ref[width : 2 * width] = (probe_ref[...].astype(F32) * scale).astype(BF16)
    o_ref[2 * width : 3 * width] = kept2_ref[...]
    o_ref[3 * width :] = (probe2_ref[...].astype(F32) * scale).astype(BF16)


def gate_kernel(x_ref, o_ref, up_slope_ref, act_ref):
    width = act_ref.shape[1]

    def part(j):
        cols = slice(j * width, (j + 1) * width)
        acc = x_ref[0, :, cols].astype(F32)
        for i in range(1, 8):
            acc = acc + x_ref[i, :, cols].astype(F32)
        return acc

    gate = part(0)
    up = part(1)
    tangent_gate = part(2) * D**-0.5
    tangent_up = part(3) * D**-0.5
    sig = jax.nn.sigmoid(gate)
    act = gate * sig
    slope = sig * (1.0 + gate * (1.0 - sig))
    hid = (act * up).astype(BF16)
    tan = (slope * tangent_gate * up + act * tangent_up).astype(BF16)
    for dy, dc, place in relatives():
        q = 16 * (2 * dc + dy)
        for i in range(8):
            o_ref[place, i, :, :width] = tan[q : q + 16]
            o_ref[place, i, :, width:] = hid[q : q + 16]
    up_slope_ref[...] = up * slope
    act_ref[...] = act


def term_kernel(x_ref, down_ref, down2_ref, o_ref, hid_ref, hid2_ref):
    width = hid_ref.shape[1]
    rows = [[], []]
    for dy, dc, place in relatives():
        part = x_ref[place].reshape(128, 2 * width)
        rows[dc].append(part)
        (hid_ref, hid2_ref)[dc][dy * 128 : (dy + 1) * 128, :] = part[:, width:]
    own = jnp.concatenate(rows[0], axis=1)
    other = jnp.concatenate(rows[1], axis=1)
    for j in range(4):
        cols = slice(j * 256, (j + 1) * 256)
        y = dot(own, down_ref[:, cols]) + dot(other, down2_ref[:, cols])
        o_ref[:, :, cols] = y.astype(BF16).reshape(4, 32, 256)


def spread_kernel(x_ref, *refs):
    o_ref = refs[-1]
    acc = x_ref[0].astype(F32)
    for i in range(1, x_ref.shape[0]):
        acc = acc + x_ref[i].astype(F32)
    acc = acc.astype(BF16)
    for i in range(o_ref.shape[0]):
        o_ref[i] = acc


def back_kernel(x_ref, down_ref, down2_ref, after_ref, o_ref):
    width = o_ref.shape[3]
    for dy, dc, place in relatives():
        w_ref = (down_ref, down2_ref)[dc]
        y = dot(x_ref[...], w_ref[2 * dy * width : (2 * dy + 1) * width, :], ((1,), (1,)))
        o_ref[place] = y.astype(BF16).reshape(8, 16, width)


def later_kernel(x_ref, after_ref, o_ref):
    o_ref[...] = x_ref[...]


def bars_kernel(x_ref, up_slope_ref, act_ref, o_ref):
    width = act_ref.shape[1]
    for dy, dc, place in relatives():
        q = 16 * (2 * dc + dy)
        rows = slice(q, q + 16)
        back = x_ref[place, 0].astype(F32)
        for i in range(1, 8):
            back = back + x_ref[place, i].astype(F32)
        gate_bar = (back * up_slope_ref[rows]).astype(BF16)
        up_bar = (back * act_ref[rows]).astype(BF16)
        for i in range(8):
            o_ref[i, rows, :width] = gate_bar
            o_ref[i, rows, width:] = up_bar


def fisher_kernel(
    own_ref, other_ref, bars_ref, pgate_ref, pup_ref, after_ref, gate_ref, up_ref
):
    width = gate_ref.shape[1]
    factor = TOKENS**-0.5
    bars = [bars_ref[:, 16 * q : 16 * q + 16, :].reshape(128, 2 * width) for q in range(4)]
    y = dot(own_ref[...], jnp.concatenate(bars[:2], axis=0), ((0,), (0,)))
    y = y + dot(other_ref[...], jnp.concatenate(bars[2:], axis=0), ((0,), (0,)))
    gate_ref[...] = (pgate_ref[...].astype(F32) * y[:, :width] * factor).astype(BF16)
    up_ref[...] = (pup_ref[...].astype(F32) * y[:, width:] * factor).astype(BF16)


def fisher(own, other, bars, probe_gate, probe_up, after):
    rows, width = probe_gate.shape
    block = 256
    weight = pl.BlockSpec((block, width), lambda i: (i, 0))
    return pl.pallas_call(
        fisher_kernel,
        grid=(rows // block,),
        out_shape=[jax.ShapeDtypeStruct((rows, width), BF16)] * 2,
        in_specs=[
            pl.BlockSpec((own.shape[0], block), lambda i: (0, i)),
            pl.BlockSpec((own.shape[0], block), lambda i: (0, i)),
            pl.BlockSpec(bars.shape, lambda i: (0, 0, 0)),
            weight,
            weight,
            pl.BlockSpec(memory_space=pl.ANY),
        ],
        out_specs=[weight, weight],
        compiler_params=pltpu.CompilerParams(vmem_limit_bytes=32 * 2**20),
    )(own, other, bars, probe_gate, probe_up, after)


def on_device(
    tokens,
    gate_weight,
    up_weight,
    down_weight,
    gate_mask,
    up_mask,
    down_mask,
    probe_gate,
    probe_up,
    probe_down,
):
    width = gate_weight.shape[1]
    feats = tokens.shape[1]

    (kept_down,) = local(
        keep_kernel, [(down_weight.shape, BF16)], down_mask, down_weight, scalars=1
    )
    (mine,) = local(copies_kernel, [((16, 8, feats), BF16)], tokens)
    tok0 = exchange(mine, ("zl", "zh")).reshape(128, feats)
    kept_y = swap(kept_down, "yh")
    probe_y = step_y(probe_down, -1)
    (stacked,) = local(
        stack_kernel,
        [((feats, 4 * width), BF16)],
        gate_mask,
        up_mask,
        gate_weight,
        up_weight,
        probe_gate,
        probe_up,
        scalars=2,
    )
    tok1 = swap(tok0, "yh")
    (pair,) = local(
        pair_kernel, [((256, feats), BF16)], tok0, tok1, stacked, kept_y, probe_y, after=3
    )
    probe_y = step_y(probe_y, -1)
    pair2 = swap(pair, "c")
    (partial,) = local(pre_kernel, [((8, 64, 4 * width), BF16)], pair, pair2, stacked)
    pre = exchange(partial, TP)
    (down,) = local(
        pack_kernel,
        [((4 * width, feats), BF16)],
        kept_down,
        probe_down,
        kept_y,
        probe_y,
        partial,
        after=1,
    )
    down2 = swap(down, "c")
    send, up_slope, act = local(
        gate_kernel,
        [((4, 8, 16, 2 * width), BF16), ((64, width), F32), ((64, width), F32)],
        pre,
    )
    both = exchange(send.reshape(32, 16, 2 * width), NEAR).reshape(4, 8, 16, 2 * width)
    term, hid, hid2 = local(
        term_kernel,
        [((4, 32, feats), BF16), ((256, width), BF16), ((256, width), BF16)],
        both,
        down,
        down2,
    )
    term = exchange(term, "zl")
    hid2 = swap(hid2, "c")
    (chunk,) = local(spread_kernel, [((4, 32, feats), BF16)], term, hid2, after=1)
    far = swap(jnp.concatenate([hid[128:], hid2[128:]], axis=0), "yh")
    hidden = jnp.concatenate([hid[:128], far[:128], hid2[:128], far[128:]], axis=0)
    chunk = exchange(chunk, "zh")
    (chunk,) = local(spread_kernel, [((4, 32, feats), BF16)], chunk)
    out = exchange(chunk, "zl").reshape(128, feats)
    (back,) = local(
        back_kernel, [((4, 8, 16, width), BF16)], out, down, down2, hidden, after=1
    )
    back_sum = exchange(back.reshape(32, 16, width), NEAR).reshape(4, 8, 16, width)

    (late,) = local(later_kernel, [((128, feats), BF16)], out, back, after=1)
    outs = jnp.concatenate([late, swap(late, "yh")], axis=0)

    (bars,) = local(bars_kernel, [((8, 64, 2 * width), BF16)], back_sum, up_slope, act)
    bars = exchange(bars, TP)
    outs = jnp.concatenate([outs, swap(outs, "c")], axis=0)
    grad_down = dot(hidden, outs, ((0,), (0,)))
    fisher_down = (probe_down.astype(F32) * grad_down * TOKENS**-0.5).astype(BF16)
    fisher_gate, fisher_up = fisher(pair, pair2, bars, probe_gate, probe_up, fisher_down)
    return (fisher_gate, fisher_up, fisher_down)


def solution(mesh):
    fine = Mesh(mesh.devices.reshape(2, 4, 4, 2, 2, 4), DP + TP)
    col = P(TP, DP)
    row = P(DP, TP)
    return jax.shard_map(
        on_device,
        mesh=fine,
        in_specs=(row, col, col, row, col, col, row, col, col, row),
        out_specs=(col, col, row),
        check_vma=False,
    )
```

time: 193 us -> 222 us (1.15)
  blocking collectives: 105 us -> 50.9 us
  starting transfers between devices: 34.6 us -> 80.9 us
  waiting for transfers between devices: 33.1 us -> 62.6 us
  local copies, waits for them, and re-layouts: 5.83 us -> 10.5 us
    all_to_all x5 -> x3, blocking collectives: 105 us -> 50.9 us  [exchange(): return lax.all_to_all(pieces, axes, 0, 0, tiled=True)]
    all_to_all x3 -> x5, starting transfers between devices: 13.3 us -> 37.3 us  [exchange(): return lax.all_to_all(pieces, axes, 0, 0, tiled=True)]
    ppermute x0 -> x2, waiting for transfers between devices: none -> 16.7 us  [step_y(): return lax.ppermute(x, ('yh', 'yl'), [(i, (i + way) % 4) for i in range(4)])]
    ppermute x5 -> x8, starting transfers between devices: 21.2 us -> 32.6 us  [swap(): return lax.ppermute(x, axis, [(0, 1), (1, 0)])]
    ppermute x0 -> x2, starting transfers between devices: none -> 11 us  [step_y(): return lax.ppermute(x, ('yh', 'yl'), [(i, (i + way) % 4) for i in range(4)])]
    ppermute x5 -> x8, waiting for transfers between devices: 5.34 us -> 12.6 us  [swap(): return lax.ppermute(x, axis, [(0, 1), (1, 0)])]
    all_to_all x3 -> x5, waiting for transfers between devices: 27.7 us -> 33.3 us  [exchange(): return lax.all_to_all(pieces, axes, 0, 0, tiled=True)]
    unnamed x36 -> x48, local copies, waits for them, and re-layouts: 5.83 us -> 10.5 us
  transfers between devices with their start and end apart: 8 -> 15, of which waited for: 6 -> 9; matrix products, arithmetic and copies ran while one was open for 1% -> 2% of each run, Pallas kernels for 2% -> 2%
where the time goes in v6:
time: 222 us; the launch traced here: 221 us
  starting transfers between devices  80.9 us (36%)
  waiting for transfers between devices  62.6 us (28%)
  blocking collectives  50.9 us (23%)
  Pallas kernels  11.2 us (5%)
  local copies, waits for them, and re-layouts  10.5 us (5%)
  matrix products  2.61 us (1%)
    all_to_all x3, blocking collectives, exchange(): return lax.all_to_all(pieces, axes, 0, 0, tiled=True)  50.9 us
    all_to_all x5, starting transfers between devices, exchange(): return lax.all_to_all(pieces, axes, 0, 0, tiled=True)  37.3 us
    all_to_all x5, waiting for transfers between devices, exchange(): return lax.all_to_all(pieces, axes, 0, 0, tiled=True)  33.3 us
    ppermute x8, starting transfers between devices, swap(): return lax.ppermute(x, axis, [(0, 1), (1, 0)])  32.6 us
    ppermute x2, waiting for transfers between devices, step_y(): return lax.ppermute(x, ('yh', 'yl'), [(i, (i + way) % 4) for i in range(4)])  16.7 us
    ppermute x8, waiting for transfers between devices, swap(): return lax.ppermute(x, axis, [(0, 1), (1, 0)])  12.6 us
    ppermute x2, starting transfers between devices, step_y(): return lax.ppermute(x, ('yh', 'yl'), [(i, (i + way) % 4) for i in range(4)])  11 us
    unnamed x48, local copies, waits for them, and re-layouts  10.5 us
  transfers between devices with their start and end apart: 15, of which 9 were waited for; matrix products, arithmetic and copies ran while one was open for 2% of the time, Pallas kernels for 2%

profile of v6, /device:TPU:1, one launch (start us, length us, event | category | flops | bytes accessed | tf_op | source)
XLA Modules:
  0.0 220.7 jit_solution(6143649147351839775)
XLA Ops:
  0.6 0.0 copy-start.6
  0.6 0.0 copy-start.4
  0.7 0.8 copy-done.16
  1.5 0.7 shard_map.121
  2.2 15.7 %all-to-all-start = ((bf16[16,8,1024]{2,1,0:T(8,128)(2,1)}), bf16[16,8,1024]{2,1,0:T(8,128)(2,1)S(1)}, u32[]{:S(2)}, u32[]{:S(2)}) async-start(bf16[16,8,1024]{2,1,0:T(8,128)(2,1)} %shard_map.121), calls=%async_computation | async-start | bytes 524288 | tf_op jit(solution)/shard_map/all_to_all | solution.py:27
  17.9 0.0 copy-start.12
  17.9 1.0 copy-done.12
  19.0 0.7 copy-done.17
  19.7 0.7 shard_map.123.kept_ref
  20.3 4.8 %collective-permute-start.1 = (bf16[256,1024]{1,0:T(8,128)(2,1)S(1)}, bf16[256,1024]{1,0:T(8,128)(2,1)S(1)}, u32[]{:S(2)}, u32[]{:S(2)}) collective-permute-start(bf16[256,1024]{1,0:T(8,128)(2,1)S(1)} %shard_map.123.kept_ref), channel_id=1, source_target_pairs={{0,256},{256,0},{1,257},{257,1},{2,258},{258,2},{3,259},{259,3},{4... | collective-permute-start | bytes 1572872 | tf_op jit(solution)/shard_map/ppermute | solution.py:19
  25.2 2.7 %collective-permute-start.2 = (bf16[256,1024]{1,0:T(8,128)(2,1)}, bf16[256,1024]{1,0:T(8,128)(2,1)}, u32[]{:S(2)}, u32[]{:S(2)}) collective-permute-start(bf16[256,1024]{1,0:T(8,128)(2,1)} %probe_ref.1), channel_id=1, source_target_pairs={{0,260},{4,0},{256,4},{260,256},{1,261},{5,1},{257,5},{261,257},{2... | collective-permute-start | bytes 1572872 | tf_op jit(solution)/shard_map/ppermute | solution.py:23
  27.9 5.4 %all-to-all-done = bf16[16,8,1024]{2,1,0:T(8,128)(2,1)S(1)} async-done(((bf16[16,8,1024]{2,1,0:T(8,128)(2,1)}), bf16[16,8,1024]{2,1,0:T(8,128)(2,1)S(1)}, u32[]{:S(2)}, u32[]{:S(2)}) %all-to-all-start) | async-done | bytes 262176 | tf_op jit(solution)/shard_map/all_to_all | solution.py:27
  33.3 4.8 %collective-permute-start = (bf16[128,1024]{1,0:T(8,128)(2,1)S(1)}, bf16[128,1024]{1,0:T(8,128)(2,1)S(1)}, u32[]{:S(2)}, u32[]{:S(2)}) collective-permute-start(bf16[128,1024]{1,0:T(8,128)(2,1)S(1)} %bitcast.10), channel_id=1, source_target_pairs={{0,256},{256,0},{1,257},{257,1},{2,258},{258,2},{3,259},{259,3},{4... | collective-permute-start | bytes 786440 | tf_op jit(solution)/shard_map/ppermute | solution.py:19
  38.1 0.8 copy.13.gmask_ref
  38.8 0.8 copy.14.umask_ref
  39.6 1.0 copy-done.14
  40.6 1.0 copy-done.15
  41.7 1.0 shard_map.122.refs_0_.w_ref
  42.7 0.0 copy-start.2
  42.7 6.3 %collective-permute-done.2.refs_2_ = bf16[256,1024]{1,0:T(8,128)(2,1)} collective-permute-done((bf16[256,1024]{1,0:T(8,128)(2,1)}, bf16[256,1024]{1,0:T(8,128)(2,1)}, u32[]{:S(2)}, u32[]{:S(2)}) %collective-permute-start.2) | collective-permute-done | bytes 524320 | tf_op jit(solution)/shard_map/ppermute | solution.py:23
  49.1 0.0 copy-start.10
  49.1 4.2 %collective-permute-start.3 = (bf16[256,1024]{1,0:T(8,128)(2,1)S(1)}, bf16[256,1024]{1,0:T(8,128)(2,1)S(1)}, u32[]{:S(2)}, u32[]{:S(2)}) collective-permute-start(bf16[256,1024]{1,0:T(8,128)(2,1)S(1)} %shard_map.124.own_ref), channel_id=1, source_target_pairs={{0,8},{8,0},{1,9},{9,1},{2,10},{10,2},{3,11},{11,3},{4,12},{12,4},... | collective-permute-start | bytes 1572872 | tf_op jit(solution)/shard_map/ppermute | solution.py:19
  53.4 8.3 %collective-permute-start.4 = (bf16[256,1024]{1,0:T(8,128)(2,1)}, bf16[256,1024]{1,0:T(8,128)(2,1)S(1)}, u32[]{:S(2)}, u32[]{:S(2)}) collective-permute-start(bf16[256,1024]{1,0:T(8,128)(2,1)} %collective-permute-done.2.refs_2_), channel_id=1, source_target_pairs={{0,260},{4,0},{256,4},{260,256},{1,261},{5,1},{257,5},{261,257},{2... | collective-permute-start | bytes 1572872 | tf_op jit(solution)/shard_map/ppermute | solution.py:23
  61.7 0.0 copy-start.8
  61.7 1.2 shard_map.125.after_ref
  63.0 10.3 %collective-permute-done.4.probe2_ref = bf16[256,1024]{1,0:T(8,128)(2,1)S(1)} collective-permute-done((bf16[256,1024]{1,0:T(8,128)(2,1)}, bf16[256,1024]{1,0:T(8,128)(2,1)S(1)}, u32[]{:S(2)}, u32[]{:S(2)}) %collective-permute-start.4) | collective-permute-done | bytes 524320 | tf_op jit(solution)/shard_map/ppermute | solution.py:23
  73.4 1.0 copy-done.3
  74.4 0.2 shard_map.127.down_ref
  74.6 2.7 %collective-permute-start.5 = (bf16[1024,1024]{1,0:T(8,128)(2,1)S(1)}, bf16[1024,1024]{1,0:T(8,128)(2,1)S(1)}, u32[]{:S(2)}, u32[]{:S(2)}) collective-permute-start(bf16[1024,1024]{1,0:T(8,128)(2,1)S(1)} %shard_map.127.down_ref), channel_id=1, source_target_pairs={{0,8},{8,0},{1,9},{9,1},{2,10},{10,2},{3,11},{11,3},{4,12},{12,4},... | collective-permute-start | bytes 6291464 | tf_op jit(solution)/shard_map/ppermute | solution.py:19
  77.3 20.0 %all_to_all.40.x_ref = bf16[8,64,1024]{2,1,0:T(8,128)(2,1)S(1)} all-to-all(bf16[8,64,1024]{2,1,0:T(8,128)(2,1)S(1)} %shard_map.125.after_ref), channel_id=1, replica_groups=mesh['yh'=2,'zh'=4,'zl'=4,'c'=2,'yl'=2,'x'=4] {'yl','x'}, dimensions={0} | all-to-all | bytes 2097152 | tf_op jit(solution)/shard_map/all_to_all | solution.py:27
  97.4 0.2 shard_map.126
  97.6 18.3 %all_to_all.41 = bf16[32,16,512]{2,1,0:T(8,128)(2,1)S(1)} all-to-all(bf16[32,16,512]{2,1,0:T(8,128)(2,1)S(1)} %bitcast.13), channel_id=1, replica_groups=mesh['yh'=2,'zh'=4,'zl'=4,'c'=2,'yl'=2,'x'=4] {'yh','c','yl','x'}, dimensions={0} | all-to-all | bytes 1048576 | tf_op jit(solution)/shard_map/all_to_all | solution.py:27
  115.8 1.4 shard_map.128
  117.3 4.4 %all-to-all-start.3 = ((bf16[4,32,1024]{2,1,0:T(8,128)(2,1)}), bf16[4,32,1024]{2,1,0:T(8,128)(2,1)S(1)}, u32[]{:S(2)}, u32[]{:S(2)}) async-start(bf16[4,32,1024]{2,1,0:T(8,128)(2,1)} %get-tuple-element.12), calls=%async_computation.3 | async-start | bytes 524288 | tf_op jit(solution)/shard_map/all_to_all | solution.py:27
  121.7 2.6 %collective-permute-start.6 = (bf16[256,256]{1,0:T(8,128)(2,1)S(1)}, bf16[256,256]{1,0:T(8,128)(2,1)S(1)}, u32[]{:S(2)}, u32[]{:S(2)}) collective-permute-start(bf16[256,256]{1,0:T(8,128)(2,1)S(1)} %get-tuple-element.13), channel_id=1, source_target_pairs={{0,8},{8,0},{1,9},{9,1},{2,10},{10,2},{3,11},{11,3},{4,12},{12,4},... | collective-permute-start | bytes 393224 | tf_op jit(solution)/shard_map/ppermute | solution.py:19
  124.3 1.0 collective-permute-done.6.refs_0_
  125.3 3.9 %all-to-all-done.3.x_ref = bf16[4,32,1024]{2,1,0:T(8,128)(2,1)S(1)} async-done(((bf16[4,32,1024]{2,1,0:T(8,128)(2,1)}), bf16[4,32,1024]{2,1,0:T(8,128)(2,1)S(1)}, u32[]{:S(2)}, u32[]{:S(2)}) %all-to-all-start.3) | async-done | bytes 262176 | tf_op jit(solution)/shard_map/all_to_all | solution.py:27
  129.2 0.7 shard_map.129
  129.9 10.2 %all-to-all-start.4 = ((bf16[4,32,1024]{2,1,0:T(8,128)(2,1)}), bf16[4,32,1024]{2,1,0:T(8,128)(2,1)S(1)}, u32[]{:S(2)}, u32[]{:S(2)}) async-start(bf16[4,32,1024]{2,1,0:T(8,128)(2,1)} %shard_map.129), calls=%async_computation.4 | async-start | bytes 524288 | tf_op jit(solution)/shard_map/all_to_all | solution.py:27
  140.2 16.5 %all-to-all-done.4.x_ref = bf16[4,32,1024]{2,1,0:T(8,128)(2,1)S(1)} async-done(((bf16[4,32,1024]{2,1,0:T(8,128)(2,1)}), bf16[4,32,1024]{2,1,0:T(8,128)(2,1)S(1)}, u32[]{:S(2)}, u32[]{:S(2)}) %all-to-all-start.4) | async-done | bytes 262176 | tf_op jit(solution)/shard_map/all_to_all | solution.py:27
  156.6 0.7 shard_map.130
  157.4 3.4 %all-to-all-start.5 = ((bf16[4,32,1024]{2,1,0:T(8,128)(2,1)}), bf16[4,32,1024]{2,1,0:T(8,128)(2,1)S(1)}, u32[]{:S(2)}, u32[]{:S(2)}) async-start(bf16[4,32,1024]{2,1,0:T(8,128)(2,1)} %shard_map.130), calls=%async_computation.5 | async-start | bytes 524288 | tf_op jit(solution)/shard_map/all_to_all | solution.py:27
  160.8 2.1 collective-permute-start.7
  162.9 5.1 %collective-permute-done.7 = bf16[256,256]{1,0:T(8,128)(2,1)S(1)} collective-permute-done((bf16[256,256]{1,0:T(8,128)(2,1)S(1)}, bf16[256,256]{1,0:T(8,128)(2,1)S(1)}, u32[]{:S(2)}, u32[]{:S(2)}) %collective-permute-start.7) | collective-permute-done | bytes 131104 | tf_op jit(solution)/shard_map/ppermute | solution.py:19
  168.1 0.6 copy-done.21
  168.7 0.0 copy-done.22
  168.7 1.6 copy-done.1
  170.3 0.8 shard_map.131.after_ref
  171.2 0.0 copy-start.11
  171.2 2.2 %collective-permute-start.8 = (bf16[128,1024]{1,0:T(8,128)(2,1)S(1)}, bf16[128,1024]{1,0:T(8,128)(2,1)S(1)}, u32[]{:S(2)}, u32[]{:S(2)}) collective-permute-start(bf16[128,1024]{1,0:T(8,128)(2,1)S(1)} %shard_map.133), channel_id=1, source_target_pairs={{0,256},{256,0},{1,257},{257,1},{2,258},{258,2},{3,259},{259,3},{4... | collective-permute-start | bytes 786440 | tf_op jit(solution)/shard_map/ppermute | solution.py:19
  173.5 6.5 %collective-permute-done.8 = bf16[128,1024]{1,0:T(8,128)(2,1)S(1)} collective-permute-done((bf16[128,1024]{1,0:T(8,128)(2,1)S(1)}, bf16[128,1024]{1,0:T(8,128)(2,1)S(1)}, u32[]{:S(2)}, u32[]{:S(2)}) %collective-permute-start.8) | collective-permute-done | bytes 262176 | tf_op jit(solution)/shard_map/ppermute | solution.py:19
  180.0 0.9 pad_maximum_fusion
  180.8 9.1 %collective-permute-start.9 = (bf16[256,1024]{1,0:T(8,128)(2,1)}, bf16[256,1024]{1,0:T(8,128)(2,1)}, u32[]{:S(2)}, u32[]{:S(2)}) collective-permute-start(bf16[256,1024]{1,0:T(8,128)(2,1)} %pad_maximum_fusion), channel_id=1, source_target_pairs={{0,8},{8,0},{1,9},{9,1},{2,10},{10,2},{3,11},{11,3},{4,12},{12,4},... | collective-permute-start | bytes 1572872 | tf_op jit(solution)/shard_map/ppermute | solution.py:19
  189.9 12.6 %all_to_all.42 = bf16[32,16,256]{2,1,0:T(8,128)(2,1)S(1)} all-to-all(bf16[32,16,256]{2,1,0:T(8,128)(2,1)S(1)} %bitcast.8), channel_id=1, replica_groups=mesh['yh'=2,'zh'=4,'zl'=4,'c'=2,'yl'=2,'x'=4] {'yh','c','yl','x'}, dimensions={0} | all-to-all | bytes 524288 | tf_op jit(solution)/shard_map/all_to_all | solution.py:27
  202.5 0.8 shard_map.132
  203.4 3.5 %all-to-all-start.7 = ((bf16[8,64,512]{2,1,0:T(8,128)(2,1)}), bf16[8,64,512]{2,1,0:T(8,128)(2,1)S(1)}, u32[]{:S(2)}, u32[]{:S(2)}) async-start(bf16[8,64,512]{2,1,0:T(8,128)(2,1)} %shard_map.132), calls=%async_computation.7 | async-start | bytes 1048576 | tf_op jit(solution)/shard_map/all_to_all | solution.py:27
  206.9 0.0 copy-start.5
  206.9 0.0 copy-start.7
  206.9 0.0 copy-start.9
  206.9 2.6 %fusion.1.after_ref = bf16[256,1024]{1,0:T(8,128)(2,1)} fusion(bf16[256,1024]{1,0:T(8,128)(2,1)} %collective-permute-done.9, bf16[128,1024]{1,0:T(8,128)(2,1)} %copy-done.18, bf16[128,1024]{1,0:T(8,128)(2,1)S(1)} %shard_map.133, bf16[256,1024]{1,0:T(8,128)(2,1)S(1)} %copy-done.11, bf16[128,256]{1,0:T(8,128)(2,1)} %copy-done.22, ...), kind=kOutput, calls=%fused_computation.2 | convolution fusion | flops 273678336 | bytes 2359296 | tf_op jit(solution)/shard_map/dot_general | solution.py:31
  209.6 7.5 %all-to-all-done.7.bars_ref = bf16[8,64,512]{2,1,0:T(8,128)(2,1)S(1)} async-done(((bf16[8,64,512]{2,1,0:T(8,128)(2,1)}), bf16[8,64,512]{2,1,0:T(8,128)(2,1)S(1)}, u32[]{:S(2)}, u32[]{:S(2)}) %all-to-all-start.7) | async-done | bytes 524320 | tf_op jit(solution)/shard_map/all_to_all | solution.py:27
  217.1 0.0 copy-start.13
  217.1 1.0 copy-done.13
  218.2 2.5 %shard_map.134 = (bf16[1024,256]{1,0:T(8,128)(2,1)}, bf16[1024,256]{1,0:T(8,128)(2,1)}) custom-call(bf16[256,1024]{1,0:T(8,128)(2,1)S(1)} %shard_map.124.own_ref, bf16[256,1024]{1,0:T(8,128)(2,1)S(1)} %copy-done.9, bf16[8,64,512]{2,1,0:T(8,128)(2,1)S(1)} %all-to-all-done.7.bars_ref, bf16[1024,256]{1,0:T(8,128)(2,1)S(1)} %copy-done.5, ...), custom_call_target="tpu_custom_call" | custom-call | tf_op jit(solution)/shard_map/pallas_call | solution.py:202
  (38 shorter events, 0.2 us)
Async XLA Ops:
  0.6 39.0 %copy-start.6 = (bf16[1024,256]{1,0:T(8,128)(2,1)S(1)}, bf16[1024,256]{1,0:T(8,128)(2,1)}, u32[]{:S(2)}) copy-start(bf16[1024,256]{1,0:T(8,128)(2,1)} %pup_ref.3) | copy-start | bytes 1572868
  0.6 39.0 %copy-start.4 = (bf16[1024,256]{1,0:T(8,128)(2,1)S(1)}, bf16[1024,256]{1,0:T(8,128)(2,1)}, u32[]{:S(2)}) copy-start(bf16[1024,256]{1,0:T(8,128)(2,1)} %pgate_ref.3) | copy-start | bytes 1572868
  0.7 0.8 copy-start.16
  2.2 31.1 %all-to-all-start = ((bf16[16,8,1024]{2,1,0:T(8,128)(2,1)}), bf16[16,8,1024]{2,1,0:T(8,128)(2,1)S(1)}, u32[]{:S(2)}, u32[]{:S(2)}) async-start(bf16[16,8,1024]{2,1,0:T(8,128)(2,1)} %shard_map.121), calls=%async_computation | async-start | bytes 524288 | tf_op jit(solution)/shard_map/all_to_all | solution.py:27
  17.9 1.0 copy-start.12
  19.0 0.7 copy-start.17
  20.3 22.4 %collective-permute-start.1 = (bf16[256,1024]{1,0:T(8,128)(2,1)S(1)}, bf16[256,1024]{1,0:T(8,128)(2,1)S(1)}, u32[]{:S(2)}, u32[]{:S(2)}) collective-permute-start(bf16[256,1024]{1,0:T(8,128)(2,1)S(1)} %shard_map.123.kept_ref), channel_id=1, source_target_pairs={{0,256},{256,0},{1,257},{257,1},{2,258},{258,2},{3,259},{259,3},{4... | collective-permute-start | bytes 1572872 | tf_op jit(solution)/shard_map/ppermute | solution.py:19
  25.2 23.9 %collective-permute-start.2 = (bf16[256,1024]{1,0:T(8,128)(2,1)}, bf16[256,1024]{1,0:T(8,128)(2,1)}, u32[]{:S(2)}, u32[]{:S(2)}) collective-permute-start(bf16[256,1024]{1,0:T(8,128)(2,1)} %probe_ref.1), channel_id=1, source_target_pairs={{0,260},{4,0},{256,4},{260,256},{1,261},{5,1},{257,5},{261,257},{2... | collective-permute-start | bytes 1572872 | tf_op jit(solution)/shard_map/ppermute | solution.py:23
  33.3 15.8 %collective-permute-start = (bf16[128,1024]{1,0:T(8,128)(2,1)S(1)}, bf16[128,1024]{1,0:T(8,128)(2,1)S(1)}, u32[]{:S(2)}, u32[]{:S(2)}) collective-permute-start(bf16[128,1024]{1,0:T(8,128)(2,1)S(1)} %bitcast.10), channel_id=1, source_target_pairs={{0,256},{256,0},{1,257},{257,1},{2,258},{258,2},{3,259},{259,3},{4... | collective-permute-start | bytes 786440 | tf_op jit(solution)/shard_map/ppermute | solution.py:19
  39.6 1.0 copy-start.14
  40.6 1.0 copy-start.15
  42.7 20.3 %copy-start.2 = (bf16[256,1024]{1,0:T(8,128)(2,1)}, bf16[256,1024]{1,0:T(8,128)(2,1)S(1)}, u32[]{:S(2)}) copy-start(bf16[256,1024]{1,0:T(8,128)(2,1)S(1)} %collective-permute-done.1.refs_1_.kept2_ref) | copy-start | bytes 1572868
  49.1 24.2 %copy-start.10 = (bf16[256,1024]{1,0:T(8,128)(2,1)S(1)}, bf16[256,1024]{1,0:T(8,128)(2,1)}, u32[]{:S(2)}) copy-start(bf16[256,1024]{1,0:T(8,128)(2,1)} %probe_ref.1) | copy-start | bytes 1572868
  49.1 12.6 %collective-permute-start.3 = (bf16[256,1024]{1,0:T(8,128)(2,1)S(1)}, bf16[256,1024]{1,0:T(8,128)(2,1)S(1)}, u32[]{:S(2)}, u32[]{:S(2)}) collective-permute-start(bf16[256,1024]{1,0:T(8,128)(2,1)S(1)} %shard_map.124.own_ref), channel_id=1, source_target_pairs={{0,8},{8,0},{1,9},{9,1},{2,10},{10,2},{3,11},{11,3},{4,12},{12,4},... | collective-permute-start | bytes 1572872 | tf_op jit(solution)/shard_map/ppermute | solution.py:19
  53.4 20.0 %collective-permute-start.4 = (bf16[256,1024]{1,0:T(8,128)(2,1)}, bf16[256,1024]{1,0:T(8,128)(2,1)S(1)}, u32[]{:S(2)}, u32[]{:S(2)}) collective-permute-start(bf16[256,1024]{1,0:T(8,128)(2,1)} %collective-permute-done.2.refs_2_), channel_id=1, source_target_pairs={{0,260},{4,0},{256,4},{260,256},{1,261},{5,1},{257,5},{261,257},{2... | collective-permute-start | bytes 1572872 | tf_op jit(solution)/shard_map/ppermute | solution.py:23
  61.7 1.3 copy-start.8
  73.4 1.0 copy-start.3
  74.6 41.2 %collective-permute-start.5 = (bf16[1024,1024]{1,0:T(8,128)(2,1)S(1)}, bf16[1024,1024]{1,0:T(8,128)(2,1)S(1)}, u32[]{:S(2)}, u32[]{:S(2)}) collective-permute-start(bf16[1024,1024]{1,0:T(8,128)(2,1)S(1)} %shard_map.127.down_ref), channel_id=1, source_target_pairs={{0,8},{8,0},{1,9},{9,1},{2,10},{10,2},{3,11},{11,3},{4,12},{12,4},... | collective-permute-start | bytes 6291464 | tf_op jit(solution)/shard_map/ppermute | solution.py:19
  115.8 1.4 copy-start
  117.3 11.9 %all-to-all-start.3 = ((bf16[4,32,1024]{2,1,0:T(8,128)(2,1)}), bf16[4,32,1024]{2,1,0:T(8,128)(2,1)S(1)}, u32[]{:S(2)}, u32[]{:S(2)}) async-start(bf16[4,32,1024]{2,1,0:T(8,128)(2,1)} %get-tuple-element.12), calls=%async_computation.3 | async-start | bytes 524288 | tf_op jit(solution)/shard_map/all_to_all | solution.py:27
  121.7 3.5 %collective-permute-start.6 = (bf16[256,256]{1,0:T(8,128)(2,1)S(1)}, bf16[256,256]{1,0:T(8,128)(2,1)S(1)}, u32[]{:S(2)}, u32[]{:S(2)}) collective-permute-start(bf16[256,256]{1,0:T(8,128)(2,1)S(1)} %get-tuple-element.13), channel_id=1, source_target_pairs={{0,8},{8,0},{1,9},{9,1},{2,10},{10,2},{3,11},{11,3},{4,12},{12,4},... | collective-permute-start | bytes 393224 | tf_op jit(solution)/shard_map/ppermute | solution.py:19
  129.9 26.7 %all-to-all-start.4 = ((bf16[4,32,1024]{2,1,0:T(8,128)(2,1)}), bf16[4,32,1024]{2,1,0:T(8,128)(2,1)S(1)}, u32[]{:S(2)}, u32[]{:S(2)}) async-start(bf16[4,32,1024]{2,1,0:T(8,128)(2,1)} %shard_map.129), calls=%async_computation.4 | async-start | bytes 524288 | tf_op jit(solution)/shard_map/all_to_all | solution.py:27
  140.1 31.0 %copy-start.19 = (bf16[128,256]{1,0:T(8,128)(2,1)}, bf16[128,256]{1,0:T(8,128)(2,1)S(1)}, u32[]{:S(2)}) copy-start(bf16[128,256]{1,0:T(8,128)(2,1)S(1)} %get-tuple-element.19) | copy-start | bytes 196612
  157.4 11.4 %all-to-all-start.5 = ((bf16[4,32,1024]{2,1,0:T(8,128)(2,1)}), bf16[4,32,1024]{2,1,0:T(8,128)(2,1)S(1)}, u32[]{:S(2)}, u32[]{:S(2)}) async-start(bf16[4,32,1024]{2,1,0:T(8,128)(2,1)} %shard_map.130), calls=%async_computation.5 | async-start | bytes 524288 | tf_op jit(solution)/shard_map/all_to_all | solution.py:27
  160.8 7.3 %copy-start.20 = (bf16[128,256]{1,0:T(8,128)(2,1)}, bf16[128,256]{1,0:T(8,128)(2,1)S(1)}, u32[]{:S(2)}) copy-start(bf16[128,256]{1,0:T(8,128)(2,1)S(1)} %get-tuple-element.23) | copy-start | bytes 196612
  160.8 7.2 %collective-permute-start.7 = (bf16[256,256]{1,0:T(8,128)(2,1)S(1)}, bf16[256,256]{1,0:T(8,128)(2,1)S(1)}, u32[]{:S(2)}, u32[]{:S(2)}) collective-permute-start(bf16[256,256]{1,0:T(8,128)(2,1)S(1)} %pad_maximum_fusion.2), channel_id=1, source_target_pairs={{0,256},{256,0},{1,257},{257,1},{2,258},{258,2},{3,259},{259,3},{4... | collective-permute-start | bytes 393224 | tf_op jit(solution)/shard_map/ppermute | solution.py:19
  168.0 0.6 copy-start.21
  168.1 0.6 copy-start.22
  168.7 1.6 copy-start.1
  171.2 35.8 %copy-start.11 = (bf16[256,1024]{1,0:T(8,128)(2,1)S(1)}, bf16[256,1024]{1,0:T(8,128)(2,1)}, u32[]{:S(2)}) copy-start(bf16[256,1024]{1,0:T(8,128)(2,1)} %probe_ref.1) | copy-start | bytes 1572868
  171.2 8.8 %collective-permute-start.8 = (bf16[128,1024]{1,0:T(8,128)(2,1)S(1)}, bf16[128,1024]{1,0:T(8,128)(2,1)S(1)}, u32[]{:S(2)}, u32[]{:S(2)}) collective-permute-start(bf16[128,1024]{1,0:T(8,128)(2,1)S(1)} %shard_map.133), channel_id=1, source_target_pairs={{0,256},{256,0},{1,257},{257,1},{2,258},{258,2},{3,259},{259,3},{4... | collective-permute-start | bytes 786440 | tf_op jit(solution)/shard_map/ppermute | solution.py:19
  180.0 22.6 %copy-start.18 = (bf16[128,1024]{1,0:T(8,128)(2,1)}, bf16[128,1024]{1,0:T(8,128)(2,1)S(1)}, u32[]{:S(2)}) copy-start(bf16[128,1024]{1,0:T(8,128)(2,1)S(1)} %collective-permute-done.8) | copy-start | bytes 786436
  180.8 26.1 %collective-permute-start.9 = (bf16[256,1024]{1,0:T(8,128)(2,1)}, bf16[256,1024]{1,0:T(8,128)(2,1)}, u32[]{:S(2)}, u32[]{:S(2)}) collective-permute-start(bf16[256,1024]{1,0:T(8,128)(2,1)} %pad_maximum_fusion), channel_id=1, source_target_pairs={{0,8},{8,0},{1,9},{9,1},{2,10},{10,2},{3,11},{11,3},{4,12},{12,4},... | collective-permute-start | bytes 1572872 | tf_op jit(solution)/shard_map/ppermute | solution.py:19
  203.4 13.7 %all-to-all-start.7 = ((bf16[8,64,512]{2,1,0:T(8,128)(2,1)}), bf16[8,64,512]{2,1,0:T(8,128)(2,1)S(1)}, u32[]{:S(2)}, u32[]{:S(2)}) async-start(bf16[8,64,512]{2,1,0:T(8,128)(2,1)} %shard_map.132), calls=%async_computation.7 | async-start | bytes 1048576 | tf_op jit(solution)/shard_map/all_to_all | solution.py:27
  206.9 10.2 %copy-start.5 = (bf16[1024,256]{1,0:T(8,128)(2,1)S(1)}, bf16[1024,256]{1,0:T(8,128)(2,1)}, u32[]{:S(2)}) copy-start(bf16[1024,256]{1,0:T(8,128)(2,1)} %pgate_ref.3) | copy-start | bytes 1572868
  206.9 10.2 %copy-start.7 = (bf16[1024,256]{1,0:T(8,128)(2,1)S(1)}, bf16[1024,256]{1,0:T(8,128)(2,1)}, u32[]{:S(2)}) copy-start(bf16[1024,256]{1,0:T(8,128)(2,1)} %pup_ref.3) | copy-start | bytes 1572868
  206.9 10.2 %copy-start.9 = (bf16[256,1024]{1,0:T(8,128)(2,1)S(1)}, bf16[256,1024]{1,0:T(8,128)(2,1)}, u32[]{:S(2)}) copy-start(bf16[256,1024]{1,0:T(8,128)(2,1)} %copy-done.8) | copy-start | bytes 1572868
  217.1 1.0 copy-start.13

commit v7 on v5

--- a/solution.py
+++ b/solution.py
@@ -27,15 +27,16 @@
     return lax.dot_general(a, b, (dims, ((), ())), preferred_element_type=F32)
 
 
-def local(kernel, outs, *args, scalars=0):
+def local(kernel, outs, *args, scalars=0, after=0):
     spec = pl.BlockSpec(memory_space=pltpu.VMEM)
     small = pl.BlockSpec(memory_space=pltpu.SMEM)
+    unread = pl.BlockSpec(memory_space=pl.ANY)
     return pl.pallas_call(
         kernel,
         out_shape=[jax.ShapeDtypeStruct(shape, dtype) for shape, dtype in outs],
-        in_specs=[small] * scalars + [spec] * (len(args) - scalars),
+        in_specs=[small] * scalars + [spec] * (len(args) - scalars - after) + [unread] * after,
         out_specs=[spec] * len(outs),
-        compiler_params=pltpu.CompilerParams(vmem_limit_bytes=32 * 2**20),
+        compiler_params=pltpu.CompilerParams(vmem_limit_bytes=16 * 2**20),
     )(*args)
 
 
@@ -51,35 +52,36 @@
             o_ref[block] = (w_ref[block].astype(F32) * mask_ref[i, j].astype(F32)).astype(BF16)
 
 
-def kept_kernel(gmask_ref, umask_ref, gate_ref, up_ref, kgate_ref, kup_ref):
-    keep(gmask_ref, gate_ref, kgate_ref)
-    keep(umask_ref, up_ref, kup_ref)
-
-
-def pre_kernel(
-    dmask_ref,
-    own_ref,
-    other_ref,
-    gate_ref,
-    up_ref,
-    pgate_ref,
-    pup_ref,
-    down_ref,
-    pdown_ref,
-    o_ref,
-    down2_ref,
-):
+def stack_kernel(gmask_ref, umask_ref, gate_ref, up_ref, pgate_ref, pup_ref, o_ref):
     width = gate_ref.shape[1]
-    keep(dmask_ref, down_ref, down2_ref)
-    down2_ref[width:, :] = pdown_ref[...]
+    keep(gmask_ref, gate_ref, o_ref.at[:, :width])
+    keep(umask_ref, up_ref, o_ref.at[:, width : 2 * width])
+    o_ref[:, 2 * width : 3 * width] = pgate_ref[...]
+    o_ref[:, 3 * width :] = pup_ref[...]
+
+
+def pair_kernel(a_ref, b_ref, *refs):
+    o_ref = refs[-1]
+    rows = a_ref.shape[0]
+    o_ref[:rows] = a_ref[...]
+    o_ref[rows:] = b_ref[...]
+
+
+def pre_kernel(own_ref, other_ref, w_ref, o_ref):
+    width = w_ref.shape[1] // 4
     for half, tok_ref in enumerate((own_ref, other_ref)):
-        for j, w_ref in enumerate((gate_ref, up_ref, pgate_ref, pup_ref)):
-            y = dot(tok_ref[...], w_ref[...]).astype(BF16)
+        for j in range(4):
+            cols = slice(j * width, (j + 1) * width)
+            y = dot(tok_ref[...], w_ref[:, cols]).astype(BF16)
             for r in range(2):
                 q = 16 * (2 * half + r)
-                o_ref[:, q : q + 16, j * width : (j + 1) * width] = y[
-                    r * 128 : (r + 1) * 128
-                ].reshape(8, 16, width)
+                o_ref[:, q : q + 16, cols] = y[r * 128 : (r + 1) * 128].reshape(8, 16, width)
+
+
+def down_kernel(mask_ref, down_ref, probe_ref, o_ref):
+    width = down_ref.shape[0]
+    keep(mask_ref, down_ref, o_ref.at[:width, :])
+    o_ref[width:, :] = probe_ref[...]
 
 
 def gate_kernel(x_ref, o_ref, up_slope_ref, act_ref):
@@ -137,7 +139,8 @@
             o_ref[:, place, :, cols] = y[r * 128 : (r + 1) * 128].reshape(4, 32, 256)
 
 
-def spread_kernel(x_ref, o_ref):
+def spread_kernel(x_ref, *refs):
+    o_ref = refs[-1]
     acc = x_ref[0].astype(F32)
     for i in range(1, x_ref.shape[0]):
         acc = acc + x_ref[i].astype(F32)
@@ -159,6 +162,16 @@
             o_ref[place, :, 16 * r : 16 * r + 16, :] = y[r * 128 : (r + 1) * 128].reshape(
                 8, 16, width
             )
+
+
+def later_kernel(x_ref, after_ref, o_ref):
+    o_ref[...] = x_ref[...]
+
+
+def turn_kernel(a_ref, b_ref, after_ref, o_ref):
+    rows = a_ref.shape[0]
+    o_ref[:, :rows] = a_ref[...].T
+    o_ref[:, rows:] = b_ref[...].T
 
 
 def bars_kernel(x_ref, up_slope_ref, act_ref, o_ref):
@@ -177,17 +190,16 @@
             o_ref[i, rows, width:] = up_bar
 
 
-def fisher_kernel(own_ref, other_ref, bars_ref, pgate_ref, pup_ref, gate_ref, up_ref):
+def fisher_kernel(tok_ref, bars_ref, pgate_ref, pup_ref, after_ref, gate_ref, up_ref):
     width = gate_ref.shape[1]
     factor = TOKENS**-0.5
     bars = [bars_ref[:, 16 * q : 16 * q + 16, :].reshape(128, 2 * width) for q in range(4)]
-    y = dot(own_ref[...], jnp.concatenate(bars[:2], axis=0), ((0,), (0,)))
-    y = y + dot(other_ref[...], jnp.concatenate(bars[2:], axis=0), ((0,), (0,)))
+    y = dot(tok_ref[...], jnp.concatenate(bars, axis=0))
     gate_ref[...] = (pgate_ref[...].astype(F32) * y[:, :width] * factor).astype(BF16)
     up_ref[...] = (pup_ref[...].astype(F32) * y[:, width:] * factor).astype(BF16)
 
 
-def fisher(own, other, bars, probe_gate, probe_up):
+def fisher(tok, bars, probe_gate, probe_up, after):
     rows, width = probe_gate.shape
     block = 256
     weight = pl.BlockSpec((block, width), lambda i: (i, 0))
@@ -196,15 +208,15 @@
         grid=(rows // block,),
         out_shape=[jax.ShapeDtypeStruct((rows, width), BF16)] * 2,
         in_specs=[
-            pl.BlockSpec((own.shape[0], block), lambda i: (0, i)),
-            pl.BlockSpec((own.shape[0], block), lambda i: (0, i)),
+            pl.BlockSpec((block, tok.shape[1]), lambda i: (i, 0)),
             pl.BlockSpec(bars.shape, lambda i: (0, 0, 0)),
             weight,
             weight,
+            pl.BlockSpec(memory_space=pl.ANY),
         ],
         out_specs=[weight, weight],
-        compiler_params=pltpu.CompilerParams(vmem_limit_bytes=32 * 2**20),
-    )(own, other, bars, probe_gate, probe_up)
+        compiler_params=pltpu.CompilerParams(vmem_limit_bytes=16 * 2**20),
+    )(tok, bars, probe_gate, probe_up, after)
 
 
 def on_device(
@@ -224,33 +236,26 @@
 
     (mine,) = local(copies_kernel, [((16, 8, feats), BF16)], tokens)
     tok0 = exchange(mine, ("zl", "zh")).reshape(128, feats)
-    kept_gate, kept_up = local(
-        kept_kernel,
-        [(gate_weight.shape, BF16), (up_weight.shape, BF16)],
+    (stacked,) = local(
+        stack_kernel,
+        [((feats, 4 * width), BF16)],
         gate_mask,
         up_mask,
         gate_weight,
         up_weight,
-        scalars=2,
-    )
-    pair = jnp.concatenate([tok0, swap(tok0, "yh")], axis=0)
-    pair2 = swap(pair, "c")
-    partial, down = local(
-        pre_kernel,
-        [((8, 64, 4 * width), BF16), ((2 * width, feats), BF16)],
-        down_mask,
-        pair,
-        pair2,
-        kept_gate,
-        kept_up,
         probe_gate,
         probe_up,
-        down_weight,
-        probe_down,
-        scalars=1,
-    )
+        scalars=2,
+    )
+    (down,) = local(
+        down_kernel, [((2 * width, feats), BF16)], down_mask, down_weight, probe_down, scalars=1
+    )
+    down2 = swap(down, "c")
+    tok1 = swap(tok0, "yh")
+    (pair,) = local(pair_kernel, [((256, feats), BF16)], tok0, tok1, stacked, down2, after=2)
+    pair2 = swap(pair, "c")
+    (partial,) = local(pre_kernel, [((8, 64, 4 * width), BF16)], pair, pair2, stacked)
     pre = exchange(partial, TP)
-    down2 = swap(down, "c")
     send, up_slope, act = local(
         gate_kernel,
         [((2, 8, 32, 2 * width), BF16), ((64, width), F32), ((64, width), F32)],
@@ -265,24 +270,27 @@
         down2,
     )
     term = exchange(term.reshape(8, 32, feats), ("zl", "yh"))
-    (chunk,) = local(spread_kernel, [((4, 32, feats), BF16)], term)
+    hid2 = swap(hid2, "c")
+    (chunk,) = local(spread_kernel, [((4, 32, feats), BF16)], term, hid2, after=1)
+    (tok_t,) = local(turn_kernel, [((feats, TOKENS), BF16)], pair, pair2, chunk, after=1)
     chunk = exchange(chunk, "zh")
-    (chunk,) = local(spread_kernel, [((8, 32, feats), BF16)], chunk)
+    (chunk,) = local(spread_kernel, [((8, 32, feats), BF16)], chunk, tok_t, after=1)
     chunk = exchange(chunk, ("zl", "yh")).reshape(4, 2, 32, feats)
     back, out = local(
         back_kernel, [((2, 8, 32, width), BF16), ((256, feats), BF16)], chunk, down, down2
     )
     back = exchange(back.reshape(16, 32, width), NEAR).reshape(2, 8, 32, width)
     (bars,) = local(bars_kernel, [((8, 64, 2 * width), BF16)], back, up_slope, act)
+    (late,) = local(later_kernel, [(out.shape, BF16)], out, bars, after=1)
     bars = exchange(bars, TP)
 
     grad_down = dot(
-        jnp.concatenate([hid, swap(hid2, "c")], axis=0),
-        jnp.concatenate([out, swap(out, "c")], axis=0),
+        jnp.concatenate([hid, hid2], axis=0),
+        jnp.concatenate([late, swap(late, "c")], axis=0),
         ((0,), (0,)),
     )
     fisher_down = (probe_down.astype(F32) * grad_down * TOKENS**-0.5).astype(BF16)
-    fisher_gate, fisher_up = fisher(pair, pair2, bars, probe_gate, probe_up)
+    fisher_gate, fisher_up = fisher(tok_t, bars, probe_gate, probe_up, fisher_down)
     return (fisher_gate, fisher_up, fisher_down)
 
 

time: 193 us -> 189 us (0.979)
  blocking collectives: 105 us -> 71.4 us
  starting transfers between devices: 34.6 us -> 51 us
  waiting for transfers between devices: 33.1 us -> 41.1 us
  local copies, waits for them, and re-layouts: 5.83 us -> 9.64 us
    all_to_all x5 -> x4, blocking collectives: 105 us -> 71.4 us  [exchange(): return lax.all_to_all(pieces, axes, 0, 0, tiled=True)]
    all_to_all x3 -> x4, starting transfers between devices: 13.3 us -> 32.5 us  [exchange(): return lax.all_to_all(pieces, axes, 0, 0, tiled=True)]
    all_to_all x3 -> x4, waiting for transfers between devices: 27.7 us -> 38 us  [exchange(): return lax.all_to_all(pieces, axes, 0, 0, tiled=True)]
    unnamed x36 -> x48, local copies, waits for them, and re-layouts: 5.83 us -> 9.64 us
    ppermute x5, starting transfers between devices: 21.2 us -> 18.5 us  [swap(): return lax.ppermute(x, axis, [(0, 1), (1, 0)])]
    ppermute x5, waiting for transfers between devices: 5.34 us -> 3.08 us  [swap(): return lax.ppermute(x, axis, [(0, 1), (1, 0)])]
    pallas_call x9 -> x13, Pallas kernels: 8.01 us -> 8.84 us  [local(): pl.pallas_call(kernel, out_shape=[jax.ShapeDtypeStruct(shape, dtype) for...]
  transfers between devices with their start and end apart: 8 -> 9, of which waited for: 6 -> 7; matrix products, arithmetic and copies ran while one was open for 1% -> 1% of each run, Pallas kernels for 2% -> 1%
where the time goes in v7:
time: 189 us; the launch traced here: 188 us
  blocking collectives  71.4 us (38%)
  starting transfers between devices  51 us (27%)
  waiting for transfers between devices  41.1 us (22%)
  Pallas kernels  11.2 us (6%)
  local copies, waits for them, and re-layouts  9.64 us (5%)
  matrix products  2.47 us (1%)
    all_to_all x4, blocking collectives, exchange(): return lax.all_to_all(pieces, axes, 0, 0, tiled=True)  71.4 us
    all_to_all x4, waiting for transfers between devices, exchange(): return lax.all_to_all(pieces, axes, 0, 0, tiled=True)  38 us
    all_to_all x4, starting transfers between devices, exchange(): return lax.all_to_all(pieces, axes, 0, 0, tiled=True)  32.5 us
    ppermute x5, starting transfers between devices, swap(): return lax.ppermute(x, axis, [(0, 1), (1, 0)])  18.5 us
    unnamed x48, local copies, waits for them, and re-layouts  9.64 us
    pallas_call x13, Pallas kernels, local(): pl.pallas_call(kernel, out_shape=[jax.ShapeDtypeStruct(shape, dtype) for...  8.84 us
  transfers between devices with their start and end apart: 9, of which 7 were waited for; matrix products, arithmetic and copies ran while one was open for 1% of the time, Pallas kernels for 1%

profile of v7, /device:TPU:1, one launch (start us, length us, event | category | flops | bytes accessed | tf_op | source)
XLA Modules:
  0.0 187.7 jit_solution(14424886084160632908)
XLA Ops:
  0.6 0.0 copy-start.4
  0.6 0.0 copy-start.2
  0.7 0.0 copy-start.17
  0.7 0.8 copy-done.17
  1.5 0.7 shard_map.121
  2.2 15.7 %all-to-all-start = ((bf16[16,8,1024]{2,1,0:T(8,128)(2,1)}), bf16[16,8,1024]{2,1,0:T(8,128)(2,1)S(1)}, u32[]{:S(2)}, u32[]{:S(2)}) async-start(bf16[16,8,1024]{2,1,0:T(8,128)(2,1)} %shard_map.121), calls=%async_computation | async-start | bytes 524288 | tf_op jit(solution)/shard_map/all_to_all | solution.py:23
  17.9 0.0 copy-start.8
  17.9 1.0 copy-done.8
  19.0 1.0 copy-done.9
  20.0 0.7 copy-done.18
  20.7 0.7 shard_map.123.down_ref
  21.4 2.9 %collective-permute-start.1 = (bf16[512,1024]{1,0:T(8,128)(2,1)S(1)}, bf16[512,1024]{1,0:T(8,128)(2,1)S(1)}, u32[]{:S(2)}, u32[]{:S(2)}) collective-permute-start(bf16[512,1024]{1,0:T(8,128)(2,1)S(1)} %shard_map.123.down_ref), channel_id=1, source_target_pairs={{0,8},{8,0},{1,9},{9,1},{2,10},{10,2},{3,11},{11,3},{4,12},{12,4},... | collective-permute-start | bytes 3145736 | tf_op jit(solution)/shard_map/ppermute | solution.py:19
  24.3 9.0 %all-to-all-done = bf16[16,8,1024]{2,1,0:T(8,128)(2,1)S(1)} async-done(((bf16[16,8,1024]{2,1,0:T(8,128)(2,1)}), bf16[16,8,1024]{2,1,0:T(8,128)(2,1)S(1)}, u32[]{:S(2)}, u32[]{:S(2)}) %all-to-all-start) | async-done | bytes 262176 | tf_op jit(solution)/shard_map/all_to_all | solution.py:23
  33.3 4.8 %collective-permute-start = (bf16[128,1024]{1,0:T(8,128)(2,1)S(1)}, bf16[128,1024]{1,0:T(8,128)(2,1)}, u32[]{:S(2)}, u32[]{:S(2)}) collective-permute-start(bf16[128,1024]{1,0:T(8,128)(2,1)S(1)} %bitcast.9), channel_id=1, source_target_pairs={{0,256},{256,0},{1,257},{257,1},{2,258},{258,2},{3,259},{259,3},{4... | collective-permute-start | bytes 786440 | tf_op jit(solution)/shard_map/ppermute | solution.py:19
  38.1 0.0 copy-done.21
  38.1 0.1 copy.13.gmask_ref
  38.2 0.0 copy-done.22
  38.2 0.1 copy.14.umask_ref
  38.3 0.0 copy-done.4
  38.3 0.0 copy-done.2
  38.3 1.0 copy-done.11
  39.3 1.0 copy-done.12
  40.4 1.0 shard_map.122.refs_0_.w_ref
  41.4 0.0 collective-permute-done.1.refs_1_.down2_ref
  41.4 0.6 collective-permute-done.b_ref
  42.0 1.0 shard_map.124.own_ref.a_ref
  43.0 0.0 copy-start
  43.0 6.2 %collective-permute-start.2 = (bf16[256,1024]{1,0:T(8,128)(2,1)S(1)}, bf16[256,1024]{1,0:T(8,128)(2,1)S(1)}, u32[]{:S(2)}, u32[]{:S(2)}) collective-permute-start(bf16[256,1024]{1,0:T(8,128)(2,1)S(1)} %shard_map.124.own_ref.a_ref), channel_id=1, source_target_pairs={{0,8},{8,0},{1,9},{9,1},{2,10},{10,2},{3,11},{11,3},{4,12},{12,4},... | collective-permute-start | bytes 1572872 | tf_op jit(solution)/shard_map/ppermute | solution.py:19
  49.2 1.5 collective-permute-done.2.other_ref.b_ref
  50.7 1.2 shard_map.125
  51.9 0.0 copy-done
  51.9 19.9 %all_to_all.40.x_ref = bf16[8,64,1024]{2,1,0:T(8,128)(2,1)S(1)} all-to-all(bf16[8,64,1024]{2,1,0:T(8,128)(2,1)S(1)} %shard_map.125), channel_id=1, replica_groups=mesh['yh'=2,'zh'=4,'zl'=4,'c'=2,'yl'=2,'x'=4] {'yl','x'}, dimensions={0} | all-to-all | bytes 2097152 | tf_op jit(solution)/shard_map/all_to_all | solution.py:23
  71.9 0.0 copy-done.6
  71.9 0.2 shard_map.126
  72.1 0.0 copy-start.13
  72.1 14.7 %all_to_all.41 = bf16[16,32,512]{2,1,0:T(8,128)(2,1)S(1)} all-to-all(bf16[16,32,512]{2,1,0:T(8,128)(2,1)S(1)} %bitcast.12), channel_id=1, replica_groups=mesh['yh'=2,'zh'=4,'zl'=4,'c'=2,'yl'=2,'x'=4] {'c','yl','x'}, dimensions={0} | all-to-all | bytes 1048576 | tf_op jit(solution)/shard_map/all_to_all | solution.py:23
  86.8 1.5 shard_map.127
  88.3 0.7 copy-done.19
  89.0 8.6 %all-to-all-start.3 = ((bf16[8,32,1024]{2,1,0:T(8,128)(2,1)}), bf16[8,32,1024]{2,1,0:T(8,128)(2,1)S(1)}, u32[]{:S(2)}, u32[]{:S(2)}) async-start(bf16[8,32,1024]{2,1,0:T(8,128)(2,1)} %bitcast.3), calls=%async_computation.3 | async-start | bytes 1048576 | tf_op jit(solution)/shard_map/all_to_all | solution.py:23
  97.6 2.4 %collective-permute-start.3 = (bf16[256,256]{1,0:T(8,128)(2,1)S(1)}, bf16[256,256]{1,0:T(8,128)(2,1)S(1)}, u32[]{:S(2)}, u32[]{:S(2)}) collective-permute-start(bf16[256,256]{1,0:T(8,128)(2,1)S(1)} %get-tuple-element.15), channel_id=1, source_target_pairs={{0,8},{8,0},{1,9},{9,1},{2,10},{10,2},{3,11},{11,3},{4,12},{12,4},... | collective-permute-start | bytes 393224 | tf_op jit(solution)/shard_map/ppermute | solution.py:19
  100.0 1.0 collective-permute-done.3.refs_0_
  100.9 10.7 %all-to-all-done.3.x_ref = bf16[8,32,1024]{2,1,0:T(8,128)(2,1)S(1)} async-done(((bf16[8,32,1024]{2,1,0:T(8,128)(2,1)}), bf16[8,32,1024]{2,1,0:T(8,128)(2,1)S(1)}, u32[]{:S(2)}, u32[]{:S(2)}) %all-to-all-start.3) | async-done | bytes 524320 | tf_op jit(solution)/shard_map/all_to_all | solution.py:23
  111.7 0.8 shard_map.128.after_ref
  112.4 4.6 %all-to-all-start.4 = ((bf16[4,32,1024]{2,1,0:T(8,128)(2,1)}), bf16[4,32,1024]{2,1,0:T(8,128)(2,1)S(1)}, u32[]{:S(2)}, u32[]{:S(2)}) async-start(bf16[4,32,1024]{2,1,0:T(8,128)(2,1)} %shard_map.128.after_ref), calls=%async_computation.4 | async-start | bytes 524288 | tf_op jit(solution)/shard_map/all_to_all | solution.py:23
  117.1 1.0 copy-done.1
  118.1 1.0 copy-done.7
  119.2 0.3 shard_map.129.refs_0_.tok_ref
  119.5 10.5 %all-to-all-done.4.x_ref = bf16[4,32,1024]{2,1,0:T(8,128)(2,1)S(1)} async-done(((bf16[4,32,1024]{2,1,0:T(8,128)(2,1)}), bf16[4,32,1024]{2,1,0:T(8,128)(2,1)S(1)}, u32[]{:S(2)}, u32[]{:S(2)}) %all-to-all-start.4) | async-done | bytes 262176 | tf_op jit(solution)/shard_map/all_to_all | solution.py:23
  130.1 0.0 copy-start.14
  130.1 0.0 copy-start.16
  130.1 21.7 %all_to_all.42 = bf16[8,32,1024]{2,1,0:T(8,128)(2,1)S(1)} all-to-all(bf16[8,32,1024]{2,1,0:T(8,128)(2,1)S(1)} %shard_map.130), channel_id=1, replica_groups=mesh['yh'=2,'zh'=4,'zl'=4,'c'=2,'yl'=2,'x'=4] {'zl','yh'}, dimensions={0} | all-to-all | bytes 1048576 | tf_op jit(solution)/shard_map/all_to_all | solution.py:23
  151.8 0.5 shard_map.131
  152.3 0.0 copy-start.20
  152.3 15.1 %all_to_all.43 = bf16[16,32,256]{2,1,0:T(8,128)(2,1)S(1)} all-to-all(bf16[16,32,256]{2,1,0:T(8,128)(2,1)S(1)} %bitcast.13), channel_id=1, replica_groups=mesh['yh'=2,'zh'=4,'zl'=4,'c'=2,'yl'=2,'x'=4] {'c','yl','x'}, dimensions={0} | all-to-all | bytes 524288 | tf_op jit(solution)/shard_map/all_to_all | solution.py:23
  167.4 0.8 shard_map.132.after_ref
  168.3 0.0 copy-start.3
  168.3 0.0 copy-start.5
  168.3 2.3 %collective-permute-start.4 = (bf16[256,1024]{1,0:T(8,128)(2,1)S(1)}, bf16[256,1024]{1,0:T(8,128)(2,1)}, u32[]{:S(2)}, u32[]{:S(2)}) collective-permute-start(bf16[256,1024]{1,0:T(8,128)(2,1)S(1)} %shard_map.133), channel_id=1, source_target_pairs={{0,8},{8,0},{1,9},{9,1},{2,10},{10,2},{3,11},{11,3},{4,12},{12,4},... | collective-permute-start | bytes 1572872 | tf_op jit(solution)/shard_map/ppermute | solution.py:19
  170.6 3.5 %all-to-all-start.7 = ((bf16[8,64,512]{2,1,0:T(8,128)(2,1)}), bf16[8,64,512]{2,1,0:T(8,128)(2,1)S(1)}, u32[]{:S(2)}, u32[]{:S(2)}) async-start(bf16[8,64,512]{2,1,0:T(8,128)(2,1)} %shard_map.132.after_ref), calls=%async_computation.7 | async-start | bytes 1048576 | tf_op jit(solution)/shard_map/all_to_all | solution.py:23
  174.1 0.0 collective-permute-done.4
  174.1 2.5 %fusion.1.after_ref = bf16[256,1024]{1,0:T(8,128)(2,1)} fusion(bf16[256,1024]{1,0:T(8,128)(2,1)} %collective-permute-done.4, bf16[256,1024]{1,0:T(8,128)(2,1)S(1)} %shard_map.133, bf16[256,1024]{1,0:T(8,128)(2,1)} %probe_ref.1, bf16[256,256]{1,0:T(8,128)(2,1)S(1)} %collective-permute-done.3.refs_0_, bf16[256,256]{1,0:T(8,128)(2,1)S(1)} %copy-done.20), kind=kOutput, calls=%fused_computation.2 | convolution fusion | flops 272105472 | bytes 2359296 | tf_op jit(solution)/shard_map/dot_general | solution.py:27
  176.6 7.7 %all-to-all-done.7.bars_ref = bf16[8,64,512]{2,1,0:T(8,128)(2,1)S(1)} async-done(((bf16[8,64,512]{2,1,0:T(8,128)(2,1)}), bf16[8,64,512]{2,1,0:T(8,128)(2,1)S(1)}, u32[]{:S(2)}, u32[]{:S(2)}) %all-to-all-start.7) | async-done | bytes 524320 | tf_op jit(solution)/shard_map/all_to_all | solution.py:23
  184.3 1.0 copy-done.10
  185.4 2.3 %shard_map.134 = (bf16[1024,256]{1,0:T(8,128)(2,1)}, bf16[1024,256]{1,0:T(8,128)(2,1)}) custom-call(bf16[1024,512]{1,0:T(8,128)(2,1)S(1)} %shard_map.129.refs_0_.tok_ref, bf16[8,64,512]{2,1,0:T(8,128)(2,1)S(1)} %all-to-all-done.7.bars_ref, bf16[1024,256]{1,0:T(8,128)(2,1)S(1)} %copy-done.3, bf16[1024,256]{1,0:T(8,128)(2,1)S(1)} %copy-done.5, ...), custom_call_target="tpu_custom_call" | custom-call | tf_op jit(solution)/shard_map/pallas_call | solution.py:206
  (21 shorter events, 0.1 us)
Async XLA Ops:
  0.6 37.6 %copy-start.4 = (bf16[1024,256]{1,0:T(8,128)(2,1)S(1)}, bf16[1024,256]{1,0:T(8,128)(2,1)}, u32[]{:S(2)}) copy-start(bf16[1024,256]{1,0:T(8,128)(2,1)} %pup_ref.3) | copy-start | bytes 1572868
  0.6 37.6 %copy-start.2 = (bf16[1024,256]{1,0:T(8,128)(2,1)S(1)}, bf16[1024,256]{1,0:T(8,128)(2,1)}, u32[]{:S(2)}) copy-start(bf16[1024,256]{1,0:T(8,128)(2,1)} %pgate_ref.3) | copy-start | bytes 1572868
  0.7 0.8 copy-start.17
  2.2 31.1 %all-to-all-start = ((bf16[16,8,1024]{2,1,0:T(8,128)(2,1)}), bf16[16,8,1024]{2,1,0:T(8,128)(2,1)S(1)}, u32[]{:S(2)}, u32[]{:S(2)}) async-start(bf16[16,8,1024]{2,1,0:T(8,128)(2,1)} %shard_map.121), calls=%async_computation | async-start | bytes 524288 | tf_op jit(solution)/shard_map/all_to_all | solution.py:23
  17.9 1.0 copy-start.8
  19.0 1.0 copy-start.9
  20.0 0.7 copy-start.18
  20.7 17.4 %copy-start.21 = (s32[8,2]{0,1:T(2,128)S(1)}, s32[8,2]{0,1:T(2,128)}, u32[]{:S(2)}) copy-start(s32[8,2]{0,1:T(2,128)} %param.14) | copy-start | bytes 196
  20.7 17.5 %copy-start.22 = (s32[8,2]{0,1:T(2,128)S(1)}, s32[8,2]{0,1:T(2,128)}, u32[]{:S(2)}) copy-start(s32[8,2]{0,1:T(2,128)} %param.15) | copy-start | bytes 196
  21.4 20.0 %collective-permute-start.1 = (bf16[512,1024]{1,0:T(8,128)(2,1)S(1)}, bf16[512,1024]{1,0:T(8,128)(2,1)S(1)}, u32[]{:S(2)}, u32[]{:S(2)}) collective-permute-start(bf16[512,1024]{1,0:T(8,128)(2,1)S(1)} %shard_map.123.down_ref), channel_id=1, source_target_pairs={{0,8},{8,0},{1,9},{9,1},{2,10},{10,2},{3,11},{11,3},{4,12},{12,4},... | collective-permute-start | bytes 3145736 | tf_op jit(solution)/shard_map/ppermute | solution.py:19
  33.3 8.7 %collective-permute-start = (bf16[128,1024]{1,0:T(8,128)(2,1)S(1)}, bf16[128,1024]{1,0:T(8,128)(2,1)}, u32[]{:S(2)}, u32[]{:S(2)}) collective-permute-start(bf16[128,1024]{1,0:T(8,128)(2,1)S(1)} %bitcast.9), channel_id=1, source_target_pairs={{0,256},{256,0},{1,257},{257,1},{2,258},{258,2},{3,259},{259,3},{4... | collective-permute-start | bytes 786440 | tf_op jit(solution)/shard_map/ppermute | solution.py:19
  38.3 1.0 copy-start.11
  39.3 1.0 copy-start.12
  43.0 9.0 %copy-start = (bf16[256,1024]{1,0:T(8,128)(2,1)}, bf16[256,1024]{1,0:T(8,128)(2,1)S(1)}, u32[]{:S(2)}) copy-start(bf16[256,1024]{1,0:T(8,128)(2,1)S(1)} %shard_map.124.own_ref.a_ref) | copy-start | bytes 1572868
  43.0 7.7 %collective-permute-start.2 = (bf16[256,1024]{1,0:T(8,128)(2,1)S(1)}, bf16[256,1024]{1,0:T(8,128)(2,1)S(1)}, u32[]{:S(2)}, u32[]{:S(2)}) collective-permute-start(bf16[256,1024]{1,0:T(8,128)(2,1)S(1)} %shard_map.124.own_ref.a_ref), channel_id=1, source_target_pairs={{0,8},{8,0},{1,9},{9,1},{2,10},{10,2},{3,11},{11,3},{4,12},{12,4},... | collective-permute-start | bytes 1572872 | tf_op jit(solution)/shard_map/ppermute | solution.py:19
  50.7 21.2 %copy-start.6 = (bf16[256,1024]{1,0:T(8,128)(2,1)}, bf16[256,1024]{1,0:T(8,128)(2,1)S(1)}, u32[]{:S(2)}) copy-start(bf16[256,1024]{1,0:T(8,128)(2,1)S(1)} %collective-permute-done.2.other_ref.b_ref) | copy-start | bytes 1572868
  72.1 16.2 %copy-start.13 = (f32[64,256]{1,0:T(8,128)}, f32[64,256]{1,0:T(8,128)S(1)}, u32[]{:S(2)}) copy-start(f32[64,256]{1,0:T(8,128)S(1)} %get-tuple-element.17.up_slope_ref) | copy-start | bytes 196612
  72.1 16.9 %copy-start.15 = (f32[64,256]{1,0:T(8,128)}, f32[64,256]{1,0:T(8,128)S(1)}, u32[]{:S(2)}) copy-start(f32[64,256]{1,0:T(8,128)S(1)} %get-tuple-element.18.act_ref) | copy-start | bytes 196612
  88.3 0.7 copy-start.19
  89.0 22.7 %all-to-all-start.3 = ((bf16[8,32,1024]{2,1,0:T(8,128)(2,1)}), bf16[8,32,1024]{2,1,0:T(8,128)(2,1)S(1)}, u32[]{:S(2)}, u32[]{:S(2)}) async-start(bf16[8,32,1024]{2,1,0:T(8,128)(2,1)} %bitcast.3), calls=%async_computation.3 | async-start | bytes 1048576 | tf_op jit(solution)/shard_map/all_to_all | solution.py:23
  97.6 3.4 %collective-permute-start.3 = (bf16[256,256]{1,0:T(8,128)(2,1)S(1)}, bf16[256,256]{1,0:T(8,128)(2,1)S(1)}, u32[]{:S(2)}, u32[]{:S(2)}) collective-permute-start(bf16[256,256]{1,0:T(8,128)(2,1)S(1)} %get-tuple-element.15), channel_id=1, source_target_pairs={{0,8},{8,0},{1,9},{9,1},{2,10},{10,2},{3,11},{11,3},{4,12},{12,4},... | collective-permute-start | bytes 393224 | tf_op jit(solution)/shard_map/ppermute | solution.py:19
  112.4 17.6 %all-to-all-start.4 = ((bf16[4,32,1024]{2,1,0:T(8,128)(2,1)}), bf16[4,32,1024]{2,1,0:T(8,128)(2,1)S(1)}, u32[]{:S(2)}, u32[]{:S(2)}) async-start(bf16[4,32,1024]{2,1,0:T(8,128)(2,1)} %shard_map.128.after_ref), calls=%async_computation.4 | async-start | bytes 524288 | tf_op jit(solution)/shard_map/all_to_all | solution.py:23
  117.1 1.0 copy-start.1
  118.1 1.0 copy-start.7
  130.1 37.3 %copy-start.14 = (f32[64,256]{1,0:T(8,128)S(1)}, f32[64,256]{1,0:T(8,128)}, u32[]{:S(2)}) copy-start(f32[64,256]{1,0:T(8,128)} %copy-done.13) | copy-start | bytes 196612
  130.1 37.3 %copy-start.16 = (f32[64,256]{1,0:T(8,128)S(1)}, f32[64,256]{1,0:T(8,128)}, u32[]{:S(2)}) copy-start(f32[64,256]{1,0:T(8,128)} %copy-done.15) | copy-start | bytes 196612
  152.3 21.8 %copy-start.20 = (bf16[256,256]{1,0:T(8,128)(2,1)S(1)}, bf16[256,256]{1,0:T(8,128)(2,1)}, u32[]{:S(2)}) copy-start(bf16[256,256]{1,0:T(8,128)(2,1)} %copy-done.19) | copy-start | bytes 393220
  168.3 16.1 %copy-start.3 = (bf16[1024,256]{1,0:T(8,128)(2,1)S(1)}, bf16[1024,256]{1,0:T(8,128)(2,1)}, u32[]{:S(2)}) copy-start(bf16[1024,256]{1,0:T(8,128)(2,1)} %pgate_ref.3) | copy-start | bytes 1572868
  168.3 16.0 %copy-start.5 = (bf16[1024,256]{1,0:T(8,128)(2,1)S(1)}, bf16[1024,256]{1,0:T(8,128)(2,1)}, u32[]{:S(2)}) copy-start(bf16[1024,256]{1,0:T(8,128)(2,1)} %pup_ref.3) | copy-start | bytes 1572868
  168.3 5.8 %collective-permute-start.4 = (bf16[256,1024]{1,0:T(8,128)(2,1)S(1)}, bf16[256,1024]{1,0:T(8,128)(2,1)}, u32[]{:S(2)}, u32[]{:S(2)}) collective-permute-start(bf16[256,1024]{1,0:T(8,128)(2,1)S(1)} %shard_map.133), channel_id=1, source_target_pairs={{0,8},{8,0},{1,9},{9,1},{2,10},{10,2},{3,11},{11,3},{4,12},{12,4},... | collective-permute-start | bytes 1572872 | tf_op jit(solution)/shard_map/ppermute | solution.py:19
  170.6 13.7 %all-to-all-start.7 = ((bf16[8,64,512]{2,1,0:T(8,128)(2,1)}), bf16[8,64,512]{2,1,0:T(8,128)(2,1)S(1)}, u32[]{:S(2)}, u32[]{:S(2)}) async-start(bf16[8,64,512]{2,1,0:T(8,128)(2,1)} %shard_map.132.after_ref), calls=%async_computation.7 | async-start | bytes 1048576 | tf_op jit(solution)/shard_map/all_to_all | solution.py:23
  184.3 1.0 copy-start.10

commit v8 on v7

--- a/solution.py
+++ b/solution.py
@@ -60,14 +60,8 @@
     o_ref[:, 3 * width :] = pup_ref[...]
 
 
-def pair_kernel(a_ref, b_ref, *refs):
+def pre_kernel(own_ref, other_ref, w_ref, *refs):
     o_ref = refs[-1]
-    rows = a_ref.shape[0]
-    o_ref[:rows] = a_ref[...]
-    o_ref[rows:] = b_ref[...]
-
-
-def pre_kernel(own_ref, other_ref, w_ref, o_ref):
     width = w_ref.shape[1] // 4
     for half, tok_ref in enumerate((own_ref, other_ref)):
         for j in range(4):
@@ -139,8 +133,7 @@
             o_ref[:, place, :, cols] = y[r * 128 : (r + 1) * 128].reshape(4, 32, 256)
 
 
-def spread_kernel(x_ref, *refs):
-    o_ref = refs[-1]
+def spread_kernel(x_ref, o_ref):
     acc = x_ref[0].astype(F32)
     for i in range(1, x_ref.shape[0]):
         acc = acc + x_ref[i].astype(F32)
@@ -164,8 +157,10 @@
             )
 
 
-def later_kernel(x_ref, after_ref, o_ref):
-    o_ref[...] = x_ref[...]
+def join_kernel(a_ref, b_ref, after_ref, o_ref):
+    cols = a_ref.shape[1]
+    o_ref[:, :cols] = a_ref[...]
+    o_ref[:, cols:] = b_ref[...]
 
 
 def turn_kernel(a_ref, b_ref, after_ref, o_ref):
@@ -190,17 +185,29 @@
             o_ref[i, rows, width:] = up_bar
 
 
-def fisher_kernel(tok_ref, bars_ref, pgate_ref, pup_ref, after_ref, gate_ref, up_ref):
+def fisher_down_kernel(hid_ref, out_ref, joined_ref, probe_ref, o_ref, done_ref):
+    feats = out_ref.shape[1]
+    own = hid_ref[...].T
+    other = joined_ref[:, feats:].T
+    for j in range(4):
+        cols = slice(j * 256, (j + 1) * 256)
+        y = dot(own, out_ref[:, cols]) + dot(other, joined_ref[:, cols])
+        o_ref[:, cols] = (probe_ref[:, cols].astype(F32) * y * TOKENS**-0.5).astype(BF16)
+    done_ref[...] = joined_ref[:16, :128]
+
+
+def fisher_kernel(tok_ref, bars_ref, probe_ref, after_ref, gate_ref, up_ref):
     width = gate_ref.shape[1]
     factor = TOKENS**-0.5
     bars = [bars_ref[:, 16 * q : 16 * q + 16, :].reshape(128, 2 * width) for q in range(4)]
     y = dot(tok_ref[...], jnp.concatenate(bars, axis=0))
-    gate_ref[...] = (pgate_ref[...].astype(F32) * y[:, :width] * factor).astype(BF16)
-    up_ref[...] = (pup_ref[...].astype(F32) * y[:, width:] * factor).astype(BF16)
-
-
-def fisher(tok, bars, probe_gate, probe_up, after):
-    rows, width = probe_gate.shape
+    gate_ref[...] = (probe_ref[:, :width].astype(F32) * y[:, :width] * factor).astype(BF16)
+    up_ref[...] = (probe_ref[:, width:].astype(F32) * y[:, width:] * factor).astype(BF16)
+
+
+def fisher(tok, bars, stacked, after):
+    rows = stacked.shape[0]
+    width = stacked.shape[1] // 4
     block = 256
     weight = pl.BlockSpec((block, width), lambda i: (i, 0))
     return pl.pallas_call(
@@ -210,13 +217,12 @@
         in_specs=[
             pl.BlockSpec((block, tok.shape[1]), lambda i: (i, 0)),
             pl.BlockSpec(bars.shape, lambda i: (0, 0, 0)),
-            weight,
-            weight,
+            pl.BlockSpec((block, 2 * width), lambda i: (i, 1)),
             pl.BlockSpec(memory_space=pl.ANY),
         ],
         out_specs=[weight, weight],
         compiler_params=pltpu.CompilerParams(vmem_limit_bytes=16 * 2**20),
-    )(tok, bars, probe_gate, probe_up, after)
+    )(tok, bars, stacked, after)
 
 
 def on_device(
@@ -252,9 +258,12 @@
     )
     down2 = swap(down, "c")
     tok1 = swap(tok0, "yh")
-    (pair,) = local(pair_kernel, [((256, feats), BF16)], tok0, tok1, stacked, down2, after=2)
+    tok1, seen, seen2 = lax.optimization_barrier((tok1, stacked[:16, :128], down2[:16, :128]))
+    pair = jnp.concatenate([tok0, tok1], axis=0)
     pair2 = swap(pair, "c")
-    (partial,) = local(pre_kernel, [((8, 64, 4 * width), BF16)], pair, pair2, stacked)
+    (partial,) = local(
+        pre_kernel, [((8, 64, 4 * width), BF16)], pair, pair2, stacked, seen, seen2, after=2
+    )
     pre = exchange(partial, TP)
     send, up_slope, act = local(
         gate_kernel,
@@ -270,27 +279,30 @@
         down2,
     )
     term = exchange(term.reshape(8, 32, feats), ("zl", "yh"))
-    hid2 = swap(hid2, "c")
-    (chunk,) = local(spread_kernel, [((4, 32, feats), BF16)], term, hid2, after=1)
-    (tok_t,) = local(turn_kernel, [((feats, TOKENS), BF16)], pair, pair2, chunk, after=1)
+    (chunk,) = local(spread_kernel, [((4, 32, feats), BF16)], term)
     chunk = exchange(chunk, "zh")
-    (chunk,) = local(spread_kernel, [((8, 32, feats), BF16)], chunk, tok_t, after=1)
+    (chunk,) = local(spread_kernel, [((8, 32, feats), BF16)], chunk)
     chunk = exchange(chunk, ("zl", "yh")).reshape(4, 2, 32, feats)
     back, out = local(
         back_kernel, [((2, 8, 32, width), BF16), ((256, feats), BF16)], chunk, down, down2
     )
     back = exchange(back.reshape(16, 32, width), NEAR).reshape(2, 8, 32, width)
     (bars,) = local(bars_kernel, [((8, 64, 2 * width), BF16)], back, up_slope, act)
-    (late,) = local(later_kernel, [(out.shape, BF16)], out, bars, after=1)
+    joined, tok_t = (
+        local(join_kernel, [((256, feats + width), BF16)], out, hid2, bars, after=1)[0],
+        local(turn_kernel, [((feats, TOKENS), BF16)], pair, pair2, bars, after=1)[0],
+    )
     bars = exchange(bars, TP)
-
-    grad_down = dot(
-        jnp.concatenate([hid, hid2], axis=0),
-        jnp.concatenate([late, swap(late, "c")], axis=0),
-        ((0,), (0,)),
-    )
-    fisher_down = (probe_down.astype(F32) * grad_down * TOKENS**-0.5).astype(BF16)
-    fisher_gate, fisher_up = fisher(tok_t, bars, probe_gate, probe_up, fisher_down)
+    joined = swap(joined, "c")
+    fisher_down, done = local(
+        fisher_down_kernel,
+        [(probe_down.shape, BF16), ((16, 128), BF16)],
+        hid,
+        out,
+        joined,
+        probe_down,
+    )
+    fisher_gate, fisher_up = fisher(tok_t, bars, stacked, done)
     return (fisher_gate, fisher_up, fisher_down)
 
 

time: 189 us -> 192 us (1.016)
  blocking collectives: 71.4 us -> 111 us
  waiting for transfers between devices: 41.1 us -> 16 us
  starting transfers between devices: 51 us -> 35 us
  Pallas kernels: 11.2 us -> 15.4 us
  matrix products: 2.47 us -> 0 us
    all_to_all x4 -> x6, blocking collectives: 71.4 us -> 111 us  [exchange(): return lax.all_to_all(pieces, axes, 0, 0, tiled=True)]
    all_to_all x4 -> x2, waiting for transfers between devices: 38 us -> 14.5 us  [exchange(): return lax.all_to_all(pieces, axes, 0, 0, tiled=True)]
    all_to_all x4 -> x2, starting transfers between devices: 32.5 us -> 19.9 us  [exchange(): return lax.all_to_all(pieces, axes, 0, 0, tiled=True)]
    ppermute x5 -> x4, starting transfers between devices: 18.5 us -> 15.1 us  [swap(): return lax.ppermute(x, axis, [(0, 1), (1, 0)])]
    pallas_call x13, Pallas kernels: 8.84 us -> 12 us  [local(): pl.pallas_call(kernel, out_shape=[jax.ShapeDtypeStruct(shape, dtype) for...]
    dot_general x1 -> x0, matrix products: 2.47 us -> none  [dot(): return lax.dot_general(a, b, (dims, ((), ())), preferred_element_type=F32)]
    unnamed x48 -> x40, local copies, waits for them, and re-layouts: 9.64 us -> 10.7 us
  transfers between devices with their start and end apart: 9 -> 6, of which waited for: 7 -> 3; matrix products, arithmetic and copies ran while one was open for 1% -> 0% of each run, Pallas kernels for 1% -> 2%
where the time goes in v8:
time: 192 us; the launch traced here: 191 us
  blocking collectives  111 us (58%)
  starting transfers between devices  35 us (18%)
  waiting for transfers between devices  16 us (8%)
  Pallas kernels  15.4 us (8%)
  local copies, waits for them, and re-layouts  11.4 us (6%)
    all_to_all x6, blocking collectives, exchange(): return lax.all_to_all(pieces, axes, 0, 0, tiled=True)  111 us
    all_to_all x2, starting transfers between devices, exchange(): return lax.all_to_all(pieces, axes, 0, 0, tiled=True)  19.9 us
    ppermute x4, starting transfers between devices, swap(): return lax.ppermute(x, axis, [(0, 1), (1, 0)])  15.1 us
    all_to_all x2, waiting for transfers between devices, exchange(): return lax.all_to_all(pieces, axes, 0, 0, tiled=True)  14.5 us
    pallas_call x13, Pallas kernels, local(): pl.pallas_call(kernel, out_shape=[jax.ShapeDtypeStruct(shape, dtype) for...  12 us
    unnamed x40, local copies, waits for them, and re-layouts  10.7 us
  transfers between devices with their start and end apart: 6, of which 3 were waited for; matrix products, arithmetic and copies ran while one was open for 0% of the time, Pallas kernels for 2%

profile of v8, /device:TPU:1, one launch (start us, length us, event | category | flops | bytes accessed | tf_op | source)
XLA Modules:
  0.0 190.6 jit_solution(12125593697771752305)
XLA Ops:
  0.6 0.0 copy-start.15
  0.6 0.7 copy-done.15
  1.3 0.0 copy-start.17
  1.4 0.7 shard_map.121
  2.1 15.7 %all-to-all-start = ((bf16[16,8,1024]{2,1,0:T(8,128)(2,1)}), bf16[16,8,1024]{2,1,0:T(8,128)(2,1)S(1)}, u32[]{:S(2)}, u32[]{:S(2)}) async-start(bf16[16,8,1024]{2,1,0:T(8,128)(2,1)} %shard_map.121), calls=%async_computation | async-start | bytes 524288 | tf_op jit(solution)/shard_map/all_to_all | solution.py:23
  17.8 0.0 copy-start.6
  17.8 1.0 copy-done.6
  18.9 1.0 copy-done.10
  19.9 0.7 copy-done.16
  20.6 0.7 shard_map.123.down_ref
  21.3 2.9 %collective-permute-start.1 = (bf16[512,1024]{1,0:T(8,128)(2,1)S(1)}, bf16[512,1024]{1,0:T(8,128)(2,1)}, u32[]{:S(2)}, u32[]{:S(2)}) collective-permute-start(bf16[512,1024]{1,0:T(8,128)(2,1)S(1)} %shard_map.123.down_ref), channel_id=1, source_target_pairs={{0,8},{8,0},{1,9},{9,1},{2,10},{10,2},{3,11},{11,3},{4,12},{12,4},... | collective-permute-start | bytes 3145736 | tf_op jit(solution)/shard_map/ppermute | solution.py:19
  24.2 9.0 %all-to-all-done = bf16[16,8,1024]{2,1,0:T(8,128)(2,1)S(1)} async-done(((bf16[16,8,1024]{2,1,0:T(8,128)(2,1)}), bf16[16,8,1024]{2,1,0:T(8,128)(2,1)S(1)}, u32[]{:S(2)}, u32[]{:S(2)}) %all-to-all-start) | async-done | bytes 262176 | tf_op jit(solution)/shard_map/all_to_all | solution.py:23
  33.2 4.8 %collective-permute-start = (bf16[128,1024]{1,0:T(8,128)(2,1)S(1)}, bf16[128,1024]{1,0:T(8,128)(2,1)}, u32[]{:S(2)}, u32[]{:S(2)}) collective-permute-start(bf16[128,1024]{1,0:T(8,128)(2,1)S(1)} %bitcast.13), channel_id=1, source_target_pairs={{0,256},{256,0},{1,257},{257,1},{2,258},{258,2},{3,259},{259,3},{4... | collective-permute-start | bytes 786440 | tf_op jit(solution)/shard_map/ppermute | solution.py:19
  38.0 0.0 copy-done.17
  38.0 0.1 copy.13.gmask_ref
  38.1 0.0 copy-done.18
  38.1 0.1 copy.14.umask_ref
  38.2 1.0 copy-done.11
  39.2 1.0 copy-done.12
  40.2 1.0 copy-done.13
  41.3 1.0 copy-done.14
  42.3 1.0 shard_map.122.w_ref.probe_ref
  43.4 0.0 collective-permute-done.1.down2_ref
  43.4 0.7 slice.9.refs_1_
  44.1 0.0 collective-permute-done
  44.1 1.0 pad_maximum_fusion.own_ref.a_ref
  45.1 0.0 copy-start
  45.1 5.3 %collective-permute-start.2 = (bf16[256,1024]{1,0:T(8,128)(2,1)S(1)}, bf16[256,1024]{1,0:T(8,128)(2,1)S(1)}, u32[]{:S(2)}, u32[]{:S(2)}) collective-permute-start(bf16[256,1024]{1,0:T(8,128)(2,1)S(1)} %pad_maximum_fusion.own_ref.a_ref), channel_id=1, source_target_pairs={{0,8},{8,0},{1,9},{9,1},{2,10},{10,2},{3,11},{11,3},{4,12},{12,4},... | collective-permute-start | bytes 1572872 | tf_op jit(solution)/shard_map/ppermute | solution.py:19
  50.4 1.5 collective-permute-done.2.other_ref.b_ref
  51.9 1.2 shard_map.124
  53.1 0.0 copy-done
  53.2 0.0 copy-start.8
  53.2 0.8 copy-done.8
  53.9 19.0 %all_to_all.40.x_ref = bf16[8,64,1024]{2,1,0:T(8,128)(2,1)S(1)} all-to-all(bf16[8,64,1024]{2,1,0:T(8,128)(2,1)S(1)} %shard_map.124), channel_id=1, replica_groups=mesh['yh'=2,'zh'=4,'zl'=4,'c'=2,'yl'=2,'x'=4] {'yl','x'}, dimensions={0} | all-to-all | bytes 2097152 | tf_op jit(solution)/shard_map/all_to_all | solution.py:23
  73.0 0.2 shard_map.125
  73.1 14.7 %all_to_all.41 = bf16[16,32,512]{2,1,0:T(8,128)(2,1)S(1)} all-to-all(bf16[16,32,512]{2,1,0:T(8,128)(2,1)S(1)} %bitcast.10), channel_id=1, replica_groups=mesh['yh'=2,'zh'=4,'zl'=4,'c'=2,'yl'=2,'x'=4] {'c','yl','x'}, dimensions={0} | all-to-all | bytes 1048576 | tf_op jit(solution)/shard_map/all_to_all | solution.py:23
  87.8 1.9 %shard_map.126 = (bf16[4,2,32,1024]{3,2,1,0:T(8,128)(2,1)S(1)}, bf16[256,256]{1,0:T(8,128)(2,1)S(1)}, bf16[256,256]{1,0:T(8,128)(2,1)S(1)}) custom-call(bf16[2,8,32,512]{3,2,1,0:T(8,128)(2,1)S(1)} %bitcast.8, bf16[512,1024]{1,0:T(8,128)(2,1)S(1)} %shard_map.123.down_ref, bf16[512,1024]{1,0:T(8,128)(2,1)} %collective-permute-done.1.down2_ref), custom_call_target="tpu_custom_call" | custom-call | tf_op jit(solution)/shard_map/pallas_call | solution.py:34
  89.8 22.1 %all_to_all.42.x_ref = bf16[8,32,1024]{2,1,0:T(8,128)(2,1)S(1)} all-to-all(bf16[8,32,1024]{2,1,0:T(8,128)(2,1)S(1)} %bitcast.11), channel_id=1, replica_groups=mesh['yh'=2,'zh'=4,'zl'=4,'c'=2,'yl'=2,'x'=4] {'zl','yh'}, dimensions={0} | all-to-all | bytes 1048576 | tf_op jit(solution)/shard_map/all_to_all | solution.py:23
  111.9 0.1 shard_map.127
  111.9 19.7 %all_to_all.43.x_ref = bf16[4,32,1024]{2,1,0:T(8,128)(2,1)S(1)} all-to-all(bf16[4,32,1024]{2,1,0:T(8,128)(2,1)S(1)} %shard_map.127), channel_id=1, replica_groups=mesh['yh'=2,'zh'=4,'zl'=4,'c'=2,'yl'=2,'x'=4] {'zh'}, dimensions={0} | all-to-all | bytes 524288 | tf_op jit(solution)/shard_map/all_to_all | solution.py:23
  131.7 21.6 %all_to_all.44 = bf16[8,32,1024]{2,1,0:T(8,128)(2,1)S(1)} all-to-all(bf16[8,32,1024]{2,1,0:T(8,128)(2,1)S(1)} %shard_map.128), channel_id=1, replica_groups=mesh['yh'=2,'zh'=4,'zl'=4,'c'=2,'yl'=2,'x'=4] {'zl','yh'}, dimensions={0} | all-to-all | bytes 1048576 | tf_op jit(solution)/shard_map/all_to_all | solution.py:23
  153.2 1.7 shard_map.129
  154.9 0.0 copy-start.4
  154.9 0.0 copy-start.1
  154.9 0.0 copy-start.9
  155.0 13.9 %all_to_all.45 = bf16[16,32,256]{2,1,0:T(8,128)(2,1)S(1)} all-to-all(bf16[16,32,256]{2,1,0:T(8,128)(2,1)S(1)} %bitcast.12), channel_id=1, replica_groups=mesh['yh'=2,'zh'=4,'zl'=4,'c'=2,'yl'=2,'x'=4] {'c','yl','x'}, dimensions={0} | all-to-all | bytes 524288 | tf_op jit(solution)/shard_map/all_to_all | solution.py:23
  168.8 0.9 shard_map.130.after_ref
  169.7 0.0 copy-done.4
  169.7 0.9 shard_map.132
  170.6 2.1 %collective-permute-start.3 = (bf16[256,1280]{1,0:T(8,128)(2,1)}, bf16[256,1280]{1,0:T(8,128)(2,1)}, u32[]{:S(2)}, u32[]{:S(2)}) collective-permute-start(bf16[256,1280]{1,0:T(8,128)(2,1)} %shard_map.132), channel_id=1, source_target_pairs={{0,8},{8,0},{1,9},{9,1},{2,10},{10,2},{3,11},{11,3},{4,12},{12,4},... | collective-permute-start | bytes 1966088 | tf_op jit(solution)/shard_map/ppermute | solution.py:19
  172.7 4.2 %all-to-all-start.7 = ((bf16[8,64,512]{2,1,0:T(8,128)(2,1)}), bf16[8,64,512]{2,1,0:T(8,128)(2,1)}, u32[]{:S(2)}, u32[]{:S(2)}) async-start(bf16[8,64,512]{2,1,0:T(8,128)(2,1)} %shard_map.130.after_ref), calls=%async_computation.7 | async-start | bytes 1048576 | tf_op jit(solution)/shard_map/all_to_all | solution.py:23
  176.9 0.0 copy-done.1
  176.9 0.0 copy-done.9
  176.9 0.0 copy-start.5
  176.9 0.3 shard_map.131.tok_ref
  177.2 0.0 copy-start.2
  177.3 1.0 copy-done.2
  178.2 0.0 collective-permute-done.3.joined_ref
  178.2 0.0 copy-done.5
  178.2 1.1 copy-done.7
  179.4 2.3 %shard_map.133 = (bf16[256,1024]{1,0:T(8,128)(2,1)}, bf16[16,128]{1,0:T(8,128)(2,1)S(1)}) custom-call(bf16[256,256]{1,0:T(8,128)(2,1)S(1)} %get-tuple-element.26.hid_ref, bf16[256,1024]{1,0:T(8,128)(2,1)S(1)} %copy-done.5, bf16[256,1280]{1,0:T(8,128)(2,1)} %collective-permute-done.3.joined_ref, bf16[256,1024]{1,0:T(8,128)(2,1)S(1)} %copy-done.7), custom_call_target="tpu_custom_call" | custom-call | tf_op jit(solution)/shard_map/pallas_call | solution.py:34
  181.7 5.5 %all-to-all-done.7.bars_ref = bf16[8,64,512]{2,1,0:T(8,128)(2,1)} async-done(((bf16[8,64,512]{2,1,0:T(8,128)(2,1)}), bf16[8,64,512]{2,1,0:T(8,128)(2,1)}, u32[]{:S(2)}, u32[]{:S(2)}) %all-to-all-start.7) | async-done | bytes 524320 | tf_op jit(solution)/shard_map/all_to_all | solution.py:23
  187.2 0.0 copy-done.3
  187.2 3.4 %shard_map.134 = (bf16[1024,256]{1,0:T(8,128)(2,1)}, bf16[1024,256]{1,0:T(8,128)(2,1)}) custom-call(bf16[1024,512]{1,0:T(8,128)(2,1)S(1)} %copy-done.3, bf16[8,64,512]{2,1,0:T(8,128)(2,1)} %all-to-all-done.7.bars_ref, bf16[1024,1024]{1,0:T(8,128)(2,1)S(1)} %shard_map.122.w_ref.probe_ref, bf16[16,128]{1,0:T(8,128)(2,1)S(1)} %get-tuple-element.29.after_ref), custom_call_target="tpu_custom_call" | custom-call | tf_op jit(solution)/shard_map/pallas_call | solution.py:213
  (11 shorter events, 0.1 us)
Async XLA Ops:
  0.6 0.7 copy-start.15
  1.3 36.6 %copy-start.17 = (s32[8,2]{0,1:T(2,128)S(1)}, s32[8,2]{0,1:T(2,128)}, u32[]{:S(2)}) copy-start(s32[8,2]{0,1:T(2,128)} %param.14) | copy-start | bytes 196
  1.4 36.7 %copy-start.18 = (s32[8,2]{0,1:T(2,128)S(1)}, s32[8,2]{0,1:T(2,128)}, u32[]{:S(2)}) copy-start(s32[8,2]{0,1:T(2,128)} %param.15) | copy-start | bytes 196
  2.1 31.1 %all-to-all-start = ((bf16[16,8,1024]{2,1,0:T(8,128)(2,1)}), bf16[16,8,1024]{2,1,0:T(8,128)(2,1)S(1)}, u32[]{:S(2)}, u32[]{:S(2)}) async-start(bf16[16,8,1024]{2,1,0:T(8,128)(2,1)} %shard_map.121), calls=%async_computation | async-start | bytes 524288 | tf_op jit(solution)/shard_map/all_to_all | solution.py:23
  17.8 1.0 copy-start.6
  18.9 1.0 copy-start.10
  19.9 0.7 copy-start.16
  21.3 22.1 %collective-permute-start.1 = (bf16[512,1024]{1,0:T(8,128)(2,1)S(1)}, bf16[512,1024]{1,0:T(8,128)(2,1)}, u32[]{:S(2)}, u32[]{:S(2)}) collective-permute-start(bf16[512,1024]{1,0:T(8,128)(2,1)S(1)} %shard_map.123.down_ref), channel_id=1, source_target_pairs={{0,8},{8,0},{1,9},{9,1},{2,10},{10,2},{3,11},{11,3},{4,12},{12,4},... | collective-permute-start | bytes 3145736 | tf_op jit(solution)/shard_map/ppermute | solution.py:19
  33.2 10.9 %collective-permute-start = (bf16[128,1024]{1,0:T(8,128)(2,1)S(1)}, bf16[128,1024]{1,0:T(8,128)(2,1)}, u32[]{:S(2)}, u32[]{:S(2)}) collective-permute-start(bf16[128,1024]{1,0:T(8,128)(2,1)S(1)} %bitcast.13), channel_id=1, source_target_pairs={{0,256},{256,0},{1,257},{257,1},{2,258},{258,2},{3,259},{259,3},{4... | collective-permute-start | bytes 786440 | tf_op jit(solution)/shard_map/ppermute | solution.py:19
  38.2 1.0 copy-start.11
  39.2 1.0 copy-start.12
  40.2 1.0 copy-start.13
  41.3 1.0 copy-start.14
  45.1 8.1 %copy-start = (bf16[256,1024]{1,0:T(8,128)(2,1)}, bf16[256,1024]{1,0:T(8,128)(2,1)S(1)}, u32[]{:S(2)}) copy-start(bf16[256,1024]{1,0:T(8,128)(2,1)S(1)} %pad_maximum_fusion.own_ref.a_ref) | copy-start | bytes 1572868
  45.1 6.8 %collective-permute-start.2 = (bf16[256,1024]{1,0:T(8,128)(2,1)S(1)}, bf16[256,1024]{1,0:T(8,128)(2,1)S(1)}, u32[]{:S(2)}, u32[]{:S(2)}) collective-permute-start(bf16[256,1024]{1,0:T(8,128)(2,1)S(1)} %pad_maximum_fusion.own_ref.a_ref), channel_id=1, source_target_pairs={{0,8},{8,0},{1,9},{9,1},{2,10},{10,2},{3,11},{11,3},{4,12},{12,4},... | collective-permute-start | bytes 1572872 | tf_op jit(solution)/shard_map/ppermute | solution.py:19
  53.2 0.8 copy-start.8
  154.9 14.8 %copy-start.4 = (bf16[256,1024]{1,0:T(8,128)(2,1)}, bf16[256,1024]{1,0:T(8,128)(2,1)S(1)}, u32[]{:S(2)}) copy-start(bf16[256,1024]{1,0:T(8,128)(2,1)S(1)} %get-tuple-element.27.a_ref.out_ref) | copy-start | bytes 1572868
  154.9 21.9 %copy-start.1 = (bf16[256,1024]{1,0:T(8,128)(2,1)S(1)}, bf16[256,1024]{1,0:T(8,128)(2,1)}, u32[]{:S(2)}) copy-start(bf16[256,1024]{1,0:T(8,128)(2,1)} %copy-done) | copy-start | bytes 1572868
  154.9 21.9 %copy-start.9 = (bf16[256,1024]{1,0:T(8,128)(2,1)S(1)}, bf16[256,1024]{1,0:T(8,128)(2,1)}, u32[]{:S(2)}) copy-start(bf16[256,1024]{1,0:T(8,128)(2,1)} %copy-done.8) | copy-start | bytes 1572868
  170.6 7.7 %collective-permute-start.3 = (bf16[256,1280]{1,0:T(8,128)(2,1)}, bf16[256,1280]{1,0:T(8,128)(2,1)}, u32[]{:S(2)}, u32[]{:S(2)}) collective-permute-start(bf16[256,1280]{1,0:T(8,128)(2,1)} %shard_map.132), channel_id=1, source_target_pairs={{0,8},{8,0},{1,9},{9,1},{2,10},{10,2},{3,11},{11,3},{4,12},{12,4},... | collective-permute-start | bytes 1966088 | tf_op jit(solution)/shard_map/ppermute | solution.py:19
  172.7 14.5 %all-to-all-start.7 = ((bf16[8,64,512]{2,1,0:T(8,128)(2,1)}), bf16[8,64,512]{2,1,0:T(8,128)(2,1)}, u32[]{:S(2)}, u32[]{:S(2)}) async-start(bf16[8,64,512]{2,1,0:T(8,128)(2,1)} %shard_map.130.after_ref), calls=%async_computation.7 | async-start | bytes 1048576 | tf_op jit(solution)/shard_map/all_to_all | solution.py:23
  176.9 1.3 copy-start.5
  177.2 1.0 copy-start.2
  178.2 9.0 %copy-start.3 = (bf16[1024,512]{1,0:T(8,128)(2,1)S(1)}, bf16[1024,512]{1,0:T(8,128)(2,1)}, u32[]{:S(2)}) copy-start(bf16[1024,512]{1,0:T(8,128)(2,1)} %copy-done.2) | copy-start | bytes 3145732
  178.2 1.1 copy-start.7

commit v9 on v8

--- a/solution.py
+++ b/solution.py
@@ -36,7 +36,7 @@
         out_shape=[jax.ShapeDtypeStruct(shape, dtype) for shape, dtype in outs],
         in_specs=[small] * scalars + [spec] * (len(args) - scalars - after) + [unread] * after,
         out_specs=[spec] * len(outs),
-        compiler_params=pltpu.CompilerParams(vmem_limit_bytes=16 * 2**20),
+        compiler_params=pltpu.CompilerParams(vmem_limit_bytes=4 * 2**20),
     )(*args)
 
 
@@ -157,20 +157,17 @@
             )
 
 
-def join_kernel(a_ref, b_ref, after_ref, o_ref):
-    cols = a_ref.shape[1]
-    o_ref[:, :cols] = a_ref[...]
-    o_ref[:, cols:] = b_ref[...]
-
-
 def turn_kernel(a_ref, b_ref, after_ref, o_ref):
     rows = a_ref.shape[0]
     o_ref[:, :rows] = a_ref[...].T
     o_ref[:, rows:] = b_ref[...].T
 
 
-def bars_kernel(x_ref, up_slope_ref, act_ref, o_ref):
+def bars_kernel(x_ref, up_slope_ref, act_ref, out_ref, hid_ref, o_ref, joined_ref):
     width = act_ref.shape[1]
+    feats = out_ref.shape[1]
+    joined_ref[:, :feats] = out_ref[...]
+    joined_ref[:, feats:] = hid_ref[...]
     c = lax.axis_index("c")
     for r in range(2):
         place = c if r == 0 else 1 - c
@@ -196,32 +193,41 @@
     done_ref[...] = joined_ref[:16, :128]
 
 
-def fisher_kernel(tok_ref, bars_ref, probe_ref, after_ref, gate_ref, up_ref):
+def fisher_kernel(tok_ref, bars_ref, probe_ref, after_ref, gate_ref, up_ref, g_ref, u_ref, sem):
     width = gate_ref.shape[1]
     factor = TOKENS**-0.5
     bars = [bars_ref[:, 16 * q : 16 * q + 16, :].reshape(128, 2 * width) for q in range(4)]
-    y = dot(tok_ref[...], jnp.concatenate(bars, axis=0))
-    gate_ref[...] = (probe_ref[:, :width].astype(F32) * y[:, :width] * factor).astype(BF16)
-    up_ref[...] = (probe_ref[:, width:].astype(F32) * y[:, width:] * factor).astype(BF16)
+    bars = jnp.concatenate(bars, axis=0)
+    writes = []
+    for i in range(4):
+        rows = slice(i * 256, (i + 1) * 256)
+        y = dot(tok_ref[rows, :], bars)
+        for j, (held, target) in enumerate(((g_ref, gate_ref), (u_ref, up_ref))):
+            probe = probe_ref[rows, (2 + j) * width : (3 + j) * width].astype(F32)
+            held[rows, :] = (probe * y[:, j * width : (j + 1) * width] * factor).astype(BF16)
+            write = pltpu.make_async_copy(held.at[rows, :], target.at[rows, :], sem.at[i, j])
+            write.start()
+            writes.append(write)
+    for write in writes:
+        write.wait()
 
 
 def fisher(tok, bars, stacked, after):
     rows = stacked.shape[0]
     width = stacked.shape[1] // 4
-    block = 256
-    weight = pl.BlockSpec((block, width), lambda i: (i, 0))
+    spec = pl.BlockSpec(memory_space=pltpu.VMEM)
+    unread = pl.BlockSpec(memory_space=pl.ANY)
     return pl.pallas_call(
         fisher_kernel,
-        grid=(rows // block,),
         out_shape=[jax.ShapeDtypeStruct((rows, width), BF16)] * 2,
-        in_specs=[
-            pl.BlockSpec((block, tok.shape[1]), lambda i: (i, 0)),
-            pl.BlockSpec(bars.shape, lambda i: (0, 0, 0)),
-            pl.BlockSpec((block, 2 * width), lambda i: (i, 1)),
-            pl.BlockSpec(memory_space=pl.ANY),
+        in_specs=[spec, spec, spec, unread],
+        out_specs=[unread, unread],
+        scratch_shapes=[
+            pltpu.VMEM((rows, width), BF16),
+            pltpu.VMEM((rows, width), BF16),
+            pltpu.SemaphoreType.DMA((4, 2)),
         ],
-        out_specs=[weight, weight],
-        compiler_params=pltpu.CompilerParams(vmem_limit_bytes=16 * 2**20),
+        compiler_params=pltpu.CompilerParams(vmem_limit_bytes=8 * 2**20),
     )(tok, bars, stacked, after)
 
 
@@ -287,11 +293,16 @@
         back_kernel, [((2, 8, 32, width), BF16), ((256, feats), BF16)], chunk, down, down2
     )
     back = exchange(back.reshape(16, 32, width), NEAR).reshape(2, 8, 32, width)
-    (bars,) = local(bars_kernel, [((8, 64, 2 * width), BF16)], back, up_slope, act)
-    joined, tok_t = (
-        local(join_kernel, [((256, feats + width), BF16)], out, hid2, bars, after=1)[0],
-        local(turn_kernel, [((feats, TOKENS), BF16)], pair, pair2, bars, after=1)[0],
-    )
+    bars, joined = local(
+        bars_kernel,
+        [((8, 64, 2 * width), BF16), ((256, feats + width), BF16)],
+        back,
+        up_slope,
+        act,
+        out,
+        hid2,
+    )
+    (tok_t,) = local(turn_kernel, [((feats, TOKENS), BF16)], pair, pair2, bars, after=1)
     bars = exchange(bars, TP)
     joined = swap(joined, "c")
     fisher_down, done = local(

time: 192 us -> 189 us (0.984)
    pallas_call x13 -> x12, Pallas kernels: 12 us -> 11.3 us  [local(): pl.pallas_call(kernel, out_shape=[jax.ShapeDtypeStruct(shape, dtype) for...]
where the time goes in v9:
time: 189 us; the launch traced here: 188 us
  blocking collectives  111 us (59%)
  starting transfers between devices  35 us (19%)
  waiting for transfers between devices  16 us (8%)
  Pallas kernels  13.9 us (7%)
  local copies, waits for them, and re-layouts  10.6 us (6%)
    all_to_all x6, blocking collectives, exchange(): return lax.all_to_all(pieces, axes, 0, 0, tiled=True)  111 us
    all_to_all x2, starting transfers between devices, exchange(): return lax.all_to_all(pieces, axes, 0, 0, tiled=True)  19.9 us
    ppermute x4, starting transfers between devices, swap(): return lax.ppermute(x, axis, [(0, 1), (1, 0)])  15.1 us
    all_to_all x2, waiting for transfers between devices, exchange(): return lax.all_to_all(pieces, axes, 0, 0, tiled=True)  14.5 us
    pallas_call x12, Pallas kernels, local(): pl.pallas_call(kernel, out_shape=[jax.ShapeDtypeStruct(shape, dtype) for...  11.3 us
    unnamed x40, local copies, waits for them, and re-layouts  9.94 us
  transfers between devices with their start and end apart: 6, of which 3 were waited for; matrix products, arithmetic and copies ran while one was open for 0% of the time, Pallas kernels for 2%

profile of v9, /device:TPU:1, one launch (start us, length us, event | category | flops | bytes accessed | tf_op | source)
XLA Modules:
  0.0 188.2 jit_solution(5619788857427451656)
XLA Ops:
  0.6 0.0 copy-start.15
  0.6 0.7 copy-done.15
  1.3 0.0 copy-start.17
  1.4 0.0 copy-start.18
  1.4 0.7 shard_map.121
  2.1 15.7 %all-to-all-start = ((bf16[16,8,1024]{2,1,0:T(8,128)(2,1)}), bf16[16,8,1024]{2,1,0:T(8,128)(2,1)S(1)}, u32[]{:S(2)}, u32[]{:S(2)}) async-start(bf16[16,8,1024]{2,1,0:T(8,128)(2,1)} %shard_map.121), calls=%async_computation | async-start | bytes 524288 | tf_op jit(solution)/shard_map/all_to_all | solution.py:23
  17.8 0.0 copy-start.6
  17.8 1.0 copy-done.6
  18.9 0.0 copy-start.10
  18.9 1.0 copy-done.10
  19.9 0.7 copy-done.16
  20.6 0.7 shard_map.123.down_ref
  21.3 2.9 %collective-permute-start.1 = (bf16[512,1024]{1,0:T(8,128)(2,1)S(1)}, bf16[512,1024]{1,0:T(8,128)(2,1)}, u32[]{:S(2)}, u32[]{:S(2)}) collective-permute-start(bf16[512,1024]{1,0:T(8,128)(2,1)S(1)} %shard_map.123.down_ref), channel_id=1, source_target_pairs={{0,8},{8,0},{1,9},{9,1},{2,10},{10,2},{3,11},{11,3},{4,12},{12,4},... | collective-permute-start | bytes 3145736 | tf_op jit(solution)/shard_map/ppermute | solution.py:19
  24.2 9.0 %all-to-all-done = bf16[16,8,1024]{2,1,0:T(8,128)(2,1)S(1)} async-done(((bf16[16,8,1024]{2,1,0:T(8,128)(2,1)}), bf16[16,8,1024]{2,1,0:T(8,128)(2,1)S(1)}, u32[]{:S(2)}, u32[]{:S(2)}) %all-to-all-start) | async-done | bytes 262176 | tf_op jit(solution)/shard_map/all_to_all | solution.py:23
  33.2 4.8 %collective-permute-start = (bf16[128,1024]{1,0:T(8,128)(2,1)S(1)}, bf16[128,1024]{1,0:T(8,128)(2,1)}, u32[]{:S(2)}, u32[]{:S(2)}) collective-permute-start(bf16[128,1024]{1,0:T(8,128)(2,1)S(1)} %bitcast.13), channel_id=1, source_target_pairs={{0,256},{256,0},{1,257},{257,1},{2,258},{258,2},{3,259},{259,3},{4... | collective-permute-start | bytes 786440 | tf_op jit(solution)/shard_map/ppermute | solution.py:19
  38.0 0.0 copy-done.17
  38.0 0.1 copy.13.gmask_ref
  38.1 0.0 copy-done.18
  38.1 0.1 copy.14.umask_ref
  38.2 1.0 copy-done.11
  39.2 1.0 copy-done.12
  40.2 1.0 copy-done.13
  41.3 1.0 copy-done.14
  42.3 1.0 shard_map.122.w_ref.probe_ref
  43.4 0.0 collective-permute-done.1.down2_ref
  43.4 0.7 slice.9.refs_1_
  44.1 0.0 collective-permute-done
  44.1 1.0 pad_maximum_fusion.own_ref.a_ref
  45.0 0.0 copy-start
  45.1 5.3 %collective-permute-start.2 = (bf16[256,1024]{1,0:T(8,128)(2,1)S(1)}, bf16[256,1024]{1,0:T(8,128)(2,1)S(1)}, u32[]{:S(2)}, u32[]{:S(2)}) collective-permute-start(bf16[256,1024]{1,0:T(8,128)(2,1)S(1)} %pad_maximum_fusion.own_ref.a_ref), channel_id=1, source_target_pairs={{0,8},{8,0},{1,9},{9,1},{2,10},{10,2},{3,11},{11,3},{4,12},{12,4},... | collective-permute-start | bytes 1572872 | tf_op jit(solution)/shard_map/ppermute | solution.py:19
  50.4 1.5 collective-permute-done.2.other_ref.b_ref
  51.9 1.2 shard_map.124
  53.1 0.0 copy-done
  53.1 0.0 copy-done.8
  53.2 19.0 %all_to_all.40.x_ref = bf16[8,64,1024]{2,1,0:T(8,128)(2,1)S(1)} all-to-all(bf16[8,64,1024]{2,1,0:T(8,128)(2,1)S(1)} %shard_map.124), channel_id=1, replica_groups=mesh['yh'=2,'zh'=4,'zl'=4,'c'=2,'yl'=2,'x'=4] {'yl','x'}, dimensions={0} | all-to-all | bytes 2097152 | tf_op jit(solution)/shard_map/all_to_all | solution.py:23
  72.2 0.2 shard_map.125
  72.4 14.7 %all_to_all.41 = bf16[16,32,512]{2,1,0:T(8,128)(2,1)S(1)} all-to-all(bf16[16,32,512]{2,1,0:T(8,128)(2,1)S(1)} %bitcast.10), channel_id=1, replica_groups=mesh['yh'=2,'zh'=4,'zl'=4,'c'=2,'yl'=2,'x'=4] {'c','yl','x'}, dimensions={0} | all-to-all | bytes 1048576 | tf_op jit(solution)/shard_map/all_to_all | solution.py:23
  87.1 1.9 %shard_map.126 = (bf16[4,2,32,1024]{3,2,1,0:T(8,128)(2,1)S(1)}, bf16[256,256]{1,0:T(8,128)(2,1)S(1)}, bf16[256,256]{1,0:T(8,128)(2,1)S(1)}) custom-call(bf16[2,8,32,512]{3,2,1,0:T(8,128)(2,1)S(1)} %bitcast.8, bf16[512,1024]{1,0:T(8,128)(2,1)S(1)} %shard_map.123.down_ref, bf16[512,1024]{1,0:T(8,128)(2,1)} %collective-permute-done.1.down2_ref), custom_call_target="tpu_custom_call" | custom-call | tf_op jit(solution)/shard_map/pallas_call | solution.py:34
  89.0 22.1 %all_to_all.42.x_ref = bf16[8,32,1024]{2,1,0:T(8,128)(2,1)S(1)} all-to-all(bf16[8,32,1024]{2,1,0:T(8,128)(2,1)S(1)} %bitcast.11), channel_id=1, replica_groups=mesh['yh'=2,'zh'=4,'zl'=4,'c'=2,'yl'=2,'x'=4] {'zl','yh'}, dimensions={0} | all-to-all | bytes 1048576 | tf_op jit(solution)/shard_map/all_to_all | solution.py:23
  111.1 0.1 shard_map.127
  111.2 19.7 %all_to_all.43.x_ref = bf16[4,32,1024]{2,1,0:T(8,128)(2,1)S(1)} all-to-all(bf16[4,32,1024]{2,1,0:T(8,128)(2,1)S(1)} %shard_map.127), channel_id=1, replica_groups=mesh['yh'=2,'zh'=4,'zl'=4,'c'=2,'yl'=2,'x'=4] {'zh'}, dimensions={0} | all-to-all | bytes 524288 | tf_op jit(solution)/shard_map/all_to_all | solution.py:23
  130.9 21.5 %all_to_all.44 = bf16[8,32,1024]{2,1,0:T(8,128)(2,1)S(1)} all-to-all(bf16[8,32,1024]{2,1,0:T(8,128)(2,1)S(1)} %shard_map.128), channel_id=1, replica_groups=mesh['yh'=2,'zh'=4,'zl'=4,'c'=2,'yl'=2,'x'=4] {'zl','yh'}, dimensions={0} | all-to-all | bytes 1048576 | tf_op jit(solution)/shard_map/all_to_all | solution.py:23
  152.4 1.7 shard_map.129
  154.1 0.0 copy-start.4
  154.1 0.0 copy-start.1
  154.1 0.0 copy-start.9
  154.2 13.9 %all_to_all.45 = bf16[16,32,256]{2,1,0:T(8,128)(2,1)S(1)} all-to-all(bf16[16,32,256]{2,1,0:T(8,128)(2,1)S(1)} %bitcast.12), channel_id=1, replica_groups=mesh['yh'=2,'zh'=4,'zl'=4,'c'=2,'yl'=2,'x'=4] {'c','yl','x'}, dimensions={0} | all-to-all | bytes 524288 | tf_op jit(solution)/shard_map/all_to_all | solution.py:23
  168.0 0.0 copy-done.4
  168.0 1.1 shard_map.130
  169.1 2.1 %collective-permute-start.3 = (bf16[256,1280]{1,0:T(8,128)(2,1)}, bf16[256,1280]{1,0:T(8,128)(2,1)}, u32[]{:S(2)}, u32[]{:S(2)}) collective-permute-start(bf16[256,1280]{1,0:T(8,128)(2,1)} %get-tuple-element.32), channel_id=1, source_target_pairs={{0,8},{8,0},{1,9},{9,1},{2,10},{10,2},{3,11},{11,3},{4,12},{12,4},... | collective-permute-start | bytes 1966088 | tf_op jit(solution)/shard_map/ppermute | solution.py:19
  171.2 4.2 %all-to-all-start.7 = ((bf16[8,64,512]{2,1,0:T(8,128)(2,1)}), bf16[8,64,512]{2,1,0:T(8,128)(2,1)}, u32[]{:S(2)}, u32[]{:S(2)}) async-start(bf16[8,64,512]{2,1,0:T(8,128)(2,1)} %get-tuple-element.30.after_ref), calls=%async_computation.7 | async-start | bytes 1048576 | tf_op jit(solution)/shard_map/all_to_all | solution.py:23
  175.4 0.0 copy-done.1
  175.4 0.0 copy-done.9
  175.4 0.0 copy-start.5
  175.4 0.3 shard_map.131.tok_ref
  175.8 0.0 copy-start.2
  175.8 1.0 copy-done.2
  176.7 0.0 collective-permute-done.3.joined_ref
  176.8 0.0 copy-done.5
  176.8 1.1 copy-done.7
  177.9 2.3 %shard_map.132 = (bf16[256,1024]{1,0:T(8,128)(2,1)}, bf16[16,128]{1,0:T(8,128)(2,1)S(1)}) custom-call(bf16[256,256]{1,0:T(8,128)(2,1)S(1)} %get-tuple-element.31.hid_ref, bf16[256,1024]{1,0:T(8,128)(2,1)S(1)} %copy-done.5, bf16[256,1280]{1,0:T(8,128)(2,1)} %collective-permute-done.3.joined_ref, bf16[256,1024]{1,0:T(8,128)(2,1)S(1)} %copy-done.7), custom_call_target="tpu_custom_call" | custom-call | tf_op jit(solution)/shard_map/pallas_call | solution.py:34
  180.2 5.5 %all-to-all-done.7.bars_ref = bf16[8,64,512]{2,1,0:T(8,128)(2,1)} async-done(((bf16[8,64,512]{2,1,0:T(8,128)(2,1)}), bf16[8,64,512]{2,1,0:T(8,128)(2,1)}, u32[]{:S(2)}, u32[]{:S(2)}) %all-to-all-start.7) | async-done | bytes 524320 | tf_op jit(solution)/shard_map/all_to_all | solution.py:23
  185.7 0.0 copy-done.3
  185.7 2.5 %shard_map.133 = (bf16[1024,256]{1,0:T(8,128)(2,1)}, bf16[1024,256]{1,0:T(8,128)(2,1)}) custom-call(bf16[1024,512]{1,0:T(8,128)(2,1)S(1)} %copy-done.3, bf16[8,64,512]{2,1,0:T(8,128)(2,1)} %all-to-all-done.7.bars_ref, bf16[1024,1024]{1,0:T(8,128)(2,1)S(1)} %shard_map.122.w_ref.probe_ref, bf16[16,128]{1,0:T(8,128)(2,1)S(1)} %get-tuple-element.33.after_ref), custom_call_target="tpu_custom_call" | custom-call | tf_op jit(solution)/shard_map/pallas_call | solution.py:220
  (10 shorter events, 0.1 us)
Async XLA Ops:
  0.6 0.7 copy-start.15
  1.3 36.6 %copy-start.17 = (s32[8,2]{0,1:T(2,128)S(1)}, s32[8,2]{0,1:T(2,128)}, u32[]{:S(2)}) copy-start(s32[8,2]{0,1:T(2,128)} %param.14) | copy-start | bytes 196
  1.4 36.7 %copy-start.18 = (s32[8,2]{0,1:T(2,128)S(1)}, s32[8,2]{0,1:T(2,128)}, u32[]{:S(2)}) copy-start(s32[8,2]{0,1:T(2,128)} %param.15) | copy-start | bytes 196
  2.1 31.1 %all-to-all-start = ((bf16[16,8,1024]{2,1,0:T(8,128)(2,1)}), bf16[16,8,1024]{2,1,0:T(8,128)(2,1)S(1)}, u32[]{:S(2)}, u32[]{:S(2)}) async-start(bf16[16,8,1024]{2,1,0:T(8,128)(2,1)} %shard_map.121), calls=%async_computation | async-start | bytes 524288 | tf_op jit(solution)/shard_map/all_to_all | solution.py:23
  17.8 1.0 copy-start.6
  18.9 1.0 copy-start.10
  19.9 0.7 copy-start.16
  21.3 22.1 %collective-permute-start.1 = (bf16[512,1024]{1,0:T(8,128)(2,1)S(1)}, bf16[512,1024]{1,0:T(8,128)(2,1)}, u32[]{:S(2)}, u32[]{:S(2)}) collective-permute-start(bf16[512,1024]{1,0:T(8,128)(2,1)S(1)} %shard_map.123.down_ref), channel_id=1, source_target_pairs={{0,8},{8,0},{1,9},{9,1},{2,10},{10,2},{3,11},{11,3},{4,12},{12,4},... | collective-permute-start | bytes 3145736 | tf_op jit(solution)/shard_map/ppermute | solution.py:19
  33.2 10.9 %collective-permute-start = (bf16[128,1024]{1,0:T(8,128)(2,1)S(1)}, bf16[128,1024]{1,0:T(8,128)(2,1)}, u32[]{:S(2)}, u32[]{:S(2)}) collective-permute-start(bf16[128,1024]{1,0:T(8,128)(2,1)S(1)} %bitcast.13), channel_id=1, source_target_pairs={{0,256},{256,0},{1,257},{257,1},{2,258},{258,2},{3,259},{259,3},{4... | collective-permute-start | bytes 786440 | tf_op jit(solution)/shard_map/ppermute | solution.py:19
  38.2 1.0 copy-start.11
  39.2 1.0 copy-start.12
  40.2 1.0 copy-start.13
  41.3 1.0 copy-start.14
  45.0 8.1 %copy-start = (bf16[256,1024]{1,0:T(8,128)(2,1)}, bf16[256,1024]{1,0:T(8,128)(2,1)S(1)}, u32[]{:S(2)}) copy-start(bf16[256,1024]{1,0:T(8,128)(2,1)S(1)} %pad_maximum_fusion.own_ref.a_ref) | copy-start | bytes 1572868
  45.1 6.8 %collective-permute-start.2 = (bf16[256,1024]{1,0:T(8,128)(2,1)S(1)}, bf16[256,1024]{1,0:T(8,128)(2,1)S(1)}, u32[]{:S(2)}, u32[]{:S(2)}) collective-permute-start(bf16[256,1024]{1,0:T(8,128)(2,1)S(1)} %pad_maximum_fusion.own_ref.a_ref), channel_id=1, source_target_pairs={{0,8},{8,0},{1,9},{9,1},{2,10},{10,2},{3,11},{11,3},{4,12},{12,4},... | collective-permute-start | bytes 1572872 | tf_op jit(solution)/shard_map/ppermute | solution.py:19
  51.9 1.3 copy-start.8
  154.1 13.9 %copy-start.4 = (bf16[256,1024]{1,0:T(8,128)(2,1)}, bf16[256,1024]{1,0:T(8,128)(2,1)S(1)}, u32[]{:S(2)}) copy-start(bf16[256,1024]{1,0:T(8,128)(2,1)S(1)} %get-tuple-element.28.out_ref) | copy-start | bytes 1572868
  154.1 21.3 %copy-start.1 = (bf16[256,1024]{1,0:T(8,128)(2,1)S(1)}, bf16[256,1024]{1,0:T(8,128)(2,1)}, u32[]{:S(2)}) copy-start(bf16[256,1024]{1,0:T(8,128)(2,1)} %copy-done) | copy-start | bytes 1572868
  154.1 21.3 %copy-start.9 = (bf16[256,1024]{1,0:T(8,128)(2,1)S(1)}, bf16[256,1024]{1,0:T(8,128)(2,1)}, u32[]{:S(2)}) copy-start(bf16[256,1024]{1,0:T(8,128)(2,1)} %copy-done.8) | copy-start | bytes 1572868
  169.1 7.6 %collective-permute-start.3 = (bf16[256,1280]{1,0:T(8,128)(2,1)}, bf16[256,1280]{1,0:T(8,128)(2,1)}, u32[]{:S(2)}, u32[]{:S(2)}) collective-permute-start(bf16[256,1280]{1,0:T(8,128)(2,1)} %get-tuple-element.32), channel_id=1, source_target_pairs={{0,8},{8,0},{1,9},{9,1},{2,10},{10,2},{3,11},{11,3},{4,12},{12,4},... | collective-permute-start | bytes 1966088 | tf_op jit(solution)/shard_map/ppermute | solution.py:19
  171.2 14.5 %all-to-all-start.7 = ((bf16[8,64,512]{2,1,0:T(8,128)(2,1)}), bf16[8,64,512]{2,1,0:T(8,128)(2,1)}, u32[]{:S(2)}, u32[]{:S(2)}) async-start(bf16[8,64,512]{2,1,0:T(8,128)(2,1)} %get-tuple-element.30.after_ref), calls=%async_computation.7 | async-start | bytes 1048576 | tf_op jit(solution)/shard_map/all_to_all | solution.py:23
  175.4 1.3 copy-start.5
  175.8 1.0 copy-start.2
  176.8 9.0 %copy-start.3 = (bf16[1024,512]{1,0:T(8,128)(2,1)S(1)}, bf16[1024,512]{1,0:T(8,128)(2,1)}, u32[]{:S(2)}) copy-start(bf16[1024,512]{1,0:T(8,128)(2,1)} %copy-done.2) | copy-start | bytes 3145732
  176.8 1.1 copy-start.7

commit v10 on v9

--- a/solution.py
+++ b/solution.py
@@ -36,7 +36,7 @@
         out_shape=[jax.ShapeDtypeStruct(shape, dtype) for shape, dtype in outs],
         in_specs=[small] * scalars + [spec] * (len(args) - scalars - after) + [unread] * after,
         out_specs=[spec] * len(outs),
-        compiler_params=pltpu.CompilerParams(vmem_limit_bytes=4 * 2**20),
+        compiler_params=pltpu.CompilerParams(vmem_limit_bytes=12 * 2**20),
     )(*args)
 
 
@@ -60,16 +60,18 @@
     o_ref[:, 3 * width :] = pup_ref[...]
 
 
-def pre_kernel(own_ref, other_ref, w_ref, *refs):
-    o_ref = refs[-1]
+def pre_kernel(a_ref, b_ref, w_ref, w2_ref, after_ref, o_ref):
     width = w_ref.shape[1] // 4
-    for half, tok_ref in enumerate((own_ref, other_ref)):
+    c = lax.axis_index("c")
+    tok = jnp.concatenate([a_ref[...], b_ref[...]], axis=0)
+    for weights, place in ((w_ref, c), (w2_ref, 1 - c)):
         for j in range(4):
             cols = slice(j * width, (j + 1) * width)
-            y = dot(tok_ref[...], w_ref[:, cols]).astype(BF16)
+            y = dot(tok, weights[:, cols]).astype(BF16)
             for r in range(2):
-                q = 16 * (2 * half + r)
-                o_ref[:, q : q + 16, cols] = y[r * 128 : (r + 1) * 128].reshape(8, 16, width)
+                o_ref[place, :, 16 * r : 16 * r + 16, cols] = y[r * 128 : (r + 1) * 128].reshape(
+                    8, 16, width
+                )
 
 
 def down_kernel(mask_ref, down_ref, probe_ref, o_ref):
@@ -81,12 +83,17 @@
 def gate_kernel(x_ref, o_ref, up_slope_ref, act_ref):
     width = act_ref.shape[1]
 
+    c = lax.axis_index("c")
+
     def part(j):
         cols = slice(j * width, (j + 1) * width)
-        acc = x_ref[0, :, cols].astype(F32)
-        for i in range(1, 8):
-            acc = acc + x_ref[i, :, cols].astype(F32)
-        return acc
+        classes = []
+        for place in (c, 1 - c):
+            acc = x_ref[place, 0, :, cols].astype(F32)
+            for i in range(1, 8):
+                acc = acc + x_ref[place, i, :, cols].astype(F32)
+            classes.append(acc)
+        return jnp.concatenate(classes, axis=0)
 
     gate = part(0)
     up = part(1)
@@ -97,7 +104,6 @@
     slope = sig * (1.0 + gate * (1.0 - sig))
     hid = (act * up).astype(BF16)
     tan = (slope * tangent_gate * up + act * tangent_up).astype(BF16)
-    c = lax.axis_index("c")
     for r in range(2):
         rows = slice(r * 32, (r + 1) * 32)
         place = c if r == 0 else 1 - c
@@ -157,17 +163,22 @@
             )
 
 
-def turn_kernel(a_ref, b_ref, after_ref, o_ref):
-    rows = a_ref.shape[0]
+def turn_kernel(a_ref, b_ref, joined_ref, o_ref):
+    feats, rows = a_ref.shape[1], a_ref.shape[0]
     o_ref[:, :rows] = a_ref[...].T
-    o_ref[:, rows:] = b_ref[...].T
-
-
-def bars_kernel(x_ref, up_slope_ref, act_ref, out_ref, hid_ref, o_ref, joined_ref):
+    o_ref[:, rows : 2 * rows] = b_ref[...].T
+    o_ref[:, 2 * rows :] = joined_ref[:, -feats:].T
+
+
+def bars_kernel(
+    x_ref, up_slope_ref, act_ref, out_ref, hid_ref, a_ref, b_ref, o_ref, joined_ref
+):
     width = act_ref.shape[1]
     feats = out_ref.shape[1]
     joined_ref[:, :feats] = out_ref[...]
-    joined_ref[:, feats:] = hid_ref[...]
+    joined_ref[:, feats : feats + width] = hid_ref[...]
+    joined_ref[:128, feats + width :] = a_ref[...]
+    joined_ref[128:, feats + width :] = b_ref[...]
     c = lax.axis_index("c")
     for r in range(2):
         place = c if r == 0 else 1 - c
@@ -185,7 +196,7 @@
 def fisher_down_kernel(hid_ref, out_ref, joined_ref, probe_ref, o_ref, done_ref):
     feats = out_ref.shape[1]
     own = hid_ref[...].T
-    other = joined_ref[:, feats:].T
+    other = joined_ref[:, feats : feats + hid_ref.shape[1]].T
     for j in range(4):
         cols = slice(j * 256, (j + 1) * 256)
         y = dot(own, out_ref[:, cols]) + dot(other, joined_ref[:, cols])
@@ -227,7 +238,7 @@
             pltpu.VMEM((rows, width), BF16),
             pltpu.SemaphoreType.DMA((4, 2)),
         ],
-        compiler_params=pltpu.CompilerParams(vmem_limit_bytes=8 * 2**20),
+        compiler_params=pltpu.CompilerParams(vmem_limit_bytes=12 * 2**20),
     )(tok, bars, stacked, after)
 
 
@@ -264,13 +275,18 @@
     )
     down2 = swap(down, "c")
     tok1 = swap(tok0, "yh")
-    tok1, seen, seen2 = lax.optimization_barrier((tok1, stacked[:16, :128], down2[:16, :128]))
-    pair = jnp.concatenate([tok0, tok1], axis=0)
-    pair2 = swap(pair, "c")
+    stacked2 = swap(stacked, "c")
     (partial,) = local(
-        pre_kernel, [((8, 64, 4 * width), BF16)], pair, pair2, stacked, seen, seen2, after=2
-    )
-    pre = exchange(partial, TP)
+        pre_kernel,
+        [((2, 8, 32, 4 * width), BF16)],
+        tok0,
+        tok1,
+        stacked,
+        stacked2,
+        down2,
+        after=1,
+    )
+    pre = exchange(partial.reshape(16, 32, 4 * width), NEAR).reshape(2, 8, 32, 4 * width)
     send, up_slope, act = local(
         gate_kernel,
         [((2, 8, 32, 2 * width), BF16), ((64, width), F32), ((64, width), F32)],
@@ -295,16 +311,18 @@
     back = exchange(back.reshape(16, 32, width), NEAR).reshape(2, 8, 32, width)
     bars, joined = local(
         bars_kernel,
-        [((8, 64, 2 * width), BF16), ((256, feats + width), BF16)],
+        [((8, 64, 2 * width), BF16), ((256, 2 * feats + width), BF16)],
         back,
         up_slope,
         act,
         out,
         hid2,
-    )
-    (tok_t,) = local(turn_kernel, [((feats, TOKENS), BF16)], pair, pair2, bars, after=1)
+        tok0,
+        tok1,
+    )
     bars = exchange(bars, TP)
     joined = swap(joined, "c")
+    (tok_t,) = local(turn_kernel, [((feats, TOKENS), BF16)], tok0, tok1, joined)
     fisher_down, done = local(
         fisher_down_kernel,
         [(probe_down.shape, BF16), ((16, 128), BF16)],

time: 189 us -> 198 us (1.048)
  waiting for transfers between devices: 16 us -> 22.7 us
  blocking collectives: 111 us -> 115 us
  starting transfers between devices: 35 us -> 31.6 us
    all_to_all x2, starting transfers between devices: 19.9 us -> 13.7 us  [exchange(): return lax.all_to_all(pieces, axes, 0, 0, tiled=True)]
    all_to_all x6, blocking collectives: 111 us -> 115 us  [exchange(): return lax.all_to_all(pieces, axes, 0, 0, tiled=True)]
    all_to_all x2, waiting for transfers between devices: 14.5 us -> 18 us  [exchange(): return lax.all_to_all(pieces, axes, 0, 0, tiled=True)]
    ppermute x4, waiting for transfers between devices: 1.52 us -> 4.7 us  [swap(): return lax.ppermute(x, axis, [(0, 1), (1, 0)])]
    ppermute x4, starting transfers between devices: 15.1 us -> 17.9 us  [swap(): return lax.ppermute(x, axis, [(0, 1), (1, 0)])]
    unnamed x40 -> x38, local copies, waits for them, and re-layouts: 9.94 us -> 11.7 us
where the time goes in v10:
time: 198 us; the launch traced here: 197 us
  blocking collectives  115 us (58%)
  starting transfers between devices  31.6 us (16%)
  waiting for transfers between devices  22.7 us (11%)
  Pallas kernels  14.5 us (7%)
  local copies, waits for them, and re-layouts  11.7 us (6%)
    all_to_all x6, blocking collectives, exchange(): return lax.all_to_all(pieces, axes, 0, 0, tiled=True)  115 us
    all_to_all x2, waiting for transfers between devices, exchange(): return lax.all_to_all(pieces, axes, 0, 0, tiled=True)  18 us
    ppermute x4, starting transfers between devices, swap(): return lax.ppermute(x, axis, [(0, 1), (1, 0)])  17.9 us
    all_to_all x2, starting transfers between devices, exchange(): return lax.all_to_all(pieces, axes, 0, 0, tiled=True)  13.7 us
    pallas_call x12, Pallas kernels, local(): pl.pallas_call(kernel, out_shape=[jax.ShapeDtypeStruct(shape, dtype) for...  12 us
    unnamed x38, local copies, waits for them, and re-layouts  11.7 us
    ppermute x4, waiting for transfers between devices, swap(): return lax.ppermute(x, axis, [(0, 1), (1, 0)])  4.7 us
  transfers between devices with their start and end apart: 6, of which 3 were waited for; matrix products, arithmetic and copies ran while one was open for 0% of the time, Pallas kernels for 2%

profile of v10, /device:TPU:1, one launch (start us, length us, event | category | flops | bytes accessed | tf_op | source)
XLA Modules:
  0.0 196.7 jit_solution(16927734616074963292)
XLA Ops:
  0.6 0.8 copy.13.gmask_ref
  1.4 0.8 copy.14.umask_ref
  2.1 0.0 copy-start.10
  2.1 1.0 copy-done.10
  3.2 0.0 copy-start.11
  3.2 1.0 copy-done.11
  4.2 0.0 copy-start.12
  4.2 1.0 copy-done.12
  5.3 0.0 copy-start.13
  5.3 1.0 copy-done.13
  6.3 0.0 copy-start.16
  6.3 0.0 copy-start.17
  6.3 1.0 shard_map.122.w_ref.probe_ref
  7.3 8.8 %collective-permute-start.1 = (bf16[1024,1024]{1,0:T(8,128)(2,1)S(1)}, bf16[1024,1024]{1,0:T(8,128)(2,1)}, u32[]{:S(2)}, u32[]{:S(2)}) collective-permute-start(bf16[1024,1024]{1,0:T(8,128)(2,1)S(1)} %shard_map.122.w_ref.probe_ref), channel_id=1, source_target_pairs={{0,8},{8,0},{1,9},{9,1},{2,10},{10,2},{3,11},{11,3},{4,12},{12,4},... | collective-permute-start | bytes 6291464 | tf_op jit(solution)/shard_map/ppermute | solution.py:19
  16.1 0.0 copy-done.16
  16.1 0.7 shard_map.121
  16.9 9.5 %all-to-all-start = ((bf16[16,8,1024]{2,1,0:T(8,128)(2,1)}), bf16[16,8,1024]{2,1,0:T(8,128)(2,1)S(1)}, u32[]{:S(2)}, u32[]{:S(2)}) async-start(bf16[16,8,1024]{2,1,0:T(8,128)(2,1)} %shard_map.121), calls=%async_computation | async-start | bytes 524288 | tf_op jit(solution)/shard_map/all_to_all | solution.py:23
  26.4 0.0 copy-done.17
  26.4 0.0 copy-start.6
  26.4 1.0 copy-done.6
  27.5 0.0 copy-start.9
  27.5 1.0 copy-done.9
  28.5 0.7 shard_map.123.down_ref
  29.2 2.2 %collective-permute-start.2 = (bf16[512,1024]{1,0:T(8,128)(2,1)S(1)}, bf16[512,1024]{1,0:T(8,128)(2,1)}, u32[]{:S(2)}, u32[]{:S(2)}) collective-permute-start(bf16[512,1024]{1,0:T(8,128)(2,1)S(1)} %shard_map.123.down_ref), channel_id=1, source_target_pairs={{0,8},{8,0},{1,9},{9,1},{2,10},{10,2},{3,11},{11,3},{4,12},{12,4},... | collective-permute-start | bytes 3145736 | tf_op jit(solution)/shard_map/ppermute | solution.py:19
  31.4 11.3 %all-to-all-done = bf16[16,8,1024]{2,1,0:T(8,128)(2,1)S(1)} async-done(((bf16[16,8,1024]{2,1,0:T(8,128)(2,1)}), bf16[16,8,1024]{2,1,0:T(8,128)(2,1)S(1)}, u32[]{:S(2)}, u32[]{:S(2)}) %all-to-all-start) | async-done | bytes 262176 | tf_op jit(solution)/shard_map/all_to_all | solution.py:23
  42.7 4.8 %collective-permute-start = (bf16[128,1024]{1,0:T(8,128)(2,1)S(1)}, bf16[128,1024]{1,0:T(8,128)(2,1)S(1)}, u32[]{:S(2)}, u32[]{:S(2)}) collective-permute-start(bf16[128,1024]{1,0:T(8,128)(2,1)S(1)} %bitcast.11), channel_id=1, source_target_pairs={{0,256},{256,0},{1,257},{257,1},{2,258},{258,2},{3,259},{259,3},{4... | collective-permute-start | bytes 786440 | tf_op jit(solution)/shard_map/ppermute | solution.py:19
  47.5 0.0 collective-permute-done.2.after_ref.down2_ref
  47.5 4.7 %collective-permute-done.b_ref = bf16[128,1024]{1,0:T(8,128)(2,1)S(1)} collective-permute-done((bf16[128,1024]{1,0:T(8,128)(2,1)S(1)}, bf16[128,1024]{1,0:T(8,128)(2,1)S(1)}, u32[]{:S(2)}, u32[]{:S(2)}) %collective-permute-start) | collective-permute-done | bytes 262176 | tf_op jit(solution)/shard_map/ppermute | solution.py:19
  52.2 0.0 copy-start.2
  52.2 0.0 collective-permute-done.1.w2_ref
  52.2 2.9 %shard_map.124 = bf16[2,8,32,1024]{3,2,1,0:T(8,128)(2,1)S(1)} custom-call(bf16[128,1024]{1,0:T(8,128)(2,1)S(1)} %bitcast.12, bf16[128,1024]{1,0:T(8,128)(2,1)S(1)} %collective-permute-done.b_ref, bf16[1024,1024]{1,0:T(8,128)(2,1)S(1)} %shard_map.122.w_ref.probe_ref, bf16[1024,1024]{1,0:T(8,128)(2,1)} %collective-permute-done.1.w2_ref, ...), custom_call_target="tpu_custom_call" | custom-call | tf_op jit(solution)/shard_map/pallas_call | solution.py:34
  55.2 24.0 %all_to_all.40 = bf16[16,32,1024]{2,1,0:T(8,128)(2,1)S(1)} all-to-all(bf16[16,32,1024]{2,1,0:T(8,128)(2,1)S(1)} %bitcast.10), channel_id=1, replica_groups=mesh['yh'=2,'zh'=4,'zl'=4,'c'=2,'yl'=2,'x'=4] {'c','yl','x'}, dimensions={0} | all-to-all | bytes 2097152 | tf_op jit(solution)/shard_map/all_to_all | solution.py:23
  79.1 0.2 shard_map.125
  79.3 13.5 %all_to_all.41 = bf16[16,32,512]{2,1,0:T(8,128)(2,1)S(1)} all-to-all(bf16[16,32,512]{2,1,0:T(8,128)(2,1)S(1)} %bitcast.18), channel_id=1, replica_groups=mesh['yh'=2,'zh'=4,'zl'=4,'c'=2,'yl'=2,'x'=4] {'c','yl','x'}, dimensions={0} | all-to-all | bytes 1048576 | tf_op jit(solution)/shard_map/all_to_all | solution.py:23
  92.9 1.9 shard_map.126
  94.8 0.0 copy-start.14
  94.8 23.8 %all_to_all.42.x_ref = bf16[8,32,1024]{2,1,0:T(8,128)(2,1)S(1)} all-to-all(bf16[8,32,1024]{2,1,0:T(8,128)(2,1)S(1)} %bitcast.19), channel_id=1, replica_groups=mesh['yh'=2,'zh'=4,'zl'=4,'c'=2,'yl'=2,'x'=4] {'zl','yh'}, dimensions={0} | all-to-all | bytes 1048576 | tf_op jit(solution)/shard_map/all_to_all | solution.py:23
  118.6 0.1 shard_map.127
  118.7 18.7 %all_to_all.43.x_ref = bf16[4,32,1024]{2,1,0:T(8,128)(2,1)S(1)} all-to-all(bf16[4,32,1024]{2,1,0:T(8,128)(2,1)S(1)} %shard_map.127), channel_id=1, replica_groups=mesh['yh'=2,'zh'=4,'zl'=4,'c'=2,'yl'=2,'x'=4] {'zh'}, dimensions={0} | all-to-all | bytes 524288 | tf_op jit(solution)/shard_map/all_to_all | solution.py:23
  137.4 21.5 %all_to_all.44 = bf16[8,32,1024]{2,1,0:T(8,128)(2,1)S(1)} all-to-all(bf16[8,32,1024]{2,1,0:T(8,128)(2,1)S(1)} %shard_map.128), channel_id=1, replica_groups=mesh['yh'=2,'zh'=4,'zl'=4,'c'=2,'yl'=2,'x'=4] {'zl','yh'}, dimensions={0} | all-to-all | bytes 1048576 | tf_op jit(solution)/shard_map/all_to_all | solution.py:23
  159.0 0.0 copy-done.14
  159.0 1.7 shard_map.129
  160.7 0.0 copy-start.4
  160.7 13.7 %all_to_all.45 = bf16[16,32,256]{2,1,0:T(8,128)(2,1)S(1)} all-to-all(bf16[16,32,256]{2,1,0:T(8,128)(2,1)S(1)} %bitcast.20), channel_id=1, replica_groups=mesh['yh'=2,'zh'=4,'zl'=4,'c'=2,'yl'=2,'x'=4] {'c','yl','x'}, dimensions={0} | all-to-all | bytes 524288 | tf_op jit(solution)/shard_map/all_to_all | solution.py:23
  174.4 0.0 copy-done.2
  174.4 1.1 shard_map.130
  175.5 0.0 copy-done.4
  175.5 0.0 copy-start.8
  175.5 0.8 copy-done.8
  176.3 2.1 %collective-permute-start.3 = (bf16[256,2304]{1,0:T(8,128)(2,1)}, bf16[256,2304]{1,0:T(8,128)(2,1)S(1)}, u32[]{:S(2)}, u32[]{:S(2)}) collective-permute-start(bf16[256,2304]{1,0:T(8,128)(2,1)} %get-tuple-element.24), channel_id=1, source_target_pairs={{0,8},{8,0},{1,9},{9,1},{2,10},{10,2},{3,11},{11,3},{4,12},{12,4},... | collective-permute-start | bytes 3538952 | tf_op jit(solution)/shard_map/ppermute | solution.py:19
  178.5 4.2 %all-to-all-start.7 = ((bf16[8,64,512]{2,1,0:T(8,128)(2,1)}), bf16[8,64,512]{2,1,0:T(8,128)(2,1)}, u32[]{:S(2)}, u32[]{:S(2)}) async-start(bf16[8,64,512]{2,1,0:T(8,128)(2,1)} %copy-done.8), calls=%async_computation.7 | async-start | bytes 1048576 | tf_op jit(solution)/shard_map/all_to_all | solution.py:23
  182.6 0.0 collective-permute-done.3.joined_ref
  182.6 0.0 copy-start.3
  182.6 0.9 copy-done.3
  183.6 0.3 shard_map.131.tok_ref
  183.9 0.0 copy-start
  183.9 1.0 copy-done
  184.9 0.0 copy-done.5
  184.9 0.0 copy-done.7
  184.9 0.0 copy-done.15
  184.9 1.3 shard_map.132
  186.2 6.8 %all-to-all-done.7.bars_ref = bf16[8,64,512]{2,1,0:T(8,128)(2,1)} async-done(((bf16[8,64,512]{2,1,0:T(8,128)(2,1)}), bf16[8,64,512]{2,1,0:T(8,128)(2,1)}, u32[]{:S(2)}, u32[]{:S(2)}) %all-to-all-start.7) | async-done | bytes 524320 | tf_op jit(solution)/shard_map/all_to_all | solution.py:23
  192.9 1.2 copy-done.1
  194.2 2.5 %shard_map.133 = (bf16[1024,256]{1,0:T(8,128)(2,1)}, bf16[1024,256]{1,0:T(8,128)(2,1)}) custom-call(bf16[1024,512]{1,0:T(8,128)(2,1)S(1)} %copy-done.1, bf16[8,64,512]{2,1,0:T(8,128)(2,1)} %all-to-all-done.7.bars_ref, bf16[1024,1024]{1,0:T(8,128)(2,1)S(1)} %shard_map.122.w_ref.probe_ref, bf16[16,128]{1,0:T(8,128)(2,1)S(1)} %get-tuple-element.27.after_ref), custom_call_target="tpu_custom_call" | custom-call | tf_op jit(solution)/shard_map/pallas_call | solution.py:231
  (5 shorter events, 0.0 us)
Async XLA Ops:
  2.1 1.0 copy-start.10
  3.2 1.0 copy-start.11
  4.2 1.0 copy-start.12
  5.3 1.0 copy-start.13
  6.3 9.8 %copy-start.16 = (bf16[8,1024]{1,0:T(8,128)(2,1)S(1)}, bf16[8,1024]{1,0:T(8,128)(2,1)}, u32[]{:S(2)}) copy-start(bf16[8,1024]{1,0:T(8,128)(2,1)} %x_ref.1) | copy-start | bytes 49156
  6.3 20.1 %copy-start.17 = (s32[2,8]{1,0:T(2,128)S(1)}, s32[2,8]{1,0:T(2,128)}, u32[]{:S(2)}) copy-start(s32[2,8]{1,0:T(2,128)} %mask_ref.1) | copy-start | bytes 196
  7.3 44.9 %collective-permute-start.1 = (bf16[1024,1024]{1,0:T(8,128)(2,1)S(1)}, bf16[1024,1024]{1,0:T(8,128)(2,1)}, u32[]{:S(2)}, u32[]{:S(2)}) collective-permute-start(bf16[1024,1024]{1,0:T(8,128)(2,1)S(1)} %shard_map.122.w_ref.probe_ref), channel_id=1, source_target_pairs={{0,8},{8,0},{1,9},{9,1},{2,10},{10,2},{3,11},{11,3},{4,12},{12,4},... | collective-permute-start | bytes 6291464 | tf_op jit(solution)/shard_map/ppermute | solution.py:19
  16.9 25.8 %all-to-all-start = ((bf16[16,8,1024]{2,1,0:T(8,128)(2,1)}), bf16[16,8,1024]{2,1,0:T(8,128)(2,1)S(1)}, u32[]{:S(2)}, u32[]{:S(2)}) async-start(bf16[16,8,1024]{2,1,0:T(8,128)(2,1)} %shard_map.121), calls=%async_computation | async-start | bytes 524288 | tf_op jit(solution)/shard_map/all_to_all | solution.py:23
  26.4 1.0 copy-start.6
  27.5 1.0 copy-start.9
  29.2 18.3 %collective-permute-start.2 = (bf16[512,1024]{1,0:T(8,128)(2,1)S(1)}, bf16[512,1024]{1,0:T(8,128)(2,1)}, u32[]{:S(2)}, u32[]{:S(2)}) collective-permute-start(bf16[512,1024]{1,0:T(8,128)(2,1)S(1)} %shard_map.123.down_ref), channel_id=1, source_target_pairs={{0,8},{8,0},{1,9},{9,1},{2,10},{10,2},{3,11},{11,3},{4,12},{12,4},... | collective-permute-start | bytes 3145736 | tf_op jit(solution)/shard_map/ppermute | solution.py:19
  42.7 9.5 %collective-permute-start = (bf16[128,1024]{1,0:T(8,128)(2,1)S(1)}, bf16[128,1024]{1,0:T(8,128)(2,1)S(1)}, u32[]{:S(2)}, u32[]{:S(2)}) collective-permute-start(bf16[128,1024]{1,0:T(8,128)(2,1)S(1)} %bitcast.11), channel_id=1, source_target_pairs={{0,256},{256,0},{1,257},{257,1},{2,258},{258,2},{3,259},{259,3},{4... | collective-permute-start | bytes 786440 | tf_op jit(solution)/shard_map/ppermute | solution.py:19
  52.2 122.2 %copy-start.2 = (bf16[128,1024]{1,0:T(8,128)(2,1)}, bf16[128,1024]{1,0:T(8,128)(2,1)S(1)}, u32[]{:S(2)}) copy-start(bf16[128,1024]{1,0:T(8,128)(2,1)S(1)} %collective-permute-done.b_ref) | copy-start | bytes 786436
  94.8 64.1 %copy-start.14 = (bf16[256,256]{1,0:T(8,128)(2,1)}, bf16[256,256]{1,0:T(8,128)(2,1)S(1)}, u32[]{:S(2)}) copy-start(bf16[256,256]{1,0:T(8,128)(2,1)S(1)} %get-tuple-element.26.hid_ref) | copy-start | bytes 393220
  160.7 14.9 %copy-start.4 = (bf16[256,1024]{1,0:T(8,128)(2,1)}, bf16[256,1024]{1,0:T(8,128)(2,1)S(1)}, u32[]{:S(2)}) copy-start(bf16[256,1024]{1,0:T(8,128)(2,1)S(1)} %get-tuple-element.22.out_ref) | copy-start | bytes 1572868
  175.5 0.8 copy-start.8
  176.3 6.3 %collective-permute-start.3 = (bf16[256,2304]{1,0:T(8,128)(2,1)}, bf16[256,2304]{1,0:T(8,128)(2,1)S(1)}, u32[]{:S(2)}, u32[]{:S(2)}) collective-permute-start(bf16[256,2304]{1,0:T(8,128)(2,1)} %get-tuple-element.24), channel_id=1, source_target_pairs={{0,8},{8,0},{1,9},{9,1},{2,10},{10,2},{3,11},{11,3},{4,12},{12,4},... | collective-permute-start | bytes 3538952 | tf_op jit(solution)/shard_map/ppermute | solution.py:19
  178.5 14.5 %all-to-all-start.7 = ((bf16[8,64,512]{2,1,0:T(8,128)(2,1)}), bf16[8,64,512]{2,1,0:T(8,128)(2,1)}, u32[]{:S(2)}, u32[]{:S(2)}) async-start(bf16[8,64,512]{2,1,0:T(8,128)(2,1)} %copy-done.8), calls=%async_computation.7 | async-start | bytes 1048576 | tf_op jit(solution)/shard_map/all_to_all | solution.py:23
  182.6 1.0 copy-start.3
  183.6 1.3 copy-start.5
  183.6 1.3 copy-start.7
  183.6 1.3 copy-start.15
  183.9 1.0 copy-start
  192.9 1.2 copy-start.1

commit v11 on v9

--- a/solution.py
+++ b/solution.py
@@ -36,7 +36,7 @@
         out_shape=[jax.ShapeDtypeStruct(shape, dtype) for shape, dtype in outs],
         in_specs=[small] * scalars + [spec] * (len(args) - scalars - after) + [unread] * after,
         out_specs=[spec] * len(outs),
-        compiler_params=pltpu.CompilerParams(vmem_limit_bytes=4 * 2**20),
+        compiler_params=pltpu.CompilerParams(vmem_limit_bytes=16 * 2**20),
     )(*args)
 
 
@@ -60,8 +60,13 @@
     o_ref[:, 3 * width :] = pup_ref[...]
 
 
-def pre_kernel(own_ref, other_ref, w_ref, *refs):
-    o_ref = refs[-1]
+def pair_kernel(a_ref, b_ref, after_ref, after2_ref, o_ref):
+    rows = a_ref.shape[0]
+    o_ref[:rows] = a_ref[...]
+    o_ref[rows:] = b_ref[...]
+
+
+def pre_kernel(own_ref, other_ref, w_ref, o_ref):
     width = w_ref.shape[1] // 4
     for half, tok_ref in enumerate((own_ref, other_ref)):
         for j in range(4):
@@ -163,11 +168,9 @@
     o_ref[:, rows:] = b_ref[...].T
 
 
-def bars_kernel(x_ref, up_slope_ref, act_ref, out_ref, hid_ref, o_ref, joined_ref):
+def bars_kernel(x_ref, up_slope_ref, act_ref, out_ref, o_ref, late_ref):
     width = act_ref.shape[1]
-    feats = out_ref.shape[1]
-    joined_ref[:, :feats] = out_ref[...]
-    joined_ref[:, feats:] = hid_ref[...]
+    late_ref[...] = out_ref[...]
     c = lax.axis_index("c")
     for r in range(2):
         place = c if r == 0 else 1 - c
@@ -182,15 +185,14 @@
             o_ref[i, rows, width:] = up_bar
 
 
-def fisher_down_kernel(hid_ref, out_ref, joined_ref, probe_ref, o_ref, done_ref):
-    feats = out_ref.shape[1]
+def fisher_down_kernel(hid_ref, out_ref, hid2_ref, out2_ref, probe_ref, o_ref, done_ref):
     own = hid_ref[...].T
-    other = joined_ref[:, feats:].T
+    other = hid2_ref[...].T
     for j in range(4):
         cols = slice(j * 256, (j + 1) * 256)
-        y = dot(own, out_ref[:, cols]) + dot(other, joined_ref[:, cols])
+        y = dot(own, out_ref[:, cols]) + dot(other, out2_ref[:, cols])
         o_ref[:, cols] = (probe_ref[:, cols].astype(F32) * y * TOKENS**-0.5).astype(BF16)
-    done_ref[...] = joined_ref[:16, :128]
+    done_ref[...] = out2_ref[:16, :128]
 
 
 def fisher_kernel(tok_ref, bars_ref, probe_ref, after_ref, gate_ref, up_ref, g_ref, u_ref, sem):
@@ -227,7 +229,7 @@
             pltpu.VMEM((rows, width), BF16),
             pltpu.SemaphoreType.DMA((4, 2)),
         ],
-        compiler_params=pltpu.CompilerParams(vmem_limit_bytes=8 * 2**20),
+        compiler_params=pltpu.CompilerParams(vmem_limit_bytes=16 * 2**20),
     )(tok, bars, stacked, after)
 
 
@@ -264,12 +266,9 @@
     )
     down2 = swap(down, "c")
     tok1 = swap(tok0, "yh")
-    tok1, seen, seen2 = lax.optimization_barrier((tok1, stacked[:16, :128], down2[:16, :128]))
-    pair = jnp.concatenate([tok0, tok1], axis=0)
+    (pair,) = local(pair_kernel, [((256, feats), BF16)], tok0, tok1, stacked, down2, after=2)
     pair2 = swap(pair, "c")
-    (partial,) = local(
-        pre_kernel, [((8, 64, 4 * width), BF16)], pair, pair2, stacked, seen, seen2, after=2
-    )
+    (partial,) = local(pre_kernel, [((8, 64, 4 * width), BF16)], pair, pair2, stacked)
     pre = exchange(partial, TP)
     send, up_slope, act = local(
         gate_kernel,
@@ -293,24 +292,25 @@
         back_kernel, [((2, 8, 32, width), BF16), ((256, feats), BF16)], chunk, down, down2
     )
     back = exchange(back.reshape(16, 32, width), NEAR).reshape(2, 8, 32, width)
-    bars, joined = local(
+    bars, late = local(
         bars_kernel,
-        [((8, 64, 2 * width), BF16), ((256, feats + width), BF16)],
+        [((8, 64, 2 * width), BF16), ((256, feats), BF16)],
         back,
         up_slope,
         act,
         out,
-        hid2,
     )
     (tok_t,) = local(turn_kernel, [((feats, TOKENS), BF16)], pair, pair2, bars, after=1)
     bars = exchange(bars, TP)
-    joined = swap(joined, "c")
+    out2 = swap(late, "c")
+    hid2 = swap(hid2, "c")
     fisher_down, done = local(
         fisher_down_kernel,
         [(probe_down.shape, BF16), ((16, 128), BF16)],
         hid,
         out,
-        joined,
+        hid2,
+        out2,
         probe_down,
     )
     fisher_gate, fisher_up = fisher(tok_t, bars, stacked, done)

time: 189 us -> 191 us (1.011)
  waiting for transfers between devices: 16 us -> 13.7 us
  starting transfers between devices: 35 us -> 37.3 us
    ppermute x4 -> x5, starting transfers between devices: 15.1 us -> 17.4 us  [swap(): return lax.ppermute(x, axis, [(0, 1), (1, 0)])]
    all_to_all x2, waiting for transfers between devices: 14.5 us -> 12.2 us  [exchange(): return lax.all_to_all(pieces, axes, 0, 0, tiled=True)]
    pallas_call x12 -> x13, Pallas kernels: 11.3 us -> 12.2 us  [local(): pl.pallas_call(kernel, out_shape=[jax.ShapeDtypeStruct(shape, dtype) for...]
  transfers between devices with their start and end apart: 6 -> 7, of which waited for: 3 -> 3; matrix products, arithmetic and copies ran while one was open for 0% -> 0% of each run, Pallas kernels for 2% -> 2%
where the time goes in v11:
time: 191 us; the launch traced here: 190 us
  blocking collectives  112 us (59%)
  starting transfers between devices  37.3 us (20%)
  Pallas kernels  14.7 us (8%)
  waiting for transfers between devices  13.7 us (7%)
  local copies, waits for them, and re-layouts  11.5 us (6%)
    all_to_all x6, blocking collectives, exchange(): return lax.all_to_all(pieces, axes, 0, 0, tiled=True)  112 us
    all_to_all x2, starting transfers between devices, exchange(): return lax.all_to_all(pieces, axes, 0, 0, tiled=True)  19.9 us
    ppermute x5, starting transfers between devices, swap(): return lax.ppermute(x, axis, [(0, 1), (1, 0)])  17.4 us
    pallas_call x13, Pallas kernels, local(): pl.pallas_call(kernel, out_shape=[jax.ShapeDtypeStruct(shape, dtype) for...  12.2 us
    all_to_all x2, waiting for transfers between devices, exchange(): return lax.all_to_all(pieces, axes, 0, 0, tiled=True)  12.2 us
    unnamed x40, local copies, waits for them, and re-layouts  11.5 us
  transfers between devices with their start and end apart: 7, of which 3 were waited for; matrix products, arithmetic and copies ran while one was open for 0% of the time, Pallas kernels for 2%

profile of v11, /device:TPU:1, one launch (start us, length us, event | category | flops | bytes accessed | tf_op | source)
XLA Modules:
  0.0 189.7 jit_solution(16058082821792888650)
XLA Ops:
  0.6 0.0 copy-start.15
  0.6 0.7 copy-done.15
  1.3 0.0 copy-start.17
  1.4 0.7 shard_map.121
  2.1 15.7 %all-to-all-start = ((bf16[16,8,1024]{2,1,0:T(8,128)(2,1)}), bf16[16,8,1024]{2,1,0:T(8,128)(2,1)S(1)}, u32[]{:S(2)}, u32[]{:S(2)}) async-start(bf16[16,8,1024]{2,1,0:T(8,128)(2,1)} %shard_map.121), calls=%async_computation | async-start | bytes 524288 | tf_op jit(solution)/shard_map/all_to_all | solution.py:23
  17.8 0.0 copy-start.6
  17.8 1.0 copy-done.6
  18.9 1.0 copy-done.10
  19.9 0.7 copy-done.16
  20.6 0.7 shard_map.123.down_ref
  21.3 2.9 %collective-permute-start.1 = (bf16[512,1024]{1,0:T(8,128)(2,1)S(1)}, bf16[512,1024]{1,0:T(8,128)(2,1)}, u32[]{:S(2)}, u32[]{:S(2)}) collective-permute-start(bf16[512,1024]{1,0:T(8,128)(2,1)S(1)} %shard_map.123.down_ref), channel_id=1, source_target_pairs={{0,8},{8,0},{1,9},{9,1},{2,10},{10,2},{3,11},{11,3},{4,12},{12,4},... | collective-permute-start | bytes 3145736 | tf_op jit(solution)/shard_map/ppermute | solution.py:19
  24.2 9.0 %all-to-all-done = bf16[16,8,1024]{2,1,0:T(8,128)(2,1)S(1)} async-done(((bf16[16,8,1024]{2,1,0:T(8,128)(2,1)}), bf16[16,8,1024]{2,1,0:T(8,128)(2,1)S(1)}, u32[]{:S(2)}, u32[]{:S(2)}) %all-to-all-start) | async-done | bytes 262176 | tf_op jit(solution)/shard_map/all_to_all | solution.py:23
  33.2 4.8 %collective-permute-start = (bf16[128,1024]{1,0:T(8,128)(2,1)S(1)}, bf16[128,1024]{1,0:T(8,128)(2,1)}, u32[]{:S(2)}, u32[]{:S(2)}) collective-permute-start(bf16[128,1024]{1,0:T(8,128)(2,1)S(1)} %bitcast.9), channel_id=1, source_target_pairs={{0,256},{256,0},{1,257},{257,1},{2,258},{258,2},{3,259},{259,3},{4... | collective-permute-start | bytes 786440 | tf_op jit(solution)/shard_map/ppermute | solution.py:19
  38.0 0.0 copy-done.17
  38.0 0.1 copy.13.gmask_ref
  38.1 0.0 copy-done.18
  38.1 0.1 copy.14.umask_ref
  38.2 1.0 copy-done.11
  39.2 1.0 copy-done.12
  40.2 1.0 copy-done.13
  41.3 1.0 copy-done.14
  42.3 1.0 shard_map.122.after_ref.w_ref.probe_ref
  43.4 0.0 collective-permute-done.1.after2_ref.down2_ref
  43.4 0.0 collective-permute-done.b_ref
  43.4 1.0 shard_map.124.own_ref.a_ref
  44.4 5.3 %collective-permute-start.2 = (bf16[256,1024]{1,0:T(8,128)(2,1)S(1)}, bf16[256,1024]{1,0:T(8,128)(2,1)S(1)}, u32[]{:S(2)}, u32[]{:S(2)}) collective-permute-start(bf16[256,1024]{1,0:T(8,128)(2,1)S(1)} %shard_map.124.own_ref.a_ref), channel_id=1, source_target_pairs={{0,8},{8,0},{1,9},{9,1},{2,10},{10,2},{3,11},{11,3},{4,12},{12,4},... | collective-permute-start | bytes 1572872 | tf_op jit(solution)/shard_map/ppermute | solution.py:19
  49.7 1.5 collective-permute-done.2.other_ref.b_ref
  51.2 1.2 shard_map.125
  52.4 0.0 copy-start
  52.5 0.8 copy-done
  53.2 0.8 copy-done.8
  54.0 19.3 %all_to_all.40.x_ref = bf16[8,64,1024]{2,1,0:T(8,128)(2,1)S(1)} all-to-all(bf16[8,64,1024]{2,1,0:T(8,128)(2,1)S(1)} %shard_map.125), channel_id=1, replica_groups=mesh['yh'=2,'zh'=4,'zl'=4,'c'=2,'yl'=2,'x'=4] {'yl','x'}, dimensions={0} | all-to-all | bytes 2097152 | tf_op jit(solution)/shard_map/all_to_all | solution.py:23
  73.3 0.2 shard_map.126
  73.5 14.7 %all_to_all.41 = bf16[16,32,512]{2,1,0:T(8,128)(2,1)S(1)} all-to-all(bf16[16,32,512]{2,1,0:T(8,128)(2,1)S(1)} %bitcast.12), channel_id=1, replica_groups=mesh['yh'=2,'zh'=4,'zl'=4,'c'=2,'yl'=2,'x'=4] {'c','yl','x'}, dimensions={0} | all-to-all | bytes 1048576 | tf_op jit(solution)/shard_map/all_to_all | solution.py:23
  88.2 1.9 %shard_map.127 = (bf16[4,2,32,1024]{3,2,1,0:T(8,128)(2,1)S(1)}, bf16[256,256]{1,0:T(8,128)(2,1)S(1)}, bf16[256,256]{1,0:T(8,128)(2,1)S(1)}) custom-call(bf16[2,8,32,512]{3,2,1,0:T(8,128)(2,1)S(1)} %bitcast.8, bf16[512,1024]{1,0:T(8,128)(2,1)S(1)} %shard_map.123.down_ref, bf16[512,1024]{1,0:T(8,128)(2,1)} %collective-permute-done.1.after2_ref.down2_ref), custom_call_target="tpu_custom_call" | custom-call | tf_op jit(solution)/shard_map/pallas_call | solution.py:34
  90.1 22.5 %all_to_all.42.x_ref = bf16[8,32,1024]{2,1,0:T(8,128)(2,1)S(1)} all-to-all(bf16[8,32,1024]{2,1,0:T(8,128)(2,1)S(1)} %bitcast.13), channel_id=1, replica_groups=mesh['yh'=2,'zh'=4,'zl'=4,'c'=2,'yl'=2,'x'=4] {'zl','yh'}, dimensions={0} | all-to-all | bytes 1048576 | tf_op jit(solution)/shard_map/all_to_all | solution.py:23
  112.6 0.1 shard_map.128
  112.7 19.7 %all_to_all.43.x_ref = bf16[4,32,1024]{2,1,0:T(8,128)(2,1)S(1)} all-to-all(bf16[4,32,1024]{2,1,0:T(8,128)(2,1)S(1)} %shard_map.128), channel_id=1, replica_groups=mesh['yh'=2,'zh'=4,'zl'=4,'c'=2,'yl'=2,'x'=4] {'zh'}, dimensions={0} | all-to-all | bytes 524288 | tf_op jit(solution)/shard_map/all_to_all | solution.py:23
  132.4 21.5 %all_to_all.44 = bf16[8,32,1024]{2,1,0:T(8,128)(2,1)S(1)} all-to-all(bf16[8,32,1024]{2,1,0:T(8,128)(2,1)S(1)} %shard_map.129), channel_id=1, replica_groups=mesh['yh'=2,'zh'=4,'zl'=4,'c'=2,'yl'=2,'x'=4] {'zl','yh'}, dimensions={0} | all-to-all | bytes 1048576 | tf_op jit(solution)/shard_map/all_to_all | solution.py:23
  154.0 1.7 shard_map.130
  155.7 0.0 copy-start.4
  155.7 0.0 copy-start.1
  155.7 0.0 copy-start.9
  155.7 13.9 %all_to_all.45 = bf16[16,32,256]{2,1,0:T(8,128)(2,1)S(1)} all-to-all(bf16[16,32,256]{2,1,0:T(8,128)(2,1)S(1)} %bitcast.14), channel_id=1, replica_groups=mesh['yh'=2,'zh'=4,'zl'=4,'c'=2,'yl'=2,'x'=4] {'c','yl','x'}, dimensions={0} | all-to-all | bytes 524288 | tf_op jit(solution)/shard_map/all_to_all | solution.py:23
  169.6 0.0 copy-done.4
  169.6 1.0 shard_map.131
  170.6 2.1 %collective-permute-start.4 = (bf16[256,1024]{1,0:T(8,128)(2,1)}, bf16[256,1024]{1,0:T(8,128)(2,1)}, u32[]{:S(2)}, u32[]{:S(2)}) collective-permute-start(bf16[256,1024]{1,0:T(8,128)(2,1)} %get-tuple-element.26), channel_id=1, source_target_pairs={{0,8},{8,0},{1,9},{9,1},{2,10},{10,2},{3,11},{11,3},{4,12},{12,4},... | collective-permute-start | bytes 1572872 | tf_op jit(solution)/shard_map/ppermute | solution.py:19
  172.7 4.1 %all-to-all-start.7 = ((bf16[8,64,512]{2,1,0:T(8,128)(2,1)}), bf16[8,64,512]{2,1,0:T(8,128)(2,1)}, u32[]{:S(2)}, u32[]{:S(2)}) async-start(bf16[8,64,512]{2,1,0:T(8,128)(2,1)} %get-tuple-element.23.after_ref), calls=%async_computation.7 | async-start | bytes 1048576 | tf_op jit(solution)/shard_map/all_to_all | solution.py:23
  176.9 0.0 copy-start.5
  176.9 2.3 %collective-permute-start.3 = (bf16[256,256]{1,0:T(8,128)(2,1)S(1)}, bf16[256,256]{1,0:T(8,128)(2,1)S(1)}, u32[]{:S(2)}, u32[]{:S(2)}) collective-permute-start(bf16[256,256]{1,0:T(8,128)(2,1)S(1)} %get-tuple-element.25), channel_id=1, source_target_pairs={{0,8},{8,0},{1,9},{9,1},{2,10},{10,2},{3,11},{11,3},{4,12},{12,4},... | collective-permute-start | bytes 393224 | tf_op jit(solution)/shard_map/ppermute | solution.py:19
  179.2 0.0 copy-done.1
  179.2 0.0 copy-done.9
  179.2 0.3 shard_map.132.tok_ref
  179.6 0.0 copy-start.2
  179.6 1.0 copy-done.2
  180.5 0.0 collective-permute-done.3.hid2_ref
  180.5 0.0 collective-permute-done.4.out2_ref
  180.6 0.0 copy-done.5
  180.6 0.0 copy-start.7
  180.6 1.1 copy-done.7
  181.7 2.3 %shard_map.133 = (bf16[256,1024]{1,0:T(8,128)(2,1)}, bf16[16,128]{1,0:T(8,128)(2,1)S(1)}) custom-call(bf16[256,256]{1,0:T(8,128)(2,1)S(1)} %get-tuple-element.24.hid_ref, bf16[256,1024]{1,0:T(8,128)(2,1)S(1)} %copy-done.5, bf16[256,256]{1,0:T(8,128)(2,1)S(1)} %collective-permute-done.3.hid2_ref, bf16[256,1024]{1,0:T(8,128)(2,1)} %collective-permute-done.4.out2_ref, ...), custom_call_target="tpu_custom_call" | custom-call | tf_op jit(solution)/shard_map/pallas_call | solution.py:34
  184.0 3.2 %all-to-all-done.7.bars_ref = bf16[8,64,512]{2,1,0:T(8,128)(2,1)} async-done(((bf16[8,64,512]{2,1,0:T(8,128)(2,1)}), bf16[8,64,512]{2,1,0:T(8,128)(2,1)}, u32[]{:S(2)}, u32[]{:S(2)}) %all-to-all-start.7) | async-done | bytes 524320 | tf_op jit(solution)/shard_map/all_to_all | solution.py:23
  187.2 0.0 copy-done.3
  187.2 2.5 %shard_map.134 = (bf16[1024,256]{1,0:T(8,128)(2,1)}, bf16[1024,256]{1,0:T(8,128)(2,1)}) custom-call(bf16[1024,512]{1,0:T(8,128)(2,1)S(1)} %copy-done.3, bf16[8,64,512]{2,1,0:T(8,128)(2,1)} %all-to-all-done.7.bars_ref, bf16[1024,1024]{1,0:T(8,128)(2,1)S(1)} %shard_map.122.after_ref.w_ref.probe_ref, bf16[16,128]{1,0:T(8,128)(2,1)S(1)} %get-tuple-element.27.after_ref), custom_call_target="tpu_custom_call" | custom-call | tf_op jit(solution)/shard_map/pallas_call | solution.py:222
  (10 shorter events, 0.1 us)
Async XLA Ops:
  0.6 0.7 copy-start.15
  1.3 36.6 %copy-start.17 = (s32[8,2]{0,1:T(2,128)S(1)}, s32[8,2]{0,1:T(2,128)}, u32[]{:S(2)}) copy-start(s32[8,2]{0,1:T(2,128)} %param.14) | copy-start | bytes 196
  1.4 36.7 %copy-start.18 = (s32[8,2]{0,1:T(2,128)S(1)}, s32[8,2]{0,1:T(2,128)}, u32[]{:S(2)}) copy-start(s32[8,2]{0,1:T(2,128)} %param.15) | copy-start | bytes 196
  2.1 31.1 %all-to-all-start = ((bf16[16,8,1024]{2,1,0:T(8,128)(2,1)}), bf16[16,8,1024]{2,1,0:T(8,128)(2,1)S(1)}, u32[]{:S(2)}, u32[]{:S(2)}) async-start(bf16[16,8,1024]{2,1,0:T(8,128)(2,1)} %shard_map.121), calls=%async_computation | async-start | bytes 524288 | tf_op jit(solution)/shard_map/all_to_all | solution.py:23
  17.8 1.0 copy-start.6
  18.9 1.0 copy-start.10
  19.9 0.7 copy-start.16
  21.3 22.1 %collective-permute-start.1 = (bf16[512,1024]{1,0:T(8,128)(2,1)S(1)}, bf16[512,1024]{1,0:T(8,128)(2,1)}, u32[]{:S(2)}, u32[]{:S(2)}) collective-permute-start(bf16[512,1024]{1,0:T(8,128)(2,1)S(1)} %shard_map.123.down_ref), channel_id=1, source_target_pairs={{0,8},{8,0},{1,9},{9,1},{2,10},{10,2},{3,11},{11,3},{4,12},{12,4},... | collective-permute-start | bytes 3145736 | tf_op jit(solution)/shard_map/ppermute | solution.py:19
  33.2 10.2 %collective-permute-start = (bf16[128,1024]{1,0:T(8,128)(2,1)S(1)}, bf16[128,1024]{1,0:T(8,128)(2,1)}, u32[]{:S(2)}, u32[]{:S(2)}) collective-permute-start(bf16[128,1024]{1,0:T(8,128)(2,1)S(1)} %bitcast.9), channel_id=1, source_target_pairs={{0,256},{256,0},{1,257},{257,1},{2,258},{258,2},{3,259},{259,3},{4... | collective-permute-start | bytes 786440 | tf_op jit(solution)/shard_map/ppermute | solution.py:19
  38.2 1.0 copy-start.11
  39.2 1.0 copy-start.12
  40.2 1.0 copy-start.13
  41.3 1.0 copy-start.14
  44.4 6.8 %collective-permute-start.2 = (bf16[256,1024]{1,0:T(8,128)(2,1)S(1)}, bf16[256,1024]{1,0:T(8,128)(2,1)S(1)}, u32[]{:S(2)}, u32[]{:S(2)}) collective-permute-start(bf16[256,1024]{1,0:T(8,128)(2,1)S(1)} %shard_map.124.own_ref.a_ref), channel_id=1, source_target_pairs={{0,8},{8,0},{1,9},{9,1},{2,10},{10,2},{3,11},{11,3},{4,12},{12,4},... | collective-permute-start | bytes 1572872 | tf_op jit(solution)/shard_map/ppermute | solution.py:19
  52.4 0.8 copy-start
  53.2 0.8 copy-start.8
  155.7 13.9 %copy-start.4 = (bf16[256,1024]{1,0:T(8,128)(2,1)}, bf16[256,1024]{1,0:T(8,128)(2,1)S(1)}, u32[]{:S(2)}) copy-start(bf16[256,1024]{1,0:T(8,128)(2,1)S(1)} %get-tuple-element.22.out_ref) | copy-start | bytes 1572868
  155.7 23.5 %copy-start.1 = (bf16[256,1024]{1,0:T(8,128)(2,1)S(1)}, bf16[256,1024]{1,0:T(8,128)(2,1)}, u32[]{:S(2)}) copy-start(bf16[256,1024]{1,0:T(8,128)(2,1)} %copy-done) | copy-start | bytes 1572868
  155.7 23.5 %copy-start.9 = (bf16[256,1024]{1,0:T(8,128)(2,1)S(1)}, bf16[256,1024]{1,0:T(8,128)(2,1)}, u32[]{:S(2)}) copy-start(bf16[256,1024]{1,0:T(8,128)(2,1)} %copy-done.8) | copy-start | bytes 1572868
  170.6 10.0 %collective-permute-start.4 = (bf16[256,1024]{1,0:T(8,128)(2,1)}, bf16[256,1024]{1,0:T(8,128)(2,1)}, u32[]{:S(2)}, u32[]{:S(2)}) collective-permute-start(bf16[256,1024]{1,0:T(8,128)(2,1)} %get-tuple-element.26), channel_id=1, source_target_pairs={{0,8},{8,0},{1,9},{9,1},{2,10},{10,2},{3,11},{11,3},{4,12},{12,4},... | collective-permute-start | bytes 1572872 | tf_op jit(solution)/shard_map/ppermute | solution.py:19
  172.7 14.5 %all-to-all-start.7 = ((bf16[8,64,512]{2,1,0:T(8,128)(2,1)}), bf16[8,64,512]{2,1,0:T(8,128)(2,1)}, u32[]{:S(2)}, u32[]{:S(2)}) async-start(bf16[8,64,512]{2,1,0:T(8,128)(2,1)} %get-tuple-element.23.after_ref), calls=%async_computation.7 | async-start | bytes 1048576 | tf_op jit(solution)/shard_map/all_to_all | solution.py:23
  176.9 3.7 %copy-start.5 = (bf16[256,1024]{1,0:T(8,128)(2,1)S(1)}, bf16[256,1024]{1,0:T(8,128)(2,1)}, u32[]{:S(2)}) copy-start(bf16[256,1024]{1,0:T(8,128)(2,1)} %copy-done.4) | copy-start | bytes 1572868
  176.9 3.6 %collective-permute-start.3 = (bf16[256,256]{1,0:T(8,128)(2,1)S(1)}, bf16[256,256]{1,0:T(8,128)(2,1)S(1)}, u32[]{:S(2)}, u32[]{:S(2)}) collective-permute-start(bf16[256,256]{1,0:T(8,128)(2,1)S(1)} %get-tuple-element.25), channel_id=1, source_target_pairs={{0,8},{8,0},{1,9},{9,1},{2,10},{10,2},{3,11},{11,3},{4,12},{12,4},... | collective-permute-start | bytes 393224 | tf_op jit(solution)/shard_map/ppermute | solution.py:19
  179.6 1.0 copy-start.2
  180.5 6.7 %copy-start.3 = (bf16[1024,512]{1,0:T(8,128)(2,1)S(1)}, bf16[1024,512]{1,0:T(8,128)(2,1)}, u32[]{:S(2)}) copy-start(bf16[1024,512]{1,0:T(8,128)(2,1)} %copy-done.2) | copy-start | bytes 3145732
  180.6 1.1 copy-start.7

commit v12 on v11

--- a/solution.py
+++ b/solution.py
@@ -66,7 +66,14 @@
     o_ref[rows:] = b_ref[...]
 
 
-def pre_kernel(own_ref, other_ref, w_ref, o_ref):
+def hold_kernel(x_ref, after_ref, o_ref):
+    o_ref[...] = x_ref[...]
+
+
+def pre_kernel(own_ref, other_ref, w_ref, after_ref, o_ref, turned_ref):
+    rows = own_ref.shape[0]
+    turned_ref[:, :rows] = own_ref[...].T
+    turned_ref[:, rows:] = other_ref[...].T
     width = w_ref.shape[1] // 4
     for half, tok_ref in enumerate((own_ref, other_ref)):
         for j in range(4):
@@ -162,12 +169,6 @@
             )
 
 
-def turn_kernel(a_ref, b_ref, after_ref, o_ref):
-    rows = a_ref.shape[0]
-    o_ref[:, :rows] = a_ref[...].T
-    o_ref[:, rows:] = b_ref[...].T
-
-
 def bars_kernel(x_ref, up_slope_ref, act_ref, out_ref, o_ref, late_ref):
     width = act_ref.shape[1]
     late_ref[...] = out_ref[...]
@@ -185,17 +186,7 @@
             o_ref[i, rows, width:] = up_bar
 
 
-def fisher_down_kernel(hid_ref, out_ref, hid2_ref, out2_ref, probe_ref, o_ref, done_ref):
-    own = hid_ref[...].T
-    other = hid2_ref[...].T
-    for j in range(4):
-        cols = slice(j * 256, (j + 1) * 256)
-        y = dot(own, out_ref[:, cols]) + dot(other, out2_ref[:, cols])
-        o_ref[:, cols] = (probe_ref[:, cols].astype(F32) * y * TOKENS**-0.5).astype(BF16)
-    done_ref[...] = out2_ref[:16, :128]
-
-
-def fisher_kernel(tok_ref, bars_ref, probe_ref, after_ref, gate_ref, up_ref, g_ref, u_ref, sem):
+def fisher_kernel(tok_ref, bars_ref, probe_ref, gate_ref, up_ref, g_ref, u_ref, sem):
     width = gate_ref.shape[1]
     factor = TOKENS**-0.5
     bars = [bars_ref[:, 16 * q : 16 * q + 16, :].reshape(128, 2 * width) for q in range(4)]
@@ -214,7 +205,7 @@
         write.wait()
 
 
-def fisher(tok, bars, stacked, after):
+def fisher(tok, bars, stacked):
     rows = stacked.shape[0]
     width = stacked.shape[1] // 4
     spec = pl.BlockSpec(memory_space=pltpu.VMEM)
@@ -222,7 +213,7 @@
     return pl.pallas_call(
         fisher_kernel,
         out_shape=[jax.ShapeDtypeStruct((rows, width), BF16)] * 2,
-        in_specs=[spec, spec, spec, unread],
+        in_specs=[spec, spec, spec],
         out_specs=[unread, unread],
         scratch_shapes=[
             pltpu.VMEM((rows, width), BF16),
@@ -230,7 +221,7 @@
             pltpu.SemaphoreType.DMA((4, 2)),
         ],
         compiler_params=pltpu.CompilerParams(vmem_limit_bytes=16 * 2**20),
-    )(tok, bars, stacked, after)
+    )(tok, bars, stacked)
 
 
 def on_device(
@@ -268,7 +259,16 @@
     tok1 = swap(tok0, "yh")
     (pair,) = local(pair_kernel, [((256, feats), BF16)], tok0, tok1, stacked, down2, after=2)
     pair2 = swap(pair, "c")
-    (partial,) = local(pre_kernel, [((8, 64, 4 * width), BF16)], pair, pair2, stacked)
+    (down2,) = local(hold_kernel, [(down2.shape, BF16)], down2, pair, after=1)
+    partial, tok_t = local(
+        pre_kernel,
+        [((8, 64, 4 * width), BF16), ((feats, TOKENS), BF16)],
+        pair,
+        pair2,
+        stacked,
+        down2,
+        after=1,
+    )
     pre = exchange(partial, TP)
     send, up_slope, act = local(
         gate_kernel,
@@ -300,20 +300,14 @@
         act,
         out,
     )
-    (tok_t,) = local(turn_kernel, [((feats, TOKENS), BF16)], pair, pair2, bars, after=1)
     bars = exchange(bars, TP)
     out2 = swap(late, "c")
     hid2 = swap(hid2, "c")
-    fisher_down, done = local(
-        fisher_down_kernel,
-        [(probe_down.shape, BF16), ((16, 128), BF16)],
-        hid,
-        out,
-        hid2,
-        out2,
-        probe_down,
-    )
-    fisher_gate, fisher_up = fisher(tok_t, bars, stacked, done)
+    grad_down = dot(
+        jnp.concatenate([hid, hid2], axis=0), jnp.concatenate([out, out2], axis=0), ((0,), (0,))
+    )
+    fisher_down = (probe_down.astype(F32) * grad_down * TOKENS**-0.5).astype(BF16)
+    fisher_gate, fisher_up = fisher(tok_t, bars, stacked)
     return (fisher_gate, fisher_up, fisher_down)
 
 

time: 191 us -> 189 us (0.990)
  Pallas kernels: 14.7 us -> 9.76 us
  waiting for transfers between devices: 13.7 us -> 17.3 us
  matrix products: 0 us -> 2.31 us
    all_to_all x2, waiting for transfers between devices: 12.2 us -> 17 us  [exchange(): return lax.all_to_all(pieces, axes, 0, 0, tiled=True)]
    pallas_call x13 -> x12, Pallas kernels: 12.2 us -> 8.27 us  [local(): pl.pallas_call(kernel, out_shape=[jax.ShapeDtypeStruct(shape, dtype) for...]
    dot_general x0 -> x1, matrix products: none -> 2.31 us  [dot(): return lax.dot_general(a, b, (dims, ((), ())), preferred_element_type=F32)]
    unnamed x40 -> x34, local copies, waits for them, and re-layouts: 11.5 us -> 9.84 us
where the time goes in v12:
time: 189 us; the launch traced here: 188 us
  blocking collectives  111 us (59%)
  starting transfers between devices  36.7 us (19%)
  waiting for transfers between devices  17.3 us (9%)
  local copies, waits for them, and re-layouts  9.84 us (5%)
  Pallas kernels  9.76 us (5%)
  matrix products  2.31 us (1%)
    all_to_all x6, blocking collectives, exchange(): return lax.all_to_all(pieces, axes, 0, 0, tiled=True)  111 us
    all_to_all x2, starting transfers between devices, exchange(): return lax.all_to_all(pieces, axes, 0, 0, tiled=True)  19.4 us
    ppermute x5, starting transfers between devices, swap(): return lax.ppermute(x, axis, [(0, 1), (1, 0)])  17.3 us
    all_to_all x2, waiting for transfers between devices, exchange(): return lax.all_to_all(pieces, axes, 0, 0, tiled=True)  17 us
    unnamed x34, local copies, waits for them, and re-layouts  9.84 us
    pallas_call x12, Pallas kernels, local(): pl.pallas_call(kernel, out_shape=[jax.ShapeDtypeStruct(shape, dtype) for...  8.27 us
  transfers between devices with their start and end apart: 7, of which 3 were waited for; matrix products, arithmetic and copies ran while one was open for 0% of the time, Pallas kernels for 2%

profile of v12, /device:TPU:1, one launch (start us, length us, event | category | flops | bytes accessed | tf_op | source)
XLA Modules:
  0.0 188.1 jit_solution(10824914128693227500)
XLA Ops:
  0.6 0.0 copy-start.12
  0.6 0.7 copy-done.12
  1.3 0.0 copy-start.14
  1.4 0.0 copy-start.15
  1.4 0.7 shard_map.121
  2.1 15.7 %all-to-all-start = ((bf16[16,8,1024]{2,1,0:T(8,128)(2,1)}), bf16[16,8,1024]{2,1,0:T(8,128)(2,1)S(1)}, u32[]{:S(2)}, u32[]{:S(2)}) async-start(bf16[16,8,1024]{2,1,0:T(8,128)(2,1)} %shard_map.121), calls=%async_computation | async-start | bytes 524288 | tf_op jit(solution)/shard_map/all_to_all | solution.py:23
  17.8 0.0 copy-start.5
  17.8 1.0 copy-done.5
  18.9 0.0 copy-start.6
  18.9 1.0 copy-done.6
  19.9 0.0 copy-start.13
  19.9 0.7 copy-done.13
  20.6 0.7 shard_map.123.down_ref
  21.3 2.9 %collective-permute-start.1 = (bf16[512,1024]{1,0:T(8,128)(2,1)S(1)}, bf16[512,1024]{1,0:T(8,128)(2,1)}, u32[]{:S(2)}, u32[]{:S(2)}) collective-permute-start(bf16[512,1024]{1,0:T(8,128)(2,1)S(1)} %shard_map.123.down_ref), channel_id=1, source_target_pairs={{0,8},{8,0},{1,9},{9,1},{2,10},{10,2},{3,11},{11,3},{4,12},{12,4},... | collective-permute-start | bytes 3145736 | tf_op jit(solution)/shard_map/ppermute | solution.py:19
  24.2 9.0 %all-to-all-done = bf16[16,8,1024]{2,1,0:T(8,128)(2,1)S(1)} async-done(((bf16[16,8,1024]{2,1,0:T(8,128)(2,1)}), bf16[16,8,1024]{2,1,0:T(8,128)(2,1)S(1)}, u32[]{:S(2)}, u32[]{:S(2)}) %all-to-all-start) | async-done | bytes 262176 | tf_op jit(solution)/shard_map/all_to_all | solution.py:23
  33.2 4.8 %collective-permute-start = (bf16[128,1024]{1,0:T(8,128)(2,1)S(1)}, bf16[128,1024]{1,0:T(8,128)(2,1)}, u32[]{:S(2)}, u32[]{:S(2)}) collective-permute-start(bf16[128,1024]{1,0:T(8,128)(2,1)S(1)} %bitcast.9), channel_id=1, source_target_pairs={{0,256},{256,0},{1,257},{257,1},{2,258},{258,2},{3,259},{259,3},{4... | collective-permute-start | bytes 786440 | tf_op jit(solution)/shard_map/ppermute | solution.py:19
  38.0 0.0 copy-done.14
  38.0 0.1 copy.13.gmask_ref
  38.1 0.0 copy-done.15
  38.1 0.1 copy.14.umask_ref
  38.2 0.0 copy-start.8
  38.2 1.0 copy-done.8
  39.2 0.0 copy-start.9
  39.2 1.0 copy-done.9
  40.2 0.0 copy-start.10
  40.2 1.0 copy-done.10
  41.3 0.0 copy-start.11
  41.3 1.0 copy-done.11
  42.3 1.0 shard_map.122.after_ref.w_ref.probe_ref
  43.4 0.0 collective-permute-done.1.after2_ref.x_ref
  43.4 0.0 collective-permute-done.b_ref
  43.4 1.0 shard_map.124.after_ref.own_ref
  44.4 5.3 %collective-permute-start.2 = (bf16[256,1024]{1,0:T(8,128)(2,1)S(1)}, bf16[256,1024]{1,0:T(8,128)(2,1)S(1)}, u32[]{:S(2)}, u32[]{:S(2)}) collective-permute-start(bf16[256,1024]{1,0:T(8,128)(2,1)S(1)} %shard_map.124.after_ref.own_ref), channel_id=1, source_target_pairs={{0,8},{8,0},{1,9},{9,1},{2,10},{10,2},{3,11},{11,3},{4,12},{12,4},... | collective-permute-start | bytes 1572872 | tf_op jit(solution)/shard_map/ppermute | solution.py:19
  49.7 1.3 shard_map.125.after_ref.down2_ref
  51.0 0.2 collective-permute-done.2.other_ref
  51.2 1.2 shard_map.126
  52.4 0.0 copy-start
  52.5 19.3 %all_to_all.40.x_ref = bf16[8,64,1024]{2,1,0:T(8,128)(2,1)S(1)} all-to-all(bf16[8,64,1024]{2,1,0:T(8,128)(2,1)S(1)} %get-tuple-element.18), channel_id=1, replica_groups=mesh['yh'=2,'zh'=4,'zl'=4,'c'=2,'yl'=2,'x'=4] {'yl','x'}, dimensions={0} | all-to-all | bytes 2097152 | tf_op jit(solution)/shard_map/all_to_all | solution.py:23
  71.8 0.2 shard_map.127
  71.9 14.7 %all_to_all.41 = bf16[16,32,512]{2,1,0:T(8,128)(2,1)S(1)} all-to-all(bf16[16,32,512]{2,1,0:T(8,128)(2,1)S(1)} %bitcast.12), channel_id=1, replica_groups=mesh['yh'=2,'zh'=4,'zl'=4,'c'=2,'yl'=2,'x'=4] {'c','yl','x'}, dimensions={0} | all-to-all | bytes 1048576 | tf_op jit(solution)/shard_map/all_to_all | solution.py:23
  86.6 0.0 copy-done
  86.6 0.7 shard_map.128
  87.4 22.5 %all_to_all.42.x_ref = bf16[8,32,1024]{2,1,0:T(8,128)(2,1)S(1)} all-to-all(bf16[8,32,1024]{2,1,0:T(8,128)(2,1)S(1)} %bitcast.13), channel_id=1, replica_groups=mesh['yh'=2,'zh'=4,'zl'=4,'c'=2,'yl'=2,'x'=4] {'zl','yh'}, dimensions={0} | all-to-all | bytes 1048576 | tf_op jit(solution)/shard_map/all_to_all | solution.py:23
  109.9 0.1 shard_map.129
  109.9 19.7 %all_to_all.43.x_ref = bf16[4,32,1024]{2,1,0:T(8,128)(2,1)S(1)} all-to-all(bf16[4,32,1024]{2,1,0:T(8,128)(2,1)S(1)} %shard_map.129), channel_id=1, replica_groups=mesh['yh'=2,'zh'=4,'zl'=4,'c'=2,'yl'=2,'x'=4] {'zh'}, dimensions={0} | all-to-all | bytes 524288 | tf_op jit(solution)/shard_map/all_to_all | solution.py:23
  129.7 21.5 %all_to_all.44 = bf16[8,32,1024]{2,1,0:T(8,128)(2,1)S(1)} all-to-all(bf16[8,32,1024]{2,1,0:T(8,128)(2,1)S(1)} %shard_map.130), channel_id=1, replica_groups=mesh['yh'=2,'zh'=4,'zl'=4,'c'=2,'yl'=2,'x'=4] {'zl','yh'}, dimensions={0} | all-to-all | bytes 1048576 | tf_op jit(solution)/shard_map/all_to_all | solution.py:23
  151.2 0.5 shard_map.131
  151.7 0.0 copy-start.2
  151.7 13.7 %all_to_all.45 = bf16[16,32,256]{2,1,0:T(8,128)(2,1)S(1)} all-to-all(bf16[16,32,256]{2,1,0:T(8,128)(2,1)S(1)} %bitcast.14), channel_id=1, replica_groups=mesh['yh'=2,'zh'=4,'zl'=4,'c'=2,'yl'=2,'x'=4] {'c','yl','x'}, dimensions={0} | all-to-all | bytes 524288 | tf_op jit(solution)/shard_map/all_to_all | solution.py:23
  165.4 0.8 shard_map.132
  166.2 0.0 copy-done.2
  166.3 0.8 copy-done.4
  167.0 2.1 %collective-permute-start.4 = (bf16[256,1024]{1,0:T(8,128)(2,1)}, bf16[256,1024]{1,0:T(8,128)(2,1)}, u32[]{:S(2)}, u32[]{:S(2)}) collective-permute-start(bf16[256,1024]{1,0:T(8,128)(2,1)} %get-tuple-element.30), channel_id=1, source_target_pairs={{0,8},{8,0},{1,9},{9,1},{2,10},{10,2},{3,11},{11,3},{4,12},{12,4},... | collective-permute-start | bytes 1572872 | tf_op jit(solution)/shard_map/ppermute | solution.py:19
  169.2 0.0 copy-start.3
  169.2 3.6 %all-to-all-start.7 = ((bf16[8,64,512]{2,1,0:T(8,128)(2,1)}), bf16[8,64,512]{2,1,0:T(8,128)(2,1)S(1)}, u32[]{:S(2)}, u32[]{:S(2)}) async-start(bf16[8,64,512]{2,1,0:T(8,128)(2,1)} %copy-done.4), calls=%async_computation.7 | async-start | bytes 1048576 | tf_op jit(solution)/shard_map/all_to_all | solution.py:23
  172.8 2.2 %collective-permute-start.3 = (bf16[256,256]{1,0:T(8,128)(2,1)S(1)}, bf16[256,256]{1,0:T(8,128)(2,1)S(1)}, u32[]{:S(2)}, u32[]{:S(2)}) collective-permute-start(bf16[256,256]{1,0:T(8,128)(2,1)S(1)} %get-tuple-element.29), channel_id=1, source_target_pairs={{0,8},{8,0},{1,9},{9,1},{2,10},{10,2},{3,11},{11,3},{4,12},{12,4},... | collective-permute-start | bytes 393224 | tf_op jit(solution)/shard_map/ppermute | solution.py:19
  175.0 8.0 %all-to-all-done.7.bars_ref = bf16[8,64,512]{2,1,0:T(8,128)(2,1)S(1)} async-done(((bf16[8,64,512]{2,1,0:T(8,128)(2,1)}), bf16[8,64,512]{2,1,0:T(8,128)(2,1)S(1)}, u32[]{:S(2)}, u32[]{:S(2)}) %all-to-all-start.7) | async-done | bytes 524320 | tf_op jit(solution)/shard_map/all_to_all | solution.py:23
  183.1 1.2 copy-done.1
  184.3 1.5 shard_map.133
  185.8 0.0 collective-permute-done.3
  185.8 0.0 collective-permute-done.4
  185.8 0.0 copy-done.3
  185.8 0.0 copy-done.7
  185.8 2.3 %fusion.1 = bf16[256,1024]{1,0:T(8,128)(2,1)} fusion(bf16[256,1024]{1,0:T(8,128)(2,1)} %collective-permute-done.4, bf16[256,1024]{1,0:T(8,128)(2,1)S(1)} %copy-done.3, bf16[256,1024]{1,0:T(8,128)(2,1)S(1)} %copy-done.7, bf16[256,256]{1,0:T(8,128)(2,1)S(1)} %collective-permute-done.3, bf16[256,256]{1,0:T(8,128)(2,1)S(1)} %get-tuple-element.28), kind=kOutput, calls=%fused_computation.2 | convolution fusion | flops 272105472 | bytes 2359296 | tf_op jit(solution)/shard_map/dot_general | solution.py:27
  (4 shorter events, 0.0 us)
Async XLA Ops:
  0.6 0.7 copy-start.12
  1.3 36.6 %copy-start.14 = (s32[8,2]{0,1:T(2,128)S(1)}, s32[8,2]{0,1:T(2,128)}, u32[]{:S(2)}) copy-start(s32[8,2]{0,1:T(2,128)} %param.14) | copy-start | bytes 196
  1.4 36.7 %copy-start.15 = (s32[8,2]{0,1:T(2,128)S(1)}, s32[8,2]{0,1:T(2,128)}, u32[]{:S(2)}) copy-start(s32[8,2]{0,1:T(2,128)} %param.15) | copy-start | bytes 196
  2.1 31.1 %all-to-all-start = ((bf16[16,8,1024]{2,1,0:T(8,128)(2,1)}), bf16[16,8,1024]{2,1,0:T(8,128)(2,1)S(1)}, u32[]{:S(2)}, u32[]{:S(2)}) async-start(bf16[16,8,1024]{2,1,0:T(8,128)(2,1)} %shard_map.121), calls=%async_computation | async-start | bytes 524288 | tf_op jit(solution)/shard_map/all_to_all | solution.py:23
  17.8 1.0 copy-start.5
  18.9 1.0 copy-start.6
  19.9 0.7 copy-start.13
  21.3 22.1 %collective-permute-start.1 = (bf16[512,1024]{1,0:T(8,128)(2,1)S(1)}, bf16[512,1024]{1,0:T(8,128)(2,1)}, u32[]{:S(2)}, u32[]{:S(2)}) collective-permute-start(bf16[512,1024]{1,0:T(8,128)(2,1)S(1)} %shard_map.123.down_ref), channel_id=1, source_target_pairs={{0,8},{8,0},{1,9},{9,1},{2,10},{10,2},{3,11},{11,3},{4,12},{12,4},... | collective-permute-start | bytes 3145736 | tf_op jit(solution)/shard_map/ppermute | solution.py:19
  33.2 10.2 %collective-permute-start = (bf16[128,1024]{1,0:T(8,128)(2,1)S(1)}, bf16[128,1024]{1,0:T(8,128)(2,1)}, u32[]{:S(2)}, u32[]{:S(2)}) collective-permute-start(bf16[128,1024]{1,0:T(8,128)(2,1)S(1)} %bitcast.9), channel_id=1, source_target_pairs={{0,256},{256,0},{1,257},{257,1},{2,258},{258,2},{3,259},{259,3},{4... | collective-permute-start | bytes 786440 | tf_op jit(solution)/shard_map/ppermute | solution.py:19
  38.2 1.0 copy-start.8
  39.2 1.0 copy-start.9
  40.2 1.0 copy-start.10
  41.3 1.0 copy-start.11
  44.4 6.8 %collective-permute-start.2 = (bf16[256,1024]{1,0:T(8,128)(2,1)S(1)}, bf16[256,1024]{1,0:T(8,128)(2,1)S(1)}, u32[]{:S(2)}, u32[]{:S(2)}) collective-permute-start(bf16[256,1024]{1,0:T(8,128)(2,1)S(1)} %shard_map.124.after_ref.own_ref), channel_id=1, source_target_pairs={{0,8},{8,0},{1,9},{9,1},{2,10},{10,2},{3,11},{11,3},{4,12},{12,4},... | collective-permute-start | bytes 1572872 | tf_op jit(solution)/shard_map/ppermute | solution.py:19
  52.4 34.2 %copy-start = (bf16[1024,512]{1,0:T(8,128)(2,1)}, bf16[1024,512]{1,0:T(8,128)(2,1)S(1)}, u32[]{:S(2)}) copy-start(bf16[1024,512]{1,0:T(8,128)(2,1)S(1)} %get-tuple-element.17.tok_ref) | copy-start | bytes 3145732
  151.7 14.6 %copy-start.2 = (bf16[256,1024]{1,0:T(8,128)(2,1)}, bf16[256,1024]{1,0:T(8,128)(2,1)S(1)}, u32[]{:S(2)}) copy-start(bf16[256,1024]{1,0:T(8,128)(2,1)S(1)} %get-tuple-element.24.out_ref) | copy-start | bytes 1572868
  166.3 0.8 copy-start.4
  167.0 18.8 %collective-permute-start.4 = (bf16[256,1024]{1,0:T(8,128)(2,1)}, bf16[256,1024]{1,0:T(8,128)(2,1)}, u32[]{:S(2)}, u32[]{:S(2)}) collective-permute-start(bf16[256,1024]{1,0:T(8,128)(2,1)} %get-tuple-element.30), channel_id=1, source_target_pairs={{0,8},{8,0},{1,9},{9,1},{2,10},{10,2},{3,11},{11,3},{4,12},{12,4},... | collective-permute-start | bytes 1572872 | tf_op jit(solution)/shard_map/ppermute | solution.py:19
  169.2 16.6 %copy-start.3 = (bf16[256,1024]{1,0:T(8,128)(2,1)S(1)}, bf16[256,1024]{1,0:T(8,128)(2,1)}, u32[]{:S(2)}) copy-start(bf16[256,1024]{1,0:T(8,128)(2,1)} %copy-done.2) | copy-start | bytes 1572868
  169.2 13.9 %all-to-all-start.7 = ((bf16[8,64,512]{2,1,0:T(8,128)(2,1)}), bf16[8,64,512]{2,1,0:T(8,128)(2,1)S(1)}, u32[]{:S(2)}, u32[]{:S(2)}) async-start(bf16[8,64,512]{2,1,0:T(8,128)(2,1)} %copy-done.4), calls=%async_computation.7 | async-start | bytes 1048576 | tf_op jit(solution)/shard_map/all_to_all | solution.py:23
  172.8 12.9 %collective-permute-start.3 = (bf16[256,256]{1,0:T(8,128)(2,1)S(1)}, bf16[256,256]{1,0:T(8,128)(2,1)S(1)}, u32[]{:S(2)}, u32[]{:S(2)}) collective-permute-start(bf16[256,256]{1,0:T(8,128)(2,1)S(1)} %get-tuple-element.29), channel_id=1, source_target_pairs={{0,8},{8,0},{1,9},{9,1},{2,10},{10,2},{3,11},{11,3},{4,12},{12,4},... | collective-permute-start | bytes 393224 | tf_op jit(solution)/shard_map/ppermute | solution.py:19
  183.1 1.2 copy-start.1
  184.3 1.5 copy-start.7

commit v13 on v12

--- a/solution.py
+++ b/solution.py
@@ -169,9 +169,11 @@
             )
 
 
-def bars_kernel(x_ref, up_slope_ref, act_ref, out_ref, o_ref, late_ref):
+def bars_kernel(x_ref, up_slope_ref, act_ref, out_ref, o_ref, late_ref, late2_ref):
     width = act_ref.shape[1]
-    late_ref[...] = out_ref[...]
+    half = late_ref.shape[1]
+    late_ref[...] = out_ref[:, :half]
+    late2_ref[...] = out_ref[:, half:]
     c = lax.axis_index("c")
     for r in range(2):
         place = c if r == 0 else 1 - c
@@ -186,7 +188,20 @@
             o_ref[i, rows, width:] = up_bar
 
 
-def fisher_kernel(tok_ref, bars_ref, probe_ref, gate_ref, up_ref, g_ref, u_ref, sem):
+def fisher_down_kernel(
+    hid_ref, out_ref, hid2_ref, late_ref, late2_ref, probe_ref, o_ref, done_ref
+):
+    own = hid_ref[...].T
+    other = hid2_ref[...].T
+    for j in range(4):
+        cols = slice(j * 256, (j + 1) * 256)
+        part = slice(j % 2 * 256, (j % 2 + 1) * 256)
+        y = dot(own, out_ref[:, cols]) + dot(other, (late_ref, late2_ref)[j // 2][:, part])
+        o_ref[:, cols] = (probe_ref[:, cols].astype(F32) * y * TOKENS**-0.5).astype(BF16)
+    done_ref[...] = late2_ref[:16, :128]
+
+
+def fisher_kernel(tok_ref, bars_ref, probe_ref, after_ref, gate_ref, up_ref, g_ref, u_ref, sem):
     width = gate_ref.shape[1]
     factor = TOKENS**-0.5
     bars = [bars_ref[:, 16 * q : 16 * q + 16, :].reshape(128, 2 * width) for q in range(4)]
@@ -205,7 +220,7 @@
         write.wait()
 
 
-def fisher(tok, bars, stacked):
+def fisher(tok, bars, stacked, after):
     rows = stacked.shape[0]
     width = stacked.shape[1] // 4
     spec = pl.BlockSpec(memory_space=pltpu.VMEM)
@@ -213,7 +228,7 @@
     return pl.pallas_call(
         fisher_kernel,
         out_shape=[jax.ShapeDtypeStruct((rows, width), BF16)] * 2,
-        in_specs=[spec, spec, spec],
+        in_specs=[spec, spec, spec, unread],
         out_specs=[unread, unread],
         scratch_shapes=[
             pltpu.VMEM((rows, width), BF16),
@@ -221,7 +236,7 @@
             pltpu.SemaphoreType.DMA((4, 2)),
         ],
         compiler_params=pltpu.CompilerParams(vmem_limit_bytes=16 * 2**20),
-    )(tok, bars, stacked)
+    )(tok, bars, stacked, after)
 
 
 def on_device(
@@ -292,22 +307,26 @@
         back_kernel, [((2, 8, 32, width), BF16), ((256, feats), BF16)], chunk, down, down2
     )
     back = exchange(back.reshape(16, 32, width), NEAR).reshape(2, 8, 32, width)
-    bars, late = local(
+    bars, late, late2 = local(
         bars_kernel,
-        [((8, 64, 2 * width), BF16), ((256, feats), BF16)],
+        [((8, 64, 2 * width), BF16), ((256, feats // 2), BF16), ((256, feats // 2), BF16)],
         back,
         up_slope,
         act,
         out,
     )
     bars = exchange(bars, TP)
-    out2 = swap(late, "c")
-    hid2 = swap(hid2, "c")
-    grad_down = dot(
-        jnp.concatenate([hid, hid2], axis=0), jnp.concatenate([out, out2], axis=0), ((0,), (0,))
-    )
-    fisher_down = (probe_down.astype(F32) * grad_down * TOKENS**-0.5).astype(BF16)
-    fisher_gate, fisher_up = fisher(tok_t, bars, stacked)
+    fisher_down, done = local(
+        fisher_down_kernel,
+        [(probe_down.shape, BF16), ((16, 128), BF16)],
+        hid,
+        out,
+        swap(hid2, "c"),
+        swap(late, "c"),
+        swap(late2, "c"),
+        probe_down,
+    )
+    fisher_gate, fisher_up = fisher(tok_t, bars, stacked, done)
     return (fisher_gate, fisher_up, fisher_down)
 
 

time: 189 us -> 185 us (0.979)
  waiting for transfers between devices: 17.3 us -> 10.6 us
  local copies, waits for them, and re-layouts: 9.84 us -> 12.2 us
  matrix products: 2.31 us -> 0 us
  starting transfers between devices: 36.7 us -> 38.7 us
    all_to_all x2, waiting for transfers between devices: 17 us -> 9.12 us  [exchange(): return lax.all_to_all(pieces, axes, 0, 0, tiled=True)]
    unnamed x34 -> x38, local copies, waits for them, and re-layouts: 9.84 us -> 12.2 us
    dot_general x1 -> x0, matrix products: 2.31 us -> none  [dot(): return lax.dot_general(a, b, (dims, ((), ())), preferred_element_type=F32)]
    ppermute x5 -> x6, starting transfers between devices: 17.3 us -> 19.5 us  [swap(): return lax.ppermute(x, axis, [(0, 1), (1, 0)])]
    pallas_call x12 -> x13, Pallas kernels: 8.27 us -> 8.77 us  [local(): pl.pallas_call(kernel, out_shape=[jax.ShapeDtypeStruct(shape, dtype) for...]
  transfers between devices with their start and end apart: 7 -> 8, of which waited for: 3 -> 4; matrix products, arithmetic and copies ran while one was open for 0% -> 0% of each run, Pallas kernels for 2% -> 2%
where the time goes in v13:
time: 185 us; the launch traced here: 184 us
  blocking collectives  112 us (61%)
  starting transfers between devices  38.7 us (21%)
  local copies, waits for them, and re-layouts  12.2 us (7%)
  waiting for transfers between devices  10.6 us (6%)
  Pallas kernels  10.2 us (6%)
    all_to_all x6, blocking collectives, exchange(): return lax.all_to_all(pieces, axes, 0, 0, tiled=True)  112 us
    ppermute x6, starting transfers between devices, swap(): return lax.ppermute(x, axis, [(0, 1), (1, 0)])  19.5 us
    all_to_all x2, starting transfers between devices, exchange(): return lax.all_to_all(pieces, axes, 0, 0, tiled=True)  19.2 us
    unnamed x38, local copies, waits for them, and re-layouts  12.2 us
    all_to_all x2, waiting for transfers between devices, exchange(): return lax.all_to_all(pieces, axes, 0, 0, tiled=True)  9.12 us
    pallas_call x13, Pallas kernels, local(): pl.pallas_call(kernel, out_shape=[jax.ShapeDtypeStruct(shape, dtype) for...  8.77 us
  transfers between devices with their start and end apart: 8, of which 4 were waited for; matrix products, arithmetic and copies ran while one was open for 0% of the time, Pallas kernels for 2%

profile of v13, /device:TPU:1, one launch (start us, length us, event | category | flops | bytes accessed | tf_op | source)
XLA Modules:
  0.0 184.2 jit_solution(13519515305631770313)
XLA Ops:
  0.6 0.0 copy-start.12
  0.6 0.7 copy-done.12
  1.3 0.0 copy-start.16
  1.4 0.7 shard_map.121
  2.1 15.7 %all-to-all-start = ((bf16[16,8,1024]{2,1,0:T(8,128)(2,1)}), bf16[16,8,1024]{2,1,0:T(8,128)(2,1)S(1)}, u32[]{:S(2)}, u32[]{:S(2)}) async-start(bf16[16,8,1024]{2,1,0:T(8,128)(2,1)} %shard_map.121), calls=%async_computation | async-start | bytes 524288 | tf_op jit(solution)/shard_map/all_to_all | solution.py:23
  17.8 0.0 copy-start.2
  17.8 1.0 copy-done.2
  18.9 1.0 copy-done.7
  19.9 0.7 copy-done.13
  20.6 0.7 shard_map.123.down_ref
  21.3 2.9 %collective-permute-start.1 = (bf16[512,1024]{1,0:T(8,128)(2,1)S(1)}, bf16[512,1024]{1,0:T(8,128)(2,1)}, u32[]{:S(2)}, u32[]{:S(2)}) collective-permute-start(bf16[512,1024]{1,0:T(8,128)(2,1)S(1)} %shard_map.123.down_ref), channel_id=1, source_target_pairs={{0,8},{8,0},{1,9},{9,1},{2,10},{10,2},{3,11},{11,3},{4,12},{12,4},... | collective-permute-start | bytes 3145736 | tf_op jit(solution)/shard_map/ppermute | solution.py:19
  24.2 9.0 %all-to-all-done = bf16[16,8,1024]{2,1,0:T(8,128)(2,1)S(1)} async-done(((bf16[16,8,1024]{2,1,0:T(8,128)(2,1)}), bf16[16,8,1024]{2,1,0:T(8,128)(2,1)S(1)}, u32[]{:S(2)}, u32[]{:S(2)}) %all-to-all-start) | async-done | bytes 262176 | tf_op jit(solution)/shard_map/all_to_all | solution.py:23
  33.2 4.8 %collective-permute-start = (bf16[128,1024]{1,0:T(8,128)(2,1)S(1)}, bf16[128,1024]{1,0:T(8,128)(2,1)}, u32[]{:S(2)}, u32[]{:S(2)}) collective-permute-start(bf16[128,1024]{1,0:T(8,128)(2,1)S(1)} %bitcast.9), channel_id=1, source_target_pairs={{0,256},{256,0},{1,257},{257,1},{2,258},{258,2},{3,259},{259,3},{4... | collective-permute-start | bytes 786440 | tf_op jit(solution)/shard_map/ppermute | solution.py:19
  38.0 0.0 copy-done.16
  38.0 0.1 copy.13.gmask_ref
  38.1 0.0 copy-done.17
  38.1 0.1 copy.14.umask_ref
  38.2 1.0 copy-done.8
  39.2 1.0 copy-done.9
  40.2 1.0 copy-done.10
  41.3 1.0 copy-done.11
  42.3 1.0 shard_map.122.after_ref.w_ref.probe_ref
  43.4 0.0 collective-permute-done.1.after2_ref.x_ref
  43.4 0.0 collective-permute-done.b_ref
  43.4 1.0 shard_map.124.after_ref.own_ref
  44.4 5.3 %collective-permute-start.2 = (bf16[256,1024]{1,0:T(8,128)(2,1)S(1)}, bf16[256,1024]{1,0:T(8,128)(2,1)S(1)}, u32[]{:S(2)}, u32[]{:S(2)}) collective-permute-start(bf16[256,1024]{1,0:T(8,128)(2,1)S(1)} %shard_map.124.after_ref.own_ref), channel_id=1, source_target_pairs={{0,8},{8,0},{1,9},{9,1},{2,10},{10,2},{3,11},{11,3},{4,12},{12,4},... | collective-permute-start | bytes 1572872 | tf_op jit(solution)/shard_map/ppermute | solution.py:19
  49.7 1.3 shard_map.125.after_ref.down2_ref
  51.0 0.2 collective-permute-done.2.other_ref
  51.2 1.2 shard_map.126
  52.4 0.0 copy-start.4
  52.5 19.3 %all_to_all.40.x_ref = bf16[8,64,1024]{2,1,0:T(8,128)(2,1)S(1)} all-to-all(bf16[8,64,1024]{2,1,0:T(8,128)(2,1)S(1)} %get-tuple-element.21), channel_id=1, replica_groups=mesh['yh'=2,'zh'=4,'zl'=4,'c'=2,'yl'=2,'x'=4] {'yl','x'}, dimensions={0} | all-to-all | bytes 2097152 | tf_op jit(solution)/shard_map/all_to_all | solution.py:23
  71.8 0.2 shard_map.127
  71.9 14.7 %all_to_all.41 = bf16[16,32,512]{2,1,0:T(8,128)(2,1)S(1)} all-to-all(bf16[16,32,512]{2,1,0:T(8,128)(2,1)S(1)} %bitcast.12), channel_id=1, replica_groups=mesh['yh'=2,'zh'=4,'zl'=4,'c'=2,'yl'=2,'x'=4] {'c','yl','x'}, dimensions={0} | all-to-all | bytes 1048576 | tf_op jit(solution)/shard_map/all_to_all | solution.py:23
  86.6 0.0 copy-done.4
  86.6 0.7 shard_map.128
  87.4 0.0 copy-start.15
  87.4 0.6 copy-done.15
  88.0 22.5 %all_to_all.42.x_ref = bf16[8,32,1024]{2,1,0:T(8,128)(2,1)S(1)} all-to-all(bf16[8,32,1024]{2,1,0:T(8,128)(2,1)S(1)} %bitcast.13), channel_id=1, replica_groups=mesh['yh'=2,'zh'=4,'zl'=4,'c'=2,'yl'=2,'x'=4] {'zl','yh'}, dimensions={0} | all-to-all | bytes 1048576 | tf_op jit(solution)/shard_map/all_to_all | solution.py:23
  110.5 0.1 shard_map.129
  110.6 19.7 %all_to_all.43.x_ref = bf16[4,32,1024]{2,1,0:T(8,128)(2,1)S(1)} all-to-all(bf16[4,32,1024]{2,1,0:T(8,128)(2,1)S(1)} %shard_map.129), channel_id=1, replica_groups=mesh['yh'=2,'zh'=4,'zl'=4,'c'=2,'yl'=2,'x'=4] {'zh'}, dimensions={0} | all-to-all | bytes 524288 | tf_op jit(solution)/shard_map/all_to_all | solution.py:23
  130.3 21.5 %all_to_all.44 = bf16[8,32,1024]{2,1,0:T(8,128)(2,1)S(1)} all-to-all(bf16[8,32,1024]{2,1,0:T(8,128)(2,1)S(1)} %shard_map.130), channel_id=1, replica_groups=mesh['yh'=2,'zh'=4,'zl'=4,'c'=2,'yl'=2,'x'=4] {'zl','yh'}, dimensions={0} | all-to-all | bytes 1048576 | tf_op jit(solution)/shard_map/all_to_all | solution.py:23
  151.8 0.5 shard_map.131
  152.3 0.0 copy-start
  152.3 0.0 copy-start.3
  152.3 13.9 %all_to_all.45 = bf16[16,32,256]{2,1,0:T(8,128)(2,1)S(1)} all-to-all(bf16[16,32,256]{2,1,0:T(8,128)(2,1)S(1)} %bitcast.14), channel_id=1, replica_groups=mesh['yh'=2,'zh'=4,'zl'=4,'c'=2,'yl'=2,'x'=4] {'c','yl','x'}, dimensions={0} | all-to-all | bytes 524288 | tf_op jit(solution)/shard_map/all_to_all | solution.py:23
  166.2 0.0 copy-done
  166.2 0.1 shard_map.132
  166.3 0.0 copy-start.6
  166.3 0.8 copy-done.6
  167.1 0.7 copy-done.14
  167.8 3.5 %all-to-all-start.7 = ((bf16[8,64,512]{2,1,0:T(8,128)(2,1)}), bf16[8,64,512]{2,1,0:T(8,128)(2,1)S(1)}, u32[]{:S(2)}, u32[]{:S(2)}) async-start(bf16[8,64,512]{2,1,0:T(8,128)(2,1)} %copy-done.6), calls=%async_computation.7 | async-start | bytes 1048576 | tf_op jit(solution)/shard_map/all_to_all | solution.py:23
  171.3 2.1 %collective-permute-start.4 = (bf16[256,512]{1,0:T(8,128)(2,1)}, bf16[256,512]{1,0:T(8,128)(2,1)S(1)}, u32[]{:S(2)}, u32[]{:S(2)}) collective-permute-start(bf16[256,512]{1,0:T(8,128)(2,1)} %copy-done.14), channel_id=1, source_target_pairs={{0,8},{8,0},{1,9},{9,1},{2,10},{10,2},{3,11},{11,3},{4,12},{12,4},... | collective-permute-start | bytes 786440 | tf_op jit(solution)/shard_map/ppermute | solution.py:19
  173.4 2.2 %collective-permute-start.5 = (bf16[256,512]{1,0:T(8,128)(2,1)S(1)}, bf16[256,512]{1,0:T(8,128)(2,1)S(1)}, u32[]{:S(2)}, u32[]{:S(2)}) collective-permute-start(bf16[256,512]{1,0:T(8,128)(2,1)S(1)} %get-tuple-element.32), channel_id=1, source_target_pairs={{0,8},{8,0},{1,9},{9,1},{2,10},{10,2},{3,11},{11,3},{4,12},{12,4},... | collective-permute-start | bytes 786440 | tf_op jit(solution)/shard_map/ppermute | solution.py:19
  175.6 2.1 %collective-permute-start.3 = (bf16[256,256]{1,0:T(8,128)(2,1)}, bf16[256,256]{1,0:T(8,128)(2,1)S(1)}, u32[]{:S(2)}, u32[]{:S(2)}) collective-permute-start(bf16[256,256]{1,0:T(8,128)(2,1)} %copy-done.15), channel_id=1, source_target_pairs={{0,8},{8,0},{1,9},{9,1},{2,10},{10,2},{3,11},{11,3},{4,12},{12,4},... | collective-permute-start | bytes 393224 | tf_op jit(solution)/shard_map/ppermute | solution.py:19
  177.8 1.3 collective-permute-done.3.hid2_ref
  179.1 0.0 collective-permute-done.4.late_ref
  179.1 0.0 collective-permute-done.5.late2_ref
  179.1 0.0 copy-done.3
  179.1 0.0 copy-start.1
  179.1 1.0 copy-done.1
  180.1 1.3 shard_map.133
  181.4 0.1 all-to-all-done.7.bars_ref
  181.5 1.2 copy-done.5
  182.7 1.5 shard_map.134
  (10 shorter events, 0.1 us)
Async XLA Ops:
  0.6 0.7 copy-start.12
  1.3 36.6 %copy-start.16 = (s32[8,2]{0,1:T(2,128)S(1)}, s32[8,2]{0,1:T(2,128)}, u32[]{:S(2)}) copy-start(s32[8,2]{0,1:T(2,128)} %param.14) | copy-start | bytes 196
  1.4 36.7 %copy-start.17 = (s32[8,2]{0,1:T(2,128)S(1)}, s32[8,2]{0,1:T(2,128)}, u32[]{:S(2)}) copy-start(s32[8,2]{0,1:T(2,128)} %param.15) | copy-start | bytes 196
  2.1 31.1 %all-to-all-start = ((bf16[16,8,1024]{2,1,0:T(8,128)(2,1)}), bf16[16,8,1024]{2,1,0:T(8,128)(2,1)S(1)}, u32[]{:S(2)}, u32[]{:S(2)}) async-start(bf16[16,8,1024]{2,1,0:T(8,128)(2,1)} %shard_map.121), calls=%async_computation | async-start | bytes 524288 | tf_op jit(solution)/shard_map/all_to_all | solution.py:23
  17.8 1.0 copy-start.2
  18.9 1.0 copy-start.7
  19.9 0.7 copy-start.13
  21.3 22.1 %collective-permute-start.1 = (bf16[512,1024]{1,0:T(8,128)(2,1)S(1)}, bf16[512,1024]{1,0:T(8,128)(2,1)}, u32[]{:S(2)}, u32[]{:S(2)}) collective-permute-start(bf16[512,1024]{1,0:T(8,128)(2,1)S(1)} %shard_map.123.down_ref), channel_id=1, source_target_pairs={{0,8},{8,0},{1,9},{9,1},{2,10},{10,2},{3,11},{11,3},{4,12},{12,4},... | collective-permute-start | bytes 3145736 | tf_op jit(solution)/shard_map/ppermute | solution.py:19
  33.2 10.2 %collective-permute-start = (bf16[128,1024]{1,0:T(8,128)(2,1)S(1)}, bf16[128,1024]{1,0:T(8,128)(2,1)}, u32[]{:S(2)}, u32[]{:S(2)}) collective-permute-start(bf16[128,1024]{1,0:T(8,128)(2,1)S(1)} %bitcast.9), channel_id=1, source_target_pairs={{0,256},{256,0},{1,257},{257,1},{2,258},{258,2},{3,259},{259,3},{4... | collective-permute-start | bytes 786440 | tf_op jit(solution)/shard_map/ppermute | solution.py:19
  38.2 1.0 copy-start.8
  39.2 1.0 copy-start.9
  40.2 1.0 copy-start.10
  41.3 1.0 copy-start.11
  44.4 6.8 %collective-permute-start.2 = (bf16[256,1024]{1,0:T(8,128)(2,1)S(1)}, bf16[256,1024]{1,0:T(8,128)(2,1)S(1)}, u32[]{:S(2)}, u32[]{:S(2)}) collective-permute-start(bf16[256,1024]{1,0:T(8,128)(2,1)S(1)} %shard_map.124.after_ref.own_ref), channel_id=1, source_target_pairs={{0,8},{8,0},{1,9},{9,1},{2,10},{10,2},{3,11},{11,3},{4,12},{12,4},... | collective-permute-start | bytes 1572872 | tf_op jit(solution)/shard_map/ppermute | solution.py:19
  52.4 34.2 %copy-start.4 = (bf16[1024,512]{1,0:T(8,128)(2,1)}, bf16[1024,512]{1,0:T(8,128)(2,1)S(1)}, u32[]{:S(2)}) copy-start(bf16[1024,512]{1,0:T(8,128)(2,1)S(1)} %get-tuple-element.20.tok_ref) | copy-start | bytes 3145732
  87.4 0.7 copy-start.15
  152.3 13.9 %copy-start = (bf16[256,1024]{1,0:T(8,128)(2,1)}, bf16[256,1024]{1,0:T(8,128)(2,1)S(1)}, u32[]{:S(2)}) copy-start(bf16[256,1024]{1,0:T(8,128)(2,1)S(1)} %get-tuple-element.27.out_ref) | copy-start | bytes 1572868
  152.3 26.8 %copy-start.3 = (bf16[256,1024]{1,0:T(8,128)(2,1)S(1)}, bf16[256,1024]{1,0:T(8,128)(2,1)}, u32[]{:S(2)}) copy-start(bf16[256,1024]{1,0:T(8,128)(2,1)} %probe_ref.3) | copy-start | bytes 1572868
  166.3 0.8 copy-start.6
  167.1 0.7 copy-start.14
  167.8 13.7 %all-to-all-start.7 = ((bf16[8,64,512]{2,1,0:T(8,128)(2,1)}), bf16[8,64,512]{2,1,0:T(8,128)(2,1)S(1)}, u32[]{:S(2)}, u32[]{:S(2)}) async-start(bf16[8,64,512]{2,1,0:T(8,128)(2,1)} %copy-done.6), calls=%async_computation.7 | async-start | bytes 1048576 | tf_op jit(solution)/shard_map/all_to_all | solution.py:23
  171.3 7.8 %collective-permute-start.4 = (bf16[256,512]{1,0:T(8,128)(2,1)}, bf16[256,512]{1,0:T(8,128)(2,1)S(1)}, u32[]{:S(2)}, u32[]{:S(2)}) collective-permute-start(bf16[256,512]{1,0:T(8,128)(2,1)} %copy-done.14), channel_id=1, source_target_pairs={{0,8},{8,0},{1,9},{9,1},{2,10},{10,2},{3,11},{11,3},{4,12},{12,4},... | collective-permute-start | bytes 786440 | tf_op jit(solution)/shard_map/ppermute | solution.py:19
  173.4 5.6 %collective-permute-start.5 = (bf16[256,512]{1,0:T(8,128)(2,1)S(1)}, bf16[256,512]{1,0:T(8,128)(2,1)S(1)}, u32[]{:S(2)}, u32[]{:S(2)}) collective-permute-start(bf16[256,512]{1,0:T(8,128)(2,1)S(1)} %get-tuple-element.32), channel_id=1, source_target_pairs={{0,8},{8,0},{1,9},{9,1},{2,10},{10,2},{3,11},{11,3},{4,12},{12,4},... | collective-permute-start | bytes 786440 | tf_op jit(solution)/shard_map/ppermute | solution.py:19
  175.6 3.5 %collective-permute-start.3 = (bf16[256,256]{1,0:T(8,128)(2,1)}, bf16[256,256]{1,0:T(8,128)(2,1)S(1)}, u32[]{:S(2)}, u32[]{:S(2)}) collective-permute-start(bf16[256,256]{1,0:T(8,128)(2,1)} %copy-done.15), channel_id=1, source_target_pairs={{0,8},{8,0},{1,9},{9,1},{2,10},{10,2},{3,11},{11,3},{4,12},{12,4},... | collective-permute-start | bytes 393224 | tf_op jit(solution)/shard_map/ppermute | solution.py:19
  179.1 1.0 copy-start.1
  181.5 1.2 copy-start.5

commit v14 on v13

--- a/solution.py
+++ b/solution.py
@@ -169,11 +169,15 @@
             )
 
 
-def bars_kernel(x_ref, up_slope_ref, act_ref, out_ref, o_ref, late_ref, late2_ref):
+def bars_kernel(
+    x_ref, up_slope_ref, act_ref, out_ref, hid2_ref, o_ref, late_ref, late2_ref, own_ref
+):
     width = act_ref.shape[1]
     half = late_ref.shape[1]
     late_ref[...] = out_ref[:, :half]
-    late2_ref[...] = out_ref[:, half:]
+    late2_ref[:, : half - width] = out_ref[:, half:]
+    late2_ref[:, half - width :] = hid2_ref[...]
+    own_ref[...] = out_ref[...]
     c = lax.axis_index("c")
     for r in range(2):
         place = c if r == 0 else 1 - c
@@ -188,15 +192,19 @@
             o_ref[i, rows, width:] = up_bar
 
 
-def fisher_down_kernel(
-    hid_ref, out_ref, hid2_ref, late_ref, late2_ref, probe_ref, o_ref, done_ref
-):
+def fisher_down_kernel(hid_ref, out_ref, late_ref, late2_ref, probe_ref, o_ref, done_ref):
+    width = hid_ref.shape[1]
+    half = late_ref.shape[1]
+    rest = half - width
     own = hid_ref[...].T
-    other = hid2_ref[...].T
-    for j in range(4):
-        cols = slice(j * 256, (j + 1) * 256)
-        part = slice(j % 2 * 256, (j % 2 + 1) * 256)
-        y = dot(own, out_ref[:, cols]) + dot(other, (late_ref, late2_ref)[j // 2][:, part])
+    other = late2_ref[:, rest:].T
+    for part_ref, start, count, column in (
+        (late_ref, 0, rest, 0),
+        (late_ref, rest, width, rest),
+        (late2_ref, 0, rest, half),
+    ):
+        cols = slice(column, column + count)
+        y = dot(own, out_ref[:, cols]) + dot(other, part_ref[:, start : start + count])
         o_ref[:, cols] = (probe_ref[:, cols].astype(F32) * y * TOKENS**-0.5).astype(BF16)
     done_ref[...] = late2_ref[:16, :128]
 
@@ -307,13 +315,20 @@
         back_kernel, [((2, 8, 32, width), BF16), ((256, feats), BF16)], chunk, down, down2
     )
     back = exchange(back.reshape(16, 32, width), NEAR).reshape(2, 8, 32, width)
-    bars, late, late2 = local(
+    half = (feats + width) // 2
+    bars, late, late2, out = local(
         bars_kernel,
-        [((8, 64, 2 * width), BF16), ((256, feats // 2), BF16), ((256, feats // 2), BF16)],
+        [
+            ((8, 64, 2 * width), BF16),
+            ((256, half), BF16),
+            ((256, half), BF16),
+            ((256, feats), BF16),
+        ],
         back,
         up_slope,
         act,
         out,
+        hid2,
     )
     bars = exchange(bars, TP)
     fisher_down, done = local(
@@ -321,7 +336,6 @@
         [(probe_down.shape, BF16), ((16, 128), BF16)],
         hid,
         out,
-        swap(hid2, "c"),
         swap(late, "c"),
         swap(late2, "c"),
         probe_down,

time: 185 us -> 186 us (level)
  starting transfers between devices: 38.7 us -> 36.5 us
  waiting for transfers between devices: 10.6 us -> 12.7 us
    ppermute x6 -> x5, starting transfers between devices: 19.5 us -> 17.3 us  [swap(): return lax.ppermute(x, axis, [(0, 1), (1, 0)])]
  transfers between devices with their start and end apart: 8 -> 7, of which waited for: 4 -> 4; matrix products, arithmetic and copies ran while one was open for 0% -> 0% of each run, Pallas kernels for 2% -> 2%
where the time goes in v14:
time: 186 us; the launch traced here: 185 us
  blocking collectives  112 us (60%)
  starting transfers between devices  36.5 us (20%)
  local copies, waits for them, and re-layouts  13.1 us (7%)
  waiting for transfers between devices  12.7 us (7%)
  Pallas kernels  10.4 us (6%)
    all_to_all x6, blocking collectives, exchange(): return lax.all_to_all(pieces, axes, 0, 0, tiled=True)  112 us
    all_to_all x2, starting transfers between devices, exchange(): return lax.all_to_all(pieces, axes, 0, 0, tiled=True)  19.2 us
    ppermute x5, starting transfers between devices, swap(): return lax.ppermute(x, axis, [(0, 1), (1, 0)])  17.3 us
    unnamed x38, local copies, waits for them, and re-layouts  13.1 us
    all_to_all x2, waiting for transfers between devices, exchange(): return lax.all_to_all(pieces, axes, 0, 0, tiled=True)  11 us
    pallas_call x13, Pallas kernels, local(): pl.pallas_call(kernel, out_shape=[jax.ShapeDtypeStruct(shape, dtype) for...  8.88 us
  transfers between devices with their start and end apart: 7, of which 4 were waited for; matrix products, arithmetic and copies ran while one was open for 0% of the time, Pallas kernels for 2%

profile of v14, /device:TPU:1, one launch (start us, length us, event | category | flops | bytes accessed | tf_op | source)
XLA Modules:
  0.0 185.1 jit_solution(7459266893299545762)
XLA Ops:
  0.6 0.0 copy-start.12
  0.6 0.7 copy-done.12
  1.3 0.0 copy-start.16
  1.4 0.0 copy-start.17
  1.4 0.7 shard_map.121
  2.1 15.7 %all-to-all-start = ((bf16[16,8,1024]{2,1,0:T(8,128)(2,1)}), bf16[16,8,1024]{2,1,0:T(8,128)(2,1)S(1)}, u32[]{:S(2)}, u32[]{:S(2)}) async-start(bf16[16,8,1024]{2,1,0:T(8,128)(2,1)} %shard_map.121), calls=%async_computation | async-start | bytes 524288 | tf_op jit(solution)/shard_map/all_to_all | solution.py:23
  17.8 0.0 copy-start
  17.8 1.0 copy-done
  18.9 0.0 copy-start.7
  18.9 1.0 copy-done.7
  19.9 0.0 copy-start.13
  19.9 0.7 copy-done.13
  20.6 0.7 shard_map.123.down_ref
  21.3 2.9 %collective-permute-start.1 = (bf16[512,1024]{1,0:T(8,128)(2,1)S(1)}, bf16[512,1024]{1,0:T(8,128)(2,1)}, u32[]{:S(2)}, u32[]{:S(2)}) collective-permute-start(bf16[512,1024]{1,0:T(8,128)(2,1)S(1)} %shard_map.123.down_ref), channel_id=1, source_target_pairs={{0,8},{8,0},{1,9},{9,1},{2,10},{10,2},{3,11},{11,3},{4,12},{12,4},... | collective-permute-start | bytes 3145736 | tf_op jit(solution)/shard_map/ppermute | solution.py:19
  24.2 9.0 %all-to-all-done = bf16[16,8,1024]{2,1,0:T(8,128)(2,1)S(1)} async-done(((bf16[16,8,1024]{2,1,0:T(8,128)(2,1)}), bf16[16,8,1024]{2,1,0:T(8,128)(2,1)S(1)}, u32[]{:S(2)}, u32[]{:S(2)}) %all-to-all-start) | async-done | bytes 262176 | tf_op jit(solution)/shard_map/all_to_all | solution.py:23
  33.2 4.8 %collective-permute-start = (bf16[128,1024]{1,0:T(8,128)(2,1)S(1)}, bf16[128,1024]{1,0:T(8,128)(2,1)}, u32[]{:S(2)}, u32[]{:S(2)}) collective-permute-start(bf16[128,1024]{1,0:T(8,128)(2,1)S(1)} %bitcast.9), channel_id=1, source_target_pairs={{0,256},{256,0},{1,257},{257,1},{2,258},{258,2},{3,259},{259,3},{4... | collective-permute-start | bytes 786440 | tf_op jit(solution)/shard_map/ppermute | solution.py:19
  38.0 0.0 copy-done.16
  38.0 0.1 copy.13.gmask_ref
  38.1 0.0 copy-done.17
  38.1 0.1 copy.14.umask_ref
  38.2 0.0 copy-start.8
  38.2 1.0 copy-done.8
  39.2 0.0 copy-start.9
  39.2 1.0 copy-done.9
  40.2 1.0 copy-done.10
  41.3 1.0 copy-done.11
  42.3 1.0 shard_map.122.after_ref.w_ref.probe_ref
  43.4 0.0 collective-permute-done.1.after2_ref.x_ref
  43.4 0.0 collective-permute-done.b_ref
  43.4 1.0 shard_map.124.after_ref.own_ref
  44.4 5.3 %collective-permute-start.2 = (bf16[256,1024]{1,0:T(8,128)(2,1)S(1)}, bf16[256,1024]{1,0:T(8,128)(2,1)S(1)}, u32[]{:S(2)}, u32[]{:S(2)}) collective-permute-start(bf16[256,1024]{1,0:T(8,128)(2,1)S(1)} %shard_map.124.after_ref.own_ref), channel_id=1, source_target_pairs={{0,8},{8,0},{1,9},{9,1},{2,10},{10,2},{3,11},{11,3},{4,12},{12,4},... | collective-permute-start | bytes 1572872 | tf_op jit(solution)/shard_map/ppermute | solution.py:19
  49.7 1.3 shard_map.125.after_ref.down2_ref
  51.0 0.2 collective-permute-done.2.other_ref
  51.2 1.2 shard_map.126
  52.4 0.0 copy-start.2
  52.5 19.3 %all_to_all.40.x_ref = bf16[8,64,1024]{2,1,0:T(8,128)(2,1)S(1)} all-to-all(bf16[8,64,1024]{2,1,0:T(8,128)(2,1)S(1)} %get-tuple-element.22), channel_id=1, replica_groups=mesh['yh'=2,'zh'=4,'zl'=4,'c'=2,'yl'=2,'x'=4] {'yl','x'}, dimensions={0} | all-to-all | bytes 2097152 | tf_op jit(solution)/shard_map/all_to_all | solution.py:23
  71.8 0.2 shard_map.127
  71.9 14.7 %all_to_all.41 = bf16[16,32,512]{2,1,0:T(8,128)(2,1)S(1)} all-to-all(bf16[16,32,512]{2,1,0:T(8,128)(2,1)S(1)} %bitcast.12), channel_id=1, replica_groups=mesh['yh'=2,'zh'=4,'zl'=4,'c'=2,'yl'=2,'x'=4] {'c','yl','x'}, dimensions={0} | all-to-all | bytes 1048576 | tf_op jit(solution)/shard_map/all_to_all | solution.py:23
  86.6 0.0 copy-done.2
  86.6 0.7 shard_map.128
  87.4 22.5 %all_to_all.42.x_ref = bf16[8,32,1024]{2,1,0:T(8,128)(2,1)S(1)} all-to-all(bf16[8,32,1024]{2,1,0:T(8,128)(2,1)S(1)} %bitcast.13), channel_id=1, replica_groups=mesh['yh'=2,'zh'=4,'zl'=4,'c'=2,'yl'=2,'x'=4] {'zl','yh'}, dimensions={0} | all-to-all | bytes 1048576 | tf_op jit(solution)/shard_map/all_to_all | solution.py:23
  109.9 0.1 shard_map.129
  109.9 19.7 %all_to_all.43.x_ref = bf16[4,32,1024]{2,1,0:T(8,128)(2,1)S(1)} all-to-all(bf16[4,32,1024]{2,1,0:T(8,128)(2,1)S(1)} %shard_map.129), channel_id=1, replica_groups=mesh['yh'=2,'zh'=4,'zl'=4,'c'=2,'yl'=2,'x'=4] {'zh'}, dimensions={0} | all-to-all | bytes 524288 | tf_op jit(solution)/shard_map/all_to_all | solution.py:23
  129.7 21.5 %all_to_all.44 = bf16[8,32,1024]{2,1,0:T(8,128)(2,1)S(1)} all-to-all(bf16[8,32,1024]{2,1,0:T(8,128)(2,1)S(1)} %shard_map.130), channel_id=1, replica_groups=mesh['yh'=2,'zh'=4,'zl'=4,'c'=2,'yl'=2,'x'=4] {'zl','yh'}, dimensions={0} | all-to-all | bytes 1048576 | tf_op jit(solution)/shard_map/all_to_all | solution.py:23
  151.2 0.5 shard_map.131
  151.7 0.0 copy-start.1
  151.7 13.9 %all_to_all.45 = bf16[16,32,256]{2,1,0:T(8,128)(2,1)S(1)} all-to-all(bf16[16,32,256]{2,1,0:T(8,128)(2,1)S(1)} %bitcast.14), channel_id=1, replica_groups=mesh['yh'=2,'zh'=4,'zl'=4,'c'=2,'yl'=2,'x'=4] {'c','yl','x'}, dimensions={0} | all-to-all | bytes 524288 | tf_op jit(solution)/shard_map/all_to_all | solution.py:23
  165.5 0.1 shard_map.132
  165.7 0.0 copy-start.4
  165.7 0.8 copy-done.4
  166.5 0.8 copy-done.6
  167.3 0.7 copy-done.14
  168.0 0.7 copy-done.15
  168.7 3.5 %all-to-all-start.7 = ((bf16[8,64,512]{2,1,0:T(8,128)(2,1)}), bf16[8,64,512]{2,1,0:T(8,128)(2,1)S(1)}, u32[]{:S(2)}, u32[]{:S(2)}) async-start(bf16[8,64,512]{2,1,0:T(8,128)(2,1)} %copy-done.6), calls=%async_computation.7 | async-start | bytes 1048576 | tf_op jit(solution)/shard_map/all_to_all | solution.py:23
  172.2 2.1 %collective-permute-start.3 = (bf16[256,640]{1,0:T(8,128)(2,1)}, bf16[256,640]{1,0:T(8,128)(2,1)S(1)}, u32[]{:S(2)}, u32[]{:S(2)}) collective-permute-start(bf16[256,640]{1,0:T(8,128)(2,1)} %copy-done.15), channel_id=1, source_target_pairs={{0,8},{8,0},{1,9},{9,1},{2,10},{10,2},{3,11},{11,3},{4,12},{12,4},... | collective-permute-start | bytes 983048 | tf_op jit(solution)/shard_map/ppermute | solution.py:19
  174.4 2.2 %collective-permute-start.4 = (bf16[256,640]{1,0:T(8,128)(2,1)}, bf16[256,640]{1,0:T(8,128)(2,1)S(1)}, u32[]{:S(2)}, u32[]{:S(2)}) collective-permute-start(bf16[256,640]{1,0:T(8,128)(2,1)} %copy-done.14), channel_id=1, source_target_pairs={{0,8},{8,0},{1,9},{9,1},{2,10},{10,2},{3,11},{11,3},{4,12},{12,4},... | collective-permute-start | bytes 983048 | tf_op jit(solution)/shard_map/ppermute | solution.py:19
  176.5 0.0 collective-permute-done.3.late_ref
  176.6 1.5 collective-permute-done.4.late2_ref
  178.1 0.0 copy-done.1
  178.1 1.0 copy-done.5
  179.1 1.3 shard_map.133
  180.5 2.0 %all-to-all-done.7.bars_ref = bf16[8,64,512]{2,1,0:T(8,128)(2,1)S(1)} async-done(((bf16[8,64,512]{2,1,0:T(8,128)(2,1)}), bf16[8,64,512]{2,1,0:T(8,128)(2,1)S(1)}, u32[]{:S(2)}, u32[]{:S(2)}) %all-to-all-start.7) | async-done | bytes 524320 | tf_op jit(solution)/shard_map/all_to_all | solution.py:23
  182.4 1.2 copy-done.3
  183.7 1.5 shard_map.134
  (8 shorter events, 0.1 us)
Async XLA Ops:
  0.6 0.7 copy-start.12
  1.3 36.6 %copy-start.16 = (s32[8,2]{0,1:T(2,128)S(1)}, s32[8,2]{0,1:T(2,128)}, u32[]{:S(2)}) copy-start(s32[8,2]{0,1:T(2,128)} %param.14) | copy-start | bytes 196
  1.4 36.7 %copy-start.17 = (s32[8,2]{0,1:T(2,128)S(1)}, s32[8,2]{0,1:T(2,128)}, u32[]{:S(2)}) copy-start(s32[8,2]{0,1:T(2,128)} %param.15) | copy-start | bytes 196
  2.1 31.1 %all-to-all-start = ((bf16[16,8,1024]{2,1,0:T(8,128)(2,1)}), bf16[16,8,1024]{2,1,0:T(8,128)(2,1)S(1)}, u32[]{:S(2)}, u32[]{:S(2)}) async-start(bf16[16,8,1024]{2,1,0:T(8,128)(2,1)} %shard_map.121), calls=%async_computation | async-start | bytes 524288 | tf_op jit(solution)/shard_map/all_to_all | solution.py:23
  17.8 1.0 copy-start
  18.9 1.0 copy-start.7
  19.9 0.7 copy-start.13
  21.3 22.1 %collective-permute-start.1 = (bf16[512,1024]{1,0:T(8,128)(2,1)S(1)}, bf16[512,1024]{1,0:T(8,128)(2,1)}, u32[]{:S(2)}, u32[]{:S(2)}) collective-permute-start(bf16[512,1024]{1,0:T(8,128)(2,1)S(1)} %shard_map.123.down_ref), channel_id=1, source_target_pairs={{0,8},{8,0},{1,9},{9,1},{2,10},{10,2},{3,11},{11,3},{4,12},{12,4},... | collective-permute-start | bytes 3145736 | tf_op jit(solution)/shard_map/ppermute | solution.py:19
  33.2 10.2 %collective-permute-start = (bf16[128,1024]{1,0:T(8,128)(2,1)S(1)}, bf16[128,1024]{1,0:T(8,128)(2,1)}, u32[]{:S(2)}, u32[]{:S(2)}) collective-permute-start(bf16[128,1024]{1,0:T(8,128)(2,1)S(1)} %bitcast.9), channel_id=1, source_target_pairs={{0,256},{256,0},{1,257},{257,1},{2,258},{258,2},{3,259},{259,3},{4... | collective-permute-start | bytes 786440 | tf_op jit(solution)/shard_map/ppermute | solution.py:19
  38.2 1.0 copy-start.8
  39.2 1.0 copy-start.9
  40.2 1.0 copy-start.10
  41.3 1.0 copy-start.11
  44.4 6.8 %collective-permute-start.2 = (bf16[256,1024]{1,0:T(8,128)(2,1)S(1)}, bf16[256,1024]{1,0:T(8,128)(2,1)S(1)}, u32[]{:S(2)}, u32[]{:S(2)}) collective-permute-start(bf16[256,1024]{1,0:T(8,128)(2,1)S(1)} %shard_map.124.after_ref.own_ref), channel_id=1, source_target_pairs={{0,8},{8,0},{1,9},{9,1},{2,10},{10,2},{3,11},{11,3},{4,12},{12,4},... | collective-permute-start | bytes 1572872 | tf_op jit(solution)/shard_map/ppermute | solution.py:19
  52.4 34.2 %copy-start.2 = (bf16[1024,512]{1,0:T(8,128)(2,1)}, bf16[1024,512]{1,0:T(8,128)(2,1)S(1)}, u32[]{:S(2)}) copy-start(bf16[1024,512]{1,0:T(8,128)(2,1)S(1)} %get-tuple-element.21.tok_ref) | copy-start | bytes 3145732
  151.7 26.4 %copy-start.1 = (bf16[256,1024]{1,0:T(8,128)(2,1)S(1)}, bf16[256,1024]{1,0:T(8,128)(2,1)}, u32[]{:S(2)}) copy-start(bf16[256,1024]{1,0:T(8,128)(2,1)} %probe_ref.3) | copy-start | bytes 1572868
  165.7 0.8 copy-start.4
  166.5 0.8 copy-start.6
  167.3 0.7 copy-start.14
  168.0 0.7 copy-start.15
  168.7 13.7 %all-to-all-start.7 = ((bf16[8,64,512]{2,1,0:T(8,128)(2,1)}), bf16[8,64,512]{2,1,0:T(8,128)(2,1)S(1)}, u32[]{:S(2)}, u32[]{:S(2)}) async-start(bf16[8,64,512]{2,1,0:T(8,128)(2,1)} %copy-done.6), calls=%async_computation.7 | async-start | bytes 1048576 | tf_op jit(solution)/shard_map/all_to_all | solution.py:23
  172.2 4.3 %collective-permute-start.3 = (bf16[256,640]{1,0:T(8,128)(2,1)}, bf16[256,640]{1,0:T(8,128)(2,1)S(1)}, u32[]{:S(2)}, u32[]{:S(2)}) collective-permute-start(bf16[256,640]{1,0:T(8,128)(2,1)} %copy-done.15), channel_id=1, source_target_pairs={{0,8},{8,0},{1,9},{9,1},{2,10},{10,2},{3,11},{11,3},{4,12},{12,4},... | collective-permute-start | bytes 983048 | tf_op jit(solution)/shard_map/ppermute | solution.py:19
  174.4 3.7 %collective-permute-start.4 = (bf16[256,640]{1,0:T(8,128)(2,1)}, bf16[256,640]{1,0:T(8,128)(2,1)S(1)}, u32[]{:S(2)}, u32[]{:S(2)}) collective-permute-start(bf16[256,640]{1,0:T(8,128)(2,1)} %copy-done.14), channel_id=1, source_target_pairs={{0,8},{8,0},{1,9},{9,1},{2,10},{10,2},{3,11},{11,3},{4,12},{12,4},... | collective-permute-start | bytes 983048 | tf_op jit(solution)/shard_map/ppermute | solution.py:19
  178.1 1.0 copy-start.5
  182.4 1.2 copy-start.3
